TPU v7x, 32 devices: a whole 2x2x4 slice. The times are simulated.
32 devices in a mesh: dp: 8 (over z, x), seq: 4 (over y, core).
Axes of the slice: x: 2, y: 2, z: 4, core: 2. Of those that a mesh axis runs over, the one named last changes fastest.
Arguments:
- tokens: bfloat16 [16, 1024, 1152], P('dp', 'seq'), may hold values from -6 to 6
- conditioning: float32 [16, 1152], P('dp'), may hold values from -6 to 6
- w_mod: bfloat16 [1152, 6912], P('dp'), may hold values from -0.1875 to 0.1875
- b_mod: bfloat16 [6912], P('dp'), may hold values from -3 to 3
- w_qkv: bfloat16 [1152, 3456], P('dp'), may hold values from -0.1875 to 0.1875
- w_proj: bfloat16 [1152, 1152], P('dp'), may hold values from -1 to 1
- w_fc1: bfloat16 [1152, 4608], P('dp'), may hold values from -0.1875 to 0.1875
- b_fc1: bfloat16 [4608], P('dp'), may hold values from -3 to 3
- w_fc2: bfloat16 [4608, 1152], P('dp'), may hold values from -0.09375 to 0.09375
- cotangent: bfloat16 [16, 1024, 1152], P('dp', 'seq'), may hold values from -6 to 6
Outputs:
- output: bfloat16 [16, 1024, 1152], P('dp', 'seq')
- grad_tokens: float32 [16, 1024, 1152], P('dp', 'seq')
- grad_cond: float32 [16, 1152], P('dp')
- grad_w_mod: float32 [1152, 6912], P(None, ('dp', 'seq'))
- grad_b_mod: float32 [6912], P(('dp', 'seq'))
- grad_w_qkv: float32 [1152, 3456], P('dp', 'seq')
- grad_w_proj: float32 [1152, 1152], P('dp', 'seq')
- grad_w_fc1: float32 [1152, 4608], P('dp', 'seq')
- grad_b_fc1: float32 [4608], P(('dp', 'seq'))
- grad_w_fc2: float32 [4608, 1152], P('dp', 'seq')
All inputs are finite; a program needn't handle non-finite values.
Results may differ from a plain program's by a relative error of at most 0.02.
The roundings to bfloat16 on the way count: a program that leaves them out, or rounds other values in their place, can miss the bound.
Values may be sent and summed in bfloat16 or wider, within the bound.
No kernel may reach another device: no remote copies, remote signals or barrier semaphores. Data moves between devices by JAX's collectives and lax.ppermute only.
A program may use at most 256 MiB of HBM per device.

v0:
```python
from functools import partial

import jax
import jax.numpy as jnp
from jax import lax
from jax.sharding import PartitionSpec as P

HEADS = 16
HEAD_DIM = 72


def layer_norm(values):
    row_mean = jnp.mean(values, axis=-1, keepdims=True)
    centred = values - row_mean
    row_var = jnp.mean(centred * centred, axis=-1, keepdims=True)
    return centred * lax.rsqrt(row_var + 1e-06)


def modulate(values, shift_rows, scale_rows):
    return layer_norm(values) * (1.0 + scale_rows[:, None]) + shift_rows[:, None]


def project(left, right):
    return jnp.einsum("btd,dn->btn", left, right, preferred_element_type=jnp.float32)


def project_back(left, right):
    return jnp.einsum("btn,dn->btd", left, right, preferred_element_type=jnp.float32)


def outer_sum(left, right):
    return jnp.einsum("btd,btn->dn", left, right, preferred_element_type=jnp.float32)


def attend_forward(packed):
    inv_root = HEAD_DIM ** (-0.5)
    queries = packed[:, 0]
    key_rows = packed[:, 1]
    values = packed[:, 2]
    scores = (
        jnp.einsum("qhd,khd->hqk", queries, key_rows, preferred_element_type=jnp.float32) * inv_root
    )
    row_max = jnp.max(scores, axis=-1, keepdims=True)
    exponent = jnp.exp(scores - row_max)
    row_sum = jnp.sum(exponent, axis=-1, keepdims=True)
    weights = (exponent / row_sum).astype(jnp.bfloat16)
    mixed = jnp.einsum("hqk,khd->qhd", weights, values, preferred_element_type=jnp.float32)
    seq_len = mixed.shape[0]
    heads_here = mixed.shape[1]
    mixed = mixed.reshape(seq_len, 1, heads_here * HEAD_DIM).astype(jnp.bfloat16)
    return (mixed, (row_max + jnp.log(row_sum))[..., 0])


def attend_backward(group):
    packed, log_sum, d_mixed = group
    inv_root = HEAD_DIM ** (-0.5)
    queries = packed[:, 0]
    key_rows = packed[:, 1]
    values = packed[:, 2]
    scores = (
        jnp.einsum("qhd,khd->hqk", queries, key_rows, preferred_element_type=jnp.float32) * inv_root
    )
    weights = jnp.exp(scores - log_sum[..., None])
    d_values = jnp.einsum(
        "hqk,qhd->khd", weights.astype(jnp.bfloat16), d_mixed, preferred_element_type=jnp.float32
    )
    d_weights = jnp.einsum("qhd,khd->hqk", d_mixed, values, preferred_element_type=jnp.float32)
    row_inner = jnp.sum(weights * d_weights, axis=-1, keepdims=True)
    d_scores = (weights * (d_weights - row_inner)).astype(jnp.bfloat16)
    d_queries = (
        jnp.einsum("hqk,khd->qhd", d_scores, key_rows, preferred_element_type=jnp.float32)
        * inv_root
    )
    d_keys = (
        jnp.einsum("hqk,qhd->khd", d_scores, queries, preferred_element_type=jnp.float32) * inv_root
    )
    stacked = jnp.stack([d_queries, d_keys, d_values], axis=1)
    seq_len = stacked.shape[0]
    heads_here = stacked.shape[2]
    return stacked.reshape(seq_len, 3, 1, heads_here * HEAD_DIM).astype(jnp.bfloat16)


def own_columns(array_in, seq_index, dp_count, seq_count):
    rows = array_in.shape[0]
    piece = array_in.shape[1] // (dp_count * seq_count)
    split = array_in.reshape(rows, dp_count, seq_count, piece)
    chosen = lax.dynamic_index_in_dim(split, seq_index, axis=2, keepdims=False)
    return chosen.reshape(rows, dp_count * piece)


def on_device(tokens, conditioning, w_mod, b_mod, w_qkv, w_proj, w_fc1, b_fc1, w_fc2, cotangent):
    batch_here, tok_here, width = tokens.shape
    seq_count = lax.axis_size("seq")
    dp_count = lax.axis_size("dp")
    seq_index = lax.axis_index("seq")
    heads_here = HEADS // seq_count
    head_cols = heads_here * HEAD_DIM
    seq_len = tok_here * seq_count
    qkv_full, proj_full, fc1_full, fc1_bias, fc2_full = (
        lax.all_gather(w_qkv, "dp", axis=0, tiled=True),
        lax.all_gather(w_proj, "dp", axis=0, tiled=True),
        lax.all_gather(w_fc1, "dp", axis=0, tiled=True),
        lax.all_gather(b_fc1, "dp", axis=0, tiled=True),
        lax.all_gather(w_fc2, "dp", axis=0, tiled=True),
    )
    cond_silu, silu_back = jax.vjp(jax.nn.silu, conditioning)
    cond_act = cond_silu.astype(jnp.bfloat16)
    mod_full, mod_bias = (
        lax.all_gather(w_mod, "dp", axis=0, tiled=True),
        lax.all_gather(b_mod, "dp", axis=0, tiled=True),
    )
    modulation = jnp.dot(cond_act, mod_full, preferred_element_type=jnp.float32) + mod_bias.astype(
        jnp.float32
    )
    shift_attn = modulation[:, 0:width]
    scale_attn = modulation[:, width : 2 * width]
    gate_attn = modulation[:, 2 * width : 3 * width]
    shift_mlp = modulation[:, 3 * width : 4 * width]
    scale_mlp = modulation[:, 4 * width : 5 * width]
    gate_mlp = modulation[:, 5 * width : 6 * width]
    token_values = tokens.astype(jnp.float32)
    normed_first, attn_back = jax.vjp(modulate, token_values, shift_attn, scale_attn)
    normed_attn = normed_first.astype(jnp.bfloat16)
    packed = (
        project(normed_attn, qkv_full)
        .astype(jnp.bfloat16)
        .reshape(batch_here, tok_here, 3, seq_count, head_cols)
    )
    grouped = lax.all_to_all(packed, "seq", split_axis=3, concat_axis=1, tiled=True).reshape(
        batch_here, seq_len, 3, heads_here, HEAD_DIM
    )
    mixed, log_sums = lax.map(attend_forward, grouped)
    attended = lax.all_to_all(mixed, "seq", split_axis=1, concat_axis=2, tiled=True).reshape(
        batch_here, tok_here, width
    )
    attn_out = project(attended, proj_full)
    resid_mid = token_values + gate_attn[:, None] * attn_out
    normed_second, mlp_back = jax.vjp(modulate, resid_mid, shift_mlp, scale_mlp)
    normed_mlp = normed_second.astype(jnp.bfloat16)
    hidden = project(normed_mlp, fc1_full) + fc1_bias.astype(jnp.float32)
    gelu_out, gelu_back = jax.vjp(partial(jax.nn.gelu, approximate=True), hidden)
    activated = gelu_out.astype(jnp.bfloat16)
    mlp_out = project(activated, fc2_full)
    output = (resid_mid + gate_mlp[:, None] * mlp_out).astype(jnp.bfloat16)
    upstream = cotangent.astype(jnp.float32)
    d_gate_mlp = jnp.sum(upstream * mlp_out, axis=1)
    d_mlp = (gate_mlp[:, None] * upstream).astype(jnp.bfloat16)
    grad_fc2 = outer_sum(activated, d_mlp)
    (d_gelu,) = gelu_back(project_back(d_mlp, fc2_full))
    d_hidden = d_gelu.astype(jnp.bfloat16)
    grad_fc1 = outer_sum(normed_mlp, d_hidden)
    grad_bias1 = jnp.sum(d_hidden.astype(jnp.float32), axis=(0, 1))
    d_resid_norm, d_shift_mlp, d_scale_mlp = mlp_back(project_back(d_hidden, fc1_full))
    d_resid = upstream + d_resid_norm
    d_gate_attn = jnp.sum(d_resid * attn_out, axis=1)
    d_attn = (gate_attn[:, None] * d_resid).astype(jnp.bfloat16)
    grad_proj = outer_sum(attended, d_attn)
    d_attended = (
        project_back(d_attn, proj_full)
        .astype(jnp.bfloat16)
        .reshape(batch_here, tok_here, seq_count, head_cols)
    )
    d_grouped = lax.all_to_all(d_attended, "seq", split_axis=2, concat_axis=1, tiled=True).reshape(
        batch_here, seq_len, heads_here, HEAD_DIM
    )
    d_packed = lax.map(attend_backward, (grouped, log_sums, d_grouped))
    d_qkv = lax.all_to_all(d_packed, "seq", split_axis=1, concat_axis=3, tiled=True).reshape(
        batch_here, tok_here, 3 * width
    )
    grad_qkv = outer_sum(normed_attn, d_qkv)
    d_tokens_norm, d_shift_attn, d_scale_attn = attn_back(project_back(d_qkv, qkv_full))
    grad_tokens = d_resid + d_tokens_norm
    d_mod_part = jnp.concatenate(
        [d_shift_attn, d_scale_attn, d_gate_attn, d_shift_mlp, d_scale_mlp, d_gate_mlp], axis=1
    )
    d_mod = lax.psum(d_mod_part.astype(jnp.bfloat16), "seq")
    grad_wmod_all = jnp.einsum("ld,ln->dn", cond_act, d_mod, preferred_element_type=jnp.float32)
    grad_bmod_all = jnp.sum(d_mod.astype(jnp.float32), axis=0)[None]
    grad_wmod, grad_bmod = (
        lax.psum_scatter(
            own_columns(grad_wmod_all, seq_index, dp_count, seq_count).astype(jnp.bfloat16),
            "dp",
            scatter_dimension=1,
            tiled=True,
        ).astype(jnp.float32),
        lax.psum_scatter(
            own_columns(grad_bmod_all, seq_index, dp_count, seq_count).astype(jnp.bfloat16),
            "dp",
            scatter_dimension=1,
            tiled=True,
        ).astype(jnp.float32),
    )
    d_cond = jnp.einsum("ln,dn->ld", d_mod, mod_full, preferred_element_type=jnp.float32)
    (grad_cond,) = silu_back(d_cond)
    rows_qkv, rows_proj, rows_fc1, rows_bias1, rows_fc2 = (
        lax.psum_scatter(
            grad_qkv.astype(jnp.bfloat16), "dp", scatter_dimension=0, tiled=True
        ).astype(jnp.float32),
        lax.psum_scatter(
            grad_proj.astype(jnp.bfloat16), "dp", scatter_dimension=0, tiled=True
        ).astype(jnp.float32),
        lax.psum_scatter(
            grad_fc1.astype(jnp.bfloat16), "dp", scatter_dimension=0, tiled=True
        ).astype(jnp.float32),
        lax.psum_scatter(
            grad_bias1.astype(jnp.bfloat16), "dp", scatter_dimension=0, tiled=True
        ).astype(jnp.float32),
        lax.psum_scatter(
            grad_fc2.astype(jnp.bfloat16), "dp", scatter_dimension=0, tiled=True
        ).astype(jnp.float32),
    )
    part_qkv, part_proj, part_fc1, part_bias1, part_fc2 = (
        lax.psum_scatter(
            rows_qkv.astype(jnp.bfloat16), "seq", scatter_dimension=1, tiled=True
        ).astype(jnp.float32),
        lax.psum_scatter(
            rows_proj.astype(jnp.bfloat16), "seq", scatter_dimension=1, tiled=True
        ).astype(jnp.float32),
        lax.psum_scatter(
            rows_fc1.astype(jnp.bfloat16), "seq", scatter_dimension=1, tiled=True
        ).astype(jnp.float32),
        lax.psum_scatter(
            rows_bias1[None].astype(jnp.bfloat16), "seq", scatter_dimension=1, tiled=True
        ).astype(jnp.float32),
        lax.psum_scatter(
            rows_fc2.astype(jnp.bfloat16), "seq", scatter_dimension=1, tiled=True
        ).astype(jnp.float32),
    )
    bias_out = part_bias1[0]
    return (
        output,
        grad_tokens,
        grad_cond,
        grad_wmod,
        grad_bmod[0],
        part_qkv,
        part_proj,
        part_fc1,
        bias_out,
        part_fc2,
    )


def solution(mesh):
    placed = (
        P("dp", "seq", None),
        P("dp", None),
        P("dp", None),
        P("dp"),
        P("dp", None),
        P("dp", None),
        P("dp", None),
        P("dp"),
        P("dp", None),
        P("dp", "seq", None),
    )
    return jax.shard_map(
        on_device,
        mesh=mesh,
        in_specs=placed,
        out_specs=(
            P("dp", "seq", None),
            P("dp", "seq", None),
            P("dp", None),
            P(None, ("dp", "seq")),
            P(("dp", "seq")),
            P("dp", "seq"),
            P("dp", "seq"),
            P("dp", "seq"),
            P(("dp", "seq")),
            P("dp", "seq"),
        ),
        check_vma=False,
    )
```

profile of v0, /device:TPU:0, one launch (start us, length us, event | category | flops | bytes accessed | tf_op | source)
XLA Modules:
  0.0 1710.5 jit_solution(11704754140268656972)
XLA Ops:
  13.0 40.6 %all-reduce.6 = (bf16[6912]{0:T(1024)(128)(2,1)S(1)}, bf16[4608]{0:T(1024)(128)(2,1)}) all-reduce(bf16[6912]{0:T(1024)(128)(2,1)S(1)} %dynamic-update-slice, bf16[4608]{0:T(1024)(128)(2,1)S(1)} %dynamic-update-slice.1), channel_id=1, replica_groups=mesh['dp'=8,'seq'=4] {'dp'}, use_global_device_ids=true, to_apply=%add | all-reduce | flops 11520 | bytes 46080
  54.9 175.6 %all-gather.6.cloned.1.call-done = bf16[1152,6912]{1,0:T(8,128)(2,1)} async-done(((bf16[144,6912]{1,0:T(8,128)(2,1)}), bf16[1152,6912]{1,0:T(8,128)(2,1)}) %all-gather.6.cloned.1.call-update) | async-done | bytes 15925264 | tf_op jit(solution)/shard_map/all_gather | solution.py:109
  230.4 7.7 convolution_add_fusion
  238.8 111.7 %all-gather.8.cloned.1.call-done = bf16[1152,3456]{1,0:T(8,128)(2,1)} async-done(((bf16[144,3456]{1,0:T(8,128)(2,1)}), bf16[1152,3456]{1,0:T(8,128)(2,1)}) %all-gather.8.cloned.1.call-update) | async-done | bytes 7962640 | tf_op jit(solution)/shard_map/all_gather | solution.py:100
  350.4 10.0 fusion.47
  360.4 4.4 copy.118
  366.9 4.0 all-to-all-start
  371.0 41.1 %all-to-all-done = bf16[2,256,3,4,288]{1,4,2,0,3:T(8,128)(2,1)S(1)} async-done(((bf16[2,256,3,4,288]{1,4,2,0,3:T(8,128)(2,1)}), bf16[2,256,3,4,288]{1,4,2,0,3:T(8,128)(2,1)S(1)}, u32[]{:S(2)}, u32[]{:S(2)}) %all-to-all-start) | async-done | bytes 3538976 | tf_op jit(solution)/shard_map/all_to_all | solution.py:129
  412.0 4.6 copy.120
  416.6 6.2 reshape.239
  422.8 53.5 %while.22 = (s32[]{:T(128)}, bf16[2,1024,1,288]{1,3,2,0:T(8,128)(2,1)}, f32[2,4,1024]{2,1,0:T(4,128)}, bf16[2,1024,3,4,72]{1,4,3,2,0:T(8,128)(2,1)S(1)}, s32[]{:T(128)}) while((s32[]{:T(128)}, bf16[2,1024,1,288]{1,3,2,0:T(8,128)(2,1)}, f32[2,4,1024]{2,1,0:T(4,128)}, bf16[2,1024,3,4,72]{1,4,3,2,0:T(8,128)(2,1)S(1)}, s32[]{:T(128)}) %tuple.68), condition=%wide.region_5.6_spmd, body=%wide.region_2.5_spmd.sunk | while | flops 1245999104 | bytes 57541696 | solution.py:132
  423.0 8.2 multiply_reduce_fusion.8
  431.2 8.6 fusion.105
  440.4 7.7 fusion.106
  449.1 8.2 multiply_reduce_fusion.8
  457.3 8.5 fusion.105
  466.5 9.0 fusion.106
  476.4 4.8 copy.121
  481.1 4.9 all-to-all-start.1
  486.7 19.5 %all-to-all-done.1 = bf16[2,1024,1,288]{3,0,2,1:T(2,128)(2,1)} async-done(((bf16[2,1024,1,288]{3,0,2,1:T(2,128)(2,1)}), bf16[2,1024,1,288]{3,0,2,1:T(2,128)(2,1)}, u32[]{:S(2)}, u32[]{:S(2)}) %all-to-all-start.1) | async-done | bytes 1179680 | tf_op jit(solution)/shard_map/all_to_all | solution.py:133
  506.2 5.1 copy.149
  513.7 5.9 fusion.77
  522.0 37.0 %all-gather.12.cloned.1.call-done = bf16[1152,4608]{1,0:T(8,128)(2,1)} async-done(((bf16[144,4608]{1,0:T(8,128)(2,1)}), bf16[1152,4608]{1,0:T(8,128)(2,1)}) %all-gather.12.cloned.1.call-update) | async-done | bytes 10616848 | tf_op jit(solution)/shard_map/all_gather | solution.py:102
  558.9 12.3 fusion.31
  571.3 140.4 %all-gather.14.cloned.1.call-done = bf16[4608,1152]{1,0:T(8,128)(2,1)} async-done(((bf16[576,1152]{1,0:T(8,128)(2,1)}), bf16[4608,1152]{1,0:T(8,128)(2,1)}) %all-gather.14.cloned.1.call-update) | async-done | bytes 10616848 | tf_op jit(solution)/shard_map/all_gather | solution.py:104
  711.7 17.9 %fusion.80 = (bf16[4608]{0:T(1024)(128)(2,1)}, bf16[2,256,4608]{2,1,0:T(8,128)(2,1)}) fusion(f32[2,256,4608]{2,1,0:T(8,128)} %fusion.31, f32[4608]{0:T(1024)} %convert_element_type.153, bf16[4608,1152]{1,0:T(8,128)(2,1)} %all-gather.14.cloned.1.call-done, bf16[2,256,1152]{2,1,0:T(8,128)(2,1)} %param.23, f32[2,1152]{1,0:T(2,128)} %get-tuple-element.163), kind=kOutput, calls=%fused_computation.139 | convolution fusion | flops 5489487360 | bytes 25989120 | tf_op jit(solution)/shard_map/btn,dn->btd/dot_general | solution.py:28
  729.5 12.3 multiply_reduce_fusion.2
  753.1 4.3 all-to-all-start.2
  757.5 4.9 fusion.46
  762.4 10.9 all-to-all-done.2
  773.3 3.2 copy.127
  776.6 3.6 reshape.242
  780.1 84.1 %while.23 = (s32[]{:T(128)}, bf16[2,1024,3,1,288]{1,4,3,2,0:T(8,128)(2,1)}, bf16[2,1024,3,4,72]{1,4,3,2,0:T(8,128)(2,1)S(1)}, f32[2,4,1024]{2,1,0:T(4,128)}, bf16[2,1024,4,72]{1,3,2,0:T(8,128)(2,1)}, /*index=5*/s32[]{:T(128)}) while((s32[]{:T(128)}, bf16[2,1024,3,1,288]{1,4,3,2,0:T(8,128)(2,1)}, ...), condition=%wide.region_12.13_spmd, body=%wide.region_10.12_spmd.sunk | while | flops 3077009408 | bytes 200787616 | solution.py:166
  786.8 9.2 multiply_reduce_fusion.9
  796.0 8.0 multiply_convert_fusion.9
  807.6 6.9 fusion.113
  814.5 4.9 fusion.112
  829.0 9.1 multiply_reduce_fusion.9
  838.1 7.9 multiply_convert_fusion.9
  849.5 6.9 fusion.113
  856.4 4.9 fusion.112
  864.2 12.4 copy.128
  876.6 60.2 %all_to_all.60 = bf16[2,1024,3,1,288]{4,0,3,2,1:T(2,128)(2,1)} all-to-all(bf16[2,1024,3,1,288]{4,0,3,2,1:T(2,128)(2,1)} %copy.128), channel_id=1, replica_groups=mesh['dp'=8,'seq'=4] {'seq'}, dimensions={1} | all-to-all | bytes 7077888 | tf_op jit(solution)/shard_map/all_to_all | solution.py:167
  936.8 13.0 copy.150
  954.3 7.4 fusion.24
  963.4 10.8 fusion.22
  974.2 13.7 fusion.23
  988.8 9.7 fusion.63
  1001.1 15.3 fusion.65
  1018.7 11.6 psum.7
  1030.7 35.2 %all-reduce.5 = (bf16[1,1728]{1,0:T(2,128)(2,1)S(1)}, bf16[4608]{0:T(1024)(128)(2,1)S(1)}) all-reduce(bf16[1,1728]{1,0:T(2,128)(2,1)S(1)} %convert_element_type.166, bf16[4608]{0:T(1024)(128)(2,1)} %get-tuple-element.175), channel_id=3, replica_groups=mesh['dp'=8,'seq'=4] {'dp'}, use_global_device_ids=true, to_apply=%region_24.25.clone | all-reduce | flops 6336 | bytes 25344
  1069.2 7.9 fusion.75
  1077.0 4.3 dynamic-slice_convert_fusion
  1081.4 20.8 %reduce-scatter.24.cloned.1.call-done = bf16[144,3456]{1,0:T(8,128)(2,1)} async-done(((bf16[1152,3456]{1,0:T(8,128)(2,1)}), bf16[144,3456]{1,0:T(8,128)(2,1)}) %reduce-scatter.24.cloned.1.call-update) | async-done | bytes 995344 | tf_op jit(solution)/shard_map/reduce_scatter | solution.py:196
  1104.9 180.4 %reduce-scatter.28.cloned.1.call-done = bf16[144,4608]{1,0:T(8,128)(2,1)} async-done(((bf16[1152,4608]{1,0:T(8,128)(2,1)}), bf16[144,4608]{1,0:T(8,128)(2,1)}) %reduce-scatter.28.cloned.1.call-update) | async-done | bytes 1327120 | tf_op jit(solution)/shard_map/reduce_scatter | solution.py:202
  1285.4 3.8 copy.157
  1289.2 178.8 %reduce-scatter.30.cloned.1.call-done = bf16[576,1152]{1,0:T(8,128)(2,1)} async-done(((bf16[4608,1152]{1,0:T(8,128)(2,1)}), bf16[576,1152]{1,0:T(8,128)(2,1)}) %reduce-scatter.30.cloned.1.call-update) | async-done | bytes 1327120 | tf_op jit(solution)/shard_map/reduce_scatter | solution.py:208
  1472.0 10.4 fusion.72
  1482.4 7.5 reduce-scatter.38.cloned.1.call-done
  1491.3 23.9 %reduce-scatter.34.cloned.1.call-done = bf16[288,144]{1,0:T(8,128)(2,1)} async-done(((bf16[1152,144]{1,0:T(8,128)(2,1)}), bf16[288,144]{1,0:T(8,128)(2,1)}) %reduce-scatter.34.cloned.1.call-update) | async-done | bytes 82960
  1517.0 86.8 %reduce-scatter.42.cloned.1.call-done = bf16[1152,216]{0,1:T(8,128)(2,1)} async-done(((bf16[1152,1728]{0,1:T(8,128)(2,1)}), bf16[1152,216]{0,1:T(8,128)(2,1)}) %reduce-scatter.42.cloned.1.call-update) | async-done | bytes 497680
  1605.9 29.9 %reduce-scatter.32.cloned.1.call-done = bf16[864,144]{1,0:T(8,128)(2,1)} async-done(((bf16[3456,144]{1,0:T(8,128)(2,1)}), bf16[864,144]{1,0:T(8,128)(2,1)}) %reduce-scatter.32.cloned.1.call-update) | async-done | bytes 248848
  1637.8 33.5 %reduce-scatter.36.cloned.1.call-done = bf16[1152,144]{1,0:T(8,128)(2,1)} async-done(((bf16[4608,144]{1,0:T(8,128)(2,1)}), bf16[1152,144]{1,0:T(8,128)(2,1)}) %reduce-scatter.36.cloned.1.call-update) | async-done | bytes 331792
  1673.5 28.0 %reduce-scatter.40.cloned.1.call-done = bf16[288,576]{1,0:T(8,128)(2,1)} async-done(((bf16[1152,576]{1,0:T(8,128)(2,1)}), bf16[288,576]{1,0:T(8,128)(2,1)}) %reduce-scatter.40.cloned.1.call-update) | async-done | bytes 331792
  (202 shorter events, 87.2 us)
Async XLA Ops:
  7.2 223.3 %all-gather.6.cloned.1.call-start = ((), (), s32[]{:S(2)}) async-start(), calls=%async_computation.14 | async-start | bytes 17915904 | tf_op jit(solution)/shard_map/all_gather | solution.py:109
  7.9 2.7 copy-start.42
  7.9 4.6 copy-start.43
  7.9 4.9 copy-start.44
  7.9 45.7 %copy-start.6 = (bf16[2,256,1152]{2,1,0:T(8,128)(2,1)S(1)}, bf16[2,256,1152]{2,1,0:T(8,128)(2,1)}, u32[]{:S(2)}) copy-start(bf16[2,256,1152]{2,1,0:T(8,128)(2,1)} %param.14) | copy-start | bytes 3538948
  8.0 342.5 %all-gather.8.cloned.1.call-start = ((), (), s32[]{:S(2)}) async-start(), calls=%async_computation.15 | async-start | bytes 8957952 | tf_op jit(solution)/shard_map/all_gather | solution.py:100
  8.7 505.0 %all-gather.10.cloned.1.call-start = ((), (), s32[]{:S(2)}) async-start(), calls=%async_computation.16 | async-start | bytes 2985984 | tf_op jit(solution)/shard_map/all_gather | solution.py:101
  9.4 221.0 %copy-start.17 = (f32[2,1152]{1,0:T(2,128)S(1)}, f32[2,1152]{1,0:T(2,128)}, u32[]{:S(2)}) copy-start(f32[2,1152]{1,0:T(2,128)} %param.15) | copy-start | bytes 27652
  9.5 549.5 %all-gather.12.cloned.1.call-start = ((), (), s32[]{:S(2)}) async-start(), calls=%async_computation.17 | async-start | bytes 11943936 | tf_op jit(solution)/shard_map/all_gather | solution.py:102
  10.0 701.6 %all-gather.14.cloned.1.call-start = ((), (), s32[]{:S(2)}) async-start(), calls=%async_computation.18 | async-start | bytes 11943936 | tf_op jit(solution)/shard_map/all_gather | solution.py:104
  53.8 296.6 %copy-start.24 = (f32[2,256]{1,0:T(2,128)}, f32[2,256]{1,0:T(2,128)S(1)}, u32[]{:S(2)}) copy-start(f32[2,256]{1,0:T(2,128)S(1)} %broadcast_multiply_fusion.1) | copy-start | bytes 6148
  54.9 295.6 %copy-start.36 = (f32[2,256]{1,0:T(2,128)}, f32[2,256]{1,0:T(2,128)S(1)}, u32[]{:S(2)}) copy-start(f32[2,256]{1,0:T(2,128)S(1)} %fusion.73) | copy-start | bytes 6148
  238.8 111.7 %copy-start.19 = (f32[2,1152]{1,0:T(2,128)}, f32[2,1152]{1,0:T(2,128)S(1)}, u32[]{:S(2)}) copy-start(f32[2,1152]{1,0:T(2,128)S(1)} %get-tuple-element.167) | copy-start | bytes 27652
  238.8 111.7 %copy-start.32 = (f32[2,1152]{1,0:T(2,128)}, f32[2,1152]{1,0:T(2,128)S(1)}, u32[]{:S(2)}) copy-start(f32[2,1152]{1,0:T(2,128)S(1)} %get-tuple-element.166) | copy-start | bytes 27652
  366.9 45.1 %all-to-all-start = ((bf16[2,256,3,4,288]{1,4,2,0,3:T(8,128)(2,1)}), bf16[2,256,3,4,288]{1,4,2,0,3:T(8,128)(2,1)S(1)}, u32[]{:S(2)}, u32[]{:S(2)}) async-start(bf16[2,256,3,4,288]{1,4,2,0,3:T(8,128)(2,1)} %copy.119), calls=%async_computation | async-start | bytes 7077888 | tf_op jit(solution)/shard_map/all_to_all | solution.py:129
  476.4 9.7 copy-start.30
  481.1 25.0 %all-to-all-start.1 = ((bf16[2,1024,1,288]{3,0,2,1:T(2,128)(2,1)}), bf16[2,1024,1,288]{3,0,2,1:T(2,128)(2,1)}, u32[]{:S(2)}, u32[]{:S(2)}) async-start(bf16[2,1024,1,288]{3,0,2,1:T(2,128)(2,1)} %copy.121), calls=%async_computation.1 | async-start | bytes 3145728 | tf_op jit(solution)/shard_map/all_to_all | solution.py:133
  506.2 7.6 copy-start.16
  519.6 1.4 copy-start.3
  519.7 1.8 copy-start.28
  711.6 17.9 %copy-start.4 = (f32[2,256,1152]{2,1,0:T(8,128)S(1)}, f32[2,256,1152]{2,1,0:T(8,128)}, u32[]{:S(2)}) copy-start(f32[2,256,1152]{2,1,0:T(8,128)} %copy-done.3) | copy-start | bytes 7077892
  711.6 17.9 %copy-start.22 = (f32[2,1152]{1,0:T(2,128)S(1)}, f32[2,1152]{1,0:T(2,128)}, u32[]{:S(2)}) copy-start(f32[2,1152]{1,0:T(2,128)} %get-tuple-element.165) | copy-start | bytes 27652
  711.6 17.9 %copy-start.29 = (f32[2,256]{1,0:T(2,128)S(1)}, f32[2,256]{1,0:T(2,128)}, u32[]{:S(2)}) copy-start(f32[2,256]{1,0:T(2,128)} %copy-done.28) | copy-start | bytes 6148
  711.7 17.9 %copy-start.39 = (f32[2,256]{1,0:T(2,128)S(1)}, f32[2,256]{1,0:T(2,128)}, u32[]{:S(2)}) copy-start(f32[2,256]{1,0:T(2,128)} %fusion.74) | copy-start | bytes 6148
  741.8 1.3 copy-start.13
  742.5 1.4 copy-start.8
  742.5 1.4 copy-start.34
  743.1 2.4 copy-start.11
  753.1 20.2 %all-to-all-start.2 = ((bf16[2,256,4,288]{1,3,0,2:T(8,128)(2,1)}), bf16[2,256,4,288]{1,3,0,2:T(8,128)(2,1)}, u32[]{:S(2)}, u32[]{:S(2)}) async-start(bf16[2,256,4,288]{1,3,0,2:T(8,128)(2,1)} %copy.126), calls=%async_computation.2 | async-start | bytes 2359296 | tf_op jit(solution)/shard_map/all_to_all | solution.py:163
  757.4 309.4 %reduce-scatter.26.cloned.1.call-start = ((), (), s32[]{:S(2)}) async-start(), calls=%async_computation.20 | async-start | bytes 2985984 | tf_op jit(solution)/shard_map/reduce_scatter | solution.py:199
  762.4 339.9 %reduce-scatter.24.cloned.1.call-start = ((), (), s32[]{:S(2)}) async-start(), calls=%async_computation.19 | async-start | bytes 8957952 | tf_op jit(solution)/shard_map/reduce_scatter | solution.py:196
  780.1 1.9 copy-start.1
  804.1 3.5 copy-start
  819.4 2.9 copy-start.2
  822.3 1.9 copy-start.1
  846.0 3.5 copy-start
  861.3 2.9 copy-start.2
  949.8 4.5 copy-start.7
  949.8 4.5 copy-start.20
  949.8 4.5 copy-start.25
  949.8 4.5 copy-start.33
  949.8 4.5 copy-start.37
  952.5 1.8 copy-start.10
  961.7 1.7 copy-start.5
  961.7 323.6 %reduce-scatter.28.cloned.1.call-start = ((), (), s32[]{:S(2)}) async-start(), calls=%async_computation.21 | async-start | bytes 11943936 | tf_op jit(solution)/shard_map/reduce_scatter | solution.py:202
  974.2 493.9 %reduce-scatter.30.cloned.1.call-start = ((), (), s32[]{:S(2)}) async-start(), calls=%async_computation.22 | async-start | bytes 11943936 | tf_op jit(solution)/shard_map/reduce_scatter | solution.py:208
  987.9 502.0 %reduce-scatter.38.cloned.1.call-start = ((), (), s32[]{:S(2)}) async-start(), calls=%async_computation.26 | async-start | bytes 184320
  988.8 9.8 copy-start.27
  988.8 9.8 copy-start.38
  988.8 12.2 copy-start.12
  998.5 2.5 copy-start.9
  998.5 2.5 copy-start.14
  998.5 2.4 copy-start.21
  998.6 2.4 copy-start.23
  998.6 2.4 copy-start.31
  998.6 2.4 copy-start.35
  1001.0 15.9 copy-start.41
  1001.0 16.5 copy-start.40
  1001.0 68.1 %copy-start.18 = (f32[2,1152]{1,0:T(2,128)S(1)}, f32[2,1152]{1,0:T(2,128)}, u32[]{:S(2)}) copy-start(f32[2,1152]{1,0:T(2,128)} %param.15) | copy-start | bytes 27652
  1066.8 448.5 %reduce-scatter.34.cloned.1.call-start = ((), (), s32[]{:S(2)}) async-start(), calls=%async_computation.24 | async-start | bytes 737280
  1068.9 534.9 %reduce-scatter.42.cloned.1.call-start = ((), (), s32[]{:S(2)}) async-start(), calls=%async_computation.28 | async-start | bytes 4478976
  1081.4 554.4 %reduce-scatter.32.cloned.1.call-start = ((), (), s32[]{:S(2)}) async-start(), calls=%async_computation.23 | async-start | bytes 2211840
  1104.9 566.4 %reduce-scatter.36.cloned.1.call-start = ((), (), s32[]{:S(2)}) async-start(), calls=%async_computation.25 | async-start | bytes 2949120
  1289.2 412.3 %reduce-scatter.40.cloned.1.call-start = ((), (), s32[]{:S(2)}) async-start(), calls=%async_computation.27 | async-start | bytes 1843200
  (2 other events, 1.6 us)
Sparse Core Ops, SparseCore 0:
  10.2 220.1 all-gather.5
  232.6 117.7 all-gather.7
  352.6 53.1 all-gather.9
  407.9 151.0 all-gather.11
  561.0 150.6 all-gather.13
  762.5 69.1 reduce-scatter.25
  961.8 140.3 reduce-scatter.23
  1106.3 179.0 reduce-scatter.27
  1289.0 179.0 reduce-scatter.29
  1471.0 18.7 reduce-scatter.37
  1493.1 22.0 reduce-scatter.33
  1519.1 84.6 reduce-scatter.41
  1606.6 29.1 reduce-scatter.31
  1638.2 33.0 reduce-scatter.35
  1673.9 27.5 reduce-scatter.39
where the time goes:
time: 1720 us; the launch traced here: 1710 us
  waiting for transfers between devices  1130 us (66%)
  matrix products  235 us (14%)
  blocking collectives  148 us (9%)
  local copies, waits for them, and re-layouts  116 us (7%)
  other arithmetic  51.3 us (3%)
  between operations  17.3 us (1%)
    unnamed x21, waiting for transfers between devices  213 us
    reduce_scatter x1, waiting for transfers between devices, on_device(): lax.psum_scatter(grad_fc1.astype(jnp.bfloat16), 'dp', scatter_dimension=0...  180 us
    reduce_scatter x1, waiting for transfers between devices, on_device(): lax.psum_scatter(grad_fc2.astype(jnp.bfloat16), 'dp', scatter_dimension=0...  179 us
    all_gather x1, waiting for transfers between devices, on_device(): lax.all_gather(w_mod, 'dp', axis=0, tiled=True)  176 us
    all_gather x1, waiting for transfers between devices, on_device(): lax.all_gather(w_fc2, 'dp', axis=0, tiled=True)  140 us
    all_gather x1, waiting for transfers between devices, on_device(): lax.all_gather(w_qkv, 'dp', axis=0, tiled=True)  112 us
    unnamed x2, blocking collectives  75.7 us
    all_to_all x1, blocking collectives, on_device(): lax.all_to_all(d_packed, 'seq', split_axis=1, concat_axis=3, tiled=True)  60.2 us
  transfers between devices with their start and end apart: 18, of which 16 were waited for; matrix products, arithmetic and copies ran while one was open for 20% of the time, Pallas kernels for 0%

commit v1 on v0

v1 whole, which is shorter than its diff:
```python
from functools import partial

import jax
import jax.numpy as jnp
from jax import lax
from jax.sharding import PartitionSpec as P

HEADS = 16
HEAD_DIM = 72
BF = jnp.bfloat16
F32 = jnp.float32
GELU_C = 0.7978845608028654
GELU_A = 0.044715


def hop(value, axis, bits):
    count = lax.axis_size(axis)
    return lax.ppermute(value, axis, [(i, i ^ bits) for i in range(count)])


def matmul(left, right):
    return jnp.dot(left, right, preferred_element_type=F32)


def matmul_nt(left, right):
    return lax.dot_general(left, right, (((1,), (1,)), ((), ())), preferred_element_type=F32)


def matmul_tn(left, right):
    return lax.dot_general(left, right, (((0,), (0,)), ((), ())), preferred_element_type=F32)


def ln_parts(values):
    row_mean = jnp.mean(values, axis=-1, keepdims=True)
    centred = values - row_mean
    row_var = jnp.mean(centred * centred, axis=-1, keepdims=True)
    inv_std = lax.rsqrt(row_var + 1e-06)
    return centred * inv_std, inv_std


def ln_backward(grad, normed, inv_std):
    mean_grad = jnp.mean(grad, axis=-1, keepdims=True)
    mean_inner = jnp.mean(grad * normed, axis=-1, keepdims=True)
    return (grad - mean_grad - normed * mean_inner) * inv_std


def seq_gather(mine):
    slots = {0: mine}
    bit = lax.axis_size("seq") // 2
    while bit:
        for j in list(slots):
            slots[j | bit] = hop(slots[j], "seq", bit)
        bit //= 2
    return [slots[j] for j in range(len(slots))]


def seq_reduce(slots):
    slots = dict(enumerate(slots))
    bit = 1
    while len(slots) > 1:
        for j in [j for j in slots if j & bit]:
            slots[j ^ bit] = slots[j ^ bit] + hop(slots.pop(j).astype(BF), "seq", bit).astype(F32)
        bit *= 2
    return slots[0]


def seq_exchange(blocks):
    return [blocks[0]] + [hop(blocks[j], "seq", j) for j in range(1, len(blocks))]


def dp_exchange(value):
    return lax.all_to_all(value, "dp", 0, 0, tiled=True)


GATHER = "sc"
SCATTER = "sc"


def dp_gather(mine):
    if GATHER == "sc":
        return lax.all_gather(mine, "dp", axis=0, tiled=True)
    count = lax.axis_size("dp")
    index = lax.axis_index("dp")
    rows = mine.shape[0]
    slots = {0: mine}
    for j in range(2, count, 2):
        slots[j] = hop(mine, "dp", j)
    for j in range(0, count, 2):
        slots[j + 1] = hop(slots[j], "dp", 1)
    whole = jnp.zeros((count * rows,) + mine.shape[1:], mine.dtype)
    for j in range(count):
        whole = lax.dynamic_update_slice(whole, slots[j], ((index ^ j) * rows, 0))
    return whole


def dp_scatter(terms):
    if SCATTER == "sc":
        return lax.psum_scatter(terms, "dp", scatter_dimension=0, tiled=True).astype(F32)
    count = lax.axis_size("dp")
    index = lax.axis_index("dp")
    rows = terms.shape[0] // count

    def block(j):
        return lax.dynamic_slice(terms, ((index ^ j) * rows, 0), (rows, terms.shape[1]))

    half = {}
    for j in list(range(2, count, 2)) + [0]:
        half[j] = block(j).astype(F32) + hop(block(j + 1), "dp", 1).astype(F32)
    total = half[0]
    for j in range(2, count, 2):
        total = total + hop(half[j].astype(BF), "dp", j).astype(F32)
    return total


def attend_forward(packed):
    inv_root = HEAD_DIM ** (-0.5)
    queries = packed[:, 0]
    key_rows = packed[:, 1]
    values = packed[:, 2]
    scores = (
        jnp.einsum("qhd,khd->hqk", queries, key_rows, preferred_element_type=jnp.float32) * inv_root
    )
    row_max = jnp.max(scores, axis=-1, keepdims=True)
    exponent = jnp.exp(scores - row_max)
    row_sum = jnp.sum(exponent, axis=-1, keepdims=True)
    weights = (exponent / row_sum).astype(jnp.bfloat16)
    mixed = jnp.einsum("hqk,khd->qhd", weights, values, preferred_element_type=jnp.float32)
    seq_len = mixed.shape[0]
    heads_here = mixed.shape[1]
    mixed = mixed.reshape(seq_len, heads_here * HEAD_DIM).astype(jnp.bfloat16)
    return (mixed, (row_max + jnp.log(row_sum))[..., 0])


def attend_backward(group):
    packed, log_sum, d_mixed = group
    inv_root = HEAD_DIM ** (-0.5)
    queries = packed[:, 0]
    key_rows = packed[:, 1]
    values = packed[:, 2]
    scores = (
        jnp.einsum("qhd,khd->hqk", queries, key_rows, preferred_element_type=jnp.float32) * inv_root
    )
    weights = jnp.exp(scores - log_sum[..., None])
    d_values = jnp.einsum(
        "hqk,qhd->khd", weights.astype(jnp.bfloat16), d_mixed, preferred_element_type=jnp.float32
    )
    d_weights = jnp.einsum("qhd,khd->hqk", d_mixed, values, preferred_element_type=jnp.float32)
    row_inner = jnp.sum(weights * d_weights, axis=-1, keepdims=True)
    d_scores = (weights * (d_weights - row_inner)).astype(jnp.bfloat16)
    d_queries = (
        jnp.einsum("hqk,khd->qhd", d_scores, key_rows, preferred_element_type=jnp.float32)
        * inv_root
    )
    d_keys = (
        jnp.einsum("hqk,qhd->khd", d_scores, queries, preferred_element_type=jnp.float32) * inv_root
    )
    stacked = jnp.stack([d_queries, d_keys, d_values], axis=1)
    seq_len = stacked.shape[0]
    heads_here = stacked.shape[2]
    return stacked.reshape(seq_len, 3 * heads_here * HEAD_DIM).astype(jnp.bfloat16)


def attention(packed, heads_here):
    lat, seq_len, _ = packed.shape
    return lax.map(attend_forward, packed.reshape(lat, seq_len, 3, heads_here, HEAD_DIM))


def attention_grad(packed, mixed, log_sums, d_mixed, heads_here):
    lat, seq_len, _ = packed.shape
    return lax.map(
        attend_backward,
        (
            packed.reshape(lat, seq_len, 3, heads_here, HEAD_DIM),
            log_sums,
            d_mixed.reshape(lat, seq_len, heads_here, HEAD_DIM),
        ),
    )


def on_device(tokens, conditioning, w_mod, b_mod, w_qkv, w_proj, w_fc1, b_fc1, w_fc2, cotangent):
    lat, tok, width = tokens.shape
    seq_n = lax.axis_size("seq")
    dp_n = lax.axis_size("dp")
    seq = lax.axis_index("seq")
    dp = lax.axis_index("dp")
    core = seq % 2
    heads_here = HEADS // seq_n
    cols = heads_here * HEAD_DIM
    seq_len = tok * seq_n
    rows = w_qkv.shape[0]
    hid_here = w_fc2.shape[0] // 2
    hid = hid_here * dp_n
    own = lat * tok
    every = ("dp", "seq")
    n_all = dp_n * seq_n

    tok_slots = seq_gather(tokens)

    cond_silu, silu_back = jax.vjp(jax.nn.silu, conditioning)
    cond_act = cond_silu.astype(BF)
    bias_half = lax.dynamic_slice(b_fc1, (core * hid_here,), (hid_here,))
    small = jnp.concatenate(
        [
            cond_act.reshape(lat, dp_n, rows).transpose(1, 0, 2).reshape(dp_n, lat * rows),
            jnp.broadcast_to(bias_half[None], (dp_n, hid_here)),
        ],
        axis=1,
    )
    small = dp_exchange(small)
    cond_rows = small[:, : lat * rows].reshape(dp_n * lat, rows)
    fc1_bias = small[:, lat * rows :].reshape(hid).astype(F32)
    mod_terms = matmul(cond_rows, w_mod)
    piece = b_mod.shape[0]
    mod_terms = lax.dynamic_update_slice(
        mod_terms,
        lax.dynamic_slice(mod_terms, (0, dp * piece), (dp_n * lat, piece))
        + b_mod.astype(F32)[None],
        (0, dp * piece),
    )
    modulation = jnp.sum(dp_exchange(mod_terms.reshape(dp_n, lat, 6 * width)), axis=0)
    shift_attn, scale_attn, gate_attn, shift_mlp, scale_mlp, gate_mlp = [
        modulation[:, None, i * width : (i + 1) * width] for i in range(6)
    ]

    qkv_here = lax.dynamic_index_in_dim(
        w_qkv.reshape(rows, 3, seq_n, cols), seq, axis=2, keepdims=False
    ).reshape(rows, 3 * cols)
    qkv = dp_gather(qkv_here)
    proj_half = dp_gather(lax.dynamic_slice(w_proj, (0, core * (width // 2)), (rows, width // 2)))
    fc1_here = lax.dynamic_index_in_dim(
        w_fc1.reshape(rows, dp_n, 2, hid_here), core, axis=2, keepdims=False
    ).reshape(rows, hid)
    fc1 = dp_gather(fc1_here)
    fc2 = dp_gather(lax.dynamic_slice(w_fc2, (core * hid_here, 0), (hid_here, width)))
    proj_other = hop(proj_half, "seq", 1)
    proj = jnp.where(
        core == 0,
        jnp.concatenate([proj_half, proj_other], axis=1),
        jnp.concatenate([proj_other, proj_half], axis=1),
    )
    proj = jnp.concatenate(
        [lax.dynamic_slice(proj, ((seq ^ j) * cols, 0), (cols, width)) for j in range(seq_n)]
    )

    tok_all = jnp.concatenate(tok_slots, axis=1).astype(F32)
    normed_all = (ln_parts(tok_all)[0] * (1.0 + scale_attn) + shift_attn).astype(BF)
    normed_all = normed_all.reshape(lat * seq_len, width)
    packed = matmul(normed_all, qkv).astype(BF).reshape(lat, seq_len, 3 * cols)
    mixed, log_sums = attention(packed, heads_here)
    mixed_slots = mixed.reshape(lat, seq_n, tok, cols)
    attended = jnp.concatenate(
        seq_exchange([mixed_slots[:, j] for j in range(seq_n)]), axis=2
    ).reshape(own, width)

    attn_out = matmul(attended, proj).reshape(lat, tok, width)
    token_values = tokens.astype(F32)
    resid_mid = token_values + gate_attn * attn_out
    normed_mid, std_mid = ln_parts(resid_mid)
    normed_mlp = (normed_mid * (1.0 + scale_mlp) + shift_mlp).astype(BF).reshape(own, width)
    upstream = cotangent.astype(F32)
    d_mlp = (gate_mlp * upstream).astype(BF).reshape(own, width)
    d_mlp_pair = jnp.concatenate([d_mlp, hop(d_mlp, "seq", 1)])

    normed_pair = jnp.concatenate([normed_mlp, hop(normed_mlp, "seq", 1)])
    hidden = matmul(normed_pair, fc1) + fc1_bias
    tanh = jnp.tanh(GELU_C * (hidden + GELU_A * hidden * hidden * hidden))
    activated = (0.5 * hidden * (1.0 + tanh)).astype(BF)
    gelu_slope = 0.5 * (1.0 + tanh) + 0.5 * hidden * (1.0 - tanh * tanh) * GELU_C * (
        1.0 + 3.0 * GELU_A * hidden * hidden
    )
    d_hidden = (matmul_nt(d_mlp_pair, fc2) * gelu_slope).astype(BF)
    d_norm_part = matmul_nt(d_hidden, fc1)
    d_norm = d_norm_part[:own] + hop(d_norm_part[own:].astype(BF), "seq", 1).astype(F32)
    d_norm = d_norm.reshape(lat, tok, width)
    grad_fc2 = matmul_tn(activated, d_mlp_pair).astype(BF)
    grad_fc1 = matmul_tn(normed_pair, d_hidden).astype(BF)
    grad_bias1 = jnp.sum(d_hidden.astype(F32), axis=0)
    mlp_part = matmul(activated, fc2)
    mlp_out = mlp_part[:own] + hop(mlp_part[own:].astype(BF), "seq", 1).astype(F32)
    mlp_out = mlp_out.reshape(lat, tok, width)
    output = (resid_mid + gate_mlp * mlp_out).astype(BF)
    d_gate_mlp = jnp.sum(upstream * mlp_out, axis=1)

    d_shift_mlp = jnp.sum(d_norm, axis=1)
    d_scale_mlp = jnp.sum(d_norm * normed_mid, axis=1)
    d_resid = upstream + ln_backward(d_norm * (1.0 + scale_mlp), normed_mid, std_mid)
    d_gate_attn = jnp.sum(d_resid * attn_out, axis=1)
    d_attn = (gate_attn * d_resid).astype(BF).reshape(own, width)
    grad_proj = matmul_tn(attended, d_attn).astype(BF)
    d_attended = matmul_nt(d_attn, proj).astype(BF).reshape(lat, tok, width)
    d_mixed = jnp.concatenate(
        seq_exchange([d_attended[:, :, j * cols : (j + 1) * cols] for j in range(seq_n)]), axis=1
    )
    d_packed = attention_grad(packed, mixed, log_sums, d_mixed, heads_here)
    d_packed = d_packed.reshape(lat * seq_len, 3 * cols)
    grad_qkv = matmul_tn(normed_all, d_packed).astype(BF)
    first_parts = matmul_nt(d_packed, qkv).reshape(lat, seq_n, tok, width)
    d_first = seq_reduce([first_parts[:, j] for j in range(seq_n)])
    normed_tok, std_tok = ln_parts(token_values)
    d_shift_attn = jnp.sum(d_first, axis=1)
    d_scale_attn = jnp.sum(d_first * normed_tok, axis=1)
    grad_tokens = d_resid + ln_backward(d_first * (1.0 + scale_attn), normed_tok, std_tok)

    mod_part = jnp.concatenate(
        [d_shift_attn, d_scale_attn, d_gate_attn, d_shift_mlp, d_scale_mlp, d_gate_mlp], axis=1
    )
    share = 6 * width // n_all
    mod_cols = lax.all_to_all(
        mod_part.reshape(lat, n_all, share).transpose(1, 0, 2), every, 0, 0, tiled=True
    )
    d_mod = jnp.sum(mod_cols.reshape(dp_n, seq_n, lat, share), axis=1).reshape(dp_n * lat, share)
    d_mod = d_mod.astype(BF)
    cond_all = lax.all_to_all(
        jnp.broadcast_to(cond_act[None], (dp_n, lat, width)), "dp", 0, 0, tiled=True
    ).reshape(dp_n * lat, width)
    grad_wmod = matmul_tn(cond_all, d_mod)
    grad_bmod = jnp.sum(d_mod.astype(F32), axis=0)
    mod_rows = lax.all_to_all(
        jnp.broadcast_to(d_mod[None], (dp_n, dp_n * lat, share)), "dp", 0, 0, tiled=True
    )
    mod_here = mod_rows.transpose(1, 0, 2).reshape(dp_n * lat, dp_n * share)
    w_mod_here = lax.dynamic_index_in_dim(
        w_mod.reshape(rows, dp_n, seq_n, share), seq, axis=2, keepdims=False
    ).reshape(rows, dp_n * share)
    cond_terms = matmul_nt(mod_here, w_mod_here)
    cond_terms = jnp.broadcast_to(
        cond_terms.reshape(dp_n, 1, lat, rows), (dp_n, seq_n, lat, rows)
    ).reshape(n_all, lat, rows)
    cond_back = lax.all_to_all(cond_terms, every, 0, 0, tiled=True)
    d_cond = jnp.sum(cond_back.reshape(dp_n, seq_n, lat, rows), axis=1)
    (grad_cond,) = silu_back(d_cond.transpose(1, 0, 2).reshape(lat, width))

    spread = jnp.zeros((dp_n, 2, hid_here), F32)
    spread = lax.dynamic_update_slice(spread, grad_bias1.reshape(dp_n, 1, hid_here), (0, core, 0))
    bias_cols = lax.all_to_all(
        spread.reshape(n_all, 2 * hid_here // seq_n), every, 0, 0, tiled=True
    )
    bias_out = jnp.sum(bias_cols, axis=0)

    sum_fc2 = dp_scatter(grad_fc2).astype(BF)
    sum_fc1 = dp_scatter(grad_fc1).astype(BF)
    grad_proj = jnp.concatenate(
        [
            lax.dynamic_slice(grad_proj, ((seq ^ j) * cols, 0), (cols, width))
            for j in range(seq_n)
        ]
    )
    sum_proj = dp_scatter(grad_proj).astype(BF)
    sum_qkv = dp_scatter(grad_qkv).astype(BF)

    def to_owner(blocks):
        return lax.all_to_all(blocks, "seq", 0, 0, tiled=True).astype(F32)

    def pair_sum(received):
        return jnp.sum(received.reshape((seq_n // 2, 2) + received.shape[1:]), axis=0)

    fc2_cols = width // seq_n
    out_fc2 = pair_sum(to_owner(sum_fc2.reshape(hid_here, seq_n, fc2_cols).transpose(1, 0, 2)))
    out_fc2 = out_fc2.reshape(2 * hid_here, fc2_cols)
    per = dp_n * 2 // seq_n
    if per >= 2:
        blocks = sum_fc1.reshape(rows, seq_n, dp_n // seq_n, hid_here).transpose(1, 0, 2, 3)
        out_fc1 = pair_sum(to_owner(blocks)).transpose(1, 2, 0, 3)
    else:
        parts = to_owner(
            jnp.broadcast_to(sum_fc1.reshape(1, rows, hid), (seq_n, rows, hid))
        )
        parts = pair_sum(parts).reshape(2, rows, dp_n, hid_here).transpose(1, 2, 0, 3)
        out_fc1 = lax.dynamic_slice(
            parts.reshape(rows, 2 * hid), (0, seq * (2 * hid // seq_n)), (rows, 2 * hid // seq_n)
        )
    out_fc1 = out_fc1.reshape(rows, 2 * hid // seq_n)
    out_proj = jnp.sum(
        to_owner(sum_proj.reshape(rows, seq_n, width // seq_n).transpose(1, 0, 2)), axis=0
    )
    qkv_slots = seq_gather(sum_qkv)
    qkv_whole = jnp.zeros((rows, 3, seq_n, cols), BF)
    for j in range(seq_n):
        qkv_whole = lax.dynamic_update_slice(
            qkv_whole, qkv_slots[j].reshape(rows, 3, 1, cols), (0, 0, seq ^ j, 0)
        )
    out_qkv = lax.dynamic_slice(
        qkv_whole.reshape(rows, 3 * width), (0, seq * 3 * cols), (rows, 3 * cols)
    ).astype(F32)
    return (
        output,
        grad_tokens,
        grad_cond,
        grad_wmod,
        grad_bmod,
        out_qkv,
        out_proj,
        out_fc1,
        bias_out,
        out_fc2,
    )


def solution(mesh):
    placed = (
        P("dp", "seq", None),
        P("dp", None),
        P("dp", None),
        P("dp"),
        P("dp", None),
        P("dp", None),
        P("dp", None),
        P("dp"),
        P("dp", None),
        P("dp", "seq", None),
    )
    return jax.shard_map(
        on_device,
        mesh=mesh,
        in_specs=placed,
        out_specs=(
            P("dp", "seq", None),
            P("dp", "seq", None),
            P("dp", None),
            P(None, ("dp", "seq")),
            P(("dp", "seq")),
            P("dp", "seq"),
            P("dp", "seq"),
            P("dp", "seq"),
            P(("dp", "seq")),
            P("dp", "seq"),
        ),
        check_vma=False,
    )
```

time: 1720 us -> 788 us (0.46)
  waiting for transfers between devices: 1130 us -> 254 us
  blocking collectives: 148 us -> 10.5 us
  local copies, waits for them, and re-layouts: 116 us -> 173 us
  matrix products: 235 us -> 189 us
  starting transfers between devices: 14.2 us -> 50.2 us
  other arithmetic: 51.3 us -> 85.8 us
    all_gather x5 -> x4, waiting for transfers between devices: 465 us -> 70.7 us  [dp_gather(): return lax.all_gather(mine, 'dp', axis=0, tiled=True)]
    reduce_scatter x4, waiting for transfers between devices: 380 us -> 90.2 us  [dp_scatter(): lax.psum_scatter(terms, 'dp', scatter_dimension=0, tiled=True).astype(F32)]
    unnamed x21 -> x8, waiting for transfers between devices: 213 us -> 0.13 us
    unnamed x2 -> x0, blocking collectives: 75.7 us -> none
    ppermute x0 -> x20, waiting for transfers between devices: none -> 64.3 us  [hop(): return lax.ppermute(value, axis, [(i, i ^ bits) for i in range(count)])]
    all_to_all x1, blocking collectives: 60.2 us -> 10.5 us  [on_device(): lax.all_to_all(mod_part.reshape(lat, n_all, share).transpose(1, 0, 2), ev...]
    dynamic_update_slice x2 -> x10, local copies, waits for them, and re-layouts: 1.72 us -> 44.9 us  [the longest x4 41.3 us: on_device(): lax.dynamic_update_slice(qkv_whole, qkv_slots[j].reshape(rows, 3, 1, cols...]
    all_to_all x3 -> x9, waiting for transfers between devices: 71.5 us -> 28.7 us  [the longest x2 12.7 us: dp_exchange(): return lax.all_to_all(value, 'dp', 0, 0, tiled=True)]
  transfers between devices with their start and end apart: 18 -> 37, of which waited for: 16 -> 18; matrix products, arithmetic and copies ran while one was open for 20% -> 49% of each run, Pallas kernels for 0% -> 0%
where the time goes in v1:
time: 788 us; the launch traced here: 779 us
  waiting for transfers between devices  254 us (32%)
  matrix products  189 us (24%)
  local copies, waits for them, and re-layouts  173 us (22%)
  other arithmetic  85.8 us (11%)
  starting transfers between devices  50.2 us (6%)
  between operations  15.6 us (2%)
  blocking collectives  10.5 us (1%)
    reduce_scatter x4, waiting for transfers between devices, dp_scatter(): lax.psum_scatter(terms, 'dp', scatter_dimension=0, tiled=True).astype(F32)  90.2 us
    all_gather x4, waiting for transfers between devices, dp_gather(): return lax.all_gather(mine, 'dp', axis=0, tiled=True)  70.7 us
    ppermute x20, waiting for transfers between devices, hop(): return lax.ppermute(value, axis, [(i, i ^ bits) for i in range(count)])  64.3 us
    dot_general x5, matrix products, matmul(): return jnp.dot(left, right, preferred_element_type=F32)  42.3 us
    dynamic_update_slice x4, local copies, waits for them, and re-layouts, on_device(): lax.dynamic_update_slice(qkv_whole, qkv_slots[j].reshape(rows, 3, 1, cols...  41.3 us
    dot_general x5, matrix products, matmul_tn(): lax.dot_general(left, right, (((0,), (0,)), ((), ())), preferred_element_...  35.6 us
    dot_general x5, matrix products, matmul_nt(): lax.dot_general(left, right, (((1,), (1,)), ((), ())), preferred_element_...  31.5 us
    dot_general x2, matrix products, attend_backward(): jnp.einsum('qhd,khd->hqk', d_mixed, values, preferred_element_type=jnp.fl...  18.7 us
  transfers between devices with their start and end apart: 37, of which 18 were waited for; matrix products, arithmetic and copies ran while one was open for 49% of the time, Pallas kernels for 0%

profile of v1, /device:TPU:0, one launch (start us, length us, event | category | flops | bytes accessed | tf_op | source)
XLA Modules:
  0.0 778.6 jit_solution(6628576466884396623)
XLA Ops:
  15.0 6.2 reshape.339
  21.2 7.2 dynamic-slice_reduce_fusion
  35.2 5.8 all-to-all-start
  41.0 6.7 all-to-all-done
  52.3 3.5 all-to-all-start.1
  61.0 6.0 all-to-all-done.1
  77.3 4.8 fusion.34
  82.1 26.0 %all-gather.5.cloned.1.call-done = bf16[1152,864]{1,0:T(8,128)(2,1)} async-done(((bf16[144,864]{1,0:T(8,128)(2,1)}), bf16[1152,864]{1,0:T(8,128)(2,1)}) %all-gather.5.cloned.1.call-update) | async-done | bytes 1990672 | tf_op jit(solution)/shard_map/all_gather | solution.py:81
  108.1 9.6 %convolution_convert_fusion.2 = bf16[2048,864]{0,1:T(8,128)(2,1)} fusion(bf16[2048,1152]{1,0:T(8,128)(2,1)} %fusion.34, bf16[1152,864]{1,0:T(8,128)(2,1)} %all-gather.5.cloned.1.call-done), kind=kOutput, calls=%fused_computation.82 | convolution fusion | flops 4078632960 | bytes 10248192 | tf_op jit(solution)/shard_map/dot_general | solution.py:22
  117.8 9.2 %reshape_reshape.4 = bf16[2,1024,3,4,72]{1,0,4,3,2:T(2,128)(2,1)} reshape(bf16[2048,864]{0,1:T(8,128)(2,1)} %convolution_convert_fusion.2) | data formatting | bytes 7077888 | tf_op jit(solution)/shard_map/reshape;reshape | solution.py:165
  127.0 5.1 copy.198
  132.1 53.0 %while.22 = (s32[]{:T(128)}, bf16[2,1024,288]{1,2,0:T(8,128)(2,1)S(1)}, f32[2,4,1024]{2,1,0:T(4,128)S(1)}, bf16[2,1024,3,4,72]{1,4,3,2,0:T(8,128)(2,1)}, s32[]{:T(128)}) while((s32[]{:T(128)}, bf16[2,1024,288]{1,2,0:T(8,128)(2,1)S(1)}, f32[2,4,1024]{2,1,0:T(4,128)S(1)}, bf16[2,1024,3,4,72]{1,4,3,2,0:T(8,128)(2,1)}, s32[]{:T(128)}) %tuple.117), condition=%wide.region_6.7_spmd, body=%wide.region_3.6_spmd.sunk | while | flops 1245999104 | bytes 57540680 | solution.py:165
  133.9 8.1 %multiply_reduce_fusion.9 = (f32[4,1024]{1,0:T(4,128)S(1)}, f32[4,1024,1024]{1,2,0:T(8,128)}) fusion(bf16[1024,3,4,72]{0,3,2,1:T(8,128)(2,1)S(1)} %dynamic-slice_bitcast_fusion.6), kind=kOutput, calls=%fused_computation.2.clone.1 | convolution fusion | flops 612364288 | bytes 17973248 | tf_op jit(solution)/shard_map/while/body/eval_jaxpr/qhd,khd->hqk/dot_general | solution.py:121
  142.1 9.0 %fusion.119 = f32[4,1024]{1,0:T(4,128)S(1)} fusion(f32[4,1024,1024]{1,2,0:T(8,128)} %get-tuple-element.250, f32[4,1024]{1,0:T(4,128)S(1)} %get-tuple-element.251), kind=kLoop, calls=%fused_computation.3.clone.1 | loop fusion | flops 12578816 | bytes 16809984 | tf_op jit(solution)/shard_map/while/body/eval_jaxpr/reduce_sum | solution.py:125
  151.1 7.7 fusion.120
  160.5 8.1 %multiply_reduce_fusion.9 = (f32[4,1024]{1,0:T(4,128)S(1)}, f32[4,1024,1024]{1,2,0:T(8,128)}) fusion(bf16[1024,3,4,72]{0,3,2,1:T(8,128)(2,1)S(1)} %dynamic-slice_bitcast_fusion.6), kind=kOutput, calls=%fused_computation.2.clone.1 | convolution fusion | flops 612364288 | bytes 17973248 | tf_op jit(solution)/shard_map/while/body/eval_jaxpr/qhd,khd->hqk/dot_general | solution.py:121
  168.6 8.6 %fusion.119 = f32[4,1024]{1,0:T(4,128)S(1)} fusion(f32[4,1024,1024]{1,2,0:T(8,128)} %get-tuple-element.250, f32[4,1024]{1,0:T(4,128)S(1)} %get-tuple-element.251), kind=kLoop, calls=%fused_computation.3.clone.1 | loop fusion | flops 12578816 | bytes 16809984 | tf_op jit(solution)/shard_map/while/body/eval_jaxpr/reduce_sum | solution.py:125
  177.2 7.9 %fusion.120 = bf16[4,72,1024]{2,1,0:T(8,128)(2,1)S(1)} fusion(f32[4,1024,1024]{1,2,0:T(8,128)} %get-tuple-element.250, f32[4,1024]{1,0:T(4,128)S(1)} %fusion.119, f32[4,1024]{1,0:T(4,128)S(1)} %get-tuple-element.251, bf16[1024,3,4,72]{0,3,2,1:T(8,128)(2,1)S(1)} %dynamic-slice_bitcast_fusion.6), kind=kOutput, calls=%fused_computation.6.clone.1 | convolution fusion | flops 621051904 | bytes 17989632 | tf_op jit(solution)/shard_map/while/body/eval_jaxpr/hqk,khd->qhd/dot_general | solution.py:127
  199.9 4.7 maximum_select_fusion
  206.2 6.1 collective-permute-done.5
  212.3 3.5 concatenate.40
  215.8 6.0 fusion.84
  226.3 12.3 %fusion.67 = f32[1024,2304]{1,0:T(8,128)} fusion(bf16[1152,2304]{1,0:T(8,128)(2,1)} %all-gather.9.cloned.1.call-done, bf16[512,1152]{1,0:T(8,128)(2,1)S(1)} %collective-permute-done.7, bf16[512,1152]{1,0:T(8,128)(2,1)S(1)} %bitcast.255), kind=kOutput, calls=%fused_computation.133 | convolution fusion | flops 5440536576 | bytes 17104896 | tf_op jit(solution)/shard_map/dot_general | solution.py:22
  238.6 44.6 %all-gather.11.cloned.1.call-done = bf16[2304,1152]{1,0:T(8,128)(2,1)} async-done(((bf16[288,1152]{1,0:T(8,128)(2,1)}), bf16[2304,1152]{1,0:T(8,128)(2,1)}) %all-gather.11.cloned.1.call-update) | async-done | bytes 5308432 | tf_op jit(solution)/shard_map/all_gather | solution.py:81
  283.2 12.4 %fusion.82 = f32[1024,1152]{1,0:T(8,128)S(1)} fusion(bf16[2304,1152]{1,0:T(8,128)(2,1)} %all-gather.11.cloned.1.call-done, f32[1024,2304]{1,0:T(8,128)} %fusion.67, f32[2304]{0:T(1024)S(1)} %reshape.371), kind=kOutput, calls=%fused_computation.199 | convolution fusion | flops 5459410944 | bytes 19473408 | tf_op jit(solution)/shard_map/dot_general | solution.py:22
  304.3 13.5 %convert_reduce_fusion = (f32[2304]{0:T(1024)}, bf16[1024,2304]{1,0:T(8,128)(2,1)S(1)}) fusion(f32[1024,2304]{1,0:T(8,128)} %fusion.67, f32[2304]{0:T(1024)S(1)} %reshape.371, bf16[2304,1152]{1,0:T(8,128)(2,1)S(1)} %copy-done.55, bf16[512,1152]{1,0:T(8,128)(2,1)S(1)} %collective-permute-done.9, bf16[512,1152]{1,0:T(8,128)(2,1)S(1)} %bitcast.252), kind=kOutput, calls=%fused_computation.59 | convolution fusion | flops 5492439040 | bytes 21841920 | tf_op jit(solution)/shard_map/dot_general | solution.py:26
  317.8 6.3 fusion.90
  329.0 5.8 multiply_reduce_fusion.3
  338.9 6.1 pad_maximum_fusion.3
  346.1 3.7 convolution_convert_fusion.3
  353.0 11.9 %convolution_convert_fusion = bf16[2304,1152]{1,0:T(8,128)(2,1)} fusion(bf16[512,1152]{1,0:T(8,128)(2,1)S(1)} %copy-done.60, bf16[512,1152]{1,0:T(8,128)(2,1)S(1)} %bitcast.253, f32[1024,2304]{1,0:T(8,128)} %fusion.67, f32[2304]{0:T(1024)S(1)} %reshape.371), kind=kOutput, calls=%fused_computation.45 | convolution fusion | flops 5466783744 | bytes 17114112 | tf_op jit(solution)/shard_map/dot_general | solution.py:30
  365.1 5.7 collective-permute-done.13
  372.2 78.3 %while.23 = (s32[]{:T(128)}, bf16[2,1024,864]{1,2,0:T(8,128)(2,1)}, bf16[2,1024,3,4,72]{1,4,3,2,0:T(8,128)(2,1)}, f32[2,4,1024]{2,1,0:T(4,128)S(1)}, bf16[2,1024,4,72]{1,3,2,0:T(8,128)(2,1)S(1)}, /*index=5*/s32[]{:T(128)}) while((s32[]{:T(128)}, bf16[2,1024,864]{1,2,0:T(8,128)(2,1)}, bf16[2,1024,3,4,72]{1,4,3,2,0:T(8,128)(2,1)}, ...), condition=%wide.region_13.14_spmd, body=%wide.region_11.13_spmd.sunk | while | flops 3073470464 | bytes 199608032 | solution.py:170
  376.7 9.3 %multiply_reduce_fusion.10 = (f32[4,1024]{1,0:T(4,128)S(1)}, f32[4,1024,1024]{1,2,0:T(8,128)}) fusion(f32[4,1024,1024]{1,2,0:T(8,128)S(1)} %fusion.125, f32[4,1024]{1,0:T(4,128)S(1)} %dynamic-slice_bitcast_fusion.8, bf16[1024,3,4,72]{0,3,2,1:T(8,128)(2,1)} %copy-done.3, bf16[2,1024,4,72]{1,3,2,0:T(8,128)(2,1)S(1)} %get-tuple-element.290, ...), kind=kOutput, calls=%fused_computation.15.clone.1 | convolution fusion | flops 620752896 | bytes 34767360 | tf_op jit(solution)/shard_map/while/body/eval_jaxpr/qhd,khd->hqk/dot_general | solution.py:147
  386.0 8.1 %multiply_convert_fusion.7 = bf16[4,1024,1024]{1,2,0:T(8,128)(2,1)S(1)} fusion(f32[4,1024,1024]{1,2,0:T(8,128)} %get-tuple-element.257, f32[4,1024,1024]{1,2,0:T(8,128)S(1)} %fusion.125, f32[4,1024]{1,0:T(4,128)S(1)} %get-tuple-element.258, f32[4,1024]{1,0:T(4,128)S(1)} %dynamic-slice_bitcast_fusion.8), kind=kLoop, calls=%fused_computation.14.clone.1 | loop fusion | flops 20971520 | bytes 41975808 | tf_op jit(solution)/shard_map/while/body/eval_jaxpr/convert_element_type | solution.py:149
  399.0 6.1 fusion.127
  405.0 4.2 fusion.126
  415.8 9.4 %multiply_reduce_fusion.10 = (f32[4,1024]{1,0:T(4,128)S(1)}, f32[4,1024,1024]{1,2,0:T(8,128)}) fusion(f32[4,1024,1024]{1,2,0:T(8,128)S(1)} %fusion.125, f32[4,1024]{1,0:T(4,128)S(1)} %dynamic-slice_bitcast_fusion.8, bf16[1024,3,4,72]{0,3,2,1:T(8,128)(2,1)} %copy-done.3, bf16[2,1024,4,72]{1,3,2,0:T(8,128)(2,1)S(1)} %get-tuple-element.290, ...), kind=kOutput, calls=%fused_computation.15.clone.1 | convolution fusion | flops 620752896 | bytes 34767360 | tf_op jit(solution)/shard_map/while/body/eval_jaxpr/qhd,khd->hqk/dot_general | solution.py:147
  425.2 8.1 %multiply_convert_fusion.7 = bf16[4,1024,1024]{1,2,0:T(8,128)(2,1)S(1)} fusion(f32[4,1024,1024]{1,2,0:T(8,128)} %get-tuple-element.257, f32[4,1024,1024]{1,2,0:T(8,128)S(1)} %fusion.125, f32[4,1024]{1,0:T(4,128)S(1)} %get-tuple-element.258, f32[4,1024]{1,0:T(4,128)S(1)} %dynamic-slice_bitcast_fusion.8), kind=kLoop, calls=%fused_computation.14.clone.1 | loop fusion | flops 20971520 | bytes 41975808 | tf_op jit(solution)/shard_map/while/body/eval_jaxpr/convert_element_type | solution.py:149
  438.1 6.2 fusion.127
  444.2 4.3 fusion.126
  450.5 10.7 %bitcast_convert_fusion = bf16[1152,864]{1,0:T(8,128)(2,1)} fusion(bf16[2,1024,864]{1,2,0:T(8,128)(2,1)} %get-tuple-element.62, f32[2,1024]{1,0:T(2,128)S(1)} %copy-done.51, f32[2,1152]{1,0:T(2,128)S(1)} %copy-done.36, f32[2,1152]{1,0:T(2,128)S(1)} %copy-done.30, f32[2,1024]{1,0:T(2,128)S(1)} %copy-done.46, ...), kind=kOutput, calls=%fused_computation.72 | convolution fusion | flops 4108529664 | bytes 10283008 | tf_op jit(solution)/shard_map/dot_general | solution.py:30
  461.3 10.0 %convolution_convert_fusion.1 = bf16[1152,2304]{1,0:T(8,128)(2,1)} fusion(bf16[1024,2304]{1,0:T(8,128)(2,1)} %copy-done.61, bf16[512,1152]{1,0:T(8,128)(2,1)S(1)} %copy-done.58, bf16[512,1152]{1,0:T(8,128)(2,1)S(1)} %bitcast.256), kind=kOutput, calls=%fused_computation.46 | convolution fusion | flops 5443190784 | bytes 12386304 | tf_op jit(solution)/shard_map/dot_general | solution.py:30
  472.9 7.8 fusion.88
  485.9 26.7 %collective-permute-done.16 = bf16[2,256,1152]{2,1,0:T(8,128)(2,1)S(1)} collective-permute-done((bf16[2,256,1152]{2,1,0:T(8,128)(2,1)S(1)}, bf16[2,256,1152]{2,1,0:T(8,128)(2,1)S(1)}, u32[]{:S(2)}, u32[]{:S(2)}) %collective-permute-start.16) | collective-permute-done | bytes 1179680 | tf_op jit(solution)/shard_map/ppermute | solution.py:18
  516.0 10.5 %all_to_all.61 = f32[32,2,216]{2,1,0:T(2,128)S(1)} all-to-all(f32[32,2,216]{2,1,0:T(2,128)S(1)} %copy.213), channel_id=1, replica_groups=mesh['dp'=8,'seq'=4] {'dp','seq'}, dimensions={0} | all-to-all | bytes 110592 | tf_op jit(solution)/shard_map/all_to_all | solution.py:308
  527.2 3.4 all-to-all-start.3
  530.5 8.1 %reshape.350 = bf16[144,8,4,216]{3,2,1,0:T(4,128)(2,1)} reshape(bf16[144,6912]{1,0:T(8,128)(2,1)S(1)} %copy-done.14) | data formatting | bytes 3981312 | tf_op jit(solution)/shard_map/reshape | solution.py:323
  539.3 6.2 all-to-all-start.5
  545.5 5.5 dynamic-slice_reduce_fusion.1
  552.7 5.0 all-to-all-start.8
  558.0 7.0 all-to-all-done.8
  571.1 4.6 all-to-all-done.4
  575.6 3.5 all-to-all-start.6
  582.6 4.5 all-to-all-done.6
  587.1 3.5 all-to-all-start.9
  590.6 4.6 fusion.55
  599.3 9.6 %collective-permute-done.18 = bf16[144,864]{1,0:T(8,128)(2,1)} collective-permute-done((bf16[144,864]{1,0:T(8,128)(2,1)}, bf16[144,864]{1,0:T(8,128)(2,1)}, u32[]{:S(2)}, u32[]{:S(2)}) %collective-permute-start.18) | collective-permute-done | bytes 248864 | tf_op jit(solution)/shard_map/ppermute | solution.py:18
  608.9 90.2 %reduce-scatter.9.cloned.1.call-done = bf16[144,2304]{1,0:T(8,128)(2,1)} async-done(((bf16[1152,2304]{1,0:T(8,128)(2,1)}), bf16[144,2304]{1,0:T(8,128)(2,1)}) %reduce-scatter.9.cloned.1.call-update) | async-done | bytes 663568 | tf_op jit(solution)/shard_map/reduce_scatter | solution.py:98
  703.9 3.8 all-to-all-start.7
  709.8 10.3 %dynamic_update_slice.31 = bf16[144,3,4,288]{3,2,1,0:T(4,128)(2,1)S(1)} dynamic-update-slice(bf16[144,3,4,288]{3,2,1,0:T(4,128)(2,1)S(1)} %broadcast_in_dim.32, bf16[144,3,1,288]{3,2,1,0:T(2,128)(2,1)} %reshape.383, s32[]{:T(128)} %constant.63.clone.1, s32[]{:T(128)} %constant.63.clone.1, s32[]{:T(128)S(6)} %select_n.69, s32[]{:T(128)} %constant.63.clone.1) | dynamic-update-slice | bytes 497668 | tf_op jit(solution)/shard_map/dynamic_update_slice | solution.py:379
  723.2 10.3 %dynamic_update_slice.32 = bf16[144,3,4,288]{3,2,1,0:T(4,128)(2,1)S(1)} dynamic-update-slice(bf16[144,3,4,288]{3,2,1,0:T(4,128)(2,1)S(1)} %dynamic_update_slice.31, bf16[144,3,1,288]{3,2,1,0:T(2,128)(2,1)} %reshape.384, s32[]{:T(128)} %constant.63.clone.1, s32[]{:T(128)} %constant.63.clone.1, s32[]{:T(128)S(6)} %select_n.78, s32[]{:T(128)} %constant.63.clone.1) | dynamic-update-slice | bytes 497668 | tf_op jit(solution)/shard_map/dynamic_update_slice | solution.py:379
  736.6 10.3 %dynamic_update_slice.33 = bf16[144,3,4,288]{3,2,1,0:T(4,128)(2,1)S(1)} dynamic-update-slice(bf16[144,3,4,288]{3,2,1,0:T(4,128)(2,1)S(1)} %dynamic_update_slice.32, bf16[144,3,1,288]{3,2,1,0:T(2,128)(2,1)} %reshape.385, s32[]{:T(128)} %constant.63.clone.1, s32[]{:T(128)} %constant.63.clone.1, s32[]{:T(128)S(6)} %select_n.79, s32[]{:T(128)} %constant.63.clone.1) | dynamic-update-slice | bytes 497668 | tf_op jit(solution)/shard_map/dynamic_update_slice | solution.py:379
  750.0 10.3 %dynamic_update_slice.34 = bf16[144,3,4,288]{3,2,1,0:T(4,128)(2,1)S(1)} dynamic-update-slice(bf16[144,3,4,288]{3,2,1,0:T(4,128)(2,1)S(1)} %dynamic_update_slice.33, bf16[144,3,1,288]{3,2,1,0:T(2,128)(2,1)} %reshape.386, s32[]{:T(128)} %constant.63.clone.1, s32[]{:T(128)} %constant.63.clone.1, s32[]{:T(128)S(6)} %select_n.80, s32[]{:T(128)} %constant.63.clone.1) | dynamic-update-slice | bytes 497668 | tf_op jit(solution)/shard_map/dynamic_update_slice | solution.py:379
  (338 shorter events, 158.5 us)
Async XLA Ops:
  7.2 51.8 %copy-start = (bf16[576,1152]{1,0:T(8,128)(2,1)S(1)}, bf16[576,1152]{1,0:T(8,128)(2,1)}, u32[]{:S(2)}) copy-start(bf16[576,1152]{1,0:T(8,128)(2,1)} %param.22) | copy-start | bytes 3981316
  7.2 60.6 %all-gather.7.cloned.1.call-start = ((), (), s32[]{:S(2)}) async-start(), calls=%async_computation.15 | async-start | bytes 1658880 | tf_op jit(solution)/shard_map/all_gather | solution.py:81
  9.1 99.0 %all-gather.5.cloned.1.call-start = ((), (), s32[]{:S(2)}) async-start(), calls=%async_computation.14 | async-start | bytes 2322432 | tf_op jit(solution)/shard_map/all_gather | solution.py:81
  14.4 211.9 %all-gather.9.cloned.1.call-start = ((), (), s32[]{:S(2)}) async-start(), calls=%async_computation.16 | async-start | bytes 5971968 | tf_op jit(solution)/shard_map/all_gather | solution.py:81
  21.2 11.8 %copy-start.41 = (f32[2,1152]{1,0:T(2,128)S(1)}, f32[2,1152]{1,0:T(2,128)}, u32[]{:S(2)}) copy-start(f32[2,1152]{1,0:T(2,128)} %param.15) | copy-start | bytes 27652
  21.2 12.0 %copy-start.54 = (bf16[576]{0:T(1024)(128)(2,1)S(1)}, bf16[576]{0:T(1024)(128)(2,1)}, u32[]{:S(2)}) copy-start(bf16[576]{0:T(1024)(128)(2,1)} %param.21) | copy-start | bytes 3460
  21.2 19.8 %copy-start.52 = (bf16[864]{0:T(1024)(128)(2,1)S(1)}, bf16[864]{0:T(1024)(128)(2,1)}, u32[]{:S(2)}) copy-start(bf16[864]{0:T(1024)(128)(2,1)} %param.17) | copy-start | bytes 5188
  30.0 29.0 %collective-permute-start.1 = (bf16[2,256,1152]{2,1,0:T(8,128)(2,1)S(1)}, bf16[2,256,1152]{2,1,0:T(8,128)(2,1)}, u32[]{:S(2)}, u32[]{:S(2)}) collective-permute-start(bf16[2,256,1152]{2,1,0:T(8,128)(2,1)S(1)} %copy-done.5), channel_id=1, source_target_pairs={{0,2},{1,3},{2,0},{3,1},{4,6},{5,7},{6,4},{7,5},{8,10},{9,11},{10,... | collective-permute-start | bytes 3538952 | tf_op jit(solution)/shard_map/ppermute | solution.py:18
  35.2 12.5 %all-to-all-start = ((bf16[8,2,288]{2,1,0:T(2,128)(2,1)}), bf16[8,2,288]{2,1,0:T(2,128)(2,1)S(1)}, u32[]{:S(2)}, u32[]{:S(2)}) async-start(bf16[8,2,288]{2,1,0:T(2,128)(2,1)} %reshape.392), calls=%async_computation | async-start | bytes 24576 | tf_op jit(solution)/shard_map/all_to_all | solution.py:72
  52.3 14.8 %all-to-all-start.1 = ((f32[8,2,6912]{2,1,0:T(2,128)}), f32[8,2,6912]{2,1,0:T(2,128)S(1)}, u32[]{:S(2)}, u32[]{:S(2)}) async-start(f32[8,2,6912]{2,1,0:T(2,128)} %reshape.334), calls=%async_computation.1 | async-start | bytes 884736 | tf_op jit(solution)/shard_map/all_to_all | solution.py:72
  55.7 227.5 %all-gather.11.cloned.1.call-start = ((), (), s32[]{:S(2)}) async-start(), calls=%async_computation.17 | async-start | bytes 5971968 | tf_op jit(solution)/shard_map/all_gather | solution.py:81
  55.8 14.6 %collective-permute-start = (bf16[2,256,1152]{2,1,0:T(8,128)(2,1)S(1)}, bf16[2,256,1152]{2,1,0:T(8,128)(2,1)}, u32[]{:S(2)}, u32[]{:S(2)}) collective-permute-start(bf16[2,256,1152]{2,1,0:T(8,128)(2,1)S(1)} %copy-done.5), channel_id=1, source_target_pairs={{0,1},{1,0},{2,3},{3,2},{4,5},{5,4},{6,7},{7,6},{8,9},{9,8},{10,11... | collective-permute-start | bytes 3538952 | tf_op jit(solution)/shard_map/ppermute | solution.py:18
  59.0 11.4 %collective-permute-start.2 = (bf16[2,256,1152]{2,1,0:T(8,128)(2,1)}, bf16[2,256,1152]{2,1,0:T(8,128)(2,1)}, u32[]{:S(2)}, u32[]{:S(2)}) collective-permute-start(bf16[2,256,1152]{2,1,0:T(8,128)(2,1)} %collective-permute-done.1), channel_id=1, source_target_pairs={{0,1},{1,0},{2,3},{3,2},{4,5},{5,4},{6,7},{7,6},{8,9},{9,8},{10,11... | collective-permute-start | bytes 3538952 | tf_op jit(solution)/shard_map/ppermute | solution.py:18
  59.9 509.0 %reduce-scatter.7.cloned.1.call-start = ((), (), s32[]{:S(2)}) async-start(), calls=%async_computation.19 | async-start | bytes 2985984 | tf_op jit(solution)/shard_map/reduce_scatter | solution.py:98
  70.4 126.9 %collective-permute-start.6 = (bf16[1152,576]{0,1:T(8,128)(2,1)}, bf16[1152,576]{0,1:T(8,128)(2,1)}, u32[]{:S(2)}, u32[]{:S(2)}) collective-permute-start(bf16[1152,576]{0,1:T(8,128)(2,1)} %copy.203), channel_id=1, source_target_pairs={{0,1},{1,0},{2,3},{3,2},{4,5},{5,4},{6,7},{7,6},{8,9},{9,8},{10,11... | collective-permute-start | bytes 3981320 | tf_op jit(solution)/shard_map/ppermute | solution.py:18
  190.3 15.9 %collective-permute-start.3 = (bf16[2,256,288]{2,1,0:T(8,128)(2,1)}, bf16[2,256,288]{2,1,0:T(8,128)(2,1)}, u32[]{:S(2)}, u32[]{:S(2)}) collective-permute-start(bf16[2,256,288]{2,1,0:T(8,128)(2,1)} %bitcast.26), channel_id=1, source_target_pairs={{0,1},{1,0},{2,3},{3,2},{4,5},{5,4},{6,7},{7,6},{8,9},{9,8},{10,11... | collective-permute-start | bytes 884744 | tf_op jit(solution)/shard_map/ppermute | solution.py:18
  192.4 13.8 %collective-permute-start.4 = (bf16[2,256,288]{2,1,0:T(8,128)(2,1)}, bf16[2,256,288]{2,1,0:T(8,128)(2,1)}, u32[]{:S(2)}, u32[]{:S(2)}) collective-permute-start(bf16[2,256,288]{2,1,0:T(8,128)(2,1)} %bitcast.27), channel_id=1, source_target_pairs={{0,2},{1,3},{2,0},{3,1},{4,6},{5,7},{6,4},{7,5},{8,10},{9,11},{10,... | collective-permute-start | bytes 884744 | tf_op jit(solution)/shard_map/ppermute | solution.py:18
  195.5 16.8 %collective-permute-start.5 = (bf16[2,256,288]{2,1,0:T(8,128)(2,1)}, bf16[2,256,288]{2,1,0:T(8,128)(2,1)}, u32[]{:S(2)}, u32[]{:S(2)}) collective-permute-start(bf16[2,256,288]{2,1,0:T(8,128)(2,1)} %bitcast.28), channel_id=1, source_target_pairs={{0,3},{1,2},{2,1},{3,0},{4,7},{5,6},{6,5},{7,4},{8,11},{9,10},{10,... | collective-permute-start | bytes 884744 | tf_op jit(solution)/shard_map/ppermute | solution.py:18
  223.3 15.3 %copy-start.19 = (bf16[2,256,1152]{2,1,0:T(8,128)(2,1)}, bf16[2,256,1152]{2,1,0:T(8,128)(2,1)S(1)}, u32[]{:S(2)}) copy-start(bf16[2,256,1152]{2,1,0:T(8,128)(2,1)S(1)} %add_convert_fusion.5) | copy-start | bytes 3538948
  223.3 3.0 collective-permute-start.7
  226.3 12.3 %copy-start.57 = (bf16[512,1152]{1,0:T(8,128)(2,1)}, bf16[512,1152]{1,0:T(8,128)(2,1)S(1)}, u32[]{:S(2)}) copy-start(bf16[512,1152]{1,0:T(8,128)(2,1)S(1)} %collective-permute-done.7) | copy-start | bytes 3538948
  238.6 60.1 %copy-start.31 = (f32[2,1152]{1,0:T(2,128)S(1)}, f32[2,1152]{1,0:T(2,128)}, u32[]{:S(2)}) copy-start(f32[2,1152]{1,0:T(2,128)} %get-tuple-element.176) | copy-start | bytes 27652
  295.8 2.9 collective-permute-start.8
  301.4 16.4 %slice-start = ((s8[5308416]{0:T(1024)(128)(4,1)}), s8[4194304]{0:T(1024)(128)(4,1)S(1)}, s32[]{:S(2)}) async-start(s8[5308416]{0:T(1024)(128)(4,1)} %bitcast.263), calls=%async_computation.22 | async-start | bytes 8388608
  301.4 16.4 %slice-start.1 = ((s8[5308416]{0:T(1024)(128)(4,1)}), s8[1114112]{0:T(1024)(128)(4,1)S(1)}, s32[]{:S(2)}) async-start(s8[5308416]{0:T(1024)(128)(4,1)} %bitcast.263), calls=%async_computation.23 | async-start | bytes 2228224
  301.4 2.8 collective-permute-start.9
  304.3 13.5 %copy-start.59 = (bf16[512,1152]{1,0:T(8,128)(2,1)}, bf16[512,1152]{1,0:T(8,128)(2,1)S(1)}, u32[]{:S(2)}) copy-start(bf16[512,1152]{1,0:T(8,128)(2,1)S(1)} %collective-permute-done.9) | copy-start | bytes 3538948
  324.3 2.9 collective-permute-start.10
  345.0 234.1 %reduce-scatter.11.cloned.1.call-start = ((), (), s32[]{:S(2)}) async-start(), calls=%async_computation.21 | async-start | bytes 5971968 | tf_op jit(solution)/shard_map/reduce_scatter | solution.py:98
  351.2 13.9 %collective-permute-start.11 = (bf16[2,256,288]{2,1,0:T(8,128)(2,1)}, bf16[2,256,288]{2,1,0:T(8,128)(2,1)S(1)}, u32[]{:S(2)}, u32[]{:S(2)}) collective-permute-start(bf16[2,256,288]{2,1,0:T(8,128)(2,1)} %get-tuple-element.169), channel_id=1, source_target_pairs={{0,1},{1,0},{2,3},{3,2},{4,5},{5,4},{6,7},{7,6},{8,9},{9,8},{10,11... | collective-permute-start | bytes 884744 | tf_op jit(solution)/shard_map/ppermute | solution.py:18
  351.3 13.7 %collective-permute-start.12 = (bf16[2,256,288]{2,1,0:T(8,128)(2,1)}, bf16[2,256,288]{2,1,0:T(8,128)(2,1)S(1)}, u32[]{:S(2)}, u32[]{:S(2)}) collective-permute-start(bf16[2,256,288]{2,1,0:T(8,128)(2,1)} %get-tuple-element.168), channel_id=1, source_target_pairs={{0,2},{1,3},{2,0},{3,1},{4,6},{5,7},{6,4},{7,5},{8,10},{9,11},{10,... | collective-permute-start | bytes 884744 | tf_op jit(solution)/shard_map/ppermute | solution.py:18
  352.8 18.0 %collective-permute-start.13 = (bf16[2,256,288]{2,1,0:T(8,128)(2,1)S(1)}, bf16[2,256,288]{2,1,0:T(8,128)(2,1)S(1)}, u32[]{:S(2)}, u32[]{:S(2)}) collective-permute-start(bf16[2,256,288]{2,1,0:T(8,128)(2,1)S(1)} %get-tuple-element.167), channel_id=1, source_target_pairs={{0,3},{1,2},{2,1},{3,0},{4,7},{5,6},{6,5},{7,4},{8,11},{9,10},{10,... | collective-permute-start | bytes 884744 | tf_op jit(solution)/shard_map/ppermute | solution.py:18
  365.0 230.2 %reduce-scatter.5.cloned.1.call-start = ((), (), s32[]{:S(2)}) async-start(), calls=%async_computation.18 | async-start | bytes 2322432 | tf_op jit(solution)/shard_map/reduce_scatter | solution.py:98
  372.1 78.4 %copy-start.30 = (f32[2,1152]{1,0:T(2,128)S(1)}, f32[2,1152]{1,0:T(2,128)}, u32[]{:S(2)}) copy-start(f32[2,1152]{1,0:T(2,128)} %copy-done.29) | copy-start | bytes 27652
  372.1 78.4 %copy-start.36 = (f32[2,1152]{1,0:T(2,128)S(1)}, f32[2,1152]{1,0:T(2,128)}, u32[]{:S(2)}) copy-start(f32[2,1152]{1,0:T(2,128)} %copy-done.35) | copy-start | bytes 27652
  372.2 78.3 %copy-start.46 = (f32[2,1024]{1,0:T(2,128)S(1)}, f32[2,1024]{1,0:T(2,128)}, u32[]{:S(2)}) copy-start(f32[2,1024]{1,0:T(2,128)} %copy-done.45) | copy-start | bytes 24580
  372.2 78.3 %copy-start.51 = (f32[2,1024]{1,0:T(2,128)S(1)}, f32[2,1024]{1,0:T(2,128)}, u32[]{:S(2)}) copy-start(f32[2,1024]{1,0:T(2,128)} %get-tuple-element.184) | copy-start | bytes 24580
  386.0 11.4 %copy-start.4 = (bf16[1024,3,4,72]{0,3,2,1:T(8,128)(2,1)S(1)}, bf16[1024,3,4,72]{0,3,2,1:T(8,128)(2,1)}, u32[]{:S(2)}) copy-start(bf16[1024,3,4,72]{0,3,2,1:T(8,128)(2,1)} %copy-done.3) | copy-start | bytes 5308420 | tf_op jit(solution)/shard_map/while
  461.2 237.8 %reduce-scatter.9.cloned.1.call-start = ((), (), s32[]{:S(2)}) async-start(), calls=%async_computation.20 | async-start | bytes 5971968 | tf_op jit(solution)/shard_map/reduce_scatter | solution.py:98
  480.9 31.7 %copy-start.7 = (bf16[2,256,1152]{2,1,0:T(8,128)(2,1)S(1)}, bf16[2,256,1152]{2,1,0:T(8,128)(2,1)}, u32[]{:S(2)}) copy-start(bf16[2,256,1152]{2,1,0:T(8,128)(2,1)} %param.14) | copy-start | bytes 3538948
  480.9 31.7 %copy-start.48 = (f32[2,256]{1,0:T(2,128)S(1)}, f32[2,256]{1,0:T(2,128)}, u32[]{:S(2)}) copy-start(f32[2,256]{1,0:T(2,128)} %broadcast_multiply_fusion.3) | copy-start | bytes 6148
  480.9 3.1 collective-permute-start.15
  481.5 4.4 collective-permute-start.14
  484.3 28.3 %collective-permute-start.16 = (bf16[2,256,1152]{2,1,0:T(8,128)(2,1)S(1)}, bf16[2,256,1152]{2,1,0:T(8,128)(2,1)S(1)}, u32[]{:S(2)}, u32[]{:S(2)}) collective-permute-start(bf16[2,256,1152]{2,1,0:T(8,128)(2,1)S(1)} %fusion.61), channel_id=1, source_target_pairs={{0,2},{1,3},{2,0},{3,1},{4,6},{5,7},{6,4},{7,5},{8,10},{9,11},{10,... | collective-permute-start | bytes 3538952 | tf_op jit(solution)/shard_map/ppermute | solution.py:18
  485.8 29.9 %copy-start.40 = (f32[2,1152]{1,0:T(2,128)S(1)}, f32[2,1152]{1,0:T(2,128)}, u32[]{:S(2)}) copy-start(f32[2,1152]{1,0:T(2,128)} %get-tuple-element.144) | copy-start | bytes 27652
  485.8 29.9 %copy-start.39 = (f32[2,1152]{1,0:T(2,128)S(1)}, f32[2,1152]{1,0:T(2,128)}, u32[]{:S(2)}) copy-start(f32[2,1152]{1,0:T(2,128)} %get-tuple-element.122) | copy-start | bytes 27652
  485.8 29.9 %copy-start.38 = (f32[2,1152]{1,0:T(2,128)S(1)}, f32[2,1152]{1,0:T(2,128)}, u32[]{:S(2)}) copy-start(f32[2,1152]{1,0:T(2,128)} %get-tuple-element.120) | copy-start | bytes 27652
  485.8 29.9 %copy-start.37 = (f32[2,1152]{1,0:T(2,128)S(1)}, f32[2,1152]{1,0:T(2,128)}, u32[]{:S(2)}) copy-start(f32[2,1152]{1,0:T(2,128)} %get-tuple-element.142) | copy-start | bytes 27652
  485.9 44.7 %copy-start.14 = (bf16[144,6912]{1,0:T(8,128)(2,1)S(1)}, bf16[144,6912]{1,0:T(8,128)(2,1)}, u32[]{:S(2)}) copy-start(bf16[144,6912]{1,0:T(8,128)(2,1)} %param.16) | copy-start | bytes 5971972
  515.7 22.9 %copy-start.34 = (bf16[2,1152]{1,0:T(2,128)(2,1)S(1)}, bf16[2,1152]{1,0:T(2,128)(2,1)}, u32[]{:S(2)}) copy-start(bf16[2,1152]{1,0:T(2,128)(2,1)} %copy-done.33) | copy-start | bytes 13828
  527.2 11.5 %all-to-all-start.3 = ((bf16[8,16,216]{2,1,0:T(8,128)(2,1)}), bf16[8,16,216]{2,1,0:T(8,128)(2,1)S(1)}, u32[]{:S(2)}, u32[]{:S(2)}) async-start(bf16[8,16,216]{2,1,0:T(8,128)(2,1)} %broadcast_in_dim.29), calls=%async_computation.3 | async-start | bytes 131072 | tf_op jit(solution)/shard_map/all_to_all | solution.py:318
  530.5 21.1 %copy-start.49 = (f32[2304]{0:T(1024)S(1)}, f32[2304]{0:T(1024)}, u32[]{:S(2)}) copy-start(f32[2304]{0:T(1024)} %get-tuple-element.191) | copy-start | bytes 27652
  539.3 13.5 %all-to-all-start.5 = ((bf16[8,2,1152]{2,1,0:T(2,128)(2,1)}), bf16[8,2,1152]{2,1,0:T(2,128)(2,1)S(1)}, u32[]{:S(2)}, u32[]{:S(2)}) async-start(bf16[8,2,1152]{2,1,0:T(2,128)(2,1)} %broadcast_in_dim.31), calls=%async_computation.5 | async-start | bytes 73728 | tf_op jit(solution)/shard_map/all_to_all | solution.py:313
  551.0 28.1 %copy-start.50 = (f32[2,256]{1,0:T(2,128)S(1)}, f32[2,256]{1,0:T(2,128)}, u32[]{:S(2)}) copy-start(f32[2,256]{1,0:T(2,128)} %get-tuple-element.118) | copy-start | bytes 6148
  552.7 12.3 %all-to-all-start.8 = ((f32[32,1,144]{2,1,0:T(1,128)}), f32[32,1,144]{2,1,0:T(1,128)S(1)}, u32[]{:S(2)}, u32[]{:S(2)}) async-start(f32[32,1,144]{2,1,0:T(1,128)} %all_to_all.48), calls=%async_computation.11 | async-start | bytes 65536 | tf_op jit(solution)/shard_map/all_to_all | solution.py:335
  565.7 10.0 %all-to-all-start.4 = ((f32[32,2,144]{2,1,0:T(2,128)}), f32[32,2,144]{2,1,0:T(2,128)S(1)}, u32[]{:S(2)}, u32[]{:S(2)}) async-start(f32[32,2,144]{2,1,0:T(2,128)} %bitcast.46), calls=%async_computation.4 | async-start | bytes 131072 | tf_op jit(solution)/shard_map/all_to_all | solution.py:329
  575.6 11.4 %all-to-all-start.6 = ((bf16[4,144,288]{2,1,0:T(8,128)(2,1)}), bf16[4,144,288]{2,1,0:T(8,128)(2,1)S(1)}, u32[]{:S(2)}, u32[]{:S(2)}) async-start(bf16[4,144,288]{2,1,0:T(8,128)(2,1)} %bitcast.195), calls=%async_computation.8 | async-start | bytes 884736 | tf_op jit(solution)/shard_map/all_to_all | solution.py:352
  587.1 116.8 %all-to-all-start.9 = ((bf16[4,288,288]{2,1,0:T(8,128)(2,1)}), bf16[4,288,288]{2,1,0:T(8,128)(2,1)S(1)}, u32[]{:S(2)}, u32[]{:S(2)}) async-start(bf16[4,288,288]{2,1,0:T(8,128)(2,1)} %bitcast.193), calls=%async_computation.13 | async-start | bytes 1769472 | tf_op jit(solution)/shard_map/all_to_all | solution.py:352
  595.2 13.7 %collective-permute-start.18 = (bf16[144,864]{1,0:T(8,128)(2,1)}, bf16[144,864]{1,0:T(8,128)(2,1)}, u32[]{:S(2)}, u32[]{:S(2)}) collective-permute-start(bf16[144,864]{1,0:T(8,128)(2,1)} %reduce-scatter.5.cloned.1.call-done), channel_id=1, source_target_pairs={{0,2},{1,3},{2,0},{3,1},{4,6},{5,7},{6,4},{7,5},{8,10},{9,11},{10,... | collective-permute-start | bytes 746504 | tf_op jit(solution)/shard_map/ppermute | solution.py:18
  599.1 108.6 %copy-start.42 = (f32[2,1152]{1,0:T(2,128)S(1)}, f32[2,1152]{1,0:T(2,128)}, u32[]{:S(2)}) copy-start(f32[2,1152]{1,0:T(2,128)} %param.15) | copy-start | bytes 27652
  599.1 109.2 %copy-start.25 = (bf16[144,864]{1,0:T(8,128)(2,1)S(1)}, bf16[144,864]{1,0:T(8,128)(2,1)}, u32[]{:S(2)}) copy-start(bf16[144,864]{1,0:T(8,128)(2,1)} %reduce-scatter.5.cloned.1.call-done) | copy-start | bytes 746500
  599.2 121.0 %collective-permute-start.17 = (bf16[144,864]{1,0:T(8,128)(2,1)}, bf16[144,864]{1,0:T(8,128)(2,1)}, u32[]{:S(2)}, u32[]{:S(2)}) collective-permute-start(bf16[144,864]{1,0:T(8,128)(2,1)} %reduce-scatter.5.cloned.1.call-done), channel_id=1, source_target_pairs={{0,1},{1,0},{2,3},{3,2},{4,5},{5,4},{6,7},{7,6},{8,9},{9,8},{10,11... | collective-permute-start | bytes 746504 | tf_op jit(solution)/shard_map/ppermute | solution.py:18
  608.9 138.1 %collective-permute-start.19 = (bf16[144,864]{1,0:T(8,128)(2,1)}, bf16[144,864]{1,0:T(8,128)(2,1)}, u32[]{:S(2)}, u32[]{:S(2)}) collective-permute-start(bf16[144,864]{1,0:T(8,128)(2,1)} %collective-permute-done.18), channel_id=1, source_target_pairs={{0,1},{1,0},{2,3},{3,2},{4,5},{5,4},{6,7},{7,6},{8,9},{9,8},{10,11... | collective-permute-start | bytes 746504 | tf_op jit(solution)/shard_map/ppermute | solution.py:18
  703.9 64.3 %all-to-all-start.7 = ((bf16[4,144,2,288]{3,2,1,0:T(2,128)(2,1)}), bf16[4,144,2,288]{3,2,1,0:T(2,128)(2,1)S(1)}, u32[]{:S(2)}, u32[]{:S(2)}) async-start(bf16[4,144,2,288]{3,2,1,0:T(2,128)(2,1)} %bitcast.194), calls=%async_computation.10 | async-start | bytes 1769472 | tf_op jit(solution)/shard_map/all_to_all | solution.py:352
  (42 other events, 219.6 us)
Sparse Core Ops, SparseCore 0:
  10.8 46.4 all-gather.6
  60.0 48.1 all-gather.4
  110.3 85.5 all-gather.8
  197.9 85.2 all-gather.10
  345.2 68.7 reduce-scatter.6
  417.8 103.2 reduce-scatter.10
  524.7 67.5 reduce-scatter.4
  595.8 103.1 reduce-scatter.8

commit v2 on v1

v2 whole, which is shorter than its diff:
```python
import math
from functools import partial

import jax
import jax.numpy as jnp
from jax import lax
from jax.experimental import pallas as pl
from jax.experimental.pallas import tpu as pltpu
from jax.sharding import PartitionSpec as P

HEADS = 16
HEAD_DIM = 72
BF = jnp.bfloat16
F32 = jnp.float32
GELU_C = 0.7978845608028654
GELU_A = 0.044715
EXP2_SCALE = HEAD_DIM ** (-0.5) * math.log2(math.e)


def hop(value, axis, bits):
    count = lax.axis_size(axis)
    return lax.ppermute(value, axis, [(i, i ^ bits) for i in range(count)])


def matmul(left, right):
    return jnp.dot(left, right, preferred_element_type=F32)


def matmul_nt(left, right):
    return lax.dot_general(left, right, (((1,), (1,)), ((), ())), preferred_element_type=F32)


def matmul_tn(left, right):
    return lax.dot_general(left, right, (((0,), (0,)), ((), ())), preferred_element_type=F32)


def ln_parts(values):
    row_mean = jnp.mean(values, axis=-1, keepdims=True)
    centred = values - row_mean
    row_var = jnp.mean(centred * centred, axis=-1, keepdims=True)
    inv_std = lax.rsqrt(row_var + 1e-06)
    return centred * inv_std, inv_std


def ln_backward(grad, normed, inv_std):
    mean_grad = jnp.mean(grad, axis=-1, keepdims=True)
    mean_inner = jnp.mean(grad * normed, axis=-1, keepdims=True)
    return (grad - mean_grad - normed * mean_inner) * inv_std


def seq_gather(mine):
    slots = {0: mine}
    bit = lax.axis_size("seq") // 2
    while bit:
        for j in list(slots):
            slots[j | bit] = hop(slots[j], "seq", bit)
        bit //= 2
    return [slots[j] for j in range(len(slots))]


def seq_reduce(slots):
    slots = dict(enumerate(slots))
    bit = 1
    while len(slots) > 1:
        for j in [j for j in slots if j & bit]:
            slots[j ^ bit] = slots[j ^ bit] + hop(slots.pop(j).astype(BF), "seq", bit).astype(F32)
        bit *= 2
    return slots[0]


def seq_exchange(blocks):
    return [blocks[0]] + [hop(blocks[j], "seq", j) for j in range(1, len(blocks))]


def dp_exchange(value):
    return lax.all_to_all(value, "dp", 0, 0, tiled=True)


def dp_gather(mine, place):
    count = lax.axis_size("dp")
    index = lax.axis_index("dp")
    slots = {0: mine}
    for j in range(2, count, 2):
        slots[j] = hop(mine, "dp", j)
    for j in range(0, count, 2):
        slots[j + 1] = hop(slots[j], "dp", 1)
    whole = jnp.zeros((count,) + mine.shape, mine.dtype)
    for j in range(count):
        whole = lax.dynamic_update_index_in_dim(whole, slots[j], place(index ^ j), 0)
    return whole


def dp_scatter(terms, place):
    count = lax.axis_size("dp")
    index = lax.axis_index("dp")

    def block(j):
        return lax.dynamic_index_in_dim(terms, place(index ^ j), 0, keepdims=False)

    half = {}
    for j in list(range(2, count, 2)) + [0]:
        half[j] = block(j).astype(F32) + hop(block(j + 1), "dp", 1).astype(F32)
    total = half[0]
    for j in range(2, count, 2):
        total = total + hop(half[j].astype(BF), "dp", j).astype(F32)
    return total


def attend_kernel(heads, block, packed, mixed, log_sum, mixed_t):
    seq_len = packed.shape[1]
    cols = heads * HEAD_DIM
    for h in range(heads):
        at = h * HEAD_DIM
        keys = packed[0, :, cols + at : cols + at + HEAD_DIM]
        values_t = packed[0, :, 2 * cols + at : 2 * cols + at + HEAD_DIM].astype(F32).T.astype(BF)
        for start in range(0, seq_len, block):
            queries = packed[0, start : start + block, at : at + HEAD_DIM]
            scores = matmul_nt(keys, queries)
            top = jnp.max(scores, axis=0, keepdims=True)
            exponent = jnp.exp2((scores - top) * EXP2_SCALE)
            total = jnp.sum(exponent, axis=0, keepdims=True)
            part = matmul(values_t, exponent.astype(BF)) / total
            mixed_t[at : at + HEAD_DIM, start : start + block] = part
            log_sum[0, h : h + 1, start : start + block] = top * EXP2_SCALE + jnp.log2(total)
    mixed[0] = mixed_t[...].T.astype(BF)


def attend_grad_kernel(heads, block, packed, mixed, log_sum, d_mixed, d_packed, d_queries_t):
    seq_len = packed.shape[1]
    cols = heads * HEAD_DIM
    inv_root = HEAD_DIM ** (-0.5)
    for h in range(heads):
        at = h * HEAD_DIM
        keys = packed[0, :, cols + at : cols + at + HEAD_DIM]
        values = packed[0, :, 2 * cols + at : 2 * cols + at + HEAD_DIM]
        keys_t = keys.astype(F32).T.astype(BF)
        d_keys = d_values = None
        for start in range(0, seq_len, block):
            queries = packed[0, start : start + block, at : at + HEAD_DIM]
            grads = d_mixed[0, start : start + block, at : at + HEAD_DIM]
            outs = mixed[0, start : start + block, at : at + HEAD_DIM]
            inner = jnp.sum(grads.astype(F32) * outs.astype(F32), axis=1, keepdims=True)
            inner = jnp.broadcast_to(inner, (block, 128)).T[0:1]
            scores = matmul_nt(keys, queries)
            probs = jnp.exp2(scores * EXP2_SCALE - log_sum[0, h : h + 1, start : start + block])
            d_probs = matmul_nt(values, grads)
            d_scores = (probs * (d_probs - inner)).astype(BF)
            d_v = matmul(probs.astype(BF), grads)
            d_k = matmul(d_scores, queries)
            d_values = d_v if d_values is None else d_values + d_v
            d_keys = d_k if d_keys is None else d_keys + d_k
            d_queries_t[at : at + HEAD_DIM, start : start + block] = matmul(keys_t, d_scores) * inv_root
        d_packed[0, :, cols + at : cols + at + HEAD_DIM] = (d_keys * inv_root).astype(BF)
        d_packed[0, :, 2 * cols + at : 2 * cols + at + HEAD_DIM] = d_values.astype(BF)
    d_packed[0, :, 0:cols] = d_queries_t[...].T.astype(BF)


def row_spec(*shape):
    return pl.BlockSpec((1,) + shape, lambda i: (i, 0, 0))


def attention(packed, heads, block=512):
    lat, seq_len, _ = packed.shape
    cols = heads * HEAD_DIM
    return pl.pallas_call(
        partial(attend_kernel, heads, block),
        grid=(lat,),
        in_specs=[row_spec(seq_len, 3 * cols)],
        out_specs=[row_spec(seq_len, cols), row_spec(heads, seq_len)],
        out_shape=[
            jax.ShapeDtypeStruct((lat, seq_len, cols), BF),
            jax.ShapeDtypeStruct((lat, heads, seq_len), F32),
        ],
        scratch_shapes=[pltpu.VMEM((cols, seq_len), F32)],
        compiler_params=pltpu.CompilerParams(vmem_limit_bytes=48 * 2**20),
        name="attend",
    )(packed)


def attention_grad(packed, mixed, log_sum, d_mixed, heads, block=512):
    lat, seq_len, _ = packed.shape
    cols = heads * HEAD_DIM
    return pl.pallas_call(
        partial(attend_grad_kernel, heads, block),
        grid=(lat,),
        in_specs=[
            row_spec(seq_len, 3 * cols),
            row_spec(seq_len, cols),
            row_spec(heads, seq_len),
            row_spec(seq_len, cols),
        ],
        out_specs=row_spec(seq_len, 3 * cols),
        out_shape=jax.ShapeDtypeStruct((lat, seq_len, 3 * cols), BF),
        scratch_shapes=[pltpu.VMEM((cols, seq_len), F32)],
        compiler_params=pltpu.CompilerParams(vmem_limit_bytes=48 * 2**20),
        name="attend_grad",
    )(packed, mixed, log_sum, d_mixed)


def on_device(tokens, conditioning, w_mod, b_mod, w_qkv, w_proj, w_fc1, b_fc1, w_fc2, cotangent):
    lat, tok, width = tokens.shape
    seq_n = lax.axis_size("seq")
    dp_n = lax.axis_size("dp")
    seq = lax.axis_index("seq")
    dp = lax.axis_index("dp")
    core = seq % 2
    heads_here = HEADS // seq_n
    cols = heads_here * HEAD_DIM
    seq_len = tok * seq_n
    rows = w_qkv.shape[0]
    hid_here = w_fc2.shape[0] // 2
    hid = hid_here * dp_n
    every = ("dp", "seq")
    n_all = dp_n * seq_n
    groups = 2
    per = lat // groups
    own = per * tok

    cond_silu, silu_back = jax.vjp(jax.nn.silu, conditioning)
    cond_act = cond_silu.astype(BF)
    bias_half = lax.dynamic_slice(b_fc1, (core * hid_here,), (hid_here,))
    small = jnp.concatenate(
        [
            cond_act.reshape(lat, dp_n, rows).transpose(1, 0, 2).reshape(dp_n, lat * rows),
            jnp.broadcast_to(bias_half[None], (dp_n, hid_here)),
        ],
        axis=1,
    )
    small = dp_exchange(small)
    cond_rows = small[:, : lat * rows].reshape(dp_n * lat, rows)
    fc1_bias = small[:, lat * rows :].reshape(hid).astype(F32)
    mod_terms = matmul(cond_rows, w_mod)
    piece = b_mod.shape[0]
    mod_terms = lax.dynamic_update_slice(
        mod_terms,
        lax.dynamic_slice(mod_terms, (0, dp * piece), (dp_n * lat, piece))
        + b_mod.astype(F32)[None],
        (0, dp * piece),
    )
    modulation = jnp.sum(dp_exchange(mod_terms.reshape(dp_n, lat, 6 * width)), axis=0)

    tok_slots = seq_gather(tokens)

    qkv_here = lax.dynamic_index_in_dim(
        w_qkv.reshape(rows, 3, seq_n, cols), seq, axis=2, keepdims=False
    ).reshape(rows, 3 * cols)
    qkv = dp_gather(qkv_here, lambda d: d).reshape(width, 3 * cols)
    fc1_here = lax.dynamic_index_in_dim(
        w_fc1.reshape(rows, dp_n, 2, hid_here), core, axis=2, keepdims=False
    ).reshape(rows, hid)
    fc1 = lax.all_gather(fc1_here, "dp", axis=0, tiled=True)
    fc2 = lax.all_gather(
        lax.dynamic_slice(w_fc2, (core * hid_here, 0), (hid_here, width)), "dp", axis=0, tiled=True
    )
    ratio = cols // rows
    half = rows // 2

    def proj_place(d):
        return ((d // ratio) ^ seq) * ratio + d % ratio

    def flip(halves):
        return halves.reshape(seq_n // 2, 2, ratio * half, width)[:, ::-1].reshape(
            dp_n, half, width
        )

    proj_mine = dp_gather(lax.dynamic_slice(w_proj, (core * half, 0), (half, width)), proj_place)
    proj_other = flip(hop(proj_mine, "seq", 1))
    proj = jnp.where(
        core == 0,
        jnp.stack([proj_mine, proj_other], axis=1),
        jnp.stack([proj_other, proj_mine], axis=1),
    ).reshape(width, width)

    def part(g):
        return slice(g * per, (g + 1) * per)

    shift_attn, scale_attn, gate_attn, shift_mlp, scale_mlp, gate_mlp = [
        [modulation[part(g), None, i * width : (i + 1) * width] for g in range(groups)]
        for i in range(6)
    ]
    token_values = [tokens[part(g)].astype(F32) for g in range(groups)]
    normed_all, packed, mixed, log_sums, attended = [], [], [], [], []
    for g in range(groups):
        tok_all = jnp.concatenate([slot[part(g)] for slot in tok_slots], axis=1).astype(F32)
        normed = (ln_parts(tok_all)[0] * (1.0 + scale_attn[g]) + shift_attn[g]).astype(BF)
        normed_all.append(normed.reshape(per * seq_len, width))
        packed.append(matmul(normed_all[g], qkv).astype(BF).reshape(per, seq_len, 3 * cols))
        out, log_sum = attention(packed[g], heads_here)
        mixed.append(out)
        log_sums.append(log_sum)
        out = out.reshape(per, seq_n, tok, cols)
        attended.append(
            jnp.concatenate(seq_exchange([out[:, j] for j in range(seq_n)]), axis=2).reshape(
                own, width
            )
        )

    attn_out, resid_mid, normed_mid, std_mid, normed_mlp, upstream, d_mlp = ([] for _ in range(7))
    for g in range(groups):
        attn_out.append(matmul(attended[g], proj).reshape(per, tok, width))
        resid_mid.append(token_values[g] + gate_attn[g] * attn_out[g])
        normed, inv_std = ln_parts(resid_mid[g])
        normed_mid.append(normed)
        std_mid.append(inv_std)
        normed_mlp.append(
            (normed * (1.0 + scale_mlp[g]) + shift_mlp[g]).astype(BF).reshape(own, width)
        )
        upstream.append(cotangent[part(g)].astype(F32))
        d_mlp.append((gate_mlp[g] * upstream[g]).astype(BF).reshape(own, width))
    d_mlp_pair = jnp.concatenate(d_mlp + [hop(v, "seq", 1) for v in d_mlp])
    normed_pair = jnp.concatenate(normed_mlp + [hop(v, "seq", 1) for v in normed_mlp])

    hidden = matmul(normed_pair, fc1) + fc1_bias
    tanh = jnp.tanh(GELU_C * (hidden + GELU_A * hidden * hidden * hidden))
    activated = (0.5 * hidden * (1.0 + tanh)).astype(BF)
    gelu_slope = 0.5 * (1.0 + tanh) + 0.5 * hidden * (1.0 - tanh * tanh) * GELU_C * (
        1.0 + 3.0 * GELU_A * hidden * hidden
    )
    d_hidden = (matmul_nt(d_mlp_pair, fc2) * gelu_slope).astype(BF)
    grad_fc2 = matmul_tn(activated, d_mlp_pair).astype(BF)
    sum_fc2 = lax.psum_scatter(grad_fc2, "dp", scatter_dimension=0, tiled=True)
    d_norm_part = matmul_nt(d_hidden, fc1)
    d_norm_sent = [
        hop(d_norm_part[(groups + g) * own : (groups + g + 1) * own].astype(BF), "seq", 1)
        for g in range(groups)
    ]
    grad_fc1 = matmul_tn(normed_pair, d_hidden).astype(BF)
    sum_fc1 = lax.psum_scatter(grad_fc1, "dp", scatter_dimension=0, tiled=True)
    grad_bias1 = jnp.sum(d_hidden.astype(F32), axis=0)
    mlp_part = matmul(activated, fc2)
    mlp_sent = hop(mlp_part[groups * own :].astype(BF), "seq", 1)
    mlp_out = mlp_part[: groups * own] + mlp_sent.astype(F32)
    mlp_out = mlp_out.reshape(groups, per, tok, width)
    output = jnp.concatenate(
        [(resid_mid[g] + gate_mlp[g] * mlp_out[g]).astype(BF) for g in range(groups)]
    )

    def stacked(terms):
        return jnp.concatenate(terms)

    d_gate_mlp = stacked([jnp.sum(upstream[g] * mlp_out[g], axis=1) for g in range(groups)])
    d_shift_mlp, d_scale_mlp, d_gate_attn, d_resid, d_attn = ([] for _ in range(5))
    d_mixed = []
    for g in range(groups):
        d_norm = d_norm_part[g * own : (g + 1) * own] + d_norm_sent[g].astype(F32)
        d_norm = d_norm.reshape(per, tok, width)
        d_shift_mlp.append(jnp.sum(d_norm, axis=1))
        d_scale_mlp.append(jnp.sum(d_norm * normed_mid[g], axis=1))
        d_resid.append(
            upstream[g] + ln_backward(d_norm * (1.0 + scale_mlp[g]), normed_mid[g], std_mid[g])
        )
        d_gate_attn.append(jnp.sum(d_resid[g] * attn_out[g], axis=1))
        d_attn.append((gate_attn[g] * d_resid[g]).astype(BF).reshape(own, width))
        d_attended = matmul_nt(d_attn[g], proj).astype(BF).reshape(per, tok, width)
        d_mixed.append(
            jnp.concatenate(
                seq_exchange([d_attended[:, :, j * cols : (j + 1) * cols] for j in range(seq_n)]),
                axis=1,
            )
        )
    grad_proj = matmul_tn(stacked(attended), stacked(d_attn)).astype(BF)
    grad_proj = grad_proj.reshape(dp_n, 2, half, width)
    proj_sent = hop(
        lax.dynamic_index_in_dim(grad_proj, 1 - core, axis=1, keepdims=False), "seq", 1
    )
    proj_terms = lax.dynamic_index_in_dim(grad_proj, core, axis=1, keepdims=False).astype(F32)
    proj_terms = (proj_terms + flip(proj_sent).astype(F32)).astype(BF)
    sum_proj = dp_scatter(proj_terms, proj_place).astype(BF)

    d_packed, d_first = [], []
    for g in range(groups):
        d_packed.append(
            attention_grad(packed[g], mixed[g], log_sums[g], d_mixed[g], heads_here).reshape(
                per * seq_len, 3 * cols
            )
        )
        parts = matmul_nt(d_packed[g], qkv).reshape(per, seq_n, tok, width)
        d_first.append(seq_reduce([parts[:, j] for j in range(seq_n)]))
    grad_qkv = matmul_tn(stacked(normed_all), stacked(d_packed)).astype(BF)
    sum_qkv = dp_scatter(grad_qkv.reshape(dp_n, rows, 3 * cols), lambda d: d).astype(BF)
    d_shift_attn, d_scale_attn, grad_tokens = [], [], []
    for g in range(groups):
        normed_tok, std_tok = ln_parts(token_values[g])
        d_shift_attn.append(jnp.sum(d_first[g], axis=1))
        d_scale_attn.append(jnp.sum(d_first[g] * normed_tok, axis=1))
        grad_tokens.append(
            d_resid[g] + ln_backward(d_first[g] * (1.0 + scale_attn[g]), normed_tok, std_tok)
        )

    mod_part = jnp.concatenate(
        [stacked(d_shift_attn), stacked(d_scale_attn), stacked(d_gate_attn)]
        + [stacked(d_shift_mlp), stacked(d_scale_mlp), d_gate_mlp],
        axis=1,
    )
    share = 6 * width // n_all
    mod_cols = lax.all_to_all(
        mod_part.reshape(lat, n_all, share).transpose(1, 0, 2), every, 0, 0, tiled=True
    )
    d_mod = jnp.sum(mod_cols.reshape(dp_n, seq_n, lat, share), axis=1).reshape(dp_n * lat, share)
    d_mod = d_mod.astype(BF)
    cond_all = lax.all_to_all(
        jnp.broadcast_to(cond_act[None], (dp_n, lat, width)), "dp", 0, 0, tiled=True
    ).reshape(dp_n * lat, width)
    grad_wmod = matmul_tn(cond_all, d_mod)
    grad_bmod = jnp.sum(d_mod.astype(F32), axis=0)
    mod_rows = lax.all_to_all(
        jnp.broadcast_to(d_mod[None], (dp_n, dp_n * lat, share)), "dp", 0, 0, tiled=True
    )
    mod_here = mod_rows.transpose(1, 0, 2).reshape(dp_n * lat, dp_n * share)
    w_mod_here = lax.dynamic_index_in_dim(
        w_mod.reshape(rows, dp_n, seq_n, share), seq, axis=2, keepdims=False
    ).reshape(rows, dp_n * share)
    cond_terms = matmul_nt(mod_here, w_mod_here)
    cond_terms = jnp.broadcast_to(
        cond_terms.reshape(dp_n, 1, lat, rows), (dp_n, seq_n, lat, rows)
    ).reshape(n_all, lat, rows)
    cond_back = lax.all_to_all(cond_terms, every, 0, 0, tiled=True)
    d_cond = jnp.sum(cond_back.reshape(dp_n, seq_n, lat, rows), axis=1)
    (grad_cond,) = silu_back(d_cond.transpose(1, 0, 2).reshape(lat, width))

    spread = jnp.zeros((dp_n, 2, hid_here), F32)
    spread = lax.dynamic_update_slice(spread, grad_bias1.reshape(dp_n, 1, hid_here), (0, core, 0))
    bias_cols = lax.all_to_all(
        spread.reshape(n_all, 2 * hid_here // seq_n), every, 0, 0, tiled=True
    )
    bias_out = jnp.sum(bias_cols, axis=0)

    def to_owner(blocks):
        received = lax.all_to_all(blocks, "seq", 0, 0, tiled=True).astype(F32)
        return jnp.sum(received.reshape((seq_n // 2, 2) + received.shape[1:]), axis=0)

    share = width // seq_n
    out_fc2 = to_owner(sum_fc2.reshape(hid_here, seq_n, share).transpose(1, 0, 2))
    out_fc2 = out_fc2.reshape(2 * hid_here, share)
    out_proj = to_owner(sum_proj.reshape(half, seq_n, share).transpose(1, 0, 2))
    out_proj = out_proj.reshape(rows, share)
    blocks = sum_fc1.reshape(rows, seq_n, dp_n // seq_n, hid_here).transpose(1, 0, 2, 3)
    out_fc1 = to_owner(blocks).transpose(1, 2, 0, 3).reshape(rows, 2 * hid // seq_n)
    qkv_slots = jnp.stack(
        seq_gather(sum_qkv.reshape(rows, 3, cols).transpose(1, 0, 2))
    ).reshape(3 * seq_n, rows, cols)
    out_qkv = []
    for i in range(3):
        block = 3 * seq + i
        at = ((block % seq_n) ^ seq) * 3 + block // seq_n
        out_qkv.append(lax.dynamic_index_in_dim(qkv_slots, at, 0, keepdims=False))
    out_qkv = jnp.concatenate(out_qkv, axis=1).astype(F32)
    return (
        output,
        stacked(grad_tokens),
        grad_cond,
        grad_wmod,
        grad_bmod,
        out_qkv,
        out_proj,
        out_fc1,
        bias_out,
        out_fc2,
    )


def solution(mesh):
    placed = (
        P("dp", "seq", None),
        P("dp", None),
        P("dp", None),
        P("dp"),
        P("dp", None),
        P("dp", None),
        P("dp", None),
        P("dp"),
        P("dp", None),
        P("dp", "seq", None),
    )
    return jax.shard_map(
        on_device,
        mesh=mesh,
        in_specs=placed,
        out_specs=(
            P("dp", "seq", None),
            P("dp", "seq", None),
            P("dp", None),
            P(None, ("dp", "seq")),
            P(("dp", "seq")),
            P("dp", "seq"),
            P("dp", "seq"),
            P("dp", "seq"),
            P(("dp", "seq")),
            P("dp", "seq"),
        ),
        check_vma=False,
    )
```

time: 788 us -> 647 us (0.82)
  waiting for transfers between devices: 254 us -> 150 us
  matrix products: 189 us -> 119 us
  starting transfers between devices: 50.2 us -> 109 us
  local copies, waits for them, and re-layouts: 173 us -> 132 us
  Pallas kernels: 0 us -> 38.8 us
  other arithmetic: 85.8 us -> 71.9 us
  blocking collectives: 10.5 us -> 0 us
    reduce_scatter x4 -> x2, waiting for transfers between devices: 90.2 us -> 0.02 us  [the longest x1 0.02 us: on_device(): sum_fc2 = lax.psum_scatter(grad_fc2, 'dp', scatter_dimension=0, tiled=True)]
    dot_general x14 -> x0, matrix products: 79.2 us -> none  [the longest x2 18.7 us: attend_backward(): jnp.einsum('qhd,khd->hqk', d_mixed, values, preferred_element_type=jnp.fl...]
    all_gather x4 -> x2, waiting for transfers between devices: 70.7 us -> 5.01 us  [the longest x1 4.98 us: on_device(): lax.all_gather(lax.dynamic_slice(w_fc2, (core * hid_here, 0), (hid_here,...]
    ppermute x20 -> x61, waiting for transfers between devices: 64.3 us -> 113 us  [hop(): return lax.ppermute(value, axis, [(i, i ^ bits) for i in range(count)])]
    ppermute x20 -> x61, starting transfers between devices: 12 us -> 56.5 us  [hop(): return lax.ppermute(value, axis, [(i, i ^ bits) for i in range(count)])]
    pallas_call x0 -> x4, Pallas kernels: none -> 38.8 us  [the longest x2 22.7 us: attention_grad(): pl.pallas_call(partial(attend_grad_kernel, heads, block), grid=(lat,), in...]
    dynamic_update_slice x8 -> x16, local copies, waits for them, and re-layouts: 44.2 us -> 15 us  [dp_gather(): lax.dynamic_update_index_in_dim(whole, slots[j], place(index ^ j), 0)]
    reshape x12 -> x6, local copies, waits for them, and re-layouts: 22.5 us -> 8.23 us  [the longest x2 3.4 us: on_device(): sum_fc2.reshape(hid_here, seq_n, share).transpose(1, 0, 2)]
  transfers between devices with their start and end apart: 37 -> 75, of which waited for: 18 -> 27; matrix products, arithmetic and copies ran while one was open for 49% -> 43% of each run, Pallas kernels for 0% -> 6%
where the time goes in v2:
time: 647 us; the launch traced here: 637 us
  waiting for transfers between devices  150 us (23%)
  local copies, waits for them, and re-layouts  132 us (20%)
  matrix products  119 us (18%)
  starting transfers between devices  109 us (17%)
  other arithmetic  71.9 us (11%)
  Pallas kernels  38.8 us (6%)
  between operations  16 us (2%)
    ppermute x61, waiting for transfers between devices, hop(): return lax.ppermute(value, axis, [(i, i ^ bits) for i in range(count)])  113 us
    ppermute x61, starting transfers between devices, hop(): return lax.ppermute(value, axis, [(i, i ^ bits) for i in range(count)])  56.5 us
    dot_general x7, matrix products, matmul_nt(): lax.dot_general(left, right, (((1,), (1,)), ((), ())), preferred_element_...  43.7 us
    dot_general x7, matrix products, matmul(): return jnp.dot(left, right, preferred_element_type=F32)  41.7 us
    dot_general x5, matrix products, matmul_tn(): lax.dot_general(left, right, (((0,), (0,)), ((), ())), preferred_element_...  33.8 us
    pallas_call x2, Pallas kernels, attention_grad(): pl.pallas_call(partial(attend_grad_kernel, heads, block), grid=(lat,), in...  22.7 us
    pallas_call x2, Pallas kernels, attention(): pl.pallas_call(partial(attend_kernel, heads, block), grid=(lat,), in_spec...  16.1 us
    dynamic_update_slice x16, local copies, waits for them, and re-layouts, dp_gather(): lax.dynamic_update_index_in_dim(whole, slots[j], place(index ^ j), 0)  15 us
  transfers between devices with their start and end apart: 75, of which 27 were waited for; matrix products, arithmetic and copies ran while one was open for 43% of the time, Pallas kernels for 6%

profile of v2, /device:TPU:0, one launch (start us, length us, event | category | flops | bytes accessed | tf_op | source)
XLA Modules:
  0.0 637.3 jit_solution(3315130954579915751)
XLA Ops:
  7.3 5.5 reshape.1004
  12.8 6.5 %dynamic-slice_reduce_fusion = bf16[144,8,288]{2,1,0:T(8,128)(2,1)} fusion(bf16[144,8,2,288]{3,2,1,0:T(2,128)(2,1)S(1)} %reshape.1004, s32[]{:T(128)S(6)} %select_n.284), kind=kLoop, calls=%fused_computation.54 | loop fusion | bytes 1327108 | tf_op jit(solution)/shard_map/jit(dynamic_index_in_dim)/dynamic_slice | solution.py:248
  19.3 2.7 reshape.1005
  23.9 2.9 collective-permute-start.13
  28.4 2.6 collective-permute-start.16
  33.5 4.9 all-to-all-start
  49.4 10.0 %all-to-all-done = bf16[8,2,288]{2,1,0:T(2,128)(2,1)S(1)} async-done(((bf16[8,2,288]{2,1,0:T(2,128)(2,1)}), bf16[8,2,288]{2,1,0:T(2,128)(2,1)S(1)}, u32[]{:S(2)}, u32[]{:S(2)}) %all-to-all-start) | async-done | bytes 9248 | tf_op jit(solution)/shard_map/all_to_all | solution.py:76
  63.4 5.6 all-to-all-start.1
  78.5 11.5 %collective-permute-done.4 = bf16[144,864]{1,0:T(8,128)(2,1)S(1)} collective-permute-done((bf16[144,864]{1,0:T(8,128)(2,1)S(1)}, bf16[144,864]{1,0:T(8,128)(2,1)S(1)}, u32[]{:S(2)}, u32[]{:S(2)}) %collective-permute-start.4) | collective-permute-done | bytes 248864 | tf_op jit(solution)/shard_map/ppermute | solution.py:22
  91.7 8.2 %collective-permute-done.15 = bf16[72,1152]{1,0:T(8,128)(2,1)S(1)} collective-permute-done((bf16[72,1152]{1,0:T(8,128)(2,1)}, bf16[72,1152]{1,0:T(8,128)(2,1)S(1)}, u32[]{:S(2)}, u32[]{:S(2)}) %collective-permute-start.15) | collective-permute-done | bytes 165920 | tf_op jit(solution)/shard_map/ppermute | solution.py:22
  105.1 4.6 collective-permute-done.17
  113.0 12.3 %collective-permute-done.6 = bf16[144,864]{1,0:T(8,128)(2,1)S(1)} collective-permute-done((bf16[144,864]{1,0:T(8,128)(2,1)S(1)}, bf16[144,864]{1,0:T(8,128)(2,1)S(1)}, u32[]{:S(2)}, u32[]{:S(2)}) %collective-permute-start.6) | collective-permute-done | bytes 248864 | tf_op jit(solution)/shard_map/ppermute | solution.py:22
  138.4 2.5 fusion.127
  141.0 2.5 fusion.126
  153.3 5.9 add_convert_fusion
  160.6 4.6 convert_bitcast_fusion.packed
  165.2 7.9 %attend.3 = (bf16[1,1024,288]{2,1,0:T(8,128)(2,1)S(1)}, f32[1,4,1024]{2,1,0:T(4,128)S(1)}) custom-call(bf16[1,1024,864]{2,1,0:T(8,128)(2,1)S(1)} %convert_bitcast_fusion.packed), custom_call_target="tpu_custom_call" | custom-call | tf_op jit(solution)/shard_map/attend/pallas_call | solution.py:165
  175.8 4.4 convert_bitcast_fusion.1.packed
  180.2 8.1 %attend.2 = (bf16[1,1024,288]{2,1,0:T(8,128)(2,1)S(1)}, f32[1,4,1024]{2,1,0:T(4,128)S(1)}) custom-call(bf16[1,1024,864]{2,1,0:T(8,128)(2,1)S(1)} %convert_bitcast_fusion.1.packed), custom_call_target="tpu_custom_call" | custom-call | tf_op jit(solution)/shard_map/attend/pallas_call | solution.py:165
  191.3 3.6 maximum_select_fusion
  202.6 3.1 fusion.113
  215.1 12.9 %fusion.89 = f32[1024,2304]{1,0:T(8,128)} fusion(bf16[1152,2304]{1,0:T(8,128)(2,1)} %all-gather.3.cloned.1.call-done, bf16[256,1152]{1,0:T(8,128)(2,1)} %collective-permute-done.25, bf16[256,1152]{1,0:T(8,128)(2,1)} %collective-permute-done.24, bf16[256,1152]{1,0:T(8,128)(2,1)} %fusion.77, bf16[256,1152]{1,0:T(8,128)(2,1)} %fusion.76), kind=kOutput, calls=%fused_computation.174 | convolution fusion | flops 5445255168 | bytes 17104896 | tf_op jit(solution)/shard_map/dot_general | solution.py:26
  228.0 5.0 all-gather.5.cloned.1.call-done
  232.9 16.2 %convert_reduce_fusion = (f32[2304]{0:T(1024)S(1)}, bf16[1024,2304]{1,0:T(8,128)(2,1)S(1)}) fusion(f32[1024,2304]{1,0:T(8,128)} %fusion.89, f32[2304]{0:T(1024)S(1)} %reshape.1046, bf16[2304,1152]{1,0:T(8,128)(2,1)} %all-gather.5.cloned.1.call-done, bf16[256,1152]{1,0:T(8,128)(2,1)} %collective-permute-done.28, ...), kind=kOutput, calls=%fused_computation.11 | convolution fusion | flops 5497157632 | bytes 21841920 | tf_op jit(solution)/shard_map/dot_general | solution.py:30
  251.4 9.1 %convolution_convert_fusion.1 = bf16[1152,2304]{1,0:T(8,128)(2,1)} fusion(bf16[1024,2304]{1,0:T(8,128)(2,1)S(1)} %get-tuple-element.143, bf16[256,1152]{1,0:T(8,128)(2,1)} %collective-permute-done.25, bf16[256,1152]{1,0:T(8,128)(2,1)} %collective-permute-done.24, bf16[256,1152]{1,0:T(8,128)(2,1)} %fusion.77, bf16[256,1152]{1,0:T(8,128)(2,1)} %fusion.76), kind=kOutput, calls=%fused_computation.3 | convolution fusion | flops 5447909376 | bytes 12386304 | tf_op jit(solution)/shard_map/dot_general | solution.py:34
  260.6 10.4 %reshape.1021 = bf16[144,8,4,216]{3,2,1,0:T(4,128)(2,1)} reshape(bf16[144,6912]{1,0:T(8,128)(2,1)} %param.12) | data formatting | bytes 3981312 | tf_op jit(solution)/shard_map/reshape | solution.py:411
  270.9 6.3 dynamic-slice_reduce_fusion.1
  277.2 2.5 reshape.1065
  280.9 12.5 %fusion.119 = f32[1024,1152]{1,0:T(8,128)S(1)} fusion(bf16[2304,1152]{1,0:T(8,128)(2,1)} %all-gather.5.cloned.1.call-done, f32[1024,2304]{1,0:T(8,128)} %fusion.89, f32[2304]{0:T(1024)S(1)} %reshape.1046), kind=kOutput, calls=%fused_computation.305 | convolution fusion | flops 5459410944 | bytes 19473408 | tf_op jit(solution)/shard_map/dot_general | solution.py:26
  296.6 11.4 %fusion.131 = (bf16[1024,1152]{1,0:T(8,128)(2,1)S(1)}, f32[1024,1152]{1,0:T(8,128)}) fusion(bf16[1024,2304]{1,0:T(8,128)(2,1)} %copy-done.85, bf16[1152,2304]{1,0:T(8,128)(2,1)} %all-gather.3.cloned.1.call-done), kind=kOutput, calls=%fused_computation.315 | convolution fusion | flops 5436997632 | bytes 17104896 | tf_op jit(solution)/shard_map/dot_general | solution.py:30
  310.5 9.9 %all-to-all-start.8 = ((f32[32,1,144]{2,1,0:T(1,128)}), f32[32,1,144]{2,1,0:T(1,128)S(1)}, u32[]{:S(2)}, u32[]{:S(2)}) async-start(f32[32,1,144]{2,1,0:T(1,128)} %all_to_all.48), calls=%async_computation.9 | async-start | bytes 65536 | tf_op jit(solution)/shard_map/all_to_all | solution.py:423
  320.6 14.7 %convolution_convert_fusion = bf16[2304,1152]{1,0:T(8,128)(2,1)} fusion(bf16[256,1152]{1,0:T(8,128)(2,1)} %collective-permute-done.28, bf16[256,1152]{1,0:T(8,128)(2,1)} %collective-permute-done.27, bf16[256,1152]{1,0:T(8,128)(2,1)} %get-tuple-element.100, bf16[256,1152]{1,0:T(8,128)(2,1)} %get-tuple-element.99, f32[1024,2304]{1,0:T(8,128)} %fusion.89, ...), kind=kOutput, calls=%fused_computation.2 | convolution fusion | flops 5471502336 | bytes 17114112 | tf_op jit(solution)/shard_map/dot_general | solution.py:34
  336.0 3.7 fusion.67
  352.5 4.5 collective-permute-done.31
  357.1 11.4 %attend_grad.2 = bf16[1,1024,864]{2,1,0:T(8,128)(2,1)S(1)} custom-call(bf16[1,1024,864]{2,1,0:T(8,128)(2,1)S(1)} %copy-done.3, bf16[1,1024,288]{2,1,0:T(8,128)(2,1)S(1)} %get-tuple-element.14.mixed, f32[1,4,1024]{2,1,0:T(4,128)S(1)} %get-tuple-element.16.log_sum, bf16[1,1024,288]{2,1,0:T(8,128)(2,1)S(1)} %pad_maximum_fusion.7.d_mixed), custom_call_target="tpu_custom_call" | custom-call | tf_op jit(solution)/shard_map/attend_grad/pallas_call | solution.py:183
  368.5 6.5 %fusion.132 = (bf16[1,4,256,1152]{3,2,1,0:T(8,128)(2,1)S(1)}, f32[1,4,256,1152]{3,2,1,0:T(8,128)}) fusion(bf16[4,256,864]{2,1,0:T(8,128)(2,1)S(1)} %bitcast.329, bf16[1152,864,1]{1,0,2:T(8,128)(2,1)} %bitcast.57), kind=kOutput, calls=%fused_computation.316 | convolution fusion | flops 2039611392 | bytes 10838016 | tf_op jit(solution)/shard_map/dot_general | solution.py:30
  390.9 3.6 collective-permute-done.38
  394.6 11.4 %attend_grad.3 = bf16[1,1024,864]{2,1,0:T(8,128)(2,1)S(1)} custom-call(bf16[1,1024,864]{2,1,0:T(8,128)(2,1)S(1)} %convert_bitcast_fusion.packed, bf16[1,1024,288]{2,1,0:T(8,128)(2,1)S(1)} %get-tuple-element.15.mixed, f32[1,4,1024]{2,1,0:T(4,128)S(1)} %get-tuple-element.17.log_sum, bf16[1,1024,288]{2,1,0:T(8,128)(2,1)S(1)} %pad_maximum_fusion.8.d_mixed), custom_call_target="tpu_custom_call" | custom-call | tf_op jit(solution)/shard_map/attend_grad/pallas_call | solution.py:183
  407.2 6.1 fusion.18
  413.3 4.2 copy.164
  422.8 6.3 fusion.133
  434.4 6.3 collective-permute-done.48
  440.7 9.2 %collective-permute-done.46 = bf16[144,864]{1,0:T(8,128)(2,1)S(1)} collective-permute-done((bf16[144,864]{1,0:T(8,128)(2,1)S(1)}, bf16[144,864]{1,0:T(8,128)(2,1)S(1)}, u32[]{:S(2)}, u32[]{:S(2)}) %collective-permute-start.46) | collective-permute-done | bytes 248864 | tf_op jit(solution)/shard_map/ppermute | solution.py:22
  450.1 5.2 collective-permute-start.49
  458.3 4.2 collective-permute-done.49
  462.4 21.1 %collective-permute-done.47 = bf16[144,864]{1,0:T(8,128)(2,1)S(1)} collective-permute-done((bf16[144,864]{1,0:T(8,128)(2,1)S(1)}, bf16[144,864]{1,0:T(8,128)(2,1)S(1)}, u32[]{:S(2)}, u32[]{:S(2)}) %collective-permute-start.47) | collective-permute-done | bytes 248864 | tf_op jit(solution)/shard_map/ppermute | solution.py:22
  488.6 11.5 %collective-permute-done.35 = bf16[1,256,1152]{2,1,0:T(8,128)(2,1)} collective-permute-done((bf16[1,256,1152]{2,1,0:T(8,128)(2,1)}, bf16[1,256,1152]{2,1,0:T(8,128)(2,1)}, u32[]{:S(2)}, u32[]{:S(2)}) %collective-permute-start.35) | collective-permute-done | bytes 589856 | tf_op jit(solution)/shard_map/ppermute | solution.py:22
  501.5 3.4 fusion.46
  505.5 3.9 collective-permute-done.51
  520.3 3.5 collective-permute-start.55
  526.1 4.4 fusion.40
  531.5 7.9 %all-to-all-start.2 = ((f32[32,2,216]{2,1,0:T(2,128)}), f32[32,2,216]{2,1,0:T(2,128)S(1)}, u32[]{:S(2)}, u32[]{:S(2)}) async-start(f32[32,2,216]{2,1,0:T(2,128)} %copy.156), calls=%async_computation.2 | async-start | bytes 131072 | tf_op jit(solution)/shard_map/all_to_all | solution.py:396
  541.9 4.9 all-to-all-done.2
  547.5 4.0 all-to-all-start.3
  553.3 3.7 collective-permute-start.60
  559.8 5.2 all-to-all-start.5
  570.0 3.4 all-to-all-done.5
  574.7 3.3 all-to-all-start.4
  585.3 4.3 all-to-all-start.6
  591.8 3.3 reshape.1037
  596.7 3.5 all-to-all-start.7
  608.8 4.0 all-to-all-done.7
  612.8 3.5 all-to-all-start.9
  622.0 7.0 %all-to-all-done.9 = bf16[4,288,288]{2,1,0:T(8,128)(2,1)S(1)} async-done(((bf16[4,288,288]{2,1,0:T(8,128)(2,1)}), bf16[4,288,288]{2,1,0:T(8,128)(2,1)S(1)}, u32[]{:S(2)}, u32[]{:S(2)}) %all-to-all-start.9) | async-done | bytes 663584 | tf_op jit(solution)/shard_map/all_to_all | solution.py:429
  (464 shorter events, 202.3 us)
Async XLA Ops:
  7.2 207.9 %all-gather.3.cloned.1.call-start = ((), (), s32[]{:S(2)}) async-start(), calls=%async_computation.12 | async-start | bytes 5971968 | tf_op jit(solution)/shard_map/all_gather | solution.py:251
  23.9 45.2 %collective-permute-start.13 = (bf16[72,1152]{1,0:T(8,128)(2,1)}, bf16[72,1152]{1,0:T(8,128)(2,1)}, u32[]{:S(2)}, u32[]{:S(2)}) collective-permute-start(bf16[72,1152]{1,0:T(8,128)(2,1)} %get-tuple-element.66), channel_id=1, source_target_pairs={{0,4},{4,0},{8,12},{12,8},{16,20},{20,16},{24,28},{28,24},{1,5},{5... | collective-permute-start | bytes 497672 | tf_op jit(solution)/shard_map/ppermute | solution.py:22
  26.9 45.9 %collective-permute-start.14 = (bf16[72,1152]{1,0:T(8,128)(2,1)}, bf16[72,1152]{1,0:T(8,128)(2,1)}, u32[]{:S(2)}, u32[]{:S(2)}) collective-permute-start(bf16[72,1152]{1,0:T(8,128)(2,1)} %get-tuple-element.66), channel_id=1, source_target_pairs={{0,8},{4,12},{8,0},{12,4},{16,24},{20,28},{24,16},{28,20},{1,9},{5... | collective-permute-start | bytes 497672 | tf_op jit(solution)/shard_map/ppermute | solution.py:22
  28.4 62.3 %collective-permute-start.16 = (bf16[72,1152]{1,0:T(8,128)(2,1)}, bf16[72,1152]{1,0:T(8,128)(2,1)}, u32[]{:S(2)}, u32[]{:S(2)}) collective-permute-start(bf16[72,1152]{1,0:T(8,128)(2,1)} %get-tuple-element.66), channel_id=1, source_target_pairs={{0,16},{4,20},{8,24},{12,28},{16,0},{20,4},{24,8},{28,12},{1,17},{... | collective-permute-start | bytes 497672 | tf_op jit(solution)/shard_map/ppermute | solution.py:22
  31.0 71.8 %collective-permute-start.18 = (bf16[72,1152]{1,0:T(8,128)(2,1)}, bf16[72,1152]{1,0:T(8,128)(2,1)}, u32[]{:S(2)}, u32[]{:S(2)}) collective-permute-start(bf16[72,1152]{1,0:T(8,128)(2,1)} %get-tuple-element.66), channel_id=1, source_target_pairs={{0,24},{4,28},{8,16},{12,20},{16,8},{20,12},{24,0},{28,4},{1,25},{... | collective-permute-start | bytes 497672 | tf_op jit(solution)/shard_map/ppermute | solution.py:22
  33.5 25.9 %all-to-all-start = ((bf16[8,2,288]{2,1,0:T(2,128)(2,1)}), bf16[8,2,288]{2,1,0:T(2,128)(2,1)S(1)}, u32[]{:S(2)}, u32[]{:S(2)}) async-start(bf16[8,2,288]{2,1,0:T(2,128)(2,1)} %reshape.1084), calls=%async_computation | async-start | bytes 24576 | tf_op jit(solution)/shard_map/all_to_all | solution.py:76
  38.4 194.6 %all-gather.5.cloned.1.call-start = ((), (), s32[]{:S(2)}) async-start(), calls=%async_computation.13 | async-start | bytes 5971968 | tf_op jit(solution)/shard_map/all_gather | solution.py:252
  38.7 97.4 %collective-permute-start.1 = (bf16[2,256,1152]{2,1,0:T(8,128)(2,1)S(1)}, bf16[2,256,1152]{2,1,0:T(8,128)(2,1)}, u32[]{:S(2)}, u32[]{:S(2)}) collective-permute-start(bf16[2,256,1152]{2,1,0:T(8,128)(2,1)S(1)} %copy-done.10), channel_id=1, source_target_pairs={{0,2},{1,3},{2,0},{3,1},{4,6},{5,7},{6,4},{7,5},{8,10},{9,11},{10,... | collective-permute-start | bytes 3538952 | tf_op jit(solution)/shard_map/ppermute | solution.py:22
  63.4 74.7 %all-to-all-start.1 = ((f32[8,2,6912]{2,1,0:T(2,128)}), f32[8,2,6912]{2,1,0:T(2,128)S(1)}, u32[]{:S(2)}, u32[]{:S(2)}) async-start(f32[8,2,6912]{2,1,0:T(2,128)} %reshape.991), calls=%async_computation.1 | async-start | bytes 884736 | tf_op jit(solution)/shard_map/all_to_all | solution.py:76
  69.1 522.8 %reduce-scatter.3.cloned.1.call-start = ((), (), s32[]{:S(2)}) async-start(), calls=%async_computation.14 | async-start | bytes 5971968 | tf_op jit(solution)/shard_map/reduce_scatter | solution.py:328
  72.7 17.3 %collective-permute-start.4 = (bf16[144,864]{1,0:T(8,128)(2,1)S(1)}, bf16[144,864]{1,0:T(8,128)(2,1)S(1)}, u32[]{:S(2)}, u32[]{:S(2)}) collective-permute-start(bf16[144,864]{1,0:T(8,128)(2,1)S(1)} %reshape.993), channel_id=1, source_target_pairs={{0,8},{4,12},{8,0},{12,4},{16,24},{20,28},{24,16},{28,20},{1,9},{5... | collective-permute-start | bytes 746504 | tf_op jit(solution)/shard_map/ppermute | solution.py:22
  77.8 63.2 %collective-permute-start = (bf16[2,256,1152]{2,1,0:T(8,128)(2,1)S(1)}, bf16[2,256,1152]{2,1,0:T(8,128)(2,1)}, u32[]{:S(2)}, u32[]{:S(2)}) collective-permute-start(bf16[2,256,1152]{2,1,0:T(8,128)(2,1)S(1)} %copy-done.10), channel_id=1, source_target_pairs={{0,1},{1,0},{2,3},{3,2},{4,5},{5,4},{6,7},{7,6},{8,9},{9,8},{10,11... | collective-permute-start | bytes 3538952 | tf_op jit(solution)/shard_map/ppermute | solution.py:22
  90.0 9.9 %collective-permute-start.15 = (bf16[72,1152]{1,0:T(8,128)(2,1)}, bf16[72,1152]{1,0:T(8,128)(2,1)S(1)}, u32[]{:S(2)}, u32[]{:S(2)}) collective-permute-start(bf16[72,1152]{1,0:T(8,128)(2,1)} %collective-permute-done.14), channel_id=1, source_target_pairs={{0,4},{4,0},{8,12},{12,8},{16,20},{20,16},{24,28},{28,24},{1,5},{5... | collective-permute-start | bytes 497672 | tf_op jit(solution)/shard_map/ppermute | solution.py:22
  90.8 34.5 %collective-permute-start.6 = (bf16[144,864]{1,0:T(8,128)(2,1)S(1)}, bf16[144,864]{1,0:T(8,128)(2,1)S(1)}, u32[]{:S(2)}, u32[]{:S(2)}) collective-permute-start(bf16[144,864]{1,0:T(8,128)(2,1)S(1)} %reshape.993), channel_id=1, source_target_pairs={{0,16},{4,20},{8,24},{12,28},{16,0},{20,4},{24,8},{28,12},{1,17},{... | collective-permute-start | bytes 746504 | tf_op jit(solution)/shard_map/ppermute | solution.py:22
  99.9 9.8 %collective-permute-start.17 = (bf16[72,1152]{1,0:T(8,128)(2,1)}, bf16[72,1152]{1,0:T(8,128)(2,1)S(1)}, u32[]{:S(2)}, u32[]{:S(2)}) collective-permute-start(bf16[72,1152]{1,0:T(8,128)(2,1)} %collective-permute-done.16), channel_id=1, source_target_pairs={{0,4},{4,0},{8,12},{12,8},{16,20},{20,16},{24,28},{28,24},{1,5},{5... | collective-permute-start | bytes 497672 | tf_op jit(solution)/shard_map/ppermute | solution.py:22
  102.8 24.7 %collective-permute-start.8 = (bf16[144,864]{1,0:T(8,128)(2,1)S(1)}, bf16[144,864]{1,0:T(8,128)(2,1)S(1)}, u32[]{:S(2)}, u32[]{:S(2)}) collective-permute-start(bf16[144,864]{1,0:T(8,128)(2,1)S(1)} %reshape.993), channel_id=1, source_target_pairs={{0,24},{4,28},{8,16},{12,20},{16,8},{20,12},{24,0},{28,4},{1,25},{... | collective-permute-start | bytes 746504 | tf_op jit(solution)/shard_map/ppermute | solution.py:22
  109.7 17.8 %collective-permute-start.19 = (bf16[72,1152]{1,0:T(8,128)(2,1)}, bf16[72,1152]{1,0:T(8,128)(2,1)S(1)}, u32[]{:S(2)}, u32[]{:S(2)}) collective-permute-start(bf16[72,1152]{1,0:T(8,128)(2,1)} %collective-permute-done.18), channel_id=1, source_target_pairs={{0,4},{4,0},{8,12},{12,8},{16,20},{20,16},{24,28},{28,24},{1,5},{5... | collective-permute-start | bytes 497672 | tf_op jit(solution)/shard_map/ppermute | solution.py:22
  127.6 9.8 %collective-permute-start.9 = (bf16[144,864]{1,0:T(8,128)(2,1)S(1)}, bf16[144,864]{1,0:T(8,128)(2,1)S(1)}, u32[]{:S(2)}, u32[]{:S(2)}) collective-permute-start(bf16[144,864]{1,0:T(8,128)(2,1)S(1)} %collective-permute-done.8), channel_id=1, source_target_pairs={{0,4},{4,0},{8,12},{12,8},{16,20},{20,16},{24,28},{28,24},{1,5},{5... | collective-permute-start | bytes 746504 | tf_op jit(solution)/shard_map/ppermute | solution.py:22
  131.8 11.7 %collective-permute-start.20 = (bf16[8,72,1152]{2,1,0:T(8,128)(2,1)}, bf16[8,72,1152]{2,1,0:T(8,128)(2,1)}, u32[]{:S(2)}, u32[]{:S(2)}) collective-permute-start(bf16[8,72,1152]{2,1,0:T(8,128)(2,1)} %bitcast_dynamic-update-slice_fusion.7), channel_id=1, source_target_pairs={{0,1},{1,0},{2,3},{3,2},{4,5},{5,4},{6,7},{7,6},{8,9},{9,8},{10,11... | collective-permute-start | bytes 3981320 | tf_op jit(solution)/shard_map/ppermute | solution.py:22
  136.0 9.9 %collective-permute-start.2 = (bf16[2,256,1152]{2,1,0:T(8,128)(2,1)}, bf16[2,256,1152]{2,1,0:T(8,128)(2,1)}, u32[]{:S(2)}, u32[]{:S(2)}) collective-permute-start(bf16[2,256,1152]{2,1,0:T(8,128)(2,1)} %collective-permute-done.1), channel_id=1, source_target_pairs={{0,1},{1,0},{2,3},{3,2},{4,5},{5,4},{6,7},{7,6},{8,9},{9,8},{10,11... | collective-permute-start | bytes 3538952 | tf_op jit(solution)/shard_map/ppermute | solution.py:22
  174.0 17.3 %collective-permute-start.21 = (bf16[1,256,288]{2,1,0:T(8,128)(2,1)S(1)}, bf16[1,256,288]{2,1,0:T(8,128)(2,1)S(1)}, u32[]{:S(2)}, u32[]{:S(2)}) collective-permute-start(bf16[1,256,288]{2,1,0:T(8,128)(2,1)S(1)} %get-tuple-element.123), channel_id=1, source_target_pairs={{0,1},{1,0},{2,3},{3,2},{4,5},{5,4},{6,7},{7,6},{8,9},{9,8},{10,11... | collective-permute-start | bytes 442376 | tf_op jit(solution)/shard_map/ppermute | solution.py:22
  174.0 20.9 %collective-permute-start.22 = (bf16[1,256,288]{2,1,0:T(8,128)(2,1)S(1)}, bf16[1,256,288]{2,1,0:T(8,128)(2,1)S(1)}, u32[]{:S(2)}, u32[]{:S(2)}) collective-permute-start(bf16[1,256,288]{2,1,0:T(8,128)(2,1)S(1)} %get-tuple-element.122), channel_id=1, source_target_pairs={{0,2},{1,3},{2,0},{3,1},{4,6},{5,7},{6,4},{7,5},{8,10},{9,11},{10,... | collective-permute-start | bytes 442376 | tf_op jit(solution)/shard_map/ppermute | solution.py:22
  175.6 19.3 %collective-permute-start.23 = (bf16[1,256,288]{2,1,0:T(8,128)(2,1)S(1)}, bf16[1,256,288]{2,1,0:T(8,128)(2,1)S(1)}, u32[]{:S(2)}, u32[]{:S(2)}) collective-permute-start(bf16[1,256,288]{2,1,0:T(8,128)(2,1)S(1)} %get-tuple-element.121), channel_id=1, source_target_pairs={{0,3},{1,2},{2,1},{3,0},{4,7},{5,6},{6,5},{7,4},{8,11},{9,10},{10,... | collective-permute-start | bytes 442376 | tf_op jit(solution)/shard_map/ppermute | solution.py:22
  214.5 13.4 %collective-permute-start.28 = (bf16[256,1152]{1,0:T(8,128)(2,1)}, bf16[256,1152]{1,0:T(8,128)(2,1)}, u32[]{:S(2)}, u32[]{:S(2)}) collective-permute-start(bf16[256,1152]{1,0:T(8,128)(2,1)} %get-tuple-element.100), channel_id=1, source_target_pairs={{0,1},{1,0},{2,3},{3,2},{4,5},{5,4},{6,7},{7,6},{8,9},{9,8},{10,11... | collective-permute-start | bytes 1769480 | tf_op jit(solution)/shard_map/ppermute | solution.py:22
  215.0 12.9 %collective-permute-start.27 = (bf16[256,1152]{1,0:T(8,128)(2,1)}, bf16[256,1152]{1,0:T(8,128)(2,1)}, u32[]{:S(2)}, u32[]{:S(2)}) collective-permute-start(bf16[256,1152]{1,0:T(8,128)(2,1)} %get-tuple-element.99), channel_id=1, source_target_pairs={{0,1},{1,0},{2,3},{3,2},{4,5},{5,4},{6,7},{7,6},{8,9},{9,8},{10,11... | collective-permute-start | bytes 1769480 | tf_op jit(solution)/shard_map/ppermute | solution.py:22
  296.6 79.5 %collective-permute-start.26 = (bf16[512,1152]{1,0:T(8,128)(2,1)}, bf16[512,1152]{1,0:T(8,128)(2,1)}, u32[]{:S(2)}, u32[]{:S(2)}) collective-permute-start(bf16[512,1152]{1,0:T(8,128)(2,1)} %slice.396), channel_id=1, source_target_pairs={{0,1},{1,0},{2,3},{3,2},{4,5},{5,4},{6,7},{7,6},{8,9},{9,8},{10,11... | collective-permute-start | bytes 3538952 | tf_op jit(solution)/shard_map/ppermute | solution.py:22
  309.0 27.0 %collective-permute-start.29 = (bf16[256,1152]{1,0:T(8,128)(2,1)}, bf16[256,1152]{1,0:T(8,128)(2,1)}, u32[]{:S(2)}, u32[]{:S(2)}) collective-permute-start(bf16[256,1152]{1,0:T(8,128)(2,1)} %get-tuple-element.76), channel_id=1, source_target_pairs={{0,1},{1,0},{2,3},{3,2},{4,5},{5,4},{6,7},{7,6},{8,9},{9,8},{10,11... | collective-permute-start | bytes 1769480 | tf_op jit(solution)/shard_map/ppermute | solution.py:22
  309.5 26.6 %collective-permute-start.36 = (bf16[256,1152]{1,0:T(8,128)(2,1)}, bf16[256,1152]{1,0:T(8,128)(2,1)}, u32[]{:S(2)}, u32[]{:S(2)}) collective-permute-start(bf16[256,1152]{1,0:T(8,128)(2,1)} %get-tuple-element.75), channel_id=1, source_target_pairs={{0,1},{1,0},{2,3},{3,2},{4,5},{5,4},{6,7},{7,6},{8,9},{9,8},{10,11... | collective-permute-start | bytes 1769480 | tf_op jit(solution)/shard_map/ppermute | solution.py:22
  310.5 24.9 %all-to-all-start.8 = ((f32[32,1,144]{2,1,0:T(1,128)}), f32[32,1,144]{2,1,0:T(1,128)S(1)}, u32[]{:S(2)}, u32[]{:S(2)}) async-start(f32[32,1,144]{2,1,0:T(1,128)} %all_to_all.48), calls=%async_computation.9 | async-start | bytes 65536 | tf_op jit(solution)/shard_map/all_to_all | solution.py:423
  320.4 285.0 %reduce-scatter.5.cloned.1.call-start = ((), (), s32[]{:S(2)}) async-start(), calls=%async_computation.15 | async-start | bytes 5971968 | tf_op jit(solution)/shard_map/reduce_scatter | solution.py:321
  347.0 10.0 %collective-permute-start.31 = (bf16[1,256,288]{2,1,0:T(8,128)(2,1)S(1)}, bf16[1,256,288]{2,1,0:T(8,128)(2,1)S(1)}, u32[]{:S(2)}, u32[]{:S(2)}) collective-permute-start(bf16[1,256,288]{2,1,0:T(8,128)(2,1)S(1)} %get-tuple-element.131), channel_id=1, source_target_pairs={{0,2},{1,3},{2,0},{3,1},{4,6},{5,7},{6,4},{7,5},{8,10},{9,11},{10,... | collective-permute-start | bytes 442376 | tf_op jit(solution)/shard_map/ppermute | solution.py:22
  347.4 9.6 %collective-permute-start.30 = (bf16[1,256,288]{2,1,0:T(8,128)(2,1)S(1)}, bf16[1,256,288]{2,1,0:T(8,128)(2,1)S(1)}, u32[]{:S(2)}, u32[]{:S(2)}) collective-permute-start(bf16[1,256,288]{2,1,0:T(8,128)(2,1)S(1)} %get-tuple-element.132), channel_id=1, source_target_pairs={{0,1},{1,0},{2,3},{3,2},{4,5},{5,4},{6,7},{7,6},{8,9},{9,8},{10,11... | collective-permute-start | bytes 442376 | tf_op jit(solution)/shard_map/ppermute | solution.py:22
  376.1 79.2 %collective-permute-start.34 = (bf16[1,256,1152]{2,1,0:T(8,128)(2,1)}, bf16[1,256,1152]{2,1,0:T(8,128)(2,1)}, u32[]{:S(2)}, u32[]{:S(2)}) collective-permute-start(bf16[1,256,1152]{2,1,0:T(8,128)(2,1)} %get-tuple-element.74), channel_id=1, source_target_pairs={{0,1},{1,0},{2,3},{3,2},{4,5},{5,4},{6,7},{7,6},{8,9},{9,8},{10,11... | collective-permute-start | bytes 1769480 | tf_op jit(solution)/shard_map/ppermute | solution.py:22
  384.4 10.1 %collective-permute-start.38 = (bf16[1,256,288]{2,1,0:T(8,128)(2,1)S(1)}, bf16[1,256,288]{2,1,0:T(8,128)(2,1)S(1)}, u32[]{:S(2)}, u32[]{:S(2)}) collective-permute-start(bf16[1,256,288]{2,1,0:T(8,128)(2,1)S(1)} %get-tuple-element.127), channel_id=1, source_target_pairs={{0,2},{1,3},{2,0},{3,1},{4,6},{5,7},{6,4},{7,5},{8,10},{9,11},{10,... | collective-permute-start | bytes 442376 | tf_op jit(solution)/shard_map/ppermute | solution.py:22
  384.9 9.6 %collective-permute-start.37 = (bf16[1,256,288]{2,1,0:T(8,128)(2,1)S(1)}, bf16[1,256,288]{2,1,0:T(8,128)(2,1)S(1)}, u32[]{:S(2)}, u32[]{:S(2)}) collective-permute-start(bf16[1,256,288]{2,1,0:T(8,128)(2,1)S(1)} %get-tuple-element.128), channel_id=1, source_target_pairs={{0,1},{1,0},{2,3},{3,2},{4,5},{5,4},{6,7},{7,6},{8,9},{9,8},{10,11... | collective-permute-start | bytes 442376 | tf_op jit(solution)/shard_map/ppermute | solution.py:22
  419.0 13.2 %collective-permute-start.44 = (bf16[144,864]{1,0:T(8,128)(2,1)S(1)}, bf16[144,864]{1,0:T(8,128)(2,1)S(1)}, u32[]{:S(2)}, u32[]{:S(2)}) collective-permute-start(bf16[144,864]{1,0:T(8,128)(2,1)S(1)} %get-tuple-element.80), channel_id=1, source_target_pairs={{0,4},{4,0},{8,12},{12,8},{16,20},{20,16},{24,28},{28,24},{1,5},{5... | collective-permute-start | bytes 746504 | tf_op jit(solution)/shard_map/ppermute | solution.py:22
  420.7 20.0 %collective-permute-start.48 = (bf16[144,864]{1,0:T(8,128)(2,1)S(1)}, bf16[144,864]{1,0:T(8,128)(2,1)S(1)}, u32[]{:S(2)}, u32[]{:S(2)}) collective-permute-start(bf16[144,864]{1,0:T(8,128)(2,1)S(1)} %get-tuple-element.78), channel_id=1, source_target_pairs={{0,4},{4,0},{8,12},{12,8},{16,20},{20,16},{24,28},{28,24},{1,5},{5... | collective-permute-start | bytes 746504 | tf_op jit(solution)/shard_map/ppermute | solution.py:22
  421.1 28.9 %collective-permute-start.46 = (bf16[144,864]{1,0:T(8,128)(2,1)S(1)}, bf16[144,864]{1,0:T(8,128)(2,1)S(1)}, u32[]{:S(2)}, u32[]{:S(2)}) collective-permute-start(bf16[144,864]{1,0:T(8,128)(2,1)S(1)} %get-tuple-element.79), channel_id=1, source_target_pairs={{0,4},{4,0},{8,12},{12,8},{16,20},{20,16},{24,28},{28,24},{1,5},{5... | collective-permute-start | bytes 746504 | tf_op jit(solution)/shard_map/ppermute | solution.py:22
  430.2 55.3 %collective-permute-start.41 = (bf16[1,256,1152]{2,1,0:T(8,128)(2,1)}, bf16[1,256,1152]{2,1,0:T(8,128)(2,1)}, u32[]{:S(2)}, u32[]{:S(2)}) collective-permute-start(bf16[1,256,1152]{2,1,0:T(8,128)(2,1)} %get-tuple-element.72), channel_id=1, source_target_pairs={{0,1},{1,0},{2,3},{3,2},{4,5},{5,4},{6,7},{7,6},{8,9},{9,8},{10,11... | collective-permute-start | bytes 1769480 | tf_op jit(solution)/shard_map/ppermute | solution.py:22
  432.2 26.1 %collective-permute-start.43 = (bf16[144,864]{1,0:T(8,128)(2,1)S(1)}, bf16[144,864]{1,0:T(8,128)(2,1)S(1)}, u32[]{:S(2)}, u32[]{:S(2)}) collective-permute-start(bf16[144,864]{1,0:T(8,128)(2,1)S(1)} %get-tuple-element.77), channel_id=1, source_target_pairs={{0,4},{4,0},{8,12},{12,8},{16,20},{20,16},{24,28},{28,24},{1,5},{5... | collective-permute-start | bytes 746504 | tf_op jit(solution)/shard_map/ppermute | solution.py:22
  450.1 12.3 %collective-permute-start.49 = (bf16[144,864]{1,0:T(8,128)(2,1)S(1)}, bf16[144,864]{1,0:T(8,128)(2,1)S(1)}, u32[]{:S(2)}, u32[]{:S(2)}) collective-permute-start(bf16[144,864]{1,0:T(8,128)(2,1)S(1)} %get-tuple-element.82), channel_id=1, source_target_pairs={{0,24},{4,28},{8,16},{12,20},{16,8},{20,12},{24,0},{28,4},{1,25},{... | collective-permute-start | bytes 746504 | tf_op jit(solution)/shard_map/ppermute | solution.py:22
  455.3 28.2 %collective-permute-start.47 = (bf16[144,864]{1,0:T(8,128)(2,1)S(1)}, bf16[144,864]{1,0:T(8,128)(2,1)S(1)}, u32[]{:S(2)}, u32[]{:S(2)}) collective-permute-start(bf16[144,864]{1,0:T(8,128)(2,1)S(1)} %get-tuple-element.83), channel_id=1, source_target_pairs={{0,16},{4,20},{8,24},{12,28},{16,0},{20,4},{24,8},{28,12},{1,17},{... | collective-permute-start | bytes 746504 | tf_op jit(solution)/shard_map/ppermute | solution.py:22
  455.3 28.2 %collective-permute-start.45 = (bf16[144,864]{1,0:T(8,128)(2,1)S(1)}, bf16[144,864]{1,0:T(8,128)(2,1)S(1)}, u32[]{:S(2)}, u32[]{:S(2)}) collective-permute-start(bf16[144,864]{1,0:T(8,128)(2,1)S(1)} %get-tuple-element.81), channel_id=1, source_target_pairs={{0,8},{4,12},{8,0},{12,4},{16,24},{20,28},{24,16},{28,20},{1,9},{5... | collective-permute-start | bytes 746504 | tf_op jit(solution)/shard_map/ppermute | solution.py:22
  458.3 30.3 %collective-permute-start.33 = (bf16[1,256,1152]{2,1,0:T(8,128)(2,1)}, bf16[1,256,1152]{2,1,0:T(8,128)(2,1)}, u32[]{:S(2)}, u32[]{:S(2)}) collective-permute-start(bf16[1,256,1152]{2,1,0:T(8,128)(2,1)} %get-tuple-element.73), channel_id=1, source_target_pairs={{0,1},{1,0},{2,3},{3,2},{4,5},{5,4},{6,7},{7,6},{8,9},{9,8},{10,11... | collective-permute-start | bytes 1769480 | tf_op jit(solution)/shard_map/ppermute | solution.py:22
  462.4 52.2 %collective-permute-start.53 = (bf16[8,72,1152]{2,1,0:T(8,128)(2,1)S(1)}, bf16[8,72,1152]{2,1,0:T(8,128)(2,1)}, u32[]{:S(2)}, u32[]{:S(2)}) collective-permute-start(bf16[8,72,1152]{2,1,0:T(8,128)(2,1)S(1)} %copy-done.49), channel_id=1, source_target_pairs={{0,1},{1,0},{2,3},{3,2},{4,5},{5,4},{6,7},{7,6},{8,9},{9,8},{10,11... | collective-permute-start | bytes 3981320 | tf_op jit(solution)/shard_map/ppermute | solution.py:22
  483.5 42.3 %collective-permute-start.40 = (bf16[1,256,1152]{2,1,0:T(8,128)(2,1)}, bf16[1,256,1152]{2,1,0:T(8,128)(2,1)}, u32[]{:S(2)}, u32[]{:S(2)}) collective-permute-start(bf16[1,256,1152]{2,1,0:T(8,128)(2,1)} %get-tuple-element.71), channel_id=1, source_target_pairs={{0,1},{1,0},{2,3},{3,2},{4,5},{5,4},{6,7},{7,6},{8,9},{9,8},{10,11... | collective-permute-start | bytes 1769480 | tf_op jit(solution)/shard_map/ppermute | solution.py:22
  483.5 16.5 %collective-permute-start.35 = (bf16[1,256,1152]{2,1,0:T(8,128)(2,1)}, bf16[1,256,1152]{2,1,0:T(8,128)(2,1)}, u32[]{:S(2)}, u32[]{:S(2)}) collective-permute-start(bf16[1,256,1152]{2,1,0:T(8,128)(2,1)} %fusion.57), channel_id=1, source_target_pairs={{0,2},{1,3},{2,0},{3,1},{4,6},{5,7},{6,4},{7,5},{8,10},{9,11},{10,... | collective-permute-start | bytes 1769480 | tf_op jit(solution)/shard_map/ppermute | solution.py:22
  485.5 23.9 %collective-permute-start.51 = (bf16[3,144,288]{2,0,1:T(4,128)(2,1)S(1)}, bf16[3,144,288]{2,0,1:T(4,128)(2,1)S(1)}, u32[]{:S(2)}, u32[]{:S(2)}) collective-permute-start(bf16[3,144,288]{2,0,1:T(4,128)(2,1)S(1)} %bitcast.351), channel_id=1, source_target_pairs={{0,2},{1,3},{2,0},{3,1},{4,6},{5,7},{6,4},{7,5},{8,10},{9,11},{10,... | collective-permute-start | bytes 746504 | tf_op jit(solution)/shard_map/ppermute | solution.py:22
  488.6 23.2 %collective-permute-start.50 = (bf16[3,144,288]{2,0,1:T(4,128)(2,1)S(1)}, bf16[3,144,288]{2,0,1:T(4,128)(2,1)S(1)}, u32[]{:S(2)}, u32[]{:S(2)}) collective-permute-start(bf16[3,144,288]{2,0,1:T(4,128)(2,1)S(1)} %bitcast.352), channel_id=1, source_target_pairs={{0,1},{1,0},{2,3},{3,2},{4,5},{5,4},{6,7},{7,6},{8,9},{9,8},{10,11... | collective-permute-start | bytes 746504 | tf_op jit(solution)/shard_map/ppermute | solution.py:22
  500.0 25.9 %collective-permute-start.42 = (bf16[1,256,1152]{2,1,0:T(8,128)(2,1)}, bf16[1,256,1152]{2,1,0:T(8,128)(2,1)S(1)}, u32[]{:S(2)}, u32[]{:S(2)}) collective-permute-start(bf16[1,256,1152]{2,1,0:T(8,128)(2,1)} %fusion.53), channel_id=1, source_target_pairs={{0,2},{1,3},{2,0},{3,1},{4,6},{5,7},{6,4},{7,5},{8,10},{9,11},{10,... | collective-permute-start | bytes 1769480 | tf_op jit(solution)/shard_map/ppermute | solution.py:22
  520.3 31.2 %collective-permute-start.55 = (bf16[72,1152]{1,0:T(8,128)(2,1)}, bf16[72,1152]{1,0:T(8,128)(2,1)S(1)}, u32[]{:S(2)}, u32[]{:S(2)}) collective-permute-start(bf16[72,1152]{1,0:T(8,128)(2,1)} %get-tuple-element.87), channel_id=1, source_target_pairs={{0,4},{4,0},{8,12},{12,8},{16,20},{20,16},{24,28},{28,24},{1,5},{5... | collective-permute-start | bytes 497672 | tf_op jit(solution)/shard_map/ppermute | solution.py:22
  523.8 27.7 %collective-permute-start.59 = (bf16[72,1152]{1,0:T(8,128)(2,1)}, bf16[72,1152]{1,0:T(8,128)(2,1)S(1)}, u32[]{:S(2)}, u32[]{:S(2)}) collective-permute-start(bf16[72,1152]{1,0:T(8,128)(2,1)} %get-tuple-element.85), channel_id=1, source_target_pairs={{0,4},{4,0},{8,12},{12,8},{16,20},{20,16},{24,28},{28,24},{1,5},{5... | collective-permute-start | bytes 497672 | tf_op jit(solution)/shard_map/ppermute | solution.py:22
  523.8 27.7 %collective-permute-start.57 = (bf16[72,1152]{1,0:T(8,128)(2,1)}, bf16[72,1152]{1,0:T(8,128)(2,1)}, u32[]{:S(2)}, u32[]{:S(2)}) collective-permute-start(bf16[72,1152]{1,0:T(8,128)(2,1)} %get-tuple-element.86), channel_id=1, source_target_pairs={{0,4},{4,0},{8,12},{12,8},{16,20},{20,16},{24,28},{28,24},{1,5},{5... | collective-permute-start | bytes 497672 | tf_op jit(solution)/shard_map/ppermute | solution.py:22
  525.8 52.1 %collective-permute-start.54 = (bf16[72,1152]{1,0:T(8,128)(2,1)}, bf16[72,1152]{1,0:T(8,128)(2,1)}, u32[]{:S(2)}, u32[]{:S(2)}) collective-permute-start(bf16[72,1152]{1,0:T(8,128)(2,1)} %get-tuple-element.84), channel_id=1, source_target_pairs={{0,4},{4,0},{8,12},{12,8},{16,20},{20,16},{24,28},{28,24},{1,5},{5... | collective-permute-start | bytes 497672 | tf_op jit(solution)/shard_map/ppermute | solution.py:22
  531.5 15.3 %all-to-all-start.2 = ((f32[32,2,216]{2,1,0:T(2,128)}), f32[32,2,216]{2,1,0:T(2,128)S(1)}, u32[]{:S(2)}, u32[]{:S(2)}) async-start(f32[32,2,216]{2,1,0:T(2,128)} %copy.156), calls=%async_computation.2 | async-start | bytes 131072 | tf_op jit(solution)/shard_map/all_to_all | solution.py:396
  547.5 10.9 %all-to-all-start.3 = ((bf16[8,16,216]{2,1,0:T(8,128)(2,1)}), bf16[8,16,216]{2,1,0:T(8,128)(2,1)}, u32[]{:S(2)}, u32[]{:S(2)}) async-start(bf16[8,16,216]{2,1,0:T(8,128)(2,1)} %broadcast_in_dim.135), calls=%async_computation.3 | async-start | bytes 131072 | tf_op jit(solution)/shard_map/all_to_all | solution.py:406
  553.3 24.6 %collective-permute-start.60 = (bf16[72,1152]{1,0:T(8,128)(2,1)}, bf16[72,1152]{1,0:T(8,128)(2,1)}, u32[]{:S(2)}, u32[]{:S(2)}) collective-permute-start(bf16[72,1152]{1,0:T(8,128)(2,1)} %get-tuple-element.89), channel_id=1, source_target_pairs={{0,24},{4,28},{8,16},{12,20},{16,8},{20,12},{24,0},{28,4},{1,25},{... | collective-permute-start | bytes 497672 | tf_op jit(solution)/shard_map/ppermute | solution.py:22
  557.0 20.9 %collective-permute-start.58 = (bf16[72,1152]{1,0:T(8,128)(2,1)}, bf16[72,1152]{1,0:T(8,128)(2,1)}, u32[]{:S(2)}, u32[]{:S(2)}) collective-permute-start(bf16[72,1152]{1,0:T(8,128)(2,1)} %get-tuple-element.90), channel_id=1, source_target_pairs={{0,16},{4,20},{8,24},{12,28},{16,0},{20,4},{24,8},{28,12},{1,17},{... | collective-permute-start | bytes 497672 | tf_op jit(solution)/shard_map/ppermute | solution.py:22
  557.0 20.9 %collective-permute-start.56 = (bf16[72,1152]{1,0:T(8,128)(2,1)}, bf16[72,1152]{1,0:T(8,128)(2,1)}, u32[]{:S(2)}, u32[]{:S(2)}) collective-permute-start(bf16[72,1152]{1,0:T(8,128)(2,1)} %get-tuple-element.88), channel_id=1, source_target_pairs={{0,8},{4,12},{8,0},{12,4},{16,24},{20,28},{24,16},{28,20},{1,9},{5... | collective-permute-start | bytes 497672 | tf_op jit(solution)/shard_map/ppermute | solution.py:22
  559.8 13.6 %all-to-all-start.5 = ((bf16[8,2,1152]{2,1,0:T(2,128)(2,1)}), bf16[8,2,1152]{2,1,0:T(2,128)(2,1)}, u32[]{:S(2)}, u32[]{:S(2)}) async-start(bf16[8,2,1152]{2,1,0:T(2,128)(2,1)} %broadcast_in_dim.137), calls=%async_computation.5 | async-start | bytes 73728 | tf_op jit(solution)/shard_map/all_to_all | solution.py:401
  574.7 10.7 %all-to-all-start.4 = ((f32[32,2,144]{2,1,0:T(2,128)}), f32[32,2,144]{2,1,0:T(2,128)}, u32[]{:S(2)}, u32[]{:S(2)}) async-start(f32[32,2,144]{2,1,0:T(2,128)} %bitcast.359), calls=%async_computation.4 | async-start | bytes 131072 | tf_op jit(solution)/shard_map/all_to_all | solution.py:417
  585.3 11.3 %all-to-all-start.6 = ((bf16[4,72,288]{2,1,0:T(8,128)(2,1)}), bf16[4,72,288]{2,1,0:T(8,128)(2,1)}, u32[]{:S(2)}, u32[]{:S(2)}) async-start(bf16[4,72,288]{2,1,0:T(8,128)(2,1)} %copy.167), calls=%async_computation.6 | async-start | bytes 442368 | tf_op jit(solution)/shard_map/all_to_all | solution.py:429
  596.7 16.2 %all-to-all-start.7 = ((bf16[4,144,2,288]{3,2,1,0:T(2,128)(2,1)}), bf16[4,144,2,288]{3,2,1,0:T(2,128)(2,1)S(1)}, u32[]{:S(2)}, u32[]{:S(2)}) async-start(bf16[4,144,2,288]{3,2,1,0:T(2,128)(2,1)} %bitcast.343), calls=%async_computation.8 | async-start | bytes 1769472 | tf_op jit(solution)/shard_map/all_to_all | solution.py:429
  612.8 16.2 %all-to-all-start.9 = ((bf16[4,288,288]{2,1,0:T(8,128)(2,1)}), bf16[4,288,288]{2,1,0:T(8,128)(2,1)S(1)}, u32[]{:S(2)}, u32[]{:S(2)}) async-start(bf16[4,288,288]{2,1,0:T(8,128)(2,1)} %bitcast.322), calls=%async_computation.11 | async-start | bytes 1769472 | tf_op jit(solution)/shard_map/all_to_all | solution.py:429
  (97 other events, 961.4 us)
Sparse Core Ops, SparseCore 0:
  22.1 121.8 all-gather.2
  146.8 86.1 all-gather.4
  260.7 109.3 reduce-scatter.2
  374.0 121.4 reduce-scatter.4

commit v3 on v2

--- a/solution.py
+++ b/solution.py
@@ -125,7 +125,9 @@
     mixed[0] = mixed_t[...].T.astype(BF)
 
 
-def attend_grad_kernel(heads, block, packed, mixed, log_sum, d_mixed, d_packed, d_queries_t):
+def attend_grad_kernel(
+    heads, block, packed, mixed, log_sum, d_mixed, after, d_packed, d_queries_t
+):
     seq_len = packed.shape[1]
     cols = heads * HEAD_DIM
     inv_root = HEAD_DIM ** (-0.5)
@@ -159,7 +161,7 @@
     return pl.BlockSpec((1,) + shape, lambda i: (i, 0, 0))
 
 
-def attention(packed, heads, block=512):
+def attention(packed, heads, block=1024):
     lat, seq_len, _ = packed.shape
     cols = heads * HEAD_DIM
     return pl.pallas_call(
@@ -177,7 +179,7 @@
     )(packed)
 
 
-def attention_grad(packed, mixed, log_sum, d_mixed, heads, block=512):
+def attention_grad(packed, mixed, log_sum, d_mixed, after, heads, block=512):
     lat, seq_len, _ = packed.shape
     cols = heads * HEAD_DIM
     return pl.pallas_call(
@@ -188,13 +190,14 @@
             row_spec(seq_len, cols),
             row_spec(heads, seq_len),
             row_spec(seq_len, cols),
+            pl.BlockSpec(memory_space=pl.ANY),
         ],
         out_specs=row_spec(seq_len, 3 * cols),
         out_shape=jax.ShapeDtypeStruct((lat, seq_len, 3 * cols), BF),
         scratch_shapes=[pltpu.VMEM((cols, seq_len), F32)],
         compiler_params=pltpu.CompilerParams(vmem_limit_bytes=48 * 2**20),
         name="attend_grad",
-    )(packed, mixed, log_sum, d_mixed)
+    )(packed, mixed, log_sum, d_mixed, after)
 
 
 def on_device(tokens, conditioning, w_mod, b_mod, w_qkv, w_proj, w_fc1, b_fc1, w_fc2, cotangent):
@@ -208,27 +211,20 @@
     cols = heads_here * HEAD_DIM
     seq_len = tok * seq_n
     rows = w_qkv.shape[0]
-    hid_here = w_fc2.shape[0] // 2
+    hid_here = w_fc2.shape[0] // seq_n
     hid = hid_here * dp_n
-    every = ("dp", "seq")
-    n_all = dp_n * seq_n
     groups = 2
     per = lat // groups
     own = per * tok
 
     cond_silu, silu_back = jax.vjp(jax.nn.silu, conditioning)
     cond_act = cond_silu.astype(BF)
-    bias_half = lax.dynamic_slice(b_fc1, (core * hid_here,), (hid_here,))
-    small = jnp.concatenate(
-        [
-            cond_act.reshape(lat, dp_n, rows).transpose(1, 0, 2).reshape(dp_n, lat * rows),
-            jnp.broadcast_to(bias_half[None], (dp_n, hid_here)),
-        ],
-        axis=1,
-    )
-    small = dp_exchange(small)
-    cond_rows = small[:, : lat * rows].reshape(dp_n * lat, rows)
-    fc1_bias = small[:, lat * rows :].reshape(hid).astype(F32)
+    bias_here = lax.dynamic_slice(b_fc1, (seq * hid_here,), (hid_here,))
+    small = jnp.concatenate([cond_act.reshape(lat * width), bias_here])
+    small = dp_exchange(jnp.broadcast_to(small[None], (dp_n, lat * width + hid_here)))
+    cond_all = small[:, : lat * width].reshape(dp_n * lat, width)
+    fc1_bias = small[:, lat * width :].reshape(hid).astype(F32)
+    cond_rows = lax.dynamic_slice(cond_all, (0, dp * rows), (dp_n * lat, rows))
     mod_terms = matmul(cond_rows, w_mod)
     piece = b_mod.shape[0]
     mod_terms = lax.dynamic_update_slice(
@@ -241,35 +237,39 @@
 
     tok_slots = seq_gather(tokens)
 
-    qkv_here = lax.dynamic_index_in_dim(
-        w_qkv.reshape(rows, 3, seq_n, cols), seq, axis=2, keepdims=False
-    ).reshape(rows, 3 * cols)
+    qkv_here = jnp.concatenate(
+        [lax.dynamic_slice(w_qkv, (0, t * width + seq * cols), (rows, cols)) for t in range(3)],
+        axis=1,
+    )
     qkv = dp_gather(qkv_here, lambda d: d).reshape(width, 3 * cols)
-    fc1_here = lax.dynamic_index_in_dim(
-        w_fc1.reshape(rows, dp_n, 2, hid_here), core, axis=2, keepdims=False
-    ).reshape(rows, hid)
+    half = rows // 2
+    proj_mine = lax.all_gather(
+        lax.dynamic_slice(w_proj, (core * half, 0), (half, width)), "dp", axis=0
+    )
+    fc1_here = jnp.concatenate(
+        [
+            lax.dynamic_slice(w_fc1, (0, (d * seq_n + seq) * hid_here), (rows, hid_here))
+            for d in range(dp_n)
+        ],
+        axis=1,
+    )
     fc1 = lax.all_gather(fc1_here, "dp", axis=0, tiled=True)
     fc2 = lax.all_gather(
-        lax.dynamic_slice(w_fc2, (core * hid_here, 0), (hid_here, width)), "dp", axis=0, tiled=True
-    )
-    ratio = cols // rows
-    half = rows // 2
-
-    def proj_place(d):
-        return ((d // ratio) ^ seq) * ratio + d % ratio
-
-    def flip(halves):
-        return halves.reshape(seq_n // 2, 2, ratio * half, width)[:, ::-1].reshape(
-            dp_n, half, width
-        )
-
-    proj_mine = dp_gather(lax.dynamic_slice(w_proj, (core * half, 0), (half, width)), proj_place)
-    proj_other = flip(hop(proj_mine, "seq", 1))
+        lax.dynamic_slice(w_fc2, (seq * hid_here, 0), (hid_here, width)), "dp", axis=0, tiled=True
+    )
+    proj_other = hop(proj_mine, "seq", 1)
     proj = jnp.where(
         core == 0,
         jnp.stack([proj_mine, proj_other], axis=1),
         jnp.stack([proj_other, proj_mine], axis=1),
-    ).reshape(width, width)
+    ).reshape(seq_n, cols, width)
+
+    def by_place(blocks):
+        return jnp.concatenate(
+            [lax.dynamic_index_in_dim(blocks, seq ^ j, 0, keepdims=False) for j in range(seq_n)]
+        )
+
+    proj = by_place(proj)
 
     def part(g):
         return slice(g * per, (g + 1) * per)
@@ -307,30 +307,28 @@
         )
         upstream.append(cotangent[part(g)].astype(F32))
         d_mlp.append((gate_mlp[g] * upstream[g]).astype(BF).reshape(own, width))
-    d_mlp_pair = jnp.concatenate(d_mlp + [hop(v, "seq", 1) for v in d_mlp])
-    normed_pair = jnp.concatenate(normed_mlp + [hop(v, "seq", 1) for v in normed_mlp])
-
-    hidden = matmul(normed_pair, fc1) + fc1_bias
-    tanh = jnp.tanh(GELU_C * (hidden + GELU_A * hidden * hidden * hidden))
-    activated = (0.5 * hidden * (1.0 + tanh)).astype(BF)
-    gelu_slope = 0.5 * (1.0 + tanh) + 0.5 * hidden * (1.0 - tanh * tanh) * GELU_C * (
-        1.0 + 3.0 * GELU_A * hidden * hidden
-    )
-    d_hidden = (matmul_nt(d_mlp_pair, fc2) * gelu_slope).astype(BF)
-    grad_fc2 = matmul_tn(activated, d_mlp_pair).astype(BF)
-    sum_fc2 = lax.psum_scatter(grad_fc2, "dp", scatter_dimension=0, tiled=True)
-    d_norm_part = matmul_nt(d_hidden, fc1)
-    d_norm_sent = [
-        hop(d_norm_part[(groups + g) * own : (groups + g + 1) * own].astype(BF), "seq", 1)
-        for g in range(groups)
-    ]
-    grad_fc1 = matmul_tn(normed_pair, d_hidden).astype(BF)
-    sum_fc1 = lax.psum_scatter(grad_fc1, "dp", scatter_dimension=0, tiled=True)
-    grad_bias1 = jnp.sum(d_hidden.astype(F32), axis=0)
-    mlp_part = matmul(activated, fc2)
-    mlp_sent = hop(mlp_part[groups * own :].astype(BF), "seq", 1)
-    mlp_out = mlp_part[: groups * own] + mlp_sent.astype(F32)
-    mlp_out = mlp_out.reshape(groups, per, tok, width)
+    d_mlp_all = [jnp.concatenate(seq_gather(v)) for v in d_mlp]
+    normed_mlp_all = [jnp.concatenate(seq_gather(v)) for v in normed_mlp]
+
+    grad_fc1 = grad_fc2 = grad_bias1 = 0.0
+    d_norm, mlp_out = [], []
+    for g in range(groups):
+        hidden = matmul(normed_mlp_all[g], fc1) + fc1_bias
+        tanh = jnp.tanh(GELU_C * (hidden + GELU_A * hidden * hidden * hidden))
+        activated = (0.5 * hidden * (1.0 + tanh)).astype(BF)
+        gelu_slope = 0.5 * (1.0 + tanh) + 0.5 * hidden * (1.0 - tanh * tanh) * GELU_C * (
+            1.0 + 3.0 * GELU_A * hidden * hidden
+        )
+        d_hidden = (matmul_nt(d_mlp_all[g], fc2) * gelu_slope).astype(BF)
+        terms = matmul_nt(d_hidden, fc1).reshape(seq_n, own, width)
+        d_norm.append(seq_reduce([terms[j] for j in range(seq_n)]).reshape(per, tok, width))
+        grad_fc2 = grad_fc2 + matmul_tn(activated, d_mlp_all[g])
+        grad_fc1 = grad_fc1 + matmul_tn(normed_mlp_all[g], d_hidden)
+        grad_bias1 = grad_bias1 + jnp.sum(d_hidden.astype(F32), axis=0)
+        terms = matmul(activated, fc2).reshape(seq_n, own, width)
+        mlp_out.append(seq_reduce([terms[j] for j in range(seq_n)]).reshape(per, tok, width))
+    sum_fc2 = lax.psum_scatter(grad_fc2.astype(BF), "dp", scatter_dimension=0, tiled=True)
+    sum_fc1 = lax.psum_scatter(grad_fc1.astype(BF), "dp", scatter_dimension=0, tiled=True)
     output = jnp.concatenate(
         [(resid_mid[g] + gate_mlp[g] * mlp_out[g]).astype(BF) for g in range(groups)]
     )
@@ -340,37 +338,40 @@
 
     d_gate_mlp = stacked([jnp.sum(upstream[g] * mlp_out[g], axis=1) for g in range(groups)])
     d_shift_mlp, d_scale_mlp, d_gate_attn, d_resid, d_attn = ([] for _ in range(5))
-    d_mixed = []
-    for g in range(groups):
-        d_norm = d_norm_part[g * own : (g + 1) * own] + d_norm_sent[g].astype(F32)
-        d_norm = d_norm.reshape(per, tok, width)
-        d_shift_mlp.append(jnp.sum(d_norm, axis=1))
-        d_scale_mlp.append(jnp.sum(d_norm * normed_mid[g], axis=1))
+    d_mixed, d_attended = [], []
+    for g in range(groups):
+        d_shift_mlp.append(jnp.sum(d_norm[g], axis=1))
+        d_scale_mlp.append(jnp.sum(d_norm[g] * normed_mid[g], axis=1))
         d_resid.append(
-            upstream[g] + ln_backward(d_norm * (1.0 + scale_mlp[g]), normed_mid[g], std_mid[g])
+            upstream[g] + ln_backward(d_norm[g] * (1.0 + scale_mlp[g]), normed_mid[g], std_mid[g])
         )
         d_gate_attn.append(jnp.sum(d_resid[g] * attn_out[g], axis=1))
         d_attn.append((gate_attn[g] * d_resid[g]).astype(BF).reshape(own, width))
-        d_attended = matmul_nt(d_attn[g], proj).astype(BF).reshape(per, tok, width)
+        d_attended.append(matmul_nt(d_attn[g], proj).astype(BF).reshape(per, tok, width))
         d_mixed.append(
             jnp.concatenate(
-                seq_exchange([d_attended[:, :, j * cols : (j + 1) * cols] for j in range(seq_n)]),
+                seq_exchange([d_attended[g][:, :, j * cols : (j + 1) * cols] for j in range(seq_n)]),
                 axis=1,
             )
         )
-    grad_proj = matmul_tn(stacked(attended), stacked(d_attn)).astype(BF)
-    grad_proj = grad_proj.reshape(dp_n, 2, half, width)
+    grad_proj = by_place(
+        matmul_tn(stacked(attended), stacked(d_attn)).astype(BF).reshape(seq_n, cols, width)
+    ).reshape(dp_n, 2, half, width)
     proj_sent = hop(
         lax.dynamic_index_in_dim(grad_proj, 1 - core, axis=1, keepdims=False), "seq", 1
     )
     proj_terms = lax.dynamic_index_in_dim(grad_proj, core, axis=1, keepdims=False).astype(F32)
-    proj_terms = (proj_terms + flip(proj_sent).astype(F32)).astype(BF)
-    sum_proj = dp_scatter(proj_terms, proj_place).astype(BF)
+    proj_terms = (proj_terms + proj_sent.astype(F32)).astype(BF)
+    sum_proj = lax.psum_scatter(
+        proj_terms.reshape(dp_n * half, width), "dp", scatter_dimension=0, tiled=True
+    )
 
     d_packed, d_first = [], []
     for g in range(groups):
         d_packed.append(
-            attention_grad(packed[g], mixed[g], log_sums[g], d_mixed[g], heads_here).reshape(
+            attention_grad(
+                packed[g], mixed[g], log_sums[g], d_mixed[g], d_attended[-1], heads_here
+            ).reshape(
                 per * seq_len, 3 * cols
             )
         )
@@ -392,50 +393,31 @@
         + [stacked(d_shift_mlp), stacked(d_scale_mlp), d_gate_mlp],
         axis=1,
     )
-    share = 6 * width // n_all
-    mod_cols = lax.all_to_all(
-        mod_part.reshape(lat, n_all, share).transpose(1, 0, 2), every, 0, 0, tiled=True
-    )
-    d_mod = jnp.sum(mod_cols.reshape(dp_n, seq_n, lat, share), axis=1).reshape(dp_n * lat, share)
-    d_mod = d_mod.astype(BF)
-    cond_all = lax.all_to_all(
-        jnp.broadcast_to(cond_act[None], (dp_n, lat, width)), "dp", 0, 0, tiled=True
-    ).reshape(dp_n * lat, width)
-    grad_wmod = matmul_tn(cond_all, d_mod)
-    grad_bmod = jnp.sum(d_mod.astype(F32), axis=0)
-    mod_rows = lax.all_to_all(
-        jnp.broadcast_to(d_mod[None], (dp_n, dp_n * lat, share)), "dp", 0, 0, tiled=True
-    )
-    mod_here = mod_rows.transpose(1, 0, 2).reshape(dp_n * lat, dp_n * share)
-    w_mod_here = lax.dynamic_index_in_dim(
-        w_mod.reshape(rows, dp_n, seq_n, share), seq, axis=2, keepdims=False
-    ).reshape(rows, dp_n * share)
-    cond_terms = matmul_nt(mod_here, w_mod_here)
-    cond_terms = jnp.broadcast_to(
-        cond_terms.reshape(dp_n, 1, lat, rows), (dp_n, seq_n, lat, rows)
-    ).reshape(n_all, lat, rows)
-    cond_back = lax.all_to_all(cond_terms, every, 0, 0, tiled=True)
-    d_cond = jnp.sum(cond_back.reshape(dp_n, seq_n, lat, rows), axis=1)
+    bit = 1
+    while bit < seq_n:
+        mod_part = mod_part + hop(mod_part, "seq", bit)
+        bit *= 2
+    d_mod = dp_exchange(jnp.broadcast_to(mod_part.astype(BF)[None], (dp_n, lat, 6 * width)))
+    d_mod = d_mod.reshape(dp_n * lat, 6 * width)
+    share = 6 * width // (dp_n * seq_n)
+    mod_cols = lax.dynamic_slice(d_mod, (0, (dp * seq_n + seq) * share), (dp_n * lat, share))
+    grad_wmod = matmul_tn(cond_all, mod_cols)
+    grad_bmod = jnp.sum(mod_cols.astype(F32), axis=0)
+    d_cond = dp_exchange(matmul_nt(d_mod, w_mod).reshape(dp_n, lat, rows))
     (grad_cond,) = silu_back(d_cond.transpose(1, 0, 2).reshape(lat, width))
 
-    spread = jnp.zeros((dp_n, 2, hid_here), F32)
-    spread = lax.dynamic_update_slice(spread, grad_bias1.reshape(dp_n, 1, hid_here), (0, core, 0))
-    bias_cols = lax.all_to_all(
-        spread.reshape(n_all, 2 * hid_here // seq_n), every, 0, 0, tiled=True
-    )
-    bias_out = jnp.sum(bias_cols, axis=0)
+    bias_out = jnp.sum(dp_exchange(grad_bias1.reshape(dp_n, hid_here)), axis=0)
 
     def to_owner(blocks):
-        received = lax.all_to_all(blocks, "seq", 0, 0, tiled=True).astype(F32)
-        return jnp.sum(received.reshape((seq_n // 2, 2) + received.shape[1:]), axis=0)
+        return lax.all_to_all(blocks, "seq", 0, 0, tiled=True).astype(F32)
 
     share = width // seq_n
     out_fc2 = to_owner(sum_fc2.reshape(hid_here, seq_n, share).transpose(1, 0, 2))
-    out_fc2 = out_fc2.reshape(2 * hid_here, share)
+    out_fc2 = out_fc2.reshape(seq_n * hid_here, share)
     out_proj = to_owner(sum_proj.reshape(half, seq_n, share).transpose(1, 0, 2))
-    out_proj = out_proj.reshape(rows, share)
+    out_proj = jnp.sum(out_proj.reshape(seq_n // 2, rows, share), axis=0)
     blocks = sum_fc1.reshape(rows, seq_n, dp_n // seq_n, hid_here).transpose(1, 0, 2, 3)
-    out_fc1 = to_owner(blocks).transpose(1, 2, 0, 3).reshape(rows, 2 * hid // seq_n)
+    out_fc1 = to_owner(blocks).transpose(1, 2, 0, 3).reshape(rows, hid)
     qkv_slots = jnp.stack(
         seq_gather(sum_qkv.reshape(rows, 3, cols).transpose(1, 0, 2))
     ).reshape(3 * seq_n, rows, cols)

time: 647 us -> 643 us (level)
  waiting for transfers between devices: 150 us -> 212 us
  local copies, waits for them, and re-layouts: 132 us -> 80.6 us
  starting transfers between devices: 109 us -> 90.6 us
  Pallas kernels: 38.8 us -> 49.1 us
    ppermute x61 -> x66, waiting for transfers between devices: 113 us -> 179 us  [hop(): return lax.ppermute(value, axis, [(i, i ^ bits) for i in range(count)])]
    all_to_all x8 -> x3, starting transfers between devices: 41.5 us -> 10.5 us  [to_owner(): return lax.all_to_all(blocks, 'seq', 0, 0, tiled=True).astype(F32)]
    reshape x14 -> x5, local copies, waits for them, and re-layouts: 26.2 us -> 2.75 us  [the longest x2 2.62 us: on_device(): out_fc1 = to_owner(blocks).transpose(1, 2, 0, 3).reshape(rows, hid)]
    all_to_all x2 -> x5, starting transfers between devices: 10.5 us -> 29.5 us  [dp_exchange(): return lax.all_to_all(value, 'dp', 0, 0, tiled=True)]
    all_to_all x2 -> x5, waiting for transfers between devices: 10 us -> 21.6 us  [dp_exchange(): return lax.all_to_all(value, 'dp', 0, 0, tiled=True)]
    all_to_all x8 -> x3, waiting for transfers between devices: 21.9 us -> 12 us  [to_owner(): return lax.all_to_all(blocks, 'seq', 0, 0, tiled=True).astype(F32)]
    pallas_call x2, Pallas kernels: 16.1 us -> 25.5 us  [attention(): pl.pallas_call(partial(attend_kernel, heads, block), grid=(lat,), in_spec...]
    dynamic_slice x5, local copies, waits for them, and re-layouts: 15.7 us -> 7.09 us  [the longest x1 1.73 us: on_device(): lax.dynamic_slice(w_fc2, (seq * hid_here, 0), (hid_here, width))]
  transfers between devices with their start and end apart: 75 -> 80, of which waited for: 27 -> 29; matrix products, arithmetic and copies ran while one was open for 43% -> 36% of each run, Pallas kernels for 6% -> 8%
where the time goes in v3:
time: 643 us; the launch traced here: 633 us
  waiting for transfers between devices  212 us (33%)
  matrix products  116 us (18%)
  starting transfers between devices  90.6 us (14%)
  local copies, waits for them, and re-layouts  80.6 us (13%)
  other arithmetic  68 us (11%)
  Pallas kernels  49.1 us (8%)
  between operations  16.3 us (3%)
    ppermute x66, waiting for transfers between devices, hop(): return lax.ppermute(value, axis, [(i, i ^ bits) for i in range(count)])  179 us
    ppermute x66, starting transfers between devices, hop(): return lax.ppermute(value, axis, [(i, i ^ bits) for i in range(count)])  50 us
    dot_general x9, matrix products, matmul_nt(): lax.dot_general(left, right, (((1,), (1,)), ((), ())), preferred_element_...  41.3 us
    dot_general x9, matrix products, matmul(): return jnp.dot(left, right, preferred_element_type=F32)  38.6 us
    dot_general x7, matrix products, matmul_tn(): lax.dot_general(left, right, (((0,), (0,)), ((), ())), preferred_element_...  36.2 us
    all_to_all x5, starting transfers between devices, dp_exchange(): return lax.all_to_all(value, 'dp', 0, 0, tiled=True)  29.5 us
    pallas_call x2, Pallas kernels, attention(): pl.pallas_call(partial(attend_kernel, heads, block), grid=(lat,), in_spec...  25.5 us
    pallas_call x2, Pallas kernels, attention_grad(): pl.pallas_call(partial(attend_grad_kernel, heads, block), grid=(lat,), in...  23.6 us
  transfers between devices with their start and end apart: 80, of which 29 were waited for; matrix products, arithmetic and copies ran while one was open for 36% of the time, Pallas kernels for 8%

profile of v3, /device:TPU:0, one launch (start us, length us, event | category | flops | bytes accessed | tf_op | source)
XLA Modules:
  0.0 633.0 jit_solution(10787389307759083954)
XLA Ops:
  15.4 2.9 collective-permute-start.3
  19.9 2.6 collective-permute-start.6
  25.7 4.9 all-to-all-start
  36.3 14.9 %all-to-all-done = bf16[8,2,1224]{2,1,0:T(2,128)(2,1)S(1)} async-done(((bf16[8,2,1224]{2,1,0:T(2,128)(2,1)}), bf16[8,2,1224]{2,1,0:T(2,128)(2,1)S(1)}, u32[]{:S(2)}, u32[]{:S(2)}) %all-to-all-start) | async-done | bytes 39200 | tf_op jit(solution)/shard_map/all_to_all | solution.py:76
  57.5 4.6 all-to-all-start.1
  69.7 6.3 collective-permute-done.5
  78.4 3.1 collective-permute-done.7
  82.9 7.0 %collective-permute-done.9 = bf16[144,864]{1,0:T(8,128)(2,1)S(1)} collective-permute-done((bf16[144,864]{1,0:T(8,128)(2,1)S(1)}, bf16[144,864]{1,0:T(8,128)(2,1)S(1)}, u32[]{:S(2)}, u32[]{:S(2)}) %collective-permute-start.9) | collective-permute-done | bytes 248864 | tf_op jit(solution)/shard_map/ppermute | solution.py:22
  92.6 2.7 fusion.147
  95.3 2.6 fusion.146
  105.4 5.9 add_convert_fusion
  112.7 4.6 convert_bitcast_fusion.1.packed
  117.3 6.9 %attend.2 = (bf16[1,1024,288]{2,1,0:T(8,128)(2,1)S(1)}, f32[1,4,1024]{2,1,0:T(4,128)S(1)}) custom-call(bf16[1,1024,864]{2,1,0:T(8,128)(2,1)S(1)} %convert_bitcast_fusion.1.packed), custom_call_target="tpu_custom_call" | custom-call | tf_op jit(solution)/shard_map/attend/pallas_call | solution.py:167
  127.6 4.4 convert_bitcast_fusion.packed
  132.0 18.6 %attend.3 = (bf16[1,1024,288]{2,1,0:T(8,128)(2,1)S(1)}, f32[1,4,1024]{2,1,0:T(4,128)S(1)}) custom-call(bf16[1,1024,864]{2,1,0:T(8,128)(2,1)S(1)} %convert_bitcast_fusion.packed), custom_call_target="tpu_custom_call" | custom-call | tf_op jit(solution)/shard_map/attend/pallas_call | solution.py:167
  159.3 3.0 collective-permute-done.21
  179.5 12.6 %collective-permute-done.24 = bf16[256,1152]{1,0:T(8,128)(2,1)} collective-permute-done((bf16[256,1152]{1,0:T(8,128)(2,1)}, bf16[256,1152]{1,0:T(8,128)(2,1)}, u32[]{:S(2)}, u32[]{:S(2)}) %collective-permute-start.24) | collective-permute-done | bytes 589856 | tf_op jit(solution)/shard_map/ppermute | solution.py:22
  193.4 11.3 %collective-permute-done.15 = bf16[256,1152]{1,0:T(8,128)(2,1)} collective-permute-done((bf16[256,1152]{1,0:T(8,128)(2,1)}, bf16[256,1152]{1,0:T(8,128)(2,1)}, u32[]{:S(2)}, u32[]{:S(2)}) %collective-permute-start.15) | collective-permute-done | bytes 589856 | tf_op jit(solution)/shard_map/ppermute | solution.py:22
  204.8 8.2 %convolution_add_fusion.2 = f32[1024,1152]{1,0:T(8,128)} fusion(bf16[1152,1152]{1,0:T(8,128)(2,1)} %all-gather.5.cloned.1.call-done, f32[1152]{0:T(1024)S(1)} %reshape.999, bf16[256,1152]{1,0:T(8,128)(2,1)} %collective-permute-done.25, bf16[256,1152]{1,0:T(8,128)(2,1)} %collective-permute-done.24, bf16[256,1152]{1,0:T(8,128)(2,1)} %collective-permute-done.23, ...), kind=kOutput, calls=%fused_computation.39 | convolution fusion | flops 2728525824 | bytes 9736704 | tf_op jit(solution)/shard_map/dot_general | solution.py:26
  213.0 7.0 %fusion.152 = (bf16[1024,1152]{1,0:T(8,128)(2,1)S(1)}, f32[1024,1152]{1,0:T(8,128)S(1)}) fusion(bf16[1152,1152]{1,0:T(8,128)(2,1)} %all-gather.7.cloned.1.call-done, f32[1024,1152]{1,0:T(8,128)} %convolution_add_fusion.2), kind=kOutput, calls=%fused_computation.349 | convolution fusion | flops 2729705472 | bytes 14450688 | tf_op jit(solution)/shard_map/dot_general | solution.py:26
  220.6 6.5 %convolution_add_fusion.3 = f32[1024,1152]{1,0:T(8,128)S(1)} fusion(bf16[1152,1152]{1,0:T(8,128)(2,1)S(1)} %copy-done.94, f32[1152]{0:T(1024)S(1)} %reshape.999, bf16[256,1152]{1,0:T(8,128)(2,1)} %collective-permute-done.16, bf16[256,1152]{1,0:T(8,128)(2,1)} %collective-permute-done.15, bf16[256,1152]{1,0:T(8,128)(2,1)} %collective-permute-done.14, ...), kind=kOutput, calls=%fused_computation.40 | convolution fusion | flops 2728525824 | bytes 9736704 | tf_op jit(solution)/shard_map/dot_general | solution.py:26
  227.1 4.2 fusion.151
  235.2 13.3 %collective-permute-done.28 = bf16[256,1152]{1,0:T(8,128)(2,1)S(1)} collective-permute-done((bf16[256,1152]{1,0:T(8,128)(2,1)S(1)}, bf16[256,1152]{1,0:T(8,128)(2,1)S(1)}, u32[]{:S(2)}, u32[]{:S(2)}) %collective-permute-start.28) | collective-permute-done | bytes 589856 | tf_op jit(solution)/shard_map/ppermute | solution.py:22
  248.4 12.2 %collective-permute-done.19 = bf16[256,1152]{1,0:T(8,128)(2,1)S(1)} collective-permute-done((bf16[256,1152]{1,0:T(8,128)(2,1)S(1)}, bf16[256,1152]{1,0:T(8,128)(2,1)S(1)}, u32[]{:S(2)}, u32[]{:S(2)}) %collective-permute-start.19) | collective-permute-done | bytes 589856 | tf_op jit(solution)/shard_map/ppermute | solution.py:22
  264.6 14.2 %collective-permute-done.39 = bf16[256,1152]{1,0:T(8,128)(2,1)S(1)} collective-permute-done((bf16[256,1152]{1,0:T(8,128)(2,1)S(1)}, bf16[256,1152]{1,0:T(8,128)(2,1)S(1)}, u32[]{:S(2)}, u32[]{:S(2)}) %collective-permute-start.39) | collective-permute-done | bytes 589856 | tf_op jit(solution)/shard_map/ppermute | solution.py:22
  279.3 10.8 %collective-permute-done.30 = bf16[256,1152]{1,0:T(8,128)(2,1)S(1)} collective-permute-done((bf16[256,1152]{1,0:T(8,128)(2,1)S(1)}, bf16[256,1152]{1,0:T(8,128)(2,1)S(1)}, u32[]{:S(2)}, u32[]{:S(2)}) %collective-permute-start.30) | collective-permute-done | bytes 589856 | tf_op jit(solution)/shard_map/ppermute | solution.py:22
  290.2 7.8 %convert_reduce_fusion.2 = (f32[1152]{0:T(1024)S(1)}, bf16[1024,1152]{1,0:T(8,128)(2,1)}) fusion(f32[1024,1152]{1,0:T(8,128)S(1)} %bitcast.322, bf16[1152,1152]{1,0:T(8,128)(2,1)S(1)} %copy-done.95, bf16[256,1152]{1,0:T(8,128)(2,1)S(1)} %collective-permute-done.40, bf16[256,1152]{1,0:T(8,128)(2,1)S(1)} %collective-permute-done.39, ...), kind=kOutput, calls=%fused_computation.33 | convolution fusion | flops 2752117760 | bytes 12096000 | tf_op jit(solution)/shard_map/dot_general | solution.py:30
  298.0 5.2 fusion.154
  304.8 7.0 %convert_reduce_fusion.3 = (f32[1152]{0:T(1024)S(1)}, bf16[1024,1152]{1,0:T(8,128)(2,1)S(1)}) fusion(f32[1024,1152]{1,0:T(8,128)S(1)} %convolution_add_fusion.3, bf16[1152,1152]{1,0:T(8,128)(2,1)S(1)} %copy-done.95, bf16[256,1152]{1,0:T(8,128)(2,1)S(1)} %collective-permute-done.31, bf16[256,1152]{1,0:T(8,128)(2,1)S(1)} %collective-permute-done.30, ...), kind=kOutput, calls=%fused_computation.34 | convolution fusion | flops 2752117760 | bytes 12096000 | tf_op jit(solution)/shard_map/dot_general | solution.py:30
  311.8 5.1 fusion.153
  323.5 12.5 %collective-permute-done.43 = bf16[256,1152]{1,0:T(8,128)(2,1)} collective-permute-done((bf16[256,1152]{1,0:T(8,128)(2,1)}, bf16[256,1152]{1,0:T(8,128)(2,1)}, u32[]{:S(2)}, u32[]{:S(2)}) %collective-permute-start.43) | collective-permute-done | bytes 589856 | tf_op jit(solution)/shard_map/ppermute | solution.py:22
  338.5 9.1 %collective-permute-done.34 = bf16[256,1152]{1,0:T(8,128)(2,1)S(1)} collective-permute-done((bf16[256,1152]{1,0:T(8,128)(2,1)S(1)}, bf16[256,1152]{1,0:T(8,128)(2,1)S(1)}, u32[]{:S(2)}, u32[]{:S(2)}) %collective-permute-start.34) | collective-permute-done | bytes 589856 | tf_op jit(solution)/shard_map/ppermute | solution.py:22
  355.1 5.0 pad_maximum_fusion.1
  361.9 3.2 collective-permute-done.65
  365.1 3.2 fusion.30
  368.4 6.8 %fusion.106 = f32[1152,1152]{1,0:T(8,128)S(1)} fusion(bf16[256,1152]{1,0:T(8,128)(2,1)} %copy-done.102, bf16[256,1152]{1,0:T(8,128)(2,1)} %copy-done.98, bf16[256,1152]{1,0:T(8,128)(2,1)} %copy-done.99, bf16[256,1152]{1,0:T(8,128)(2,1)S(1)} %copy-done.70, f32[1024,1152]{1,0:T(8,128)} %convolution_add_fusion.2), kind=kOutput, calls=%fused_computation.212 | convolution fusion | flops 2737963008 | bytes 12386304 | tf_op jit(solution)/shard_map/dot_general | solution.py:34
  375.2 7.8 %fusion.1 = bf16[1152,1152]{1,0:T(8,128)(2,1)} fusion(f32[1152,1152]{1,0:T(8,128)S(1)} %fusion.106, bf16[256,1152]{1,0:T(8,128)(2,1)S(1)} %copy-done.104, bf16[256,1152]{1,0:T(8,128)(2,1)S(1)} %copy-done.97, bf16[256,1152]{1,0:T(8,128)(2,1)S(1)} %copy-done.101, bf16[256,1152]{1,0:T(8,128)(2,1)S(1)} %copy-done.68, f32[1024,1152]{1,0:T(8,128)} %copy-done.105), kind=kOutput, calls=%fused_computation.4 | convolution fusion | flops 2740617216 | bytes 15040512 | tf_op jit(solution)/shard_map/dot_general | solution.py:34
  386.1 4.6 all-to-all-start.6
  391.2 5.8 fusion.107
  405.1 6.4 %fusion = bf16[1152,1152]{1,0:T(8,128)(2,1)} fusion(f32[1152,1152]{1,0:T(8,128)S(1)} %fusion.107, bf16[1024,1152]{1,0:T(8,128)(2,1)S(1)} %copy-done.107, bf16[256,1152]{1,0:T(8,128)(2,1)} %collective-permute-done.16, bf16[256,1152]{1,0:T(8,128)(2,1)} %collective-permute-done.15, bf16[256,1152]{1,0:T(8,128)(2,1)} %collective-permute-done.14, ...), kind=kOutput, calls=%fused_computation.3 | convolution fusion | flops 2730000384 | bytes 12681216 | tf_op jit(solution)/shard_map/dot_general | solution.py:34
  415.0 11.8 %attend_grad.3 = bf16[1,1024,864]{2,1,0:T(8,128)(2,1)S(1)} custom-call(bf16[1,1024,864]{2,1,0:T(8,128)(2,1)S(1)} %copy-done.4, bf16[1,1024,288]{2,1,0:T(8,128)(2,1)S(1)} %copy-done.8, f32[1,4,1024]{2,1,0:T(4,128)S(1)} %get-tuple-element.17.log_sum, bf16[1,1024,288]{2,1,0:T(8,128)(2,1)S(1)} %pad_maximum_fusion.12.d_mixed, bf16[1,256,1152]{2,1,0:T(8,128)(2,1)S(1)} %fusion.32.after), custom_call_target="tpu_custom_call" | custom-call | tf_op jit(solution)/shard_map/attend_grad/pallas_call | solution.py:185
  428.7 11.8 %attend_grad.2 = bf16[1,1024,864]{2,1,0:T(8,128)(2,1)S(1)} custom-call(bf16[1,1024,864]{2,1,0:T(8,128)(2,1)S(1)} %copy-done.2, bf16[1,1024,288]{2,1,0:T(8,128)(2,1)S(1)} %copy-done.6, f32[1,4,1024]{2,1,0:T(4,128)S(1)} %get-tuple-element.16.log_sum, bf16[1,1024,288]{2,1,0:T(8,128)(2,1)S(1)} %pad_maximum_fusion.11.d_mixed, bf16[1,256,1152]{2,1,0:T(8,128)(2,1)S(1)} %fusion.32.after), custom_call_target="tpu_custom_call" | custom-call | tf_op jit(solution)/shard_map/attend_grad/pallas_call | solution.py:185
  441.8 6.4 %fusion.25 = bf16[1152,864]{0,1:T(8,128)(2,1)} fusion(bf16[1024,864]{1,0:T(8,128)(2,1)S(1)} %bitcast.292, bf16[1024,864]{1,0:T(8,128)(2,1)S(1)} %bitcast.294, bf16[1024,1152]{1,0:T(8,128)(2,1)S(1)} %copy-done.38, bf16[1024,1152]{1,0:T(8,128)(2,1)S(1)} %copy-done.40), kind=kOutput, calls=%fused_computation.48 | convolution fusion | flops 4094373888 | bytes 10248192 | tf_op jit(solution)/shard_map/dot_general | solution.py:34
  448.1 4.5 copy.124
  458.2 7.3 %fusion.156 = (bf16[1,4,256,1152]{3,2,1,0:T(8,128)(2,1)S(1)}, f32[1,4,256,1152]{3,2,1,0:T(8,128)}) fusion(bf16[4,256,864]{2,1,0:T(8,128)(2,1)} %bitcast.293, bf16[1152,864,1]{1,0,2:T(8,128)(2,1)} %bitcast.56), kind=kOutput, calls=%fused_computation.353 | convolution fusion | flops 2039611392 | bytes 10838016 | tf_op jit(solution)/shard_map/dot_general | solution.py:30
  465.5 6.1 fusion.155
  472.7 8.0 %collective-permute-done.60 = bf16[144,864]{1,0:T(8,128)(2,1)S(1)} collective-permute-done((bf16[144,864]{1,0:T(8,128)(2,1)S(1)}, bf16[144,864]{1,0:T(8,128)(2,1)S(1)}, u32[]{:S(2)}, u32[]{:S(2)}) %collective-permute-start.60) | collective-permute-done | bytes 248864 | tf_op jit(solution)/shard_map/ppermute | solution.py:22
  488.4 5.4 collective-permute-done.57
  493.8 13.6 %collective-permute-done.59 = bf16[144,864]{1,0:T(8,128)(2,1)S(1)} collective-permute-done((bf16[144,864]{1,0:T(8,128)(2,1)S(1)}, bf16[144,864]{1,0:T(8,128)(2,1)S(1)}, u32[]{:S(2)}, u32[]{:S(2)}) %collective-permute-start.59) | collective-permute-done | bytes 248864 | tf_op jit(solution)/shard_map/ppermute | solution.py:22
  507.9 2.8 collective-permute-start.63
  512.8 8.9 %collective-permute-done.63 = bf16[3,144,288]{2,0,1:T(4,128)(2,1)S(1)} collective-permute-done((bf16[3,144,288]{2,0,1:T(4,128)(2,1)S(1)}, bf16[3,144,288]{2,0,1:T(4,128)(2,1)S(1)}, u32[]{:S(2)}, u32[]{:S(2)}) %collective-permute-start.63) | collective-permute-done | bytes 248864 | tf_op jit(solution)/shard_map/ppermute | solution.py:22
  528.2 6.2 collective-permute-done.46
  536.8 10.0 %collective-permute-done.52 = bf16[1,256,1152]{2,1,0:T(8,128)(2,1)S(1)} collective-permute-done((bf16[1,256,1152]{2,1,0:T(8,128)(2,1)S(1)}, bf16[1,256,1152]{2,1,0:T(8,128)(2,1)S(1)}, u32[]{:S(2)}, u32[]{:S(2)}) %collective-permute-start.52) | collective-permute-done | bytes 589856 | tf_op jit(solution)/shard_map/ppermute | solution.py:22
  546.8 3.8 fusion.49
  557.2 12.1 %all-to-all-start.2 = ((bf16[8,2,6912]{2,1,0:T(2,128)(2,1)}), bf16[8,2,6912]{2,1,0:T(2,128)(2,1)S(1)}, u32[]{:S(2)}, u32[]{:S(2)}) async-start(bf16[8,2,6912]{2,1,0:T(2,128)(2,1)} %broadcast_in_dim.41), calls=%async_computation.2 | async-start | bytes 442368 | tf_op jit(solution)/shard_map/all_to_all | solution.py:76
  569.3 3.1 fusion.48
  572.4 4.8 all-to-all-done.2
  578.5 3.3 all-to-all-start.3
  581.9 3.0 pad_maximum_fusion.8
  588.7 3.6 all-to-all-start.4
  597.8 3.5 all-to-all-start.7
  605.6 3.6 all-to-all-done.7
  610.0 3.5 all-to-all-start.5
  615.7 7.3 %all-to-all-done.5 = bf16[4,144,2,144]{3,2,1,0:T(2,128)(2,1)S(1)} async-done(((bf16[4,144,2,144]{3,2,1,0:T(2,128)(2,1)}), bf16[4,144,2,144]{3,2,1,0:T(2,128)(2,1)S(1)}, u32[]{:S(2)}, u32[]{:S(2)}) %all-to-all-start.5) | async-done | bytes 331808 | tf_op jit(solution)/shard_map/all_to_all | solution.py:412
  (510 shorter events, 178.0 us)
Async XLA Ops:
  7.2 90.7 %all-gather.9.cloned.1.call-start = ((), (), s32[]{:S(2)}) async-start(), calls=%async_computation.15 | async-start | bytes 1492992 | tf_op jit(solution)/shard_map/all_gather | solution.py:246
  9.0 195.8 %all-gather.5.cloned.1.call-start = ((), (), s32[]{:S(2)}) async-start(), calls=%async_computation.11 | async-start | bytes 2985984 | tf_op jit(solution)/shard_map/all_gather | solution.py:256
  15.4 46.8 %collective-permute-start.3 = (bf16[144,864]{1,0:T(8,128)(2,1)}, bf16[144,864]{1,0:T(8,128)(2,1)}, u32[]{:S(2)}, u32[]{:S(2)}) collective-permute-start(bf16[144,864]{1,0:T(8,128)(2,1)} %get-tuple-element.134), channel_id=1, source_target_pairs={{0,4},{4,0},{8,12},{12,8},{16,20},{20,16},{24,28},{28,24},{1,5},{5... | collective-permute-start | bytes 746504 | tf_op jit(solution)/shard_map/ppermute | solution.py:22
  18.3 43.9 %collective-permute-start.4 = (bf16[144,864]{1,0:T(8,128)(2,1)}, bf16[144,864]{1,0:T(8,128)(2,1)}, u32[]{:S(2)}, u32[]{:S(2)}) collective-permute-start(bf16[144,864]{1,0:T(8,128)(2,1)} %get-tuple-element.134), channel_id=1, source_target_pairs={{0,8},{4,12},{8,0},{12,4},{16,24},{20,28},{24,16},{28,20},{1,9},{5... | collective-permute-start | bytes 746504 | tf_op jit(solution)/shard_map/ppermute | solution.py:22
  19.9 44.4 %collective-permute-start.6 = (bf16[144,864]{1,0:T(8,128)(2,1)}, bf16[144,864]{1,0:T(8,128)(2,1)}, u32[]{:S(2)}, u32[]{:S(2)}) collective-permute-start(bf16[144,864]{1,0:T(8,128)(2,1)} %get-tuple-element.134), channel_id=1, source_target_pairs={{0,16},{4,20},{8,24},{12,28},{16,0},{20,4},{24,8},{28,12},{1,17},{... | collective-permute-start | bytes 746504 | tf_op jit(solution)/shard_map/ppermute | solution.py:22
  22.5 41.9 %collective-permute-start.8 = (bf16[144,864]{1,0:T(8,128)(2,1)}, bf16[144,864]{1,0:T(8,128)(2,1)S(1)}, u32[]{:S(2)}, u32[]{:S(2)}) collective-permute-start(bf16[144,864]{1,0:T(8,128)(2,1)} %get-tuple-element.134), channel_id=1, source_target_pairs={{0,24},{4,28},{8,16},{12,20},{16,8},{20,12},{24,0},{28,4},{1,25},{... | collective-permute-start | bytes 746504 | tf_op jit(solution)/shard_map/ppermute | solution.py:22
  25.7 25.5 %all-to-all-start = ((bf16[8,2,1224]{2,1,0:T(2,128)(2,1)}), bf16[8,2,1224]{2,1,0:T(2,128)(2,1)S(1)}, u32[]{:S(2)}, u32[]{:S(2)}) async-start(bf16[8,2,1224]{2,1,0:T(2,128)(2,1)} %reshape.1031), calls=%async_computation | async-start | bytes 81920 | tf_op jit(solution)/shard_map/all_to_all | solution.py:76
  30.6 182.4 %all-gather.7.cloned.1.call-start = ((), (), s32[]{:S(2)}) async-start(), calls=%async_computation.12 | async-start | bytes 2985984 | tf_op jit(solution)/shard_map/all_gather | solution.py:257
  30.6 52.3 %collective-permute-start.1 = (bf16[2,256,1152]{2,1,0:T(8,128)(2,1)S(1)}, bf16[2,256,1152]{2,1,0:T(8,128)(2,1)}, u32[]{:S(2)}, u32[]{:S(2)}) collective-permute-start(bf16[2,256,1152]{2,1,0:T(8,128)(2,1)S(1)} %copy-done.15), channel_id=1, source_target_pairs={{0,2},{1,3},{2,0},{3,1},{4,6},{5,7},{6,4},{7,5},{8,10},{9,11},{10,... | collective-permute-start | bytes 3538952 | tf_op jit(solution)/shard_map/ppermute | solution.py:22
  57.5 33.1 %all-to-all-start.1 = ((f32[8,2,6912]{2,1,0:T(2,128)}), f32[8,2,6912]{2,1,0:T(2,128)}, u32[]{:S(2)}, u32[]{:S(2)}) async-start(f32[8,2,6912]{2,1,0:T(2,128)} %reshape.956), calls=%async_computation.1 | async-start | bytes 884736 | tf_op jit(solution)/shard_map/all_to_all | solution.py:76
  62.1 522.8 %reduce-scatter.10.cloned.1.call-start = ((), (), s32[]{:S(2)}) async-start(), calls=%async_computation.16 | async-start | bytes 1492992
  62.2 33.1 %collective-permute-start = (bf16[2,256,1152]{2,1,0:T(8,128)(2,1)S(1)}, bf16[2,256,1152]{2,1,0:T(8,128)(2,1)}, u32[]{:S(2)}, u32[]{:S(2)}) collective-permute-start(bf16[2,256,1152]{2,1,0:T(8,128)(2,1)S(1)} %copy-done.15), channel_id=1, source_target_pairs={{0,1},{1,0},{2,3},{3,2},{4,5},{5,4},{6,7},{7,6},{8,9},{9,8},{10,11... | collective-permute-start | bytes 3538952 | tf_op jit(solution)/shard_map/ppermute | solution.py:22
  62.3 13.7 %collective-permute-start.5 = (bf16[144,864]{1,0:T(8,128)(2,1)}, bf16[144,864]{1,0:T(8,128)(2,1)S(1)}, u32[]{:S(2)}, u32[]{:S(2)}) collective-permute-start(bf16[144,864]{1,0:T(8,128)(2,1)} %collective-permute-done.4), channel_id=1, source_target_pairs={{0,4},{4,0},{8,12},{12,8},{16,20},{20,16},{24,28},{28,24},{1,5},{5... | collective-permute-start | bytes 746504 | tf_op jit(solution)/shard_map/ppermute | solution.py:22
  64.3 17.2 %collective-permute-start.7 = (bf16[144,864]{1,0:T(8,128)(2,1)}, bf16[144,864]{1,0:T(8,128)(2,1)S(1)}, u32[]{:S(2)}, u32[]{:S(2)}) collective-permute-start(bf16[144,864]{1,0:T(8,128)(2,1)} %collective-permute-done.6), channel_id=1, source_target_pairs={{0,4},{4,0},{8,12},{12,8},{16,20},{20,16},{24,28},{28,24},{1,5},{5... | collective-permute-start | bytes 746504 | tf_op jit(solution)/shard_map/ppermute | solution.py:22
  64.4 25.5 %collective-permute-start.9 = (bf16[144,864]{1,0:T(8,128)(2,1)S(1)}, bf16[144,864]{1,0:T(8,128)(2,1)S(1)}, u32[]{:S(2)}, u32[]{:S(2)}) collective-permute-start(bf16[144,864]{1,0:T(8,128)(2,1)S(1)} %collective-permute-done.8), channel_id=1, source_target_pairs={{0,4},{4,0},{8,12},{12,8},{16,20},{20,16},{24,28},{28,24},{1,5},{5... | collective-permute-start | bytes 746504 | tf_op jit(solution)/shard_map/ppermute | solution.py:22
  82.9 15.0 %collective-permute-start.2 = (bf16[2,256,1152]{2,1,0:T(8,128)(2,1)}, bf16[2,256,1152]{2,1,0:T(8,128)(2,1)}, u32[]{:S(2)}, u32[]{:S(2)}) collective-permute-start(bf16[2,256,1152]{2,1,0:T(8,128)(2,1)} %collective-permute-done.1), channel_id=1, source_target_pairs={{0,1},{1,0},{2,3},{3,2},{4,5},{5,4},{6,7},{7,6},{8,9},{9,8},{10,11... | collective-permute-start | bytes 3538952 | tf_op jit(solution)/shard_map/ppermute | solution.py:22
  97.9 69.0 %collective-permute-start.13 = (bf16[8,72,1152]{2,1,0:T(8,128)(2,1)}, bf16[8,72,1152]{2,1,0:T(8,128)(2,1)}, u32[]{:S(2)}, u32[]{:S(2)}) collective-permute-start(bf16[8,72,1152]{2,1,0:T(8,128)(2,1)} %bitcast.309), channel_id=1, source_target_pairs={{0,1},{1,0},{2,3},{3,2},{4,5},{5,4},{6,7},{7,6},{8,9},{9,8},{10,11... | collective-permute-start | bytes 3981320 | tf_op jit(solution)/shard_map/ppermute | solution.py:22
  125.6 28.5 %collective-permute-start.10 = (bf16[1,256,288]{2,1,0:T(8,128)(2,1)S(1)}, bf16[1,256,288]{2,1,0:T(8,128)(2,1)S(1)}, u32[]{:S(2)}, u32[]{:S(2)}) collective-permute-start(bf16[1,256,288]{2,1,0:T(8,128)(2,1)S(1)} %get-tuple-element.205), channel_id=1, source_target_pairs={{0,1},{1,0},{2,3},{3,2},{4,5},{5,4},{6,7},{7,6},{8,9},{9,8},{10,11... | collective-permute-start | bytes 442376 | tf_op jit(solution)/shard_map/ppermute | solution.py:22
  126.0 29.7 %collective-permute-start.11 = (bf16[1,256,288]{2,1,0:T(8,128)(2,1)S(1)}, bf16[1,256,288]{2,1,0:T(8,128)(2,1)S(1)}, u32[]{:S(2)}, u32[]{:S(2)}) collective-permute-start(bf16[1,256,288]{2,1,0:T(8,128)(2,1)S(1)} %get-tuple-element.204), channel_id=1, source_target_pairs={{0,2},{1,3},{2,0},{3,1},{4,6},{5,7},{6,4},{7,5},{8,10},{9,11},{10,... | collective-permute-start | bytes 442376 | tf_op jit(solution)/shard_map/ppermute | solution.py:22
  127.4 28.8 %collective-permute-start.12 = (bf16[1,256,288]{2,1,0:T(8,128)(2,1)S(1)}, bf16[1,256,288]{2,1,0:T(8,128)(2,1)S(1)}, u32[]{:S(2)}, u32[]{:S(2)}) collective-permute-start(bf16[1,256,288]{2,1,0:T(8,128)(2,1)S(1)} %get-tuple-element.203), channel_id=1, source_target_pairs={{0,3},{1,2},{2,1},{3,0},{4,7},{5,6},{6,5},{7,4},{8,11},{9,10},{10,... | collective-permute-start | bytes 442376 | tf_op jit(solution)/shard_map/ppermute | solution.py:22
  175.6 16.5 %collective-permute-start.24 = (bf16[256,1152]{1,0:T(8,128)(2,1)}, bf16[256,1152]{1,0:T(8,128)(2,1)}, u32[]{:S(2)}, u32[]{:S(2)}) collective-permute-start(bf16[256,1152]{1,0:T(8,128)(2,1)} %fusion.94), channel_id=1, source_target_pairs={{0,2},{1,3},{2,0},{3,1},{4,6},{5,7},{6,4},{7,5},{8,10},{9,11},{10,... | collective-permute-start | bytes 1769480 | tf_op jit(solution)/shard_map/ppermute | solution.py:22
  178.5 26.2 %collective-permute-start.15 = (bf16[256,1152]{1,0:T(8,128)(2,1)}, bf16[256,1152]{1,0:T(8,128)(2,1)}, u32[]{:S(2)}, u32[]{:S(2)}) collective-permute-start(bf16[256,1152]{1,0:T(8,128)(2,1)} %fusion.93), channel_id=1, source_target_pairs={{0,2},{1,3},{2,0},{3,1},{4,6},{5,7},{6,4},{7,5},{8,10},{9,11},{10,... | collective-permute-start | bytes 1769480 | tf_op jit(solution)/shard_map/ppermute | solution.py:22
  179.0 25.8 %collective-permute-start.23 = (bf16[256,1152]{1,0:T(8,128)(2,1)}, bf16[256,1152]{1,0:T(8,128)(2,1)}, u32[]{:S(2)}, u32[]{:S(2)}) collective-permute-start(bf16[256,1152]{1,0:T(8,128)(2,1)} %fusion.94), channel_id=1, source_target_pairs={{0,1},{1,0},{2,3},{3,2},{4,5},{5,4},{6,7},{7,6},{8,9},{9,8},{10,11... | collective-permute-start | bytes 1769480 | tf_op jit(solution)/shard_map/ppermute | solution.py:22
  192.0 12.8 %collective-permute-start.25 = (bf16[256,1152]{1,0:T(8,128)(2,1)}, bf16[256,1152]{1,0:T(8,128)(2,1)}, u32[]{:S(2)}, u32[]{:S(2)}) collective-permute-start(bf16[256,1152]{1,0:T(8,128)(2,1)} %collective-permute-done.24), channel_id=1, source_target_pairs={{0,1},{1,0},{2,3},{3,2},{4,5},{5,4},{6,7},{7,6},{8,9},{9,8},{10,11... | collective-permute-start | bytes 1769480 | tf_op jit(solution)/shard_map/ppermute | solution.py:22
  193.1 27.5 %collective-permute-start.14 = (bf16[256,1152]{1,0:T(8,128)(2,1)}, bf16[256,1152]{1,0:T(8,128)(2,1)}, u32[]{:S(2)}, u32[]{:S(2)}) collective-permute-start(bf16[256,1152]{1,0:T(8,128)(2,1)} %fusion.93), channel_id=1, source_target_pairs={{0,1},{1,0},{2,3},{3,2},{4,5},{5,4},{6,7},{7,6},{8,9},{9,8},{10,11... | collective-permute-start | bytes 1769480 | tf_op jit(solution)/shard_map/ppermute | solution.py:22
  204.7 15.9 %collective-permute-start.16 = (bf16[256,1152]{1,0:T(8,128)(2,1)}, bf16[256,1152]{1,0:T(8,128)(2,1)}, u32[]{:S(2)}, u32[]{:S(2)}) collective-permute-start(bf16[256,1152]{1,0:T(8,128)(2,1)} %collective-permute-done.15), channel_id=1, source_target_pairs={{0,1},{1,0},{2,3},{3,2},{4,5},{5,4},{6,7},{7,6},{8,9},{9,8},{10,11... | collective-permute-start | bytes 1769480 | tf_op jit(solution)/shard_map/ppermute | solution.py:22
  220.1 12.0 %collective-permute-start.27 = (bf16[256,1152]{1,0:T(8,128)(2,1)S(1)}, bf16[256,1152]{1,0:T(8,128)(2,1)S(1)}, u32[]{:S(2)}, u32[]{:S(2)}) collective-permute-start(bf16[256,1152]{1,0:T(8,128)(2,1)S(1)} %get-tuple-element.156), channel_id=1, source_target_pairs={{0,1},{1,0},{2,3},{3,2},{4,5},{5,4},{6,7},{7,6},{8,9},{9,8},{10,11... | collective-permute-start | bytes 1769480 | tf_op jit(solution)/shard_map/ppermute | solution.py:22
  232.2 16.2 %collective-permute-start.28 = (bf16[256,1152]{1,0:T(8,128)(2,1)S(1)}, bf16[256,1152]{1,0:T(8,128)(2,1)S(1)}, u32[]{:S(2)}, u32[]{:S(2)}) collective-permute-start(bf16[256,1152]{1,0:T(8,128)(2,1)S(1)} %fusion.73), channel_id=1, source_target_pairs={{0,2},{1,3},{2,0},{3,1},{4,6},{5,7},{6,4},{7,5},{8,10},{9,11},{10,... | collective-permute-start | bytes 1769480 | tf_op jit(solution)/shard_map/ppermute | solution.py:22
  233.9 26.7 %collective-permute-start.19 = (bf16[256,1152]{1,0:T(8,128)(2,1)S(1)}, bf16[256,1152]{1,0:T(8,128)(2,1)S(1)}, u32[]{:S(2)}, u32[]{:S(2)}) collective-permute-start(bf16[256,1152]{1,0:T(8,128)(2,1)S(1)} %fusion.75), channel_id=1, source_target_pairs={{0,2},{1,3},{2,0},{3,1},{4,6},{5,7},{6,4},{7,5},{8,10},{9,11},{10,... | collective-permute-start | bytes 1769480 | tf_op jit(solution)/shard_map/ppermute | solution.py:22
  262.6 16.2 %collective-permute-start.39 = (bf16[256,1152]{1,0:T(8,128)(2,1)S(1)}, bf16[256,1152]{1,0:T(8,128)(2,1)S(1)}, u32[]{:S(2)}, u32[]{:S(2)}) collective-permute-start(bf16[256,1152]{1,0:T(8,128)(2,1)S(1)} %get-tuple-element.175), channel_id=1, source_target_pairs={{0,2},{1,3},{2,0},{3,1},{4,6},{5,7},{6,4},{7,5},{8,10},{9,11},{10,... | collective-permute-start | bytes 1769480 | tf_op jit(solution)/shard_map/ppermute | solution.py:22
  264.1 26.1 %collective-permute-start.30 = (bf16[256,1152]{1,0:T(8,128)(2,1)S(1)}, bf16[256,1152]{1,0:T(8,128)(2,1)S(1)}, u32[]{:S(2)}, u32[]{:S(2)}) collective-permute-start(bf16[256,1152]{1,0:T(8,128)(2,1)S(1)} %get-tuple-element.176), channel_id=1, source_target_pairs={{0,2},{1,3},{2,0},{3,1},{4,6},{5,7},{6,4},{7,5},{8,10},{9,11},{10,... | collective-permute-start | bytes 1769480 | tf_op jit(solution)/shard_map/ppermute | solution.py:22
  264.6 25.5 %collective-permute-start.38 = (bf16[256,1152]{1,0:T(8,128)(2,1)S(1)}, bf16[256,1152]{1,0:T(8,128)(2,1)S(1)}, u32[]{:S(2)}, u32[]{:S(2)}) collective-permute-start(bf16[256,1152]{1,0:T(8,128)(2,1)S(1)} %get-tuple-element.175), channel_id=1, source_target_pairs={{0,1},{1,0},{2,3},{3,2},{4,5},{5,4},{6,7},{7,6},{8,9},{9,8},{10,11... | collective-permute-start | bytes 1769480 | tf_op jit(solution)/shard_map/ppermute | solution.py:22
  278.8 25.9 %collective-permute-start.29 = (bf16[256,1152]{1,0:T(8,128)(2,1)S(1)}, bf16[256,1152]{1,0:T(8,128)(2,1)S(1)}, u32[]{:S(2)}, u32[]{:S(2)}) collective-permute-start(bf16[256,1152]{1,0:T(8,128)(2,1)S(1)} %get-tuple-element.176), channel_id=1, source_target_pairs={{0,1},{1,0},{2,3},{3,2},{4,5},{5,4},{6,7},{7,6},{8,9},{9,8},{10,11... | collective-permute-start | bytes 1769480 | tf_op jit(solution)/shard_map/ppermute | solution.py:22
  290.1 14.6 %collective-permute-start.31 = (bf16[256,1152]{1,0:T(8,128)(2,1)S(1)}, bf16[256,1152]{1,0:T(8,128)(2,1)S(1)}, u32[]{:S(2)}, u32[]{:S(2)}) collective-permute-start(bf16[256,1152]{1,0:T(8,128)(2,1)S(1)} %collective-permute-done.30), channel_id=1, source_target_pairs={{0,1},{1,0},{2,3},{3,2},{4,5},{5,4},{6,7},{7,6},{8,9},{9,8},{10,11... | collective-permute-start | bytes 1769480 | tf_op jit(solution)/shard_map/ppermute | solution.py:22
  304.2 14.4 %collective-permute-start.42 = (bf16[256,1152]{1,0:T(8,128)(2,1)S(1)}, bf16[256,1152]{1,0:T(8,128)(2,1)S(1)}, u32[]{:S(2)}, u32[]{:S(2)}) collective-permute-start(bf16[256,1152]{1,0:T(8,128)(2,1)S(1)} %get-tuple-element.152), channel_id=1, source_target_pairs={{0,1},{1,0},{2,3},{3,2},{4,5},{5,4},{6,7},{7,6},{8,9},{9,8},{10,11... | collective-permute-start | bytes 1769480 | tf_op jit(solution)/shard_map/ppermute | solution.py:22
  319.5 16.5 %collective-permute-start.43 = (bf16[256,1152]{1,0:T(8,128)(2,1)}, bf16[256,1152]{1,0:T(8,128)(2,1)}, u32[]{:S(2)}, u32[]{:S(2)}) collective-permute-start(bf16[256,1152]{1,0:T(8,128)(2,1)} %fusion.69), channel_id=1, source_target_pairs={{0,2},{1,3},{2,0},{3,1},{4,6},{5,7},{6,4},{7,5},{8,10},{9,11},{10,... | collective-permute-start | bytes 1769480 | tf_op jit(solution)/shard_map/ppermute | solution.py:22
  321.0 17.5 %collective-permute-start.32 = (bf16[256,1152]{1,0:T(8,128)(2,1)}, bf16[256,1152]{1,0:T(8,128)(2,1)S(1)}, u32[]{:S(2)}, u32[]{:S(2)}) collective-permute-start(bf16[256,1152]{1,0:T(8,128)(2,1)} %get-tuple-element.149), channel_id=1, source_target_pairs={{0,1},{1,0},{2,3},{3,2},{4,5},{5,4},{6,7},{7,6},{8,9},{9,8},{10,11... | collective-permute-start | bytes 1769480 | tf_op jit(solution)/shard_map/ppermute | solution.py:22
  322.5 25.1 %collective-permute-start.34 = (bf16[256,1152]{1,0:T(8,128)(2,1)S(1)}, bf16[256,1152]{1,0:T(8,128)(2,1)S(1)}, u32[]{:S(2)}, u32[]{:S(2)}) collective-permute-start(bf16[256,1152]{1,0:T(8,128)(2,1)S(1)} %fusion.71), channel_id=1, source_target_pairs={{0,2},{1,3},{2,0},{3,1},{4,6},{5,7},{6,4},{7,5},{8,10},{9,11},{10,... | collective-permute-start | bytes 1769480 | tf_op jit(solution)/shard_map/ppermute | solution.py:22
  368.3 226.1 %reduce-scatter.8.cloned.1.call-start = ((), (), s32[]{:S(2)}) async-start(), calls=%async_computation.14 | async-start | bytes 2985984 | tf_op jit(solution)/shard_map/reduce_scatter | solution.py:330
  386.1 25.4 %all-to-all-start.6 = ((f32[8,1,144]{2,1,0:T(1,128)}), f32[8,1,144]{2,1,0:T(1,128)S(1)}, u32[]{:S(2)}, u32[]{:S(2)}) async-start(f32[8,1,144]{2,1,0:T(1,128)} %add.613), calls=%async_computation.7 | async-start | bytes 16384 | tf_op jit(solution)/shard_map/all_to_all | solution.py:76
  390.8 211.9 %reduce-scatter.6.cloned.1.call-start = ((), (), s32[]{:S(2)}) async-start(), calls=%async_computation.13 | async-start | bytes 2985984 | tf_op jit(solution)/shard_map/reduce_scatter | solution.py:331
  399.2 13.0 %collective-permute-start.48 = (bf16[1,256,288]{2,1,0:T(8,128)(2,1)}, bf16[1,256,288]{2,1,0:T(8,128)(2,1)}, u32[]{:S(2)}, u32[]{:S(2)}) collective-permute-start(bf16[1,256,288]{2,1,0:T(8,128)(2,1)} %get-tuple-element.213), channel_id=1, source_target_pairs={{0,2},{1,3},{2,0},{3,1},{4,6},{5,7},{6,4},{7,5},{8,10},{9,11},{10,... | collective-permute-start | bytes 442376 | tf_op jit(solution)/shard_map/ppermute | solution.py:22
  400.7 11.5 %collective-permute-start.49 = (bf16[1,256,288]{2,1,0:T(8,128)(2,1)}, bf16[1,256,288]{2,1,0:T(8,128)(2,1)}, u32[]{:S(2)}, u32[]{:S(2)}) collective-permute-start(bf16[1,256,288]{2,1,0:T(8,128)(2,1)} %get-tuple-element.212), channel_id=1, source_target_pairs={{0,3},{1,2},{2,1},{3,0},{4,7},{5,6},{6,5},{7,4},{8,11},{9,10},{10,... | collective-permute-start | bytes 442376 | tf_op jit(solution)/shard_map/ppermute | solution.py:22
  403.2 23.6 %collective-permute-start.35 = (bf16[1,256,288]{2,1,0:T(8,128)(2,1)}, bf16[1,256,288]{2,1,0:T(8,128)(2,1)}, u32[]{:S(2)}, u32[]{:S(2)}) collective-permute-start(bf16[1,256,288]{2,1,0:T(8,128)(2,1)} %get-tuple-element.218), channel_id=1, source_target_pairs={{0,1},{1,0},{2,3},{3,2},{4,5},{5,4},{6,7},{7,6},{8,9},{9,8},{10,11... | collective-permute-start | bytes 442376 | tf_op jit(solution)/shard_map/ppermute | solution.py:22
  403.5 23.3 %collective-permute-start.36 = (bf16[1,256,288]{2,1,0:T(8,128)(2,1)}, bf16[1,256,288]{2,1,0:T(8,128)(2,1)}, u32[]{:S(2)}, u32[]{:S(2)}) collective-permute-start(bf16[1,256,288]{2,1,0:T(8,128)(2,1)} %get-tuple-element.217), channel_id=1, source_target_pairs={{0,2},{1,3},{2,0},{3,1},{4,6},{5,7},{6,4},{7,5},{8,10},{9,11},{10,... | collective-permute-start | bytes 442376 | tf_op jit(solution)/shard_map/ppermute | solution.py:22
  405.0 21.8 %collective-permute-start.37 = (bf16[1,256,288]{2,1,0:T(8,128)(2,1)}, bf16[1,256,288]{2,1,0:T(8,128)(2,1)}, u32[]{:S(2)}, u32[]{:S(2)}) collective-permute-start(bf16[1,256,288]{2,1,0:T(8,128)(2,1)} %get-tuple-element.216), channel_id=1, source_target_pairs={{0,3},{1,2},{2,1},{3,0},{4,7},{5,6},{6,5},{7,4},{8,11},{9,10},{10,... | collective-permute-start | bytes 442376 | tf_op jit(solution)/shard_map/ppermute | solution.py:22
  454.0 18.7 %collective-permute-start.56 = (bf16[144,864]{1,0:T(8,128)(2,1)S(1)}, bf16[144,864]{1,0:T(8,128)(2,1)S(1)}, u32[]{:S(2)}, u32[]{:S(2)}) collective-permute-start(bf16[144,864]{1,0:T(8,128)(2,1)S(1)} %get-tuple-element.160), channel_id=1, source_target_pairs={{0,4},{4,0},{8,12},{12,8},{16,20},{20,16},{24,28},{28,24},{1,5},{5... | collective-permute-start | bytes 746504 | tf_op jit(solution)/shard_map/ppermute | solution.py:22
  456.1 16.7 %collective-permute-start.58 = (bf16[144,864]{1,0:T(8,128)(2,1)S(1)}, bf16[144,864]{1,0:T(8,128)(2,1)S(1)}, u32[]{:S(2)}, u32[]{:S(2)}) collective-permute-start(bf16[144,864]{1,0:T(8,128)(2,1)S(1)} %get-tuple-element.159), channel_id=1, source_target_pairs={{0,4},{4,0},{8,12},{12,8},{16,20},{20,16},{24,28},{28,24},{1,5},{5... | collective-permute-start | bytes 746504 | tf_op jit(solution)/shard_map/ppermute | solution.py:22
  456.1 24.5 %collective-permute-start.60 = (bf16[144,864]{1,0:T(8,128)(2,1)S(1)}, bf16[144,864]{1,0:T(8,128)(2,1)S(1)}, u32[]{:S(2)}, u32[]{:S(2)}) collective-permute-start(bf16[144,864]{1,0:T(8,128)(2,1)S(1)} %get-tuple-element.158), channel_id=1, source_target_pairs={{0,4},{4,0},{8,12},{12,8},{16,20},{20,16},{24,28},{28,24},{1,5},{5... | collective-permute-start | bytes 746504 | tf_op jit(solution)/shard_map/ppermute | solution.py:22
  458.1 30.2 %collective-permute-start.55 = (bf16[144,864]{1,0:T(8,128)(2,1)S(1)}, bf16[144,864]{1,0:T(8,128)(2,1)S(1)}, u32[]{:S(2)}, u32[]{:S(2)}) collective-permute-start(bf16[144,864]{1,0:T(8,128)(2,1)S(1)} %get-tuple-element.157), channel_id=1, source_target_pairs={{0,4},{4,0},{8,12},{12,8},{16,20},{20,16},{24,28},{28,24},{1,5},{5... | collective-permute-start | bytes 746504 | tf_op jit(solution)/shard_map/ppermute | solution.py:22
  472.7 38.0 %collective-permute-start.45 = (bf16[1,256,1152]{2,1,0:T(8,128)(2,1)}, bf16[1,256,1152]{2,1,0:T(8,128)(2,1)S(1)}, u32[]{:S(2)}, u32[]{:S(2)}) collective-permute-start(bf16[1,256,1152]{2,1,0:T(8,128)(2,1)} %get-tuple-element.148), channel_id=1, source_target_pairs={{0,1},{1,0},{2,3},{3,2},{4,5},{5,4},{6,7},{7,6},{8,9},{9,8},{10,11... | collective-permute-start | bytes 1769480 | tf_op jit(solution)/shard_map/ppermute | solution.py:22
  480.9 12.9 %collective-permute-start.57 = (bf16[144,864]{1,0:T(8,128)(2,1)S(1)}, bf16[144,864]{1,0:T(8,128)(2,1)S(1)}, u32[]{:S(2)}, u32[]{:S(2)}) collective-permute-start(bf16[144,864]{1,0:T(8,128)(2,1)S(1)} %get-tuple-element.161), channel_id=1, source_target_pairs={{0,8},{4,12},{8,0},{12,4},{16,24},{20,28},{24,16},{28,20},{1,9},{5... | collective-permute-start | bytes 746504 | tf_op jit(solution)/shard_map/ppermute | solution.py:22
  482.2 25.3 %collective-permute-start.59 = (bf16[144,864]{1,0:T(8,128)(2,1)S(1)}, bf16[144,864]{1,0:T(8,128)(2,1)S(1)}, u32[]{:S(2)}, u32[]{:S(2)}) collective-permute-start(bf16[144,864]{1,0:T(8,128)(2,1)S(1)} %get-tuple-element.163), channel_id=1, source_target_pairs={{0,16},{4,20},{8,24},{12,28},{16,0},{20,4},{24,8},{28,12},{1,17},{... | collective-permute-start | bytes 746504 | tf_op jit(solution)/shard_map/ppermute | solution.py:22
  484.7 22.8 %collective-permute-start.61 = (bf16[144,864]{1,0:T(8,128)(2,1)S(1)}, bf16[144,864]{1,0:T(8,128)(2,1)S(1)}, u32[]{:S(2)}, u32[]{:S(2)}) collective-permute-start(bf16[144,864]{1,0:T(8,128)(2,1)S(1)} %get-tuple-element.162), channel_id=1, source_target_pairs={{0,24},{4,28},{8,16},{12,20},{16,8},{20,12},{24,0},{28,4},{1,25},{... | collective-permute-start | bytes 746504 | tf_op jit(solution)/shard_map/ppermute | solution.py:22
  488.3 24.0 %collective-permute-start.51 = (bf16[1,256,1152]{2,1,0:T(8,128)(2,1)}, bf16[1,256,1152]{2,1,0:T(8,128)(2,1)}, u32[]{:S(2)}, u32[]{:S(2)}) collective-permute-start(bf16[1,256,1152]{2,1,0:T(8,128)(2,1)} %get-tuple-element.146), channel_id=1, source_target_pairs={{0,1},{1,0},{2,3},{3,2},{4,5},{5,4},{6,7},{7,6},{8,9},{9,8},{10,11... | collective-permute-start | bytes 1769480 | tf_op jit(solution)/shard_map/ppermute | solution.py:22
  493.8 43.0 %collective-permute-start.50 = (bf16[1,256,1152]{2,1,0:T(8,128)(2,1)}, bf16[1,256,1152]{2,1,0:T(8,128)(2,1)}, u32[]{:S(2)}, u32[]{:S(2)}) collective-permute-start(bf16[1,256,1152]{2,1,0:T(8,128)(2,1)} %get-tuple-element.145), channel_id=1, source_target_pairs={{0,1},{1,0},{2,3},{3,2},{4,5},{5,4},{6,7},{7,6},{8,9},{9,8},{10,11... | collective-permute-start | bytes 1769480 | tf_op jit(solution)/shard_map/ppermute | solution.py:22
  507.4 20.7 %collective-permute-start.44 = (bf16[1,256,1152]{2,1,0:T(8,128)(2,1)}, bf16[1,256,1152]{2,1,0:T(8,128)(2,1)}, u32[]{:S(2)}, u32[]{:S(2)}) collective-permute-start(bf16[1,256,1152]{2,1,0:T(8,128)(2,1)} %get-tuple-element.147), channel_id=1, source_target_pairs={{0,1},{1,0},{2,3},{3,2},{4,5},{5,4},{6,7},{7,6},{8,9},{9,8},{10,11... | collective-permute-start | bytes 1769480 | tf_op jit(solution)/shard_map/ppermute | solution.py:22
  507.9 13.8 %collective-permute-start.63 = (bf16[3,144,288]{2,0,1:T(4,128)(2,1)S(1)}, bf16[3,144,288]{2,0,1:T(4,128)(2,1)S(1)}, u32[]{:S(2)}, u32[]{:S(2)}) collective-permute-start(bf16[3,144,288]{2,0,1:T(4,128)(2,1)S(1)} %bitcast.306), channel_id=1, source_target_pairs={{0,2},{1,3},{2,0},{3,1},{4,6},{5,7},{6,4},{7,5},{8,10},{9,11},{10,... | collective-permute-start | bytes 746504 | tf_op jit(solution)/shard_map/ppermute | solution.py:22
  510.7 12.5 %collective-permute-start.62 = (bf16[3,144,288]{2,0,1:T(4,128)(2,1)S(1)}, bf16[3,144,288]{2,0,1:T(4,128)(2,1)S(1)}, u32[]{:S(2)}, u32[]{:S(2)}) collective-permute-start(bf16[3,144,288]{2,0,1:T(4,128)(2,1)S(1)} %bitcast.307), channel_id=1, source_target_pairs={{0,1},{1,0},{2,3},{3,2},{4,5},{5,4},{6,7},{7,6},{8,9},{9,8},{10,11... | collective-permute-start | bytes 746504 | tf_op jit(solution)/shard_map/ppermute | solution.py:22
  512.3 22.0 %collective-permute-start.46 = (bf16[1,256,1152]{2,1,0:T(8,128)(2,1)S(1)}, bf16[1,256,1152]{2,1,0:T(8,128)(2,1)S(1)}, u32[]{:S(2)}, u32[]{:S(2)}) collective-permute-start(bf16[1,256,1152]{2,1,0:T(8,128)(2,1)S(1)} %fusion.66), channel_id=1, source_target_pairs={{0,2},{1,3},{2,0},{3,1},{4,6},{5,7},{6,4},{7,5},{8,10},{9,11},{10,... | collective-permute-start | bytes 1769480 | tf_op jit(solution)/shard_map/ppermute | solution.py:22
  523.3 23.6 %collective-permute-start.52 = (bf16[1,256,1152]{2,1,0:T(8,128)(2,1)S(1)}, bf16[1,256,1152]{2,1,0:T(8,128)(2,1)S(1)}, u32[]{:S(2)}, u32[]{:S(2)}) collective-permute-start(bf16[1,256,1152]{2,1,0:T(8,128)(2,1)S(1)} %fusion.62), channel_id=1, source_target_pairs={{0,2},{1,3},{2,0},{3,1},{4,6},{5,7},{6,4},{7,5},{8,10},{9,11},{10,... | collective-permute-start | bytes 1769480 | tf_op jit(solution)/shard_map/ppermute | solution.py:22
  557.2 20.0 %all-to-all-start.2 = ((bf16[8,2,6912]{2,1,0:T(2,128)(2,1)}), bf16[8,2,6912]{2,1,0:T(2,128)(2,1)S(1)}, u32[]{:S(2)}, u32[]{:S(2)}) async-start(bf16[8,2,6912]{2,1,0:T(2,128)(2,1)} %broadcast_in_dim.41), calls=%async_computation.2 | async-start | bytes 442368 | tf_op jit(solution)/shard_map/all_to_all | solution.py:76
  597.8 11.4 %all-to-all-start.7 = ((bf16[4,144,288]{2,1,0:T(8,128)(2,1)}), bf16[4,144,288]{2,1,0:T(8,128)(2,1)S(1)}, u32[]{:S(2)}, u32[]{:S(2)}) async-start(bf16[4,144,288]{2,1,0:T(8,128)(2,1)} %bitcast.287), calls=%async_computation.9 | async-start | bytes 884736 | tf_op jit(solution)/shard_map/all_to_all | solution.py:412
  610.0 13.0 %all-to-all-start.5 = ((bf16[4,144,2,144]{3,2,1,0:T(2,128)(2,1)}), bf16[4,144,2,144]{3,2,1,0:T(2,128)(2,1)S(1)}, u32[]{:S(2)}, u32[]{:S(2)}) async-start(bf16[4,144,2,144]{3,2,1,0:T(2,128)(2,1)} %bitcast.304), calls=%async_computation.6 | async-start | bytes 1179648 | tf_op jit(solution)/shard_map/all_to_all | solution.py:412
  (126 other events, 1106.7 us)
Sparse Core Ops, SparseCore 0:
  10.8 57.8 all-gather.8
  70.8 58.0 all-gather.4
  131.2 53.6 all-gather.6
  368.4 62.6 reduce-scatter.9
  434.6 83.1 reduce-scatter.7
  521.8 71.3 reduce-scatter.5

commit v4 on v3

--- a/solution.py
+++ b/solution.py
@@ -106,7 +106,7 @@
     return total
 
 
-def attend_kernel(heads, block, packed, mixed, log_sum, mixed_t):
+def attend_kernel(heads, block, packed, after, mixed, log_sum, mixed_t):
     seq_len = packed.shape[1]
     cols = heads * HEAD_DIM
     for h in range(heads):
@@ -161,13 +161,13 @@
     return pl.BlockSpec((1,) + shape, lambda i: (i, 0, 0))
 
 
-def attention(packed, heads, block=1024):
+def attention(packed, after, heads, block=1024):
     lat, seq_len, _ = packed.shape
     cols = heads * HEAD_DIM
     return pl.pallas_call(
         partial(attend_kernel, heads, block),
         grid=(lat,),
-        in_specs=[row_spec(seq_len, 3 * cols)],
+        in_specs=[row_spec(seq_len, 3 * cols), pl.BlockSpec(memory_space=pl.ANY)],
         out_specs=[row_spec(seq_len, cols), row_spec(heads, seq_len)],
         out_shape=[
             jax.ShapeDtypeStruct((lat, seq_len, cols), BF),
@@ -176,7 +176,7 @@
         scratch_shapes=[pltpu.VMEM((cols, seq_len), F32)],
         compiler_params=pltpu.CompilerParams(vmem_limit_bytes=48 * 2**20),
         name="attend",
-    )(packed)
+    )(packed, after)
 
 
 def attention_grad(packed, mixed, log_sum, d_mixed, after, heads, block=512):
@@ -198,6 +198,205 @@
         compiler_params=pltpu.CompilerParams(vmem_limit_bytes=48 * 2**20),
         name="attend_grad",
     )(packed, mixed, log_sum, d_mixed, after)
+
+
+def qkv_kernel(count, *refs):
+    slots, (shift, scale, qkv, normed, packed) = refs[:count], refs[count:]
+    chunk, width = slots[0].shape[1:]
+    for j in range(count):
+        value = ln_parts(slots[j][0].astype(F32))[0] * (1.0 + scale[0]) + shift[0]
+        normed[0, j] = value.astype(BF)
+    rows = normed[0].reshape(count * chunk, width)
+    packed[0] = matmul(rows, qkv[...]).astype(BF).reshape(count, chunk, packed.shape[3])
+
+
+def qkv_forward(slots, group, per, shift, scale, qkv):
+    count = len(slots)
+    _, tok, width = slots[0].shape
+    chunk = max(16, 256 // count)
+    row = pl.BlockSpec((1, 1, width), lambda i, c: (i, 0, 0))
+    cols = qkv.shape[1]
+    return pl.pallas_call(
+        partial(qkv_kernel, count),
+        grid=(per, tok // chunk),
+        in_specs=[pl.BlockSpec((1, chunk, width), lambda i, c: (group * per + i, c, 0))] * count
+        + [row, row, pl.BlockSpec((width, cols), lambda i, c: (0, 0))],
+        out_specs=[
+            pl.BlockSpec((1, count, chunk, width), lambda i, c: (i, 0, c, 0)),
+            pl.BlockSpec((1, count, chunk, cols), lambda i, c: (i, 0, c, 0)),
+        ],
+        out_shape=[
+            jax.ShapeDtypeStruct((per, count, tok, width), BF),
+            jax.ShapeDtypeStruct((per, count, tok, cols), BF),
+        ],
+        compiler_params=pltpu.CompilerParams(vmem_limit_bytes=48 * 2**20),
+        name="qkv_forward",
+    )(*slots, shift, scale, qkv)
+
+
+def mlp_kernel(count, *refs):
+    inputs, grads = refs[:count], refs[count : 2 * count]
+    gate, fc1, bias, fc2, x_all, g_all, activated, d_hidden, d_norm, d_bias = refs[2 * count :]
+    chunk, width = inputs[0].shape[1:]
+    hid = fc1.shape[1]
+    for j in range(count):
+        x_all[0, j] = inputs[j][0]
+        g_all[0, j] = (gate[0] * grads[j][0].astype(F32)).astype(BF)
+    x = x_all[0].reshape(count * chunk, width)
+    g = g_all[0].reshape(count * chunk, width)
+    hidden = matmul(x, fc1[...]) + bias[...]
+    square = hidden * hidden
+    tanh = jnp.tanh(GELU_C * (hidden + GELU_A * hidden * square))
+    half = 0.5 * (1.0 + tanh)
+    activated[0] = (hidden * half).astype(BF).reshape(count, chunk, hid)
+    slope = half + (0.5 * GELU_C) * hidden * (1.0 - tanh * tanh) * (1.0 + 3.0 * GELU_A * square)
+    d_h = (matmul_nt(g, fc2[...]) * slope).astype(BF)
+    d_hidden[0] = d_h.reshape(count, chunk, hid)
+    d_norm[0] = matmul_nt(d_h, fc1[...]).astype(BF).reshape(count, chunk, width)
+
+    @pl.when((pl.program_id(0) == 0) & (pl.program_id(1) == 0))
+    def _():
+        d_bias[...] = jnp.zeros_like(d_bias)
+
+    d_bias[...] += jnp.sum(d_h.astype(F32), axis=0, keepdims=True)
+
+
+def mlp(inputs, grads, group, gate, fc1, bias, fc2):
+    count = len(inputs)
+    per, tok, width = inputs[0].shape
+    hid = fc1.shape[1]
+    chunk = max(16, 256 // count)
+    slot = pl.BlockSpec((1, chunk, width), lambda i, c: (i, c, 0))
+    late = pl.BlockSpec((1, chunk, width), lambda i, c: (group * per + i, c, 0))
+
+    def whole(rows, cols):
+        return pl.BlockSpec((rows, cols), lambda i, c: (0, 0))
+
+    wide = pl.BlockSpec((1, count, chunk, width), lambda i, c: (i, 0, c, 0))
+    inner = pl.BlockSpec((1, count, chunk, hid), lambda i, c: (i, 0, c, 0))
+    shape_wide = jax.ShapeDtypeStruct((per, count, tok, width), BF)
+    shape_inner = jax.ShapeDtypeStruct((per, count, tok, hid), BF)
+    return pl.pallas_call(
+        partial(mlp_kernel, count),
+        grid=(per, tok // chunk),
+        in_specs=[slot] * count
+        + [late] * count
+        + [pl.BlockSpec((1, 1, width), lambda i, c: (i, 0, 0))]
+        + [whole(width, hid), whole(1, hid), whole(hid, width)],
+        out_specs=[wide, wide, inner, inner, wide, whole(1, hid)],
+        out_shape=[shape_wide, shape_wide, shape_inner, shape_inner, shape_wide]
+        + [jax.ShapeDtypeStruct((1, hid), F32)],
+        compiler_params=pltpu.CompilerParams(vmem_limit_bytes=56 * 2**20),
+        name="mlp",
+    )(*inputs, *grads, gate, fc1, bias, fc2)
+
+
+def mlp_out_kernel(activated, fc2, after, out):
+    count, chunk, hid = activated.shape[1:]
+    rows = activated[0].reshape(count * chunk, hid)
+    out[0] = matmul(rows, fc2[...]).astype(BF).reshape(count, chunk, out.shape[3])
+
+
+def mlp_out_terms(activated, fc2, after):
+    per, count, tok, hid = activated.shape
+    width = fc2.shape[1]
+    chunk = max(16, 256 // count)
+    return pl.pallas_call(
+        mlp_out_kernel,
+        grid=(per, tok // chunk),
+        in_specs=[
+            pl.BlockSpec((1, count, chunk, hid), lambda i, c: (i, 0, c, 0)),
+            pl.BlockSpec((hid, width), lambda i, c: (0, 0)),
+            pl.BlockSpec(memory_space=pl.ANY),
+        ],
+        out_specs=pl.BlockSpec((1, count, chunk, width), lambda i, c: (i, 0, c, 0)),
+        out_shape=jax.ShapeDtypeStruct((per, count, tok, width), BF),
+        compiler_params=pltpu.CompilerParams(vmem_limit_bytes=48 * 2**20),
+        name="mlp_out_terms",
+    )(activated, fc2, after)
+
+
+def resid_grad_kernel(count, *refs):
+    d_norm, resid_mid, attn_out, cotangent, scale, gate, proj, after = refs[:8]
+    d_resid, d_attn, d_shift, d_scale, d_gate = refs[8:13]
+    d_attended = refs[13:]
+    normed, inv_std = ln_parts(resid_mid[0])
+    grad = d_norm[0]
+    total = cotangent[0].astype(F32) + ln_backward(grad * (1.0 + scale[0]), normed, inv_std)
+    d_resid[0] = total
+    d_a = (gate[0] * total).astype(BF)
+    d_attn[0] = d_a
+    back = matmul_nt(d_a, proj[...]).astype(BF)
+    cols = back.shape[1] // count
+    for j in range(count):
+        d_attended[j][0] = back[:, j * cols : (j + 1) * cols]
+
+    @pl.when(pl.program_id(1) == 0)
+    def _():
+        d_shift[...] = jnp.zeros_like(d_shift)
+        d_scale[...] = jnp.zeros_like(d_scale)
+        d_gate[...] = jnp.zeros_like(d_gate)
+
+    d_shift[0] += jnp.sum(grad, axis=0, keepdims=True)
+    d_scale[0] += jnp.sum(grad * normed, axis=0, keepdims=True)
+    d_gate[0] += jnp.sum(total * attn_out[0], axis=0, keepdims=True)
+
+
+def resid_grad(d_norm, resid_mid, attn_out, cotangent, group, scale, gate, proj, after, count):
+    per, tok, width = d_norm.shape
+    chunk = min(tok, 128)
+    block = pl.BlockSpec((1, chunk, width), lambda i, c: (i, c, 0))
+    row = pl.BlockSpec((1, 1, width), lambda i, c: (i, 0, 0))
+    part = pl.BlockSpec((1, chunk, width // count), lambda i, c: (i, c, 0))
+    row_shape = jax.ShapeDtypeStruct((per, 1, width), F32)
+    return pl.pallas_call(
+        partial(resid_grad_kernel, count),
+        grid=(per, tok // chunk),
+        in_specs=[
+            block,
+            block,
+            block,
+            pl.BlockSpec((1, chunk, width), lambda i, c: (group * per + i, c, 0)),
+            row,
+            row,
+            pl.BlockSpec((width, width), lambda i, c: (0, 0)),
+            pl.BlockSpec(memory_space=pl.ANY),
+        ],
+        out_specs=[block, block, row, row, row] + [part] * count,
+        out_shape=[
+            jax.ShapeDtypeStruct((per, tok, width), F32),
+            jax.ShapeDtypeStruct((per, tok, width), BF),
+            row_shape,
+            row_shape,
+            row_shape,
+        ]
+        + [jax.ShapeDtypeStruct((per, tok, width // count), BF)] * count,
+        compiler_params=pltpu.CompilerParams(vmem_limit_bytes=48 * 2**20),
+        name="resid_grad",
+    )(d_norm, resid_mid, attn_out, cotangent, scale, gate, proj, after)
+
+
+def unpack_kernel(joined, after, *parts):
+    start = 0
+    for part in parts:
+        part[0] = joined[0, start : start + part.shape[1]]
+        start += part.shape[1]
+
+
+def unpack(joined, after, row_counts):
+    count, rows, width = joined.shape
+    return pl.pallas_call(
+        unpack_kernel,
+        grid=(count,),
+        in_specs=[
+            pl.BlockSpec((1, rows, width), lambda i: (i, 0, 0)),
+            pl.BlockSpec(memory_space=pl.ANY),
+        ],
+        out_specs=[pl.BlockSpec((1, n, width), lambda i: (i, 0, 0)) for n in row_counts],
+        out_shape=[jax.ShapeDtypeStruct((count, n, width), joined.dtype) for n in row_counts],
+        compiler_params=pltpu.CompilerParams(vmem_limit_bytes=32 * 2**20),
+        name="unpack",
+    )(joined, after)
 
 
 def on_device(tokens, conditioning, w_mod, b_mod, w_qkv, w_proj, w_fc1, b_fc1, w_fc2, cotangent):
@@ -236,6 +435,7 @@
     modulation = jnp.sum(dp_exchange(mod_terms.reshape(dp_n, lat, 6 * width)), axis=0)
 
     tok_slots = seq_gather(tokens)
+    cot_slots = seq_gather(cotangent)
 
     qkv_here = jnp.concatenate(
         [lax.dynamic_slice(w_qkv, (0, t * width + seq * cols), (rows, cols)) for t in range(3)],
@@ -243,9 +443,6 @@
     )
     qkv = dp_gather(qkv_here, lambda d: d).reshape(width, 3 * cols)
     half = rows // 2
-    proj_mine = lax.all_gather(
-        lax.dynamic_slice(w_proj, (core * half, 0), (half, width)), "dp", axis=0
-    )
     fc1_here = jnp.concatenate(
         [
             lax.dynamic_slice(w_fc1, (0, (d * seq_n + seq) * hid_here), (rows, hid_here))
@@ -253,24 +450,15 @@
         ],
         axis=1,
     )
-    fc1 = lax.all_gather(fc1_here, "dp", axis=0, tiled=True)
-    fc2 = lax.all_gather(
-        lax.dynamic_slice(w_fc2, (seq * hid_here, 0), (hid_here, width)), "dp", axis=0, tiled=True
-    )
-    proj_other = hop(proj_mine, "seq", 1)
-    proj = jnp.where(
-        core == 0,
-        jnp.stack([proj_mine, proj_other], axis=1),
-        jnp.stack([proj_other, proj_mine], axis=1),
-    ).reshape(seq_n, cols, width)
-
-    def by_place(blocks):
-        return jnp.concatenate(
-            [lax.dynamic_index_in_dim(blocks, seq ^ j, 0, keepdims=False) for j in range(seq_n)]
-        )
-
-    proj = by_place(proj)
-
+    fc2_here = lax.dynamic_slice(w_fc2, (seq * hid_here, 0), (hid_here, width))
+    proj_here = lax.dynamic_slice(w_proj, (core * half, 0), (half, width))
+    together = hid == width
+    if together:
+        joined = lax.all_gather(jnp.concatenate([fc1_here, fc2_here, proj_here]), "dp", axis=0)
+    else:
+        proj_mine = lax.all_gather(proj_here, "dp", axis=0)
+        fc1 = lax.all_gather(fc1_here, "dp", axis=0, tiled=True)
+        fc2 = lax.all_gather(fc2_here, "dp", axis=0, tiled=True)
     def part(g):
         return slice(g * per, (g + 1) * per)
 
@@ -281,11 +469,10 @@
     token_values = [tokens[part(g)].astype(F32) for g in range(groups)]
     normed_all, packed, mixed, log_sums, attended = [], [], [], [], []
     for g in range(groups):
-        tok_all = jnp.concatenate([slot[part(g)] for slot in tok_slots], axis=1).astype(F32)
-        normed = (ln_parts(tok_all)[0] * (1.0 + scale_attn[g]) + shift_attn[g]).astype(BF)
+        normed, rows_packed = qkv_forward(tok_slots, g, per, shift_attn[g], scale_attn[g], qkv)
         normed_all.append(normed.reshape(per * seq_len, width))
-        packed.append(matmul(normed_all[g], qkv).astype(BF).reshape(per, seq_len, 3 * cols))
-        out, log_sum = attention(packed[g], heads_here)
+        packed.append(rows_packed.reshape(per, seq_len, 3 * cols))
+        out, log_sum = attention(packed[g], tokens if g == 0 else cot_slots[-1], heads_here)
         mixed.append(out)
         log_sums.append(log_sum)
         out = out.reshape(per, seq_n, tok, cols)
@@ -295,76 +482,88 @@
             )
         )
 
-    attn_out, resid_mid, normed_mid, std_mid, normed_mlp, upstream, d_mlp = ([] for _ in range(7))
+    if together:
+        fc1, fc2, proj_mine = unpack(joined, mixed[-1], [rows, hid_here, half])
+        fc1, fc2 = fc1.reshape(width, hid), fc2.reshape(hid, width)
+    proj_other = hop(proj_mine, "seq", 1)
+    proj = jnp.where(
+        core == 0,
+        jnp.stack([proj_mine, proj_other], axis=1),
+        jnp.stack([proj_other, proj_mine], axis=1),
+    ).reshape(seq_n, cols, width)
+
+    def by_place(blocks):
+        return jnp.concatenate(
+            [lax.dynamic_index_in_dim(blocks, seq ^ j, 0, keepdims=False) for j in range(seq_n)]
+        )
+
+    proj = by_place(proj)
+
+    attn_out, resid_mid, normed_mlp, upstream = [], [], [], []
     for g in range(groups):
         attn_out.append(matmul(attended[g], proj).reshape(per, tok, width))
         resid_mid.append(token_values[g] + gate_attn[g] * attn_out[g])
-        normed, inv_std = ln_parts(resid_mid[g])
-        normed_mid.append(normed)
-        std_mid.append(inv_std)
         normed_mlp.append(
-            (normed * (1.0 + scale_mlp[g]) + shift_mlp[g]).astype(BF).reshape(own, width)
+            (ln_parts(resid_mid[g])[0] * (1.0 + scale_mlp[g]) + shift_mlp[g]).astype(BF)
         )
         upstream.append(cotangent[part(g)].astype(F32))
-        d_mlp.append((gate_mlp[g] * upstream[g]).astype(BF).reshape(own, width))
-    d_mlp_all = [jnp.concatenate(seq_gather(v)) for v in d_mlp]
-    normed_mlp_all = [jnp.concatenate(seq_gather(v)) for v in normed_mlp]
 
     grad_fc1 = grad_fc2 = grad_bias1 = 0.0
-    d_norm, mlp_out = [], []
+    d_norm, activated = [], []
     for g in range(groups):
-        hidden = matmul(normed_mlp_all[g], fc1) + fc1_bias
-        tanh = jnp.tanh(GELU_C * (hidden + GELU_A * hidden * hidden * hidden))
-        activated = (0.5 * hidden * (1.0 + tanh)).astype(BF)
-        gelu_slope = 0.5 * (1.0 + tanh) + 0.5 * hidden * (1.0 - tanh * tanh) * GELU_C * (
-            1.0 + 3.0 * GELU_A * hidden * hidden
+        x_all, d_mlp, active, d_hidden, terms, d_bias = mlp(
+            seq_gather(normed_mlp[g]), cot_slots, g, gate_mlp[g], fc1, fc1_bias[None], fc2
         )
-        d_hidden = (matmul_nt(d_mlp_all[g], fc2) * gelu_slope).astype(BF)
-        terms = matmul_nt(d_hidden, fc1).reshape(seq_n, own, width)
-        d_norm.append(seq_reduce([terms[j] for j in range(seq_n)]).reshape(per, tok, width))
-        grad_fc2 = grad_fc2 + matmul_tn(activated, d_mlp_all[g])
-        grad_fc1 = grad_fc1 + matmul_tn(normed_mlp_all[g], d_hidden)
-        grad_bias1 = grad_bias1 + jnp.sum(d_hidden.astype(F32), axis=0)
-        terms = matmul(activated, fc2).reshape(seq_n, own, width)
-        mlp_out.append(seq_reduce([terms[j] for j in range(seq_n)]).reshape(per, tok, width))
-    sum_fc2 = lax.psum_scatter(grad_fc2.astype(BF), "dp", scatter_dimension=0, tiled=True)
-    sum_fc1 = lax.psum_scatter(grad_fc1.astype(BF), "dp", scatter_dimension=0, tiled=True)
+        d_norm.append(seq_reduce([terms[:, j].astype(F32) for j in range(seq_n)]))
+        activated.append(active)
+        flat = per * seq_len
+        grad_fc2 = grad_fc2 + matmul_tn(active.reshape(flat, hid), d_mlp.reshape(flat, width))
+        grad_fc1 = grad_fc1 + matmul_tn(x_all.reshape(flat, width), d_hidden.reshape(flat, hid))
+        grad_bias1 = grad_bias1 + d_bias[0]
+    grad_fc1 = grad_fc1.astype(BF).reshape(dp_n, rows, hid)
+    grad_fc2 = grad_fc2.astype(BF).reshape(dp_n, hid_here, width)
+    if together:
+        grad_fc = jnp.concatenate([grad_fc1, grad_fc2], axis=1)
+        sum_fc = lax.psum_scatter(grad_fc, "dp", scatter_dimension=0)
+        sum_fc1, sum_fc2 = sum_fc[:rows], sum_fc[rows:]
+    else:
+        grad_fc = grad_fc1
+        sum_fc1 = lax.psum_scatter(grad_fc1, "dp", scatter_dimension=0)
+        sum_fc2 = lax.psum_scatter(grad_fc2, "dp", scatter_dimension=0)
+
+    def stacked(terms):
+        return jnp.concatenate(terms)
+
+    d_shift_mlp, d_scale_mlp, d_gate_attn, d_resid, d_attn, d_attended = ([] for _ in range(6))
+    d_mixed = []
+    for g in range(groups):
+        outs = resid_grad(
+            d_norm[g], resid_mid[g], attn_out[g], cotangent, g, scale_mlp[g], gate_attn[g], proj,
+            grad_fc, seq_n,
+        )
+        d_resid.append(outs[0])
+        d_attn.append(outs[1].reshape(own, width))
+        d_shift_mlp.append(outs[2][:, 0])
+        d_scale_mlp.append(outs[3][:, 0])
+        d_gate_attn.append(outs[4][:, 0])
+        d_attended.append(outs[5])
+        d_mixed.append(jnp.concatenate(seq_exchange(outs[5:]), axis=1))
+    mlp_out = []
+    for g in range(groups):
+        terms = mlp_out_terms(activated[g], fc2, d_attended[-1])
+        mlp_out.append(seq_reduce([terms[:, j].astype(F32) for j in range(seq_n)]))
     output = jnp.concatenate(
         [(resid_mid[g] + gate_mlp[g] * mlp_out[g]).astype(BF) for g in range(groups)]
     )
-
-    def stacked(terms):
-        return jnp.concatenate(terms)
-
     d_gate_mlp = stacked([jnp.sum(upstream[g] * mlp_out[g], axis=1) for g in range(groups)])
-    d_shift_mlp, d_scale_mlp, d_gate_attn, d_resid, d_attn = ([] for _ in range(5))
-    d_mixed, d_attended = [], []
-    for g in range(groups):
-        d_shift_mlp.append(jnp.sum(d_norm[g], axis=1))
-        d_scale_mlp.append(jnp.sum(d_norm[g] * normed_mid[g], axis=1))
-        d_resid.append(
-            upstream[g] + ln_backward(d_norm[g] * (1.0 + scale_mlp[g]), normed_mid[g], std_mid[g])
-        )
-        d_gate_attn.append(jnp.sum(d_resid[g] * attn_out[g], axis=1))
-        d_attn.append((gate_attn[g] * d_resid[g]).astype(BF).reshape(own, width))
-        d_attended.append(matmul_nt(d_attn[g], proj).astype(BF).reshape(per, tok, width))
-        d_mixed.append(
-            jnp.concatenate(
-                seq_exchange([d_attended[g][:, :, j * cols : (j + 1) * cols] for j in range(seq_n)]),
-                axis=1,
-            )
-        )
     grad_proj = by_place(
         matmul_tn(stacked(attended), stacked(d_attn)).astype(BF).reshape(seq_n, cols, width)
-    ).reshape(dp_n, 2, half, width)
+    ).reshape(dp_n, rows, 2, width // 2)
     proj_sent = hop(
-        lax.dynamic_index_in_dim(grad_proj, 1 - core, axis=1, keepdims=False), "seq", 1
-    )
-    proj_terms = lax.dynamic_index_in_dim(grad_proj, core, axis=1, keepdims=False).astype(F32)
+        lax.dynamic_index_in_dim(grad_proj, 1 - core, axis=2, keepdims=False), "seq", 1
+    )
+    proj_terms = lax.dynamic_index_in_dim(grad_proj, core, axis=2, keepdims=False).astype(F32)
     proj_terms = (proj_terms + proj_sent.astype(F32)).astype(BF)
-    sum_proj = lax.psum_scatter(
-        proj_terms.reshape(dp_n * half, width), "dp", scatter_dimension=0, tiled=True
-    )
 
     d_packed, d_first = [], []
     for g in range(groups):
@@ -378,7 +577,12 @@
         parts = matmul_nt(d_packed[g], qkv).reshape(per, seq_n, tok, width)
         d_first.append(seq_reduce([parts[:, j] for j in range(seq_n)]))
     grad_qkv = matmul_tn(stacked(normed_all), stacked(d_packed)).astype(BF)
-    sum_qkv = dp_scatter(grad_qkv.reshape(dp_n, rows, 3 * cols), lambda d: d).astype(BF)
+    sum_last = lax.psum_scatter(
+        jnp.concatenate([proj_terms, grad_qkv.reshape(dp_n, rows, 3 * cols)], axis=2),
+        "dp",
+        scatter_dimension=0,
+    )
+    sum_proj, sum_qkv = sum_last[:, : width // 2], sum_last[:, width // 2 :]
     d_shift_attn, d_scale_attn, grad_tokens = [], [], []
     for g in range(groups):
         normed_tok, std_tok = ln_parts(token_values[g])
@@ -412,21 +616,40 @@
         return lax.all_to_all(blocks, "seq", 0, 0, tiled=True).astype(F32)
 
     share = width // seq_n
-    out_fc2 = to_owner(sum_fc2.reshape(hid_here, seq_n, share).transpose(1, 0, 2))
+    fc2_blocks = sum_fc2.reshape(hid_here, seq_n, share).transpose(1, 0, 2)
+    fc1_blocks = sum_fc1.reshape(rows, seq_n, hid // seq_n).transpose(1, 0, 2)
+    if together:
+        received = to_owner(jnp.concatenate([fc1_blocks, fc2_blocks], axis=1))
+        out_fc1, out_fc2 = received[:, :rows], received[:, rows:]
+    else:
+        out_fc1, out_fc2 = to_owner(fc1_blocks), to_owner(fc2_blocks)
     out_fc2 = out_fc2.reshape(seq_n * hid_here, share)
-    out_proj = to_owner(sum_proj.reshape(half, seq_n, share).transpose(1, 0, 2))
-    out_proj = jnp.sum(out_proj.reshape(seq_n // 2, rows, share), axis=0)
-    blocks = sum_fc1.reshape(rows, seq_n, dp_n // seq_n, hid_here).transpose(1, 0, 2, 3)
-    out_fc1 = to_owner(blocks).transpose(1, 2, 0, 3).reshape(rows, hid)
-    qkv_slots = jnp.stack(
-        seq_gather(sum_qkv.reshape(rows, 3, cols).transpose(1, 0, 2))
-    ).reshape(3 * seq_n, rows, cols)
-    out_qkv = []
-    for i in range(3):
-        block = 3 * seq + i
-        at = ((block % seq_n) ^ seq) * 3 + block // seq_n
-        out_qkv.append(lax.dynamic_index_in_dim(qkv_slots, at, 0, keepdims=False))
-    out_qkv = jnp.concatenate(out_qkv, axis=1).astype(F32)
+    out_fc1 = out_fc1.reshape(seq_n, rows, dp_n // seq_n, hid_here).transpose(1, 2, 0, 3)
+    out_fc1 = out_fc1.reshape(rows, hid)
+    owners = jnp.arange(seq_n)
+    proj_blocks = jnp.where(
+        (owners // (seq_n // 2) == core)[:, None, None],
+        jnp.tile(sum_proj.reshape(rows, seq_n // 2, share).transpose(1, 0, 2), (2, 1, 1)),
+        0,
+    )
+    qkv_thirds = sum_qkv.reshape(rows, 3, cols).transpose(1, 0, 2)
+    qkv_blocks = jnp.stack(
+        [
+            lax.dynamic_index_in_dim(
+                qkv_thirds, jnp.minimum((3 * to - seq + seq_n - 1) // seq_n, 2), 0, keepdims=False
+            )
+            for to in range(seq_n)
+        ]
+    )
+    received = to_owner(jnp.concatenate([proj_blocks, qkv_blocks], axis=1))
+    out_proj = jnp.sum(received[:, :rows], axis=0)
+    out_qkv = jnp.concatenate(
+        [
+            lax.dynamic_index_in_dim(received, (3 * seq + i) % seq_n, 0, keepdims=False)[rows:]
+            for i in range(3)
+        ],
+        axis=1,
+    )
     return (
         output,
         stacked(grad_tokens),

time: 643 us -> 660 us (1.026)
  matrix products: 116 us -> 38.9 us
  Pallas kernels: 49.1 us -> 114 us
  waiting for transfers between devices: 212 us -> 255 us
  starting transfers between devices: 90.6 us -> 66.7 us
  local copies, waits for them, and re-layouts: 80.6 us -> 93.2 us
    pallas_call x0 -> x9, Pallas kernels: none -> 76.3 us  [the longest x2 33.7 us: mlp(): pl.pallas_call(partial(mlp_kernel, count), grid=(per, tok // chunk), in_s...]
    reduce_scatter x2, waiting for transfers between devices: 0.02 us -> 50.6 us  [the longest x1 50.6 us: on_device(): sum_fc = lax.psum_scatter(grad_fc, 'dp', scatter_dimension=0)]
    ppermute x66 -> x53, waiting for transfers between devices: 179 us -> 136 us  [hop(): return lax.ppermute(value, axis, [(i, i ^ bits) for i in range(count)])]
    all_gather x3 -> x1, waiting for transfers between devices: 0.01 us -> 36.8 us  [on_device(): lax.all_gather(jnp.concatenate([fc1_here, fc2_here, proj_here]), 'dp', ax...]
    dot_general x9 -> x3, matrix products: 38.6 us -> 4.35 us  [matmul(): return jnp.dot(left, right, preferred_element_type=F32)]
    dot_general x9 -> x3, matrix products: 41.3 us -> 9.55 us  [matmul_nt(): lax.dot_general(left, right, (((1,), (1,)), ((), ())), preferred_element_...]
    ppermute x66 -> x53, starting transfers between devices: 50 us -> 37 us  [hop(): return lax.ppermute(value, axis, [(i, i ^ bits) for i in range(count)])]
    pallas_call x2, Pallas kernels: 25.5 us -> 13.9 us  [attention(): pl.pallas_call(partial(attend_kernel, heads, block), grid=(lat,), in_spec...]
  transfers between devices with their start and end apart: 80 -> 63, of which waited for: 29 -> 23; matrix products, arithmetic and copies ran while one was open for 36% -> 24% of each run, Pallas kernels for 8% -> 17%
where the time goes in v4:
time: 660 us; the launch traced here: 654 us
  waiting for transfers between devices  255 us (39%)
  Pallas kernels  114 us (17%)
  local copies, waits for them, and re-layouts  93.2 us (14%)
  other arithmetic  70.8 us (11%)
  starting transfers between devices  66.7 us (10%)
  matrix products  38.9 us (6%)
  between operations  15.5 us (2%)
    ppermute x53, waiting for transfers between devices, hop(): return lax.ppermute(value, axis, [(i, i ^ bits) for i in range(count)])  136 us
    reduce_scatter x1, waiting for transfers between devices, on_device(): sum_fc = lax.psum_scatter(grad_fc, 'dp', scatter_dimension=0)  50.6 us
    ppermute x53, starting transfers between devices, hop(): return lax.ppermute(value, axis, [(i, i ^ bits) for i in range(count)])  37 us
    all_gather x1, waiting for transfers between devices, on_device(): lax.all_gather(jnp.concatenate([fc1_here, fc2_here, proj_here]), 'dp', ax...  36.8 us
    pallas_call x2, Pallas kernels, mlp(): pl.pallas_call(partial(mlp_kernel, count), grid=(per, tok // chunk), in_s...  33.7 us
    unnamed x159, local copies, waits for them, and re-layouts  26.5 us
    dot_general x7, matrix products, matmul_tn(): lax.dot_general(left, right, (((0,), (0,)), ((), ())), preferred_element_...  25 us
    pallas_call x2, Pallas kernels, attention_grad(): pl.pallas_call(partial(attend_grad_kernel, heads, block), grid=(lat,), in...  23.7 us
  transfers between devices with their start and end apart: 63, of which 23 were waited for; matrix products, arithmetic and copies ran while one was open for 24% of the time, Pallas kernels for 17%

profile of v4, /device:TPU:0, one launch (start us, length us, event | category | flops | bytes accessed | tf_op | source)
XLA Modules:
  0.0 654.1 jit_solution(12753175608016345123)
XLA Ops:
  10.1 2.3 constant_dynamic-slice_fusion.8
  19.5 7.3 %all-to-all-start = ((bf16[8,2,1224]{2,1,0:T(2,128)(2,1)}), bf16[8,2,1224]{2,1,0:T(2,128)(2,1)S(1)}, u32[]{:S(2)}, u32[]{:S(2)}) async-start(bf16[8,2,1224]{2,1,0:T(2,128)(2,1)} %reshape.683), calls=%async_computation | async-start | bytes 81920 | tf_op jit(solution)/shard_map/all_to_all | solution.py:76
  32.5 2.9 collective-permute-start.6
  44.0 4.1 all-to-all-start.1
  48.7 13.1 %collective-permute-done.4 = bf16[144,864]{1,0:T(8,128)(2,1)} collective-permute-done((bf16[144,864]{1,0:T(8,128)(2,1)}, bf16[144,864]{1,0:T(8,128)(2,1)}, u32[]{:S(2)}, u32[]{:S(2)}) %collective-permute-start.4) | collective-permute-done | bytes 248864 | tf_op jit(solution)/shard_map/ppermute | solution.py:22
  67.5 15.5 %collective-permute-done.8 = bf16[144,864]{1,0:T(8,128)(2,1)S(1)} collective-permute-done((bf16[144,864]{1,0:T(8,128)(2,1)}, bf16[144,864]{1,0:T(8,128)(2,1)S(1)}, u32[]{:S(2)}, u32[]{:S(2)}) %collective-permute-start.8) | collective-permute-done | bytes 248864 | tf_op jit(solution)/shard_map/ppermute | solution.py:22
  88.0 4.8 collective-permute-done.7
  94.3 7.9 %collective-permute-done.9 = bf16[144,864]{1,0:T(8,128)(2,1)S(1)} collective-permute-done((bf16[144,864]{1,0:T(8,128)(2,1)S(1)}, bf16[144,864]{1,0:T(8,128)(2,1)S(1)}, u32[]{:S(2)}, u32[]{:S(2)}) %collective-permute-start.9) | collective-permute-done | bytes 248864 | tf_op jit(solution)/shard_map/ppermute | solution.py:22
  105.3 7.9 %qkv_forward.3 = (bf16[1,4,256,1152]{3,2,1,0:T(8,128)(2,1)}, bf16[1,4,256,864]{3,2,1,0:T(8,128)(2,1)}) custom-call(bf16[2,256,1152]{2,1,0:T(8,128)(2,1)S(1)} %copy-done.1, bf16[2,256,1152]{2,1,0:T(8,128)(2,1)} %collective-permute-done.refs_1_, bf16[2,256,1152]{2,1,0:T(8,128)(2,1)} %collective-permute-done.1.refs_2_, ...), custom_call_target="tpu_custom_call" | custom-call | tf_op jit(solution)/shard_map/qkv_forward/pallas_call | solution.py:219
  114.7 7.0 %attend.3 = (bf16[1,1024,288]{2,1,0:T(8,128)(2,1)S(1)}, f32[1,4,1024]{2,1,0:T(4,128)S(1)}) custom-call(bf16[1,1024,864]{2,1,0:T(8,128)(2,1)S(1)} %bitcast.299, bf16[2,256,1152]{2,1,0:T(8,128)(2,1)} %collective-permute-done.14.after.refs_7_), custom_call_target="tpu_custom_call" | custom-call | tf_op jit(solution)/shard_map/attend/pallas_call | solution.py:167
  122.6 36.8 %all-gather.3.cloned.1.call-done = bf16[2880,1152]{1,0:T(8,128)(2,1)} async-done(((bf16[360,1152]{1,0:T(8,128)(2,1)}), bf16[2880,1152]{1,0:T(8,128)(2,1)}) %all-gather.3.cloned.1.call-update) | async-done | bytes 6635536 | tf_op jit(solution)/shard_map/all_gather | solution.py:457
  160.5 2.9 copy-done.18
  163.4 3.0 unpack.1
  169.6 8.0 %qkv_forward.2 = (bf16[1,4,256,1152]{3,2,1,0:T(8,128)(2,1)}, bf16[1,4,256,864]{3,2,1,0:T(8,128)(2,1)}) custom-call(bf16[2,256,1152]{2,1,0:T(8,128)(2,1)S(1)} %copy-done.1, bf16[2,256,1152]{2,1,0:T(8,128)(2,1)} %collective-permute-done.refs_1_, bf16[2,256,1152]{2,1,0:T(8,128)(2,1)} %collective-permute-done.1.refs_2_, ...), custom_call_target="tpu_custom_call" | custom-call | tf_op jit(solution)/shard_map/qkv_forward/pallas_call | solution.py:219
  179.1 6.9 %attend.2 = (bf16[1,1024,288]{2,1,0:T(8,128)(2,1)S(1)}, f32[1,4,1024]{2,1,0:T(4,128)S(1)}) custom-call(bf16[1,1024,864]{2,1,0:T(8,128)(2,1)S(1)} %bitcast.301, bf16[2,256,1152]{2,1,0:T(8,128)(2,1)S(1)} %copy-done.1), custom_call_target="tpu_custom_call" | custom-call | tf_op jit(solution)/shard_map/attend/pallas_call | solution.py:167
  191.5 2.3 collective-permute-done.12
  195.1 3.9 collective-permute-done.11
  202.3 4.6 collective-permute-done.21
  209.0 3.1 maximum_select_fusion
  212.5 5.0 pad_maximum_fusion.2.refs_6_
  219.1 2.9 fusion.48
  227.0 13.4 %collective-permute-done.17.refs_2_ = bf16[1,256,1152]{2,1,0:T(8,128)(2,1)} collective-permute-done((bf16[1,256,1152]{2,1,0:T(8,128)(2,1)}, bf16[1,256,1152]{2,1,0:T(8,128)(2,1)}, u32[]{:S(2)}, u32[]{:S(2)}) %collective-permute-start.17) | collective-permute-done | bytes 589856 | tf_op jit(solution)/shard_map/ppermute | solution.py:22
  242.3 9.3 %collective-permute-done.24.refs_2_ = bf16[1,256,1152]{2,1,0:T(8,128)(2,1)} collective-permute-done((bf16[1,256,1152]{2,1,0:T(8,128)(2,1)}, bf16[1,256,1152]{2,1,0:T(8,128)(2,1)}, u32[]{:S(2)}, u32[]{:S(2)}) %collective-permute-start.24) | collective-permute-done | bytes 589856 | tf_op jit(solution)/shard_map/ppermute | solution.py:22
  252.2 16.6 %mlp.2 = (bf16[1,4,256,1152]{3,2,1,0:T(8,128)(2,1)}, bf16[1,4,256,1152]{3,2,1,0:T(8,128)(2,1)}, bf16[1,4,256,1152]{3,2,1,0:T(8,128)(2,1)}, bf16[1,4,256,1152]{3,...) custom-call(bf16[1,256,1152]{2,1,0:T(8,128)(2,1)} %add_convert_fusion.3.refs_0_, ...), custom_call_target="tpu_custom_call" | custom-call | tf_op jit(solution)/shard_map/mlp/pallas_call | solution.py:279
  273.2 17.0 %mlp.3 = (bf16[1,4,256,1152]{3,2,1,0:T(8,128)(2,1)}, bf16[1,4,256,1152]{3,2,1,0:T(8,128)(2,1)}, bf16[1,4,256,1152]{3,2,1,0:T(8,128)(2,1)}, bf16[1,4,256,1152]{3,...) custom-call(bf16[1,256,1152]{2,1,0:T(8,128)(2,1)} %add_convert_fusion.2.refs_0_, ...), custom_call_target="tpu_custom_call" | custom-call | tf_op jit(solution)/shard_map/mlp/pallas_call | solution.py:279
  290.2 2.3 slice_bitcast_fusion.19
  293.1 5.1 convolution_bitcast_fusion.2
  298.2 3.3 convolution_bitcast_fusion
  301.6 3.4 fusion.2
  305.0 3.6 fusion.3
  314.8 2.8 pad_maximum_fusion.refs_7_
  317.6 9.6 %collective-permute-done.37 = bf16[1,256,1152]{2,1,0:T(8,128)(2,1)} collective-permute-done((bf16[1,256,1152]{2,1,0:T(8,128)(2,1)}, bf16[1,256,1152]{2,1,0:T(8,128)(2,1)}, u32[]{:S(2)}, u32[]{:S(2)}) %collective-permute-start.37) | collective-permute-done | bytes 589856 | tf_op jit(solution)/shard_map/ppermute | solution.py:22
  328.8 5.6 resid_grad.3
  336.3 3.5 collective-permute-done.28
  341.5 5.6 resid_grad.2
  350.8 6.0 pad_maximum_fusion.3
  356.8 7.6 %reshape.642 = bf16[8,144,2,576]{3,2,1,0:T(2,128)(2,1)} reshape(bf16[1152,1152]{1,0:T(8,128)(2,1)} %pad_maximum_fusion.3) | data formatting | bytes 5308416 | tf_op jit(solution)/shard_map/reshape | solution.py:561
  364.7 9.7 %constant_dynamic-slice_fusion.4 = (bf16[8,144,1,576]{3,2,1,0:T(2,128)(2,1)S(1)}, f32[8,144,1,576]{3,2,1,0:T(1,128)}) fusion(bf16[8,144,2,576]{3,2,1,0:T(2,128)(2,1)} %reshape.642, s32[]{:T(128)S(6)} %select_n.213, s32[]{:T(128)S(6)} %select_n.212), kind=kLoop, calls=%fused_computation.187 | loop fusion | flops 663552 | bytes 6635528 | tf_op jit(solution)/shard_map/jit(dynamic_index_in_dim)/dynamic_slice | solution.py:563
  377.5 12.0 %attend_grad.2 = bf16[1,1024,864]{2,1,0:T(8,128)(2,1)S(1)} custom-call(bf16[1,1024,864]{2,1,0:T(8,128)(2,1)S(1)} %bitcast.302, bf16[1,1024,288]{2,1,0:T(8,128)(2,1)S(1)} %copy-done.23, f32[1,4,1024]{2,1,0:T(4,128)S(1)} %get-tuple-element.70.log_sum, bf16[1,1024,288]{2,1,0:T(8,128)(2,1)S(1)} %pad_maximum_fusion.8.d_mixed, ...), custom_call_target="tpu_custom_call" | custom-call | tf_op jit(solution)/shard_map/attend_grad/pallas_call | solution.py:185
  391.5 11.7 %attend_grad.3 = bf16[1,1024,864]{2,1,0:T(8,128)(2,1)S(1)} custom-call(bf16[1,1024,864]{2,1,0:T(8,128)(2,1)S(1)} %bitcast.300, bf16[1,1024,288]{2,1,0:T(8,128)(2,1)S(1)} %copy-done.17, f32[1,4,1024]{2,1,0:T(4,128)S(1)} %get-tuple-element.76.log_sum, bf16[1,1024,288]{2,1,0:T(8,128)(2,1)S(1)} %pad_maximum_fusion.9.d_mixed, ...), custom_call_target="tpu_custom_call" | custom-call | tf_op jit(solution)/shard_map/attend_grad/pallas_call | solution.py:185
  404.5 6.4 fusion.11
  410.9 4.1 copy.87
  414.9 2.7 fusion.16
  417.9 3.2 pad_maximum_fusion.1
  422.4 3.7 all-to-all-start.6
  426.9 5.9 all-to-all-done.6
  435.0 6.2 mlp_out_terms.3
  441.3 6.4 mlp_out_terms.2
  449.3 4.5 fusion.90
  455.3 4.5 fusion.89
  464.9 11.4 %collective-permute-done.31 = bf16[1,256,1152]{2,1,0:T(8,128)(2,1)S(1)} collective-permute-done((bf16[1,256,1152]{2,1,0:T(8,128)(2,1)S(1)}, bf16[1,256,1152]{2,1,0:T(8,128)(2,1)S(1)}, u32[]{:S(2)}, u32[]{:S(2)}) %collective-permute-start.31) | collective-permute-done | bytes 589856 | tf_op jit(solution)/shard_map/ppermute | solution.py:22
  477.8 11.1 %collective-permute-done.34 = bf16[1,256,1152]{2,1,0:T(8,128)(2,1)S(1)} collective-permute-done((bf16[1,256,1152]{2,1,0:T(8,128)(2,1)S(1)}, bf16[1,256,1152]{2,1,0:T(8,128)(2,1)S(1)}, u32[]{:S(2)}, u32[]{:S(2)}) %collective-permute-start.34) | collective-permute-done | bytes 589856 | tf_op jit(solution)/shard_map/ppermute | solution.py:22
  492.3 21.5 %collective-permute-done.43 = bf16[1,256,1152]{2,1,0:T(8,128)(2,1)S(1)} collective-permute-done((bf16[1,256,1152]{2,1,0:T(8,128)(2,1)S(1)}, bf16[1,256,1152]{2,1,0:T(8,128)(2,1)S(1)}, u32[]{:S(2)}, u32[]{:S(2)}) %collective-permute-start.43) | collective-permute-done | bytes 589856 | tf_op jit(solution)/shard_map/ppermute | solution.py:22
  515.1 2.3 fusion.41
  520.5 2.6 collective-permute-done.51
  524.0 3.4 all-to-all-start.2
  531.2 11.1 %all-to-all-done.2 = bf16[8,2,6912]{2,1,0:T(2,128)(2,1)S(1)} async-done(((bf16[8,2,6912]{2,1,0:T(2,128)(2,1)}), bf16[8,2,6912]{2,1,0:T(2,128)(2,1)S(1)}, u32[]{:S(2)}, u32[]{:S(2)}) %all-to-all-start.2) | async-done | bytes 221216 | tf_op jit(solution)/shard_map/all_to_all | solution.py:76
  543.6 3.6 all-to-all-start.3
  549.3 4.7 all-to-all-done.3
  559.0 3.5 all-to-all-start.4
  562.5 50.6 %reduce-scatter.5.cloned.1.call-done = bf16[1,288,1152]{2,1,0:T(8,128)(2,1)} async-done(((bf16[8,288,1152]{2,1,0:T(8,128)(2,1)}), bf16[1,288,1152]{2,1,0:T(8,128)(2,1)}) %reduce-scatter.5.cloned.1.call-update) | async-done | bytes 663568 | tf_op jit(solution)/shard_map/reduce_scatter | solution.py:527
  621.4 3.5 all-to-all-start.5
  628.7 9.0 %all-to-all-done.5 = bf16[4,288,288]{2,1,0:T(8,128)(2,1)S(1)} async-done(((bf16[4,288,288]{2,1,0:T(8,128)(2,1)}), bf16[4,288,288]{2,1,0:T(8,128)(2,1)S(1)}, u32[]{:S(2)}, u32[]{:S(2)}) %all-to-all-start.5) | async-done | bytes 663584 | tf_op jit(solution)/shard_map/all_to_all | solution.py:616
  639.0 2.4 copy.93
  (383 shorter events, 150.2 us)
Async XLA Ops:
  7.2 32.0 %copy-start = (bf16[144,6912]{1,0:T(8,128)(2,1)S(1)}, bf16[144,6912]{1,0:T(8,128)(2,1)}, u32[]{:S(2)}) copy-start(bf16[144,6912]{1,0:T(8,128)(2,1)} %param.12) | copy-start | bytes 5971972
  7.2 152.2 %all-gather.3.cloned.1.call-start = ((), (), s32[]{:S(2)}) async-start(), calls=%async_computation.11 | async-start | bytes 7464960 | tf_op jit(solution)/shard_map/all_gather | solution.py:457
  19.5 18.8 %all-to-all-start = ((bf16[8,2,1224]{2,1,0:T(2,128)(2,1)}), bf16[8,2,1224]{2,1,0:T(2,128)(2,1)S(1)}, u32[]{:S(2)}, u32[]{:S(2)}) async-start(bf16[8,2,1224]{2,1,0:T(2,128)(2,1)} %reshape.683), calls=%async_computation | async-start | bytes 81920 | tf_op jit(solution)/shard_map/all_to_all | solution.py:76
  26.8 58.3 %collective-permute-start.13 = (bf16[2,256,1152]{2,1,0:T(8,128)(2,1)}, bf16[2,256,1152]{2,1,0:T(8,128)(2,1)}, u32[]{:S(2)}, u32[]{:S(2)}) collective-permute-start(bf16[2,256,1152]{2,1,0:T(8,128)(2,1)} %refs_3_.3), channel_id=1, source_target_pairs={{0,2},{1,3},{2,0},{3,1},{4,6},{5,7},{6,4},{7,5},{8,10},{9,11},{10,... | collective-permute-start | bytes 3538952 | tf_op jit(solution)/shard_map/ppermute | solution.py:22
  28.3 56.8 %collective-permute-start.1 = (bf16[2,256,1152]{2,1,0:T(8,128)(2,1)S(1)}, bf16[2,256,1152]{2,1,0:T(8,128)(2,1)}, u32[]{:S(2)}, u32[]{:S(2)}) collective-permute-start(bf16[2,256,1152]{2,1,0:T(8,128)(2,1)S(1)} %copy-done.1), channel_id=1, source_target_pairs={{0,2},{1,3},{2,0},{3,1},{4,6},{5,7},{6,4},{7,5},{8,10},{9,11},{10,... | collective-permute-start | bytes 3538952 | tf_op jit(solution)/shard_map/ppermute | solution.py:22
  32.5 35.0 %collective-permute-start.6 = (bf16[144,864]{1,0:T(8,128)(2,1)}, bf16[144,864]{1,0:T(8,128)(2,1)}, u32[]{:S(2)}, u32[]{:S(2)}) collective-permute-start(bf16[144,864]{1,0:T(8,128)(2,1)} %get-tuple-element.162), channel_id=1, source_target_pairs={{0,16},{4,20},{8,24},{12,28},{16,0},{20,4},{24,8},{28,12},{1,17},{... | collective-permute-start | bytes 746504 | tf_op jit(solution)/shard_map/ppermute | solution.py:22
  35.4 26.4 %collective-permute-start.4 = (bf16[144,864]{1,0:T(8,128)(2,1)}, bf16[144,864]{1,0:T(8,128)(2,1)}, u32[]{:S(2)}, u32[]{:S(2)}) collective-permute-start(bf16[144,864]{1,0:T(8,128)(2,1)} %get-tuple-element.162), channel_id=1, source_target_pairs={{0,8},{4,12},{8,0},{12,4},{16,24},{20,28},{24,16},{28,20},{1,9},{5... | collective-permute-start | bytes 746504 | tf_op jit(solution)/shard_map/ppermute | solution.py:22
  36.9 26.3 %collective-permute-start.3 = (bf16[144,864]{1,0:T(8,128)(2,1)}, bf16[144,864]{1,0:T(8,128)(2,1)}, u32[]{:S(2)}, u32[]{:S(2)}) collective-permute-start(bf16[144,864]{1,0:T(8,128)(2,1)} %get-tuple-element.162), channel_id=1, source_target_pairs={{0,4},{4,0},{8,12},{12,8},{16,20},{20,16},{24,28},{28,24},{1,5},{5... | collective-permute-start | bytes 746504 | tf_op jit(solution)/shard_map/ppermute | solution.py:22
  44.0 58.8 %all-to-all-start.1 = ((f32[8,2,6912]{2,1,0:T(2,128)}), f32[8,2,6912]{2,1,0:T(2,128)}, u32[]{:S(2)}, u32[]{:S(2)}) async-start(f32[8,2,6912]{2,1,0:T(2,128)} %reshape.613), calls=%async_computation.1 | async-start | bytes 884736 | tf_op jit(solution)/shard_map/all_to_all | solution.py:76
  48.2 506.0 %reduce-scatter.3.cloned.1.call-start = ((), (), s32[]{:S(2)}) async-start(), calls=%async_computation.9 | async-start | bytes 3981312 | tf_op jit(solution)/shard_map/reduce_scatter | solution.py:580
  61.8 21.2 %collective-permute-start.8 = (bf16[144,864]{1,0:T(8,128)(2,1)}, bf16[144,864]{1,0:T(8,128)(2,1)S(1)}, u32[]{:S(2)}, u32[]{:S(2)}) collective-permute-start(bf16[144,864]{1,0:T(8,128)(2,1)} %get-tuple-element.162), channel_id=1, source_target_pairs={{0,24},{4,28},{8,16},{12,20},{16,8},{20,12},{24,0},{28,4},{1,25},{... | collective-permute-start | bytes 746504 | tf_op jit(solution)/shard_map/ppermute | solution.py:22
  63.2 21.3 %collective-permute-start.5 = (bf16[144,864]{1,0:T(8,128)(2,1)}, bf16[144,864]{1,0:T(8,128)(2,1)S(1)}, u32[]{:S(2)}, u32[]{:S(2)}) collective-permute-start(bf16[144,864]{1,0:T(8,128)(2,1)} %collective-permute-done.4), channel_id=1, source_target_pairs={{0,4},{4,0},{8,12},{12,8},{16,20},{20,16},{24,28},{28,24},{1,5},{5... | collective-permute-start | bytes 746504 | tf_op jit(solution)/shard_map/ppermute | solution.py:22
  67.5 37.8 %collective-permute-start = (bf16[2,256,1152]{2,1,0:T(8,128)(2,1)S(1)}, bf16[2,256,1152]{2,1,0:T(8,128)(2,1)}, u32[]{:S(2)}, u32[]{:S(2)}) collective-permute-start(bf16[2,256,1152]{2,1,0:T(8,128)(2,1)S(1)} %copy-done.1), channel_id=1, source_target_pairs={{0,1},{1,0},{2,3},{3,2},{4,5},{5,4},{6,7},{7,6},{8,9},{9,8},{10,11... | collective-permute-start | bytes 3538952 | tf_op jit(solution)/shard_map/ppermute | solution.py:22
  83.0 9.8 %collective-permute-start.7 = (bf16[144,864]{1,0:T(8,128)(2,1)}, bf16[144,864]{1,0:T(8,128)(2,1)S(1)}, u32[]{:S(2)}, u32[]{:S(2)}) collective-permute-start(bf16[144,864]{1,0:T(8,128)(2,1)} %collective-permute-done.6), channel_id=1, source_target_pairs={{0,4},{4,0},{8,12},{12,8},{16,20},{20,16},{24,28},{28,24},{1,5},{5... | collective-permute-start | bytes 746504 | tf_op jit(solution)/shard_map/ppermute | solution.py:22
  84.5 17.6 %collective-permute-start.9 = (bf16[144,864]{1,0:T(8,128)(2,1)S(1)}, bf16[144,864]{1,0:T(8,128)(2,1)S(1)}, u32[]{:S(2)}, u32[]{:S(2)}) collective-permute-start(bf16[144,864]{1,0:T(8,128)(2,1)S(1)} %collective-permute-done.8), channel_id=1, source_target_pairs={{0,4},{4,0},{8,12},{12,8},{16,20},{20,16},{24,28},{28,24},{1,5},{5... | collective-permute-start | bytes 746504 | tf_op jit(solution)/shard_map/ppermute | solution.py:22
  85.1 28.1 %collective-permute-start.14 = (bf16[2,256,1152]{2,1,0:T(8,128)(2,1)}, bf16[2,256,1152]{2,1,0:T(8,128)(2,1)}, u32[]{:S(2)}, u32[]{:S(2)}) collective-permute-start(bf16[2,256,1152]{2,1,0:T(8,128)(2,1)} %collective-permute-done.13.refs_6_), channel_id=1, source_target_pairs={{0,1},{1,0},{2,3},{3,2},{4,5},{5,4},{6,7},{7,6},{8,9},{9,8},{10,11... | collective-permute-start | bytes 3538952 | tf_op jit(solution)/shard_map/ppermute | solution.py:22
  85.1 20.2 %collective-permute-start.2 = (bf16[2,256,1152]{2,1,0:T(8,128)(2,1)}, bf16[2,256,1152]{2,1,0:T(8,128)(2,1)}, u32[]{:S(2)}, u32[]{:S(2)}) collective-permute-start(bf16[2,256,1152]{2,1,0:T(8,128)(2,1)} %collective-permute-done.1.refs_2_), channel_id=1, source_target_pairs={{0,1},{1,0},{2,3},{3,2},{4,5},{5,4},{6,7},{7,6},{8,9},{9,8},{10,11... | collective-permute-start | bytes 3538952 | tf_op jit(solution)/shard_map/ppermute | solution.py:22
  169.4 39.6 %collective-permute-start.15 = (bf16[8,72,1152]{2,1,0:T(8,128)(2,1)}, bf16[8,72,1152]{2,1,0:T(8,128)(2,1)}, u32[]{:S(2)}, u32[]{:S(2)}) collective-permute-start(bf16[8,72,1152]{2,1,0:T(8,128)(2,1)} %get-tuple-element.55), channel_id=1, source_target_pairs={{0,1},{1,0},{2,3},{3,2},{4,5},{5,4},{6,7},{7,6},{8,9},{9,8},{10,11... | collective-permute-start | bytes 3981320 | tf_op jit(solution)/shard_map/ppermute | solution.py:22
  186.9 6.8 %collective-permute-start.12 = (bf16[1,256,288]{2,1,0:T(8,128)(2,1)S(1)}, bf16[1,256,288]{2,1,0:T(8,128)(2,1)S(1)}, u32[]{:S(2)}, u32[]{:S(2)}) collective-permute-start(bf16[1,256,288]{2,1,0:T(8,128)(2,1)S(1)} %get-tuple-element.208), channel_id=1, source_target_pairs={{0,3},{1,2},{2,1},{3,0},{4,7},{5,6},{6,5},{7,4},{8,11},{9,10},{10,... | collective-permute-start | bytes 442376 | tf_op jit(solution)/shard_map/ppermute | solution.py:22
  188.5 10.4 %collective-permute-start.11 = (bf16[1,256,288]{2,1,0:T(8,128)(2,1)S(1)}, bf16[1,256,288]{2,1,0:T(8,128)(2,1)S(1)}, u32[]{:S(2)}, u32[]{:S(2)}) collective-permute-start(bf16[1,256,288]{2,1,0:T(8,128)(2,1)S(1)} %get-tuple-element.209), channel_id=1, source_target_pairs={{0,2},{1,3},{2,0},{3,1},{4,6},{5,7},{6,4},{7,5},{8,10},{9,11},{10,... | collective-permute-start | bytes 442376 | tf_op jit(solution)/shard_map/ppermute | solution.py:22
  189.0 9.9 %collective-permute-start.10 = (bf16[1,256,288]{2,1,0:T(8,128)(2,1)S(1)}, bf16[1,256,288]{2,1,0:T(8,128)(2,1)S(1)}, u32[]{:S(2)}, u32[]{:S(2)}) collective-permute-start(bf16[1,256,288]{2,1,0:T(8,128)(2,1)S(1)} %get-tuple-element.210), channel_id=1, source_target_pairs={{0,1},{1,0},{2,3},{3,2},{4,5},{5,4},{6,7},{7,6},{8,9},{9,8},{10,11... | collective-permute-start | bytes 442376 | tf_op jit(solution)/shard_map/ppermute | solution.py:22
  189.9 12.4 %collective-permute-start.22 = (bf16[1,256,288]{2,1,0:T(8,128)(2,1)}, bf16[1,256,288]{2,1,0:T(8,128)(2,1)}, u32[]{:S(2)}, u32[]{:S(2)}) collective-permute-start(bf16[1,256,288]{2,1,0:T(8,128)(2,1)} %get-tuple-element.212), channel_id=1, source_target_pairs={{0,3},{1,2},{2,1},{3,0},{4,7},{5,6},{6,5},{7,4},{8,11},{9,10},{10,... | collective-permute-start | bytes 442376 | tf_op jit(solution)/shard_map/ppermute | solution.py:22
  193.7 13.1 %collective-permute-start.21 = (bf16[1,256,288]{2,1,0:T(8,128)(2,1)}, bf16[1,256,288]{2,1,0:T(8,128)(2,1)}, u32[]{:S(2)}, u32[]{:S(2)}) collective-permute-start(bf16[1,256,288]{2,1,0:T(8,128)(2,1)} %get-tuple-element.213), channel_id=1, source_target_pairs={{0,2},{1,3},{2,0},{3,1},{4,6},{5,7},{6,4},{7,5},{8,10},{9,11},{10,... | collective-permute-start | bytes 442376 | tf_op jit(solution)/shard_map/ppermute | solution.py:22
  198.9 8.0 %collective-permute-start.20 = (bf16[1,256,288]{2,1,0:T(8,128)(2,1)}, bf16[1,256,288]{2,1,0:T(8,128)(2,1)}, u32[]{:S(2)}, u32[]{:S(2)}) collective-permute-start(bf16[1,256,288]{2,1,0:T(8,128)(2,1)} %get-tuple-element.214), channel_id=1, source_target_pairs={{0,1},{1,0},{2,3},{3,2},{4,5},{5,4},{6,7},{7,6},{8,9},{9,8},{10,11... | collective-permute-start | bytes 442376 | tf_op jit(solution)/shard_map/ppermute | solution.py:22
  199.0 53.2 %collective-permute-start.19 = (bf16[2,256,1152]{2,1,0:T(8,128)(2,1)}, bf16[2,256,1152]{2,1,0:T(8,128)(2,1)}, u32[]{:S(2)}, u32[]{:S(2)}) collective-permute-start(bf16[2,256,1152]{2,1,0:T(8,128)(2,1)} %refs_3_.3), channel_id=1, source_target_pairs={{0,1},{1,0},{2,3},{3,2},{4,5},{5,4},{6,7},{7,6},{8,9},{9,8},{10,11... | collective-permute-start | bytes 3538952 | tf_op jit(solution)/shard_map/ppermute | solution.py:22
  223.9 16.6 %collective-permute-start.17 = (bf16[1,256,1152]{2,1,0:T(8,128)(2,1)}, bf16[1,256,1152]{2,1,0:T(8,128)(2,1)}, u32[]{:S(2)}, u32[]{:S(2)}) collective-permute-start(bf16[1,256,1152]{2,1,0:T(8,128)(2,1)} %add_convert_fusion.3.refs_0_), channel_id=1, source_target_pairs={{0,2},{1,3},{2,0},{3,1},{4,6},{5,7},{6,4},{7,5},{8,10},{9,11},{10,... | collective-permute-start | bytes 1769480 | tf_op jit(solution)/shard_map/ppermute | solution.py:22
  226.5 25.1 %collective-permute-start.24 = (bf16[1,256,1152]{2,1,0:T(8,128)(2,1)}, bf16[1,256,1152]{2,1,0:T(8,128)(2,1)}, u32[]{:S(2)}, u32[]{:S(2)}) collective-permute-start(bf16[1,256,1152]{2,1,0:T(8,128)(2,1)} %add_convert_fusion.2.refs_0_), channel_id=1, source_target_pairs={{0,2},{1,3},{2,0},{3,1},{4,6},{5,7},{6,4},{7,5},{8,10},{9,11},{10,... | collective-permute-start | bytes 1769480 | tf_op jit(solution)/shard_map/ppermute | solution.py:22
  227.0 25.2 %collective-permute-start.16 = (bf16[1,256,1152]{2,1,0:T(8,128)(2,1)}, bf16[1,256,1152]{2,1,0:T(8,128)(2,1)}, u32[]{:S(2)}, u32[]{:S(2)}) collective-permute-start(bf16[1,256,1152]{2,1,0:T(8,128)(2,1)} %add_convert_fusion.3.refs_0_), channel_id=1, source_target_pairs={{0,1},{1,0},{2,3},{3,2},{4,5},{5,4},{6,7},{7,6},{8,9},{9,8},{10,11... | collective-permute-start | bytes 1769480 | tf_op jit(solution)/shard_map/ppermute | solution.py:22
  240.5 11.8 %collective-permute-start.18 = (bf16[1,256,1152]{2,1,0:T(8,128)(2,1)}, bf16[1,256,1152]{2,1,0:T(8,128)(2,1)}, u32[]{:S(2)}, u32[]{:S(2)}) collective-permute-start(bf16[1,256,1152]{2,1,0:T(8,128)(2,1)} %collective-permute-done.17.refs_2_), channel_id=1, source_target_pairs={{0,1},{1,0},{2,3},{3,2},{4,5},{5,4},{6,7},{7,6},{8,9},{9,8},{10,11... | collective-permute-start | bytes 1769480 | tf_op jit(solution)/shard_map/ppermute | solution.py:22
  241.8 29.7 %collective-permute-start.23 = (bf16[1,256,1152]{2,1,0:T(8,128)(2,1)}, bf16[1,256,1152]{2,1,0:T(8,128)(2,1)S(1)}, u32[]{:S(2)}, u32[]{:S(2)}) collective-permute-start(bf16[1,256,1152]{2,1,0:T(8,128)(2,1)} %add_convert_fusion.2.refs_0_), channel_id=1, source_target_pairs={{0,1},{1,0},{2,3},{3,2},{4,5},{5,4},{6,7},{7,6},{8,9},{9,8},{10,11... | collective-permute-start | bytes 1769480 | tf_op jit(solution)/shard_map/ppermute | solution.py:22
  251.6 19.9 %collective-permute-start.25 = (bf16[1,256,1152]{2,1,0:T(8,128)(2,1)}, bf16[1,256,1152]{2,1,0:T(8,128)(2,1)S(1)}, u32[]{:S(2)}, u32[]{:S(2)}) collective-permute-start(bf16[1,256,1152]{2,1,0:T(8,128)(2,1)} %collective-permute-done.24.refs_2_), channel_id=1, source_target_pairs={{0,1},{1,0},{2,3},{3,2},{4,5},{5,4},{6,7},{7,6},{8,9},{9,8},{10,11... | collective-permute-start | bytes 1769480 | tf_op jit(solution)/shard_map/ppermute | solution.py:22
  271.0 46.6 %collective-permute-start.35 = (bf16[1,256,1152]{2,1,0:T(8,128)(2,1)}, bf16[1,256,1152]{2,1,0:T(8,128)(2,1)}, u32[]{:S(2)}, u32[]{:S(2)}) collective-permute-start(bf16[1,256,1152]{2,1,0:T(8,128)(2,1)} %get-tuple-element.179), channel_id=1, source_target_pairs={{0,1},{1,0},{2,3},{3,2},{4,5},{5,4},{6,7},{7,6},{8,9},{9,8},{10,11... | collective-permute-start | bytes 1769480 | tf_op jit(solution)/shard_map/ppermute | solution.py:22
  271.5 37.2 %collective-permute-start.36 = (bf16[1,256,1152]{2,1,0:T(8,128)(2,1)S(1)}, bf16[1,256,1152]{2,1,0:T(8,128)(2,1)S(1)}, u32[]{:S(2)}, u32[]{:S(2)}) collective-permute-start(bf16[1,256,1152]{2,1,0:T(8,128)(2,1)S(1)} %get-tuple-element.180), channel_id=1, source_target_pairs={{0,1},{1,0},{2,3},{3,2},{4,5},{5,4},{6,7},{7,6},{8,9},{9,8},{10,11... | collective-permute-start | bytes 1769480 | tf_op jit(solution)/shard_map/ppermute | solution.py:22
  292.5 43.8 %collective-permute-start.26 = (bf16[1,256,1152]{2,1,0:T(8,128)(2,1)}, bf16[1,256,1152]{2,1,0:T(8,128)(2,1)}, u32[]{:S(2)}, u32[]{:S(2)}) collective-permute-start(bf16[1,256,1152]{2,1,0:T(8,128)(2,1)} %get-tuple-element.185), channel_id=1, source_target_pairs={{0,1},{1,0},{2,3},{3,2},{4,5},{5,4},{6,7},{7,6},{8,9},{9,8},{10,11... | collective-permute-start | bytes 1769480 | tf_op jit(solution)/shard_map/ppermute | solution.py:22
  293.1 19.2 %collective-permute-start.27 = (bf16[1,256,1152]{2,1,0:T(8,128)(2,1)S(1)}, bf16[1,256,1152]{2,1,0:T(8,128)(2,1)S(1)}, u32[]{:S(2)}, u32[]{:S(2)}) collective-permute-start(bf16[1,256,1152]{2,1,0:T(8,128)(2,1)S(1)} %get-tuple-element.186), channel_id=1, source_target_pairs={{0,1},{1,0},{2,3},{3,2},{4,5},{5,4},{6,7},{7,6},{8,9},{9,8},{10,11... | collective-permute-start | bytes 1769480 | tf_op jit(solution)/shard_map/ppermute | solution.py:22
  310.7 16.4 %collective-permute-start.37 = (bf16[1,256,1152]{2,1,0:T(8,128)(2,1)}, bf16[1,256,1152]{2,1,0:T(8,128)(2,1)}, u32[]{:S(2)}, u32[]{:S(2)}) collective-permute-start(bf16[1,256,1152]{2,1,0:T(8,128)(2,1)} %fusion.63), channel_id=1, source_target_pairs={{0,2},{1,3},{2,0},{3,1},{4,6},{5,7},{6,4},{7,5},{8,10},{9,11},{10,... | collective-permute-start | bytes 1769480 | tf_op jit(solution)/shard_map/ppermute | solution.py:22
  314.3 25.5 %collective-permute-start.28 = (bf16[1,256,1152]{2,1,0:T(8,128)(2,1)}, bf16[1,256,1152]{2,1,0:T(8,128)(2,1)}, u32[]{:S(2)}, u32[]{:S(2)}) collective-permute-start(bf16[1,256,1152]{2,1,0:T(8,128)(2,1)} %fusion.69), channel_id=1, source_target_pairs={{0,2},{1,3},{2,0},{3,1},{4,6},{5,7},{6,4},{7,5},{8,10},{9,11},{10,... | collective-permute-start | bytes 1769480 | tf_op jit(solution)/shard_map/ppermute | solution.py:22
  334.4 30.0 %collective-permute-start.38 = (bf16[1,256,288]{2,1,0:T(8,128)(2,1)}, bf16[1,256,288]{2,1,0:T(8,128)(2,1)}, u32[]{:S(2)}, u32[]{:S(2)}) collective-permute-start(bf16[1,256,288]{2,1,0:T(8,128)(2,1)} %get-tuple-element.72), channel_id=1, source_target_pairs={{0,1},{1,0},{2,3},{3,2},{4,5},{5,4},{6,7},{7,6},{8,9},{9,8},{10,11... | collective-permute-start | bytes 442376 | tf_op jit(solution)/shard_map/ppermute | solution.py:22
  334.5 41.4 %collective-permute-start.39 = (bf16[1,256,288]{2,1,0:T(8,128)(2,1)}, bf16[1,256,288]{2,1,0:T(8,128)(2,1)}, u32[]{:S(2)}, u32[]{:S(2)}) collective-permute-start(bf16[1,256,288]{2,1,0:T(8,128)(2,1)} %get-tuple-element.73), channel_id=1, source_target_pairs={{0,2},{1,3},{2,0},{3,1},{4,6},{5,7},{6,4},{7,5},{8,10},{9,11},{10,... | collective-permute-start | bytes 442376 | tf_op jit(solution)/shard_map/ppermute | solution.py:22
  336.0 40.2 %collective-permute-start.40 = (bf16[1,256,288]{2,1,0:T(8,128)(2,1)}, bf16[1,256,288]{2,1,0:T(8,128)(2,1)}, u32[]{:S(2)}, u32[]{:S(2)}) collective-permute-start(bf16[1,256,288]{2,1,0:T(8,128)(2,1)} %get-tuple-element.74), channel_id=1, source_target_pairs={{0,3},{1,2},{2,1},{3,0},{4,7},{5,6},{6,5},{7,4},{8,11},{9,10},{10,... | collective-permute-start | bytes 442376 | tf_op jit(solution)/shard_map/ppermute | solution.py:22
  347.1 42.3 %collective-permute-start.44 = (bf16[1,256,288]{2,1,0:T(8,128)(2,1)}, bf16[1,256,288]{2,1,0:T(8,128)(2,1)}, u32[]{:S(2)}, u32[]{:S(2)}) collective-permute-start(bf16[1,256,288]{2,1,0:T(8,128)(2,1)} %get-tuple-element.77), channel_id=1, source_target_pairs={{0,1},{1,0},{2,3},{3,2},{4,5},{5,4},{6,7},{7,6},{8,9},{9,8},{10,11... | collective-permute-start | bytes 442376 | tf_op jit(solution)/shard_map/ppermute | solution.py:22
  347.2 42.3 %collective-permute-start.45 = (bf16[1,256,288]{2,1,0:T(8,128)(2,1)}, bf16[1,256,288]{2,1,0:T(8,128)(2,1)}, u32[]{:S(2)}, u32[]{:S(2)}) collective-permute-start(bf16[1,256,288]{2,1,0:T(8,128)(2,1)} %get-tuple-element.78), channel_id=1, source_target_pairs={{0,2},{1,3},{2,0},{3,1},{4,6},{5,7},{6,4},{7,5},{8,10},{9,11},{10,... | collective-permute-start | bytes 442376 | tf_op jit(solution)/shard_map/ppermute | solution.py:22
  364.4 25.1 %collective-permute-start.46 = (bf16[1,256,288]{2,1,0:T(8,128)(2,1)}, bf16[1,256,288]{2,1,0:T(8,128)(2,1)S(1)}, u32[]{:S(2)}, u32[]{:S(2)}) collective-permute-start(bf16[1,256,288]{2,1,0:T(8,128)(2,1)} %copy-done.37), channel_id=1, source_target_pairs={{0,3},{1,2},{2,1},{3,0},{4,7},{5,6},{6,5},{7,4},{8,11},{9,10},{10,... | collective-permute-start | bytes 442376 | tf_op jit(solution)/shard_map/ppermute | solution.py:22
  375.9 39.1 %collective-permute-start.52 = (bf16[8,144,576]{2,1,0:T(8,128)(2,1)}, bf16[8,144,576]{2,1,0:T(8,128)(2,1)}, u32[]{:S(2)}, u32[]{:S(2)}) collective-permute-start(bf16[8,144,576]{2,1,0:T(8,128)(2,1)} %bitcast.290), channel_id=1, source_target_pairs={{0,1},{1,0},{2,3},{3,2},{4,5},{5,4},{6,7},{7,6},{8,9},{9,8},{10,11... | collective-permute-start | bytes 3981320 | tf_op jit(solution)/shard_map/ppermute | solution.py:22
  422.4 10.3 %all-to-all-start.6 = ((f32[8,1,144]{2,1,0:T(1,128)}), f32[8,1,144]{2,1,0:T(1,128)S(1)}, u32[]{:S(2)}, u32[]{:S(2)}) async-start(f32[8,1,144]{2,1,0:T(1,128)} %add.488), calls=%async_computation.8 | async-start | bytes 16384 | tf_op jit(solution)/shard_map/all_to_all | solution.py:76
  426.2 186.9 %reduce-scatter.5.cloned.1.call-start = ((), (), s32[]{:S(2)}) async-start(), calls=%async_computation.10 | async-start | bytes 5971968 | tf_op jit(solution)/shard_map/reduce_scatter | solution.py:527
  447.8 15.0 %collective-permute-start.29 = (bf16[1,256,1152]{2,1,0:T(8,128)(2,1)S(1)}, bf16[1,256,1152]{2,1,0:T(8,128)(2,1)S(1)}, u32[]{:S(2)}, u32[]{:S(2)}) collective-permute-start(bf16[1,256,1152]{2,1,0:T(8,128)(2,1)S(1)} %get-tuple-element.181), channel_id=1, source_target_pairs={{0,1},{1,0},{2,3},{3,2},{4,5},{5,4},{6,7},{7,6},{8,9},{9,8},{10,11... | collective-permute-start | bytes 1769480 | tf_op jit(solution)/shard_map/ppermute | solution.py:22
  447.8 12.0 %collective-permute-start.30 = (bf16[1,256,1152]{2,1,0:T(8,128)(2,1)S(1)}, bf16[1,256,1152]{2,1,0:T(8,128)(2,1)S(1)}, u32[]{:S(2)}, u32[]{:S(2)}) collective-permute-start(bf16[1,256,1152]{2,1,0:T(8,128)(2,1)S(1)} %get-tuple-element.182), channel_id=1, source_target_pairs={{0,1},{1,0},{2,3},{3,2},{4,5},{5,4},{6,7},{7,6},{8,9},{9,8},{10,11... | collective-permute-start | bytes 1769480 | tf_op jit(solution)/shard_map/ppermute | solution.py:22
  448.4 14.9 %collective-permute-start.32 = (bf16[1,256,1152]{2,1,0:T(8,128)(2,1)S(1)}, bf16[1,256,1152]{2,1,0:T(8,128)(2,1)S(1)}, u32[]{:S(2)}, u32[]{:S(2)}) collective-permute-start(bf16[1,256,1152]{2,1,0:T(8,128)(2,1)S(1)} %get-tuple-element.183), channel_id=1, source_target_pairs={{0,1},{1,0},{2,3},{3,2},{4,5},{5,4},{6,7},{7,6},{8,9},{9,8},{10,11... | collective-permute-start | bytes 1769480 | tf_op jit(solution)/shard_map/ppermute | solution.py:22
  448.6 11.5 %collective-permute-start.33 = (bf16[1,256,1152]{2,1,0:T(8,128)(2,1)S(1)}, bf16[1,256,1152]{2,1,0:T(8,128)(2,1)S(1)}, u32[]{:S(2)}, u32[]{:S(2)}) collective-permute-start(bf16[1,256,1152]{2,1,0:T(8,128)(2,1)S(1)} %get-tuple-element.184), channel_id=1, source_target_pairs={{0,1},{1,0},{2,3},{3,2},{4,5},{5,4},{6,7},{7,6},{8,9},{9,8},{10,11... | collective-permute-start | bytes 1769480 | tf_op jit(solution)/shard_map/ppermute | solution.py:22
  453.9 8.0 %collective-permute-start.48 = (bf16[1,256,1152]{2,1,0:T(8,128)(2,1)S(1)}, bf16[1,256,1152]{2,1,0:T(8,128)(2,1)S(1)}, u32[]{:S(2)}, u32[]{:S(2)}) collective-permute-start(bf16[1,256,1152]{2,1,0:T(8,128)(2,1)S(1)} %get-tuple-element.176), channel_id=1, source_target_pairs={{0,1},{1,0},{2,3},{3,2},{4,5},{5,4},{6,7},{7,6},{8,9},{9,8},{10,11... | collective-permute-start | bytes 1769480 | tf_op jit(solution)/shard_map/ppermute | solution.py:22
  459.9 2.7 collective-permute-start.42
  460.1 16.2 %collective-permute-start.31 = (bf16[1,256,1152]{2,1,0:T(8,128)(2,1)S(1)}, bf16[1,256,1152]{2,1,0:T(8,128)(2,1)S(1)}, u32[]{:S(2)}, u32[]{:S(2)}) collective-permute-start(bf16[1,256,1152]{2,1,0:T(8,128)(2,1)S(1)} %fusion.67), channel_id=1, source_target_pairs={{0,2},{1,3},{2,0},{3,1},{4,6},{5,7},{6,4},{7,5},{8,10},{9,11},{10,... | collective-permute-start | bytes 1769480 | tf_op jit(solution)/shard_map/ppermute | solution.py:22
  461.8 27.1 %collective-permute-start.34 = (bf16[1,256,1152]{2,1,0:T(8,128)(2,1)S(1)}, bf16[1,256,1152]{2,1,0:T(8,128)(2,1)S(1)}, u32[]{:S(2)}, u32[]{:S(2)}) collective-permute-start(bf16[1,256,1152]{2,1,0:T(8,128)(2,1)S(1)} %fusion.65), channel_id=1, source_target_pairs={{0,2},{1,3},{2,0},{3,1},{4,6},{5,7},{6,4},{7,5},{8,10},{9,11},{10,... | collective-permute-start | bytes 1769480 | tf_op jit(solution)/shard_map/ppermute | solution.py:22
  462.6 52.2 %collective-permute-start.47 = (bf16[1,256,1152]{2,1,0:T(8,128)(2,1)S(1)}, bf16[1,256,1152]{2,1,0:T(8,128)(2,1)S(1)}, u32[]{:S(2)}, u32[]{:S(2)}) collective-permute-start(bf16[1,256,1152]{2,1,0:T(8,128)(2,1)S(1)} %get-tuple-element.175), channel_id=1, source_target_pairs={{0,1},{1,0},{2,3},{3,2},{4,5},{5,4},{6,7},{7,6},{8,9},{9,8},{10,11... | collective-permute-start | bytes 1769480 | tf_op jit(solution)/shard_map/ppermute | solution.py:22
  462.8 29.6 %collective-permute-start.41 = (bf16[1,256,1152]{2,1,0:T(8,128)(2,1)S(1)}, bf16[1,256,1152]{2,1,0:T(8,128)(2,1)S(1)}, u32[]{:S(2)}, u32[]{:S(2)}) collective-permute-start(bf16[1,256,1152]{2,1,0:T(8,128)(2,1)S(1)} %get-tuple-element.177), channel_id=1, source_target_pairs={{0,1},{1,0},{2,3},{3,2},{4,5},{5,4},{6,7},{7,6},{8,9},{9,8},{10,11... | collective-permute-start | bytes 1769480 | tf_op jit(solution)/shard_map/ppermute | solution.py:22
  463.3 51.4 %collective-permute-start.49 = (bf16[1,256,1152]{2,1,0:T(8,128)(2,1)S(1)}, bf16[1,256,1152]{2,1,0:T(8,128)(2,1)S(1)}, u32[]{:S(2)}, u32[]{:S(2)}) collective-permute-start(bf16[1,256,1152]{2,1,0:T(8,128)(2,1)S(1)} %fusion.50), channel_id=1, source_target_pairs={{0,2},{1,3},{2,0},{3,1},{4,6},{5,7},{6,4},{7,5},{8,10},{9,11},{10,... | collective-permute-start | bytes 1769480 | tf_op jit(solution)/shard_map/ppermute | solution.py:22
  476.3 37.5 %collective-permute-start.43 = (bf16[1,256,1152]{2,1,0:T(8,128)(2,1)S(1)}, bf16[1,256,1152]{2,1,0:T(8,128)(2,1)S(1)}, u32[]{:S(2)}, u32[]{:S(2)}) collective-permute-start(bf16[1,256,1152]{2,1,0:T(8,128)(2,1)S(1)} %fusion.54), channel_id=1, source_target_pairs={{0,2},{1,3},{2,0},{3,1},{4,6},{5,7},{6,4},{7,5},{8,10},{9,11},{10,... | collective-permute-start | bytes 1769480 | tf_op jit(solution)/shard_map/ppermute | solution.py:22
  517.6 1.3 collective-permute-start.50
  518.9 4.2 collective-permute-start.51
  524.0 18.3 %all-to-all-start.2 = ((bf16[8,2,6912]{2,1,0:T(2,128)(2,1)}), bf16[8,2,6912]{2,1,0:T(2,128)(2,1)S(1)}, u32[]{:S(2)}, u32[]{:S(2)}) async-start(bf16[8,2,6912]{2,1,0:T(2,128)(2,1)} %broadcast_in_dim.120), calls=%async_computation.2 | async-start | bytes 442368 | tf_op jit(solution)/shard_map/all_to_all | solution.py:76
  543.6 10.5 %all-to-all-start.3 = ((f32[8,2,144]{2,1,0:T(2,128)}), f32[8,2,144]{2,1,0:T(2,128)S(1)}, u32[]{:S(2)}, u32[]{:S(2)}) async-start(f32[8,2,144]{2,1,0:T(2,128)} %copy.85), calls=%async_computation.3 | async-start | bytes 32768 | tf_op jit(solution)/shard_map/all_to_all | solution.py:76
  559.0 61.6 %all-to-all-start.4 = ((bf16[4,288,288]{2,1,0:T(8,128)(2,1)}), bf16[4,288,288]{2,1,0:T(8,128)(2,1)S(1)}, u32[]{:S(2)}, u32[]{:S(2)}) async-start(bf16[4,288,288]{2,1,0:T(8,128)(2,1)} %maximum_maximum_fusion), calls=%async_computation.5 | async-start | bytes 1769472 | tf_op jit(solution)/shard_map/all_to_all | solution.py:616
  621.4 16.2 %all-to-all-start.5 = ((bf16[4,288,288]{2,1,0:T(8,128)(2,1)}), bf16[4,288,288]{2,1,0:T(8,128)(2,1)S(1)}, u32[]{:S(2)}, u32[]{:S(2)}) async-start(bf16[4,288,288]{2,1,0:T(8,128)(2,1)} %pad_maximum_fusion.6), calls=%async_computation.7 | async-start | bytes 1769472 | tf_op jit(solution)/shard_map/all_to_all | solution.py:616
  (75 other events, 406.6 us)
Sparse Core Ops, SparseCore 0:
  16.7 142.6 all-gather.2
  421.2 78.3 reduce-scatter.2
  503.1 109.8 reduce-scatter.4

commit v5 on v4

--- a/solution.py
+++ b/solution.py
@@ -14,6 +14,7 @@
 F32 = jnp.float32
 GELU_C = 0.7978845608028654
 GELU_A = 0.044715
+VMEM_LIMIT = 60 * 2**20
 EXP2_SCALE = HEAD_DIM ** (-0.5) * math.log2(math.e)
 
 
@@ -106,7 +107,8 @@
     return total
 
 
-def attend_kernel(heads, block, packed, after, mixed, log_sum, mixed_t):
+def attend_kernel(heads, block, packed, *refs):
+    mixed, log_sum, mixed_t = refs[-3:]
     seq_len = packed.shape[1]
     cols = heads * HEAD_DIM
     for h in range(heads):
@@ -125,9 +127,8 @@
     mixed[0] = mixed_t[...].T.astype(BF)
 
 
-def attend_grad_kernel(
-    heads, block, packed, mixed, log_sum, d_mixed, after, d_packed, d_queries_t
-):
+def attend_grad_kernel(heads, block, packed, mixed, log_sum, d_mixed, qkv, *refs):
+    d_packed, terms, d_queries_t = refs[-3:]
     seq_len = packed.shape[1]
     cols = heads * HEAD_DIM
     inv_root = HEAD_DIM ** (-0.5)
@@ -155,6 +156,9 @@
         d_packed[0, :, cols + at : cols + at + HEAD_DIM] = (d_keys * inv_root).astype(BF)
         d_packed[0, :, 2 * cols + at : 2 * cols + at + HEAD_DIM] = d_values.astype(BF)
     d_packed[0, :, 0:cols] = d_queries_t[...].T.astype(BF)
+    for start in range(0, seq_len, block):
+        rows = d_packed[0, start : start + block]
+        terms[0, start : start + block] = matmul_nt(rows, qkv[...]).astype(BF)
 
 
 def row_spec(*shape):
@@ -167,19 +171,19 @@
     return pl.pallas_call(
         partial(attend_kernel, heads, block),
         grid=(lat,),
-        in_specs=[row_spec(seq_len, 3 * cols), pl.BlockSpec(memory_space=pl.ANY)],
+        in_specs=[row_spec(seq_len, 3 * cols)] + [pl.BlockSpec(memory_space=pl.ANY)] * len(after),
         out_specs=[row_spec(seq_len, cols), row_spec(heads, seq_len)],
         out_shape=[
             jax.ShapeDtypeStruct((lat, seq_len, cols), BF),
             jax.ShapeDtypeStruct((lat, heads, seq_len), F32),
         ],
         scratch_shapes=[pltpu.VMEM((cols, seq_len), F32)],
-        compiler_params=pltpu.CompilerParams(vmem_limit_bytes=48 * 2**20),
+        compiler_params=pltpu.CompilerParams(vmem_limit_bytes=VMEM_LIMIT),
         name="attend",
-    )(packed, after)
-
-
-def attention_grad(packed, mixed, log_sum, d_mixed, after, heads, block=512):
+    )(packed, *after)
+
+
+def attention_grad(packed, mixed, log_sum, d_mixed, qkv, after, heads, block=512):
     lat, seq_len, _ = packed.shape
     cols = heads * HEAD_DIM
     return pl.pallas_call(
@@ -190,14 +194,18 @@
             row_spec(seq_len, cols),
             row_spec(heads, seq_len),
             row_spec(seq_len, cols),
-            pl.BlockSpec(memory_space=pl.ANY),
-        ],
-        out_specs=row_spec(seq_len, 3 * cols),
-        out_shape=jax.ShapeDtypeStruct((lat, seq_len, 3 * cols), BF),
+            pl.BlockSpec(qkv.shape, lambda i: (0, 0)),
+        ]
+        + [pl.BlockSpec(memory_space=pl.ANY)] * len(after),
+        out_specs=[row_spec(seq_len, 3 * cols), row_spec(seq_len, qkv.shape[0])],
+        out_shape=[
+            jax.ShapeDtypeStruct((lat, seq_len, 3 * cols), BF),
+            jax.ShapeDtypeStruct((lat, seq_len, qkv.shape[0]), BF),
+        ],
         scratch_shapes=[pltpu.VMEM((cols, seq_len), F32)],
-        compiler_params=pltpu.CompilerParams(vmem_limit_bytes=48 * 2**20),
+        compiler_params=pltpu.CompilerParams(vmem_limit_bytes=VMEM_LIMIT),
         name="attend_grad",
-    )(packed, mixed, log_sum, d_mixed, after)
+    )(packed, mixed, log_sum, d_mixed, qkv, *after)
 
 
 def qkv_kernel(count, *refs):
@@ -229,7 +237,7 @@
             jax.ShapeDtypeStruct((per, count, tok, width), BF),
             jax.ShapeDtypeStruct((per, count, tok, cols), BF),
         ],
-        compiler_params=pltpu.CompilerParams(vmem_limit_bytes=48 * 2**20),
+        compiler_params=pltpu.CompilerParams(vmem_limit_bytes=VMEM_LIMIT),
         name="qkv_forward",
     )(*slots, shift, scale, qkv)
 
@@ -286,7 +294,7 @@
         out_specs=[wide, wide, inner, inner, wide, whole(1, hid)],
         out_shape=[shape_wide, shape_wide, shape_inner, shape_inner, shape_wide]
         + [jax.ShapeDtypeStruct((1, hid), F32)],
-        compiler_params=pltpu.CompilerParams(vmem_limit_bytes=56 * 2**20),
+        compiler_params=pltpu.CompilerParams(vmem_limit_bytes=VMEM_LIMIT),
         name="mlp",
     )(*inputs, *grads, gate, fc1, bias, fc2)
 
@@ -311,7 +319,7 @@
         ],
         out_specs=pl.BlockSpec((1, count, chunk, width), lambda i, c: (i, 0, c, 0)),
         out_shape=jax.ShapeDtypeStruct((per, count, tok, width), BF),
-        compiler_params=pltpu.CompilerParams(vmem_limit_bytes=48 * 2**20),
+        compiler_params=pltpu.CompilerParams(vmem_limit_bytes=VMEM_LIMIT),
         name="mlp_out_terms",
     )(activated, fc2, after)
 
@@ -371,9 +379,57 @@
             row_shape,
         ]
         + [jax.ShapeDtypeStruct((per, tok, width // count), BF)] * count,
-        compiler_params=pltpu.CompilerParams(vmem_limit_bytes=48 * 2**20),
+        compiler_params=pltpu.CompilerParams(vmem_limit_bytes=VMEM_LIMIT),
         name="resid_grad",
     )(d_norm, resid_mid, attn_out, cotangent, scale, gate, proj, after)
+
+
+def pack_kernel(first, second, after, out):
+    rows = first.shape[1]
+    out[0, :rows] = first[0]
+    out[0, rows:] = second[0]
+
+
+def pack(first, second, after):
+    count, rows, width = first.shape
+    more = second.shape[1]
+    return pl.pallas_call(
+        pack_kernel,
+        grid=(count,),
+        in_specs=[
+            pl.BlockSpec((1, rows, width), lambda i: (i, 0, 0)),
+            pl.BlockSpec((1, more, width), lambda i: (i, 0, 0)),
+            pl.BlockSpec(memory_space=pl.ANY),
+        ],
+        out_specs=pl.BlockSpec((1, rows + more, width), lambda i: (i, 0, 0)),
+        out_shape=jax.ShapeDtypeStruct((count, rows + more, width), first.dtype),
+        compiler_params=pltpu.CompilerParams(vmem_limit_bytes=VMEM_LIMIT),
+        name="pack",
+    )(first, second, after)
+
+
+def pack_last_kernel(proj_terms, qkv_terms, after, out):
+    half = proj_terms.shape[2] // 2
+    folded = jnp.concatenate([proj_terms[0, :, :half], proj_terms[0, :, half:]], axis=0)
+    out[0] = jnp.concatenate([folded, qkv_terms[0].astype(F32)], axis=1).astype(BF)
+
+
+def pack_last(proj_terms, qkv_terms, after):
+    count, half, width = proj_terms.shape
+    _, rows, cols = qkv_terms.shape
+    return pl.pallas_call(
+        pack_last_kernel,
+        grid=(count,),
+        in_specs=[
+            pl.BlockSpec((1, half, width), lambda i: (i, 0, 0)),
+            pl.BlockSpec((1, rows, cols), lambda i: (i, 0, 0)),
+            pl.BlockSpec(memory_space=pl.ANY),
+        ],
+        out_specs=pl.BlockSpec((1, rows, width // 2 + cols), lambda i: (i, 0, 0)),
+        out_shape=jax.ShapeDtypeStruct((count, rows, width // 2 + cols), BF),
+        compiler_params=pltpu.CompilerParams(vmem_limit_bytes=VMEM_LIMIT),
+        name="pack_last",
+    )(proj_terms, qkv_terms, after)
 
 
 def unpack_kernel(joined, after, *parts):
@@ -394,7 +450,7 @@
         ],
         out_specs=[pl.BlockSpec((1, n, width), lambda i: (i, 0, 0)) for n in row_counts],
         out_shape=[jax.ShapeDtypeStruct((count, n, width), joined.dtype) for n in row_counts],
-        compiler_params=pltpu.CompilerParams(vmem_limit_bytes=32 * 2**20),
+        compiler_params=pltpu.CompilerParams(vmem_limit_bytes=VMEM_LIMIT),
         name="unpack",
     )(joined, after)
 
@@ -453,12 +509,13 @@
     fc2_here = lax.dynamic_slice(w_fc2, (seq * hid_here, 0), (hid_here, width))
     proj_here = lax.dynamic_slice(w_proj, (core * half, 0), (half, width))
     together = hid == width
+    proj_mine = lax.all_gather(proj_here, "dp", axis=0)
     if together:
-        joined = lax.all_gather(jnp.concatenate([fc1_here, fc2_here, proj_here]), "dp", axis=0)
+        joined = lax.all_gather(pack(fc1_here[None], fc2_here[None], proj_mine)[0], "dp", axis=0)
     else:
-        proj_mine = lax.all_gather(proj_here, "dp", axis=0)
         fc1 = lax.all_gather(fc1_here, "dp", axis=0, tiled=True)
         fc2 = lax.all_gather(fc2_here, "dp", axis=0, tiled=True)
+
     def part(g):
         return slice(g * per, (g + 1) * per)
 
@@ -472,7 +529,9 @@
         normed, rows_packed = qkv_forward(tok_slots, g, per, shift_attn[g], scale_attn[g], qkv)
         normed_all.append(normed.reshape(per * seq_len, width))
         packed.append(rows_packed.reshape(per, seq_len, 3 * cols))
-        out, log_sum = attention(packed[g], tokens if g == 0 else cot_slots[-1], heads_here)
+        out, log_sum = attention(
+            packed[g], mixed + cot_slots[-1:] if g else [], heads_here
+        )
         mixed.append(out)
         log_sums.append(log_sum)
         out = out.reshape(per, seq_n, tok, cols)
@@ -482,9 +541,6 @@
             )
         )
 
-    if together:
-        fc1, fc2, proj_mine = unpack(joined, mixed[-1], [rows, hid_here, half])
-        fc1, fc2 = fc1.reshape(width, hid), fc2.reshape(hid, width)
     proj_other = hop(proj_mine, "seq", 1)
     proj = jnp.where(
         core == 0,
@@ -507,6 +563,9 @@
             (ln_parts(resid_mid[g])[0] * (1.0 + scale_mlp[g]) + shift_mlp[g]).astype(BF)
         )
         upstream.append(cotangent[part(g)].astype(F32))
+    if together:
+        fc1, fc2 = unpack(joined, normed_mlp[0], [rows, hid_here])
+        fc1, fc2 = fc1.reshape(width, hid), fc2.reshape(hid, width)
 
     grad_fc1 = grad_fc2 = grad_bias1 = 0.0
     d_norm, activated = [], []
@@ -523,13 +582,13 @@
     grad_fc1 = grad_fc1.astype(BF).reshape(dp_n, rows, hid)
     grad_fc2 = grad_fc2.astype(BF).reshape(dp_n, hid_here, width)
     if together:
-        grad_fc = jnp.concatenate([grad_fc1, grad_fc2], axis=1)
+        grad_fc = pack(grad_fc1, grad_fc2, grad_bias1)
         sum_fc = lax.psum_scatter(grad_fc, "dp", scatter_dimension=0)
         sum_fc1, sum_fc2 = sum_fc[:rows], sum_fc[rows:]
     else:
         grad_fc = grad_fc1
         sum_fc1 = lax.psum_scatter(grad_fc1, "dp", scatter_dimension=0)
-        sum_fc2 = lax.psum_scatter(grad_fc2, "dp", scatter_dimension=0)
+        sum_fc = sum_fc2 = lax.psum_scatter(grad_fc2, "dp", scatter_dimension=0)
 
     def stacked(terms):
         return jnp.concatenate(terms)
@@ -548,9 +607,10 @@
         d_gate_attn.append(outs[4][:, 0])
         d_attended.append(outs[5])
         d_mixed.append(jnp.concatenate(seq_exchange(outs[5:]), axis=1))
-    mlp_out = []
+    mlp_out, mlp_terms = [], []
     for g in range(groups):
         terms = mlp_out_terms(activated[g], fc2, d_attended[-1])
+        mlp_terms.append(terms)
         mlp_out.append(seq_reduce([terms[:, j].astype(F32) for j in range(seq_n)]))
     output = jnp.concatenate(
         [(resid_mid[g] + gate_mlp[g] * mlp_out[g]).astype(BF) for g in range(groups)]
@@ -558,27 +618,26 @@
     d_gate_mlp = stacked([jnp.sum(upstream[g] * mlp_out[g], axis=1) for g in range(groups)])
     grad_proj = by_place(
         matmul_tn(stacked(attended), stacked(d_attn)).astype(BF).reshape(seq_n, cols, width)
-    ).reshape(dp_n, rows, 2, width // 2)
+    ).reshape(dp_n, 2, half, width)
     proj_sent = hop(
-        lax.dynamic_index_in_dim(grad_proj, 1 - core, axis=2, keepdims=False), "seq", 1
-    )
-    proj_terms = lax.dynamic_index_in_dim(grad_proj, core, axis=2, keepdims=False).astype(F32)
-    proj_terms = (proj_terms + proj_sent.astype(F32)).astype(BF)
-
-    d_packed, d_first = [], []
+        lax.dynamic_index_in_dim(grad_proj, 1 - core, axis=1, keepdims=False), "seq", 1
+    )
+    proj_terms = lax.dynamic_index_in_dim(grad_proj, core, axis=1, keepdims=False).astype(F32)
+    proj_terms = proj_terms + proj_sent.astype(F32)
+
+    d_packed, d_first, first_terms = [], [], []
     for g in range(groups):
-        d_packed.append(
-            attention_grad(
-                packed[g], mixed[g], log_sums[g], d_mixed[g], d_attended[-1], heads_here
-            ).reshape(
-                per * seq_len, 3 * cols
-            )
+        grads, terms = attention_grad(
+            packed[g], mixed[g], log_sums[g], d_mixed[g], qkv,
+            first_terms if g else [d_attended[-1]] + mlp_terms, heads_here,
         )
-        parts = matmul_nt(d_packed[g], qkv).reshape(per, seq_n, tok, width)
-        d_first.append(seq_reduce([parts[:, j] for j in range(seq_n)]))
+        d_packed.append(grads.reshape(per * seq_len, 3 * cols))
+        first_terms.append(terms)
+        terms = terms.reshape(per, seq_n, tok, width)
+        d_first.append(seq_reduce([terms[:, j].astype(F32) for j in range(seq_n)]))
     grad_qkv = matmul_tn(stacked(normed_all), stacked(d_packed)).astype(BF)
     sum_last = lax.psum_scatter(
-        jnp.concatenate([proj_terms, grad_qkv.reshape(dp_n, rows, 3 * cols)], axis=2),
+        pack_last(proj_terms, grad_qkv.reshape(dp_n, rows, 3 * cols), sum_fc),
         "dp",
         scatter_dimension=0,
     )
@@ -607,10 +666,17 @@
     mod_cols = lax.dynamic_slice(d_mod, (0, (dp * seq_n + seq) * share), (dp_n * lat, share))
     grad_wmod = matmul_tn(cond_all, mod_cols)
     grad_bmod = jnp.sum(mod_cols.astype(F32), axis=0)
-    d_cond = dp_exchange(matmul_nt(d_mod, w_mod).reshape(dp_n, lat, rows))
+    back = jnp.concatenate(
+        [
+            matmul_nt(d_mod, w_mod).reshape(dp_n, lat * rows),
+            grad_bias1.reshape(dp_n, hid_here),
+        ],
+        axis=1,
+    )
+    back = dp_exchange(back)
+    d_cond = back[:, : lat * rows].reshape(dp_n, lat, rows)
     (grad_cond,) = silu_back(d_cond.transpose(1, 0, 2).reshape(lat, width))
-
-    bias_out = jnp.sum(dp_exchange(grad_bias1.reshape(dp_n, hid_here)), axis=0)
+    bias_out = jnp.sum(back[:, lat * rows :], axis=0)
 
     def to_owner(blocks):
         return lax.all_to_all(blocks, "seq", 0, 0, tiled=True).astype(F32)
@@ -626,12 +692,8 @@
     out_fc2 = out_fc2.reshape(seq_n * hid_here, share)
     out_fc1 = out_fc1.reshape(seq_n, rows, dp_n // seq_n, hid_here).transpose(1, 2, 0, 3)
     out_fc1 = out_fc1.reshape(rows, hid)
-    owners = jnp.arange(seq_n)
-    proj_blocks = jnp.where(
-        (owners // (seq_n // 2) == core)[:, None, None],
-        jnp.tile(sum_proj.reshape(rows, seq_n // 2, share).transpose(1, 0, 2), (2, 1, 1)),
-        0,
-    )
+    proj_blocks = sum_proj.reshape(2, half, seq_n // 2, share).transpose(0, 2, 1, 3)
+    proj_blocks = proj_blocks.reshape(seq_n, half, share)
     qkv_thirds = sum_qkv.reshape(rows, 3, cols).transpose(1, 0, 2)
     qkv_blocks = jnp.stack(
         [
@@ -642,10 +704,11 @@
         ]
     )
     received = to_owner(jnp.concatenate([proj_blocks, qkv_blocks], axis=1))
-    out_proj = jnp.sum(received[:, :rows], axis=0)
+    out_proj = jnp.sum(received[:, :half].reshape(seq_n // 2, 2, half, share), axis=0)
+    out_proj = out_proj.reshape(rows, share)
     out_qkv = jnp.concatenate(
         [
-            lax.dynamic_index_in_dim(received, (3 * seq + i) % seq_n, 0, keepdims=False)[rows:]
+            lax.dynamic_index_in_dim(received, (3 * seq + i) % seq_n, 0, keepdims=False)[half:]
             for i in range(3)
         ],
         axis=1,

time: 660 us -> 617 us (0.935)
  waiting for transfers between devices: 255 us -> 194 us
  Pallas kernels: 114 us -> 155 us
  local copies, waits for them, and re-layouts: 93.2 us -> 77.7 us
  other arithmetic: 70.8 us -> 57.9 us
  starting transfers between devices: 66.7 us -> 73.8 us
    reduce_scatter x1, waiting for transfers between devices: 50.6 us -> 0.01 us  [on_device(): sum_fc = lax.psum_scatter(grad_fc, 'dp', scatter_dimension=0)]
    reduce_scatter x1, waiting for transfers between devices: 0.02 us -> 35.3 us  [on_device(): lax.psum_scatter(pack_last(proj_terms, grad_qkv.reshape(dp_n, rows, 3 * c...]
    ppermute x53, waiting for transfers between devices: 136 us -> 108 us  [hop(): return lax.ppermute(value, axis, [(i, i ^ bits) for i in range(count)])]
    unnamed x159 -> x114, local copies, waits for them, and re-layouts: 26.5 us -> 9.99 us
    pallas_call x0 -> x3, Pallas kernels: none -> 16.1 us  [the longest x2 9.17 us: pack(): pl.pallas_call(pack_kernel, grid=(count,), in_specs=[pl.BlockSpec((1, row...]
    pallas_call x2, Pallas kernels: 23.7 us -> 36.2 us  [attention_grad(): pl.pallas_call(partial(attend_grad_kernel, heads, block), grid=(lat,), in...]
    dynamic_slice x1 -> x0, other arithmetic: 9.69 us -> none  [on_device(): lax.dynamic_index_in_dim(grad_proj, 1 - core, axis=2, keepdims=False)]
    dot_general x3 -> x1, matrix products: 9.55 us -> 0.58 us  [matmul_nt(): lax.dot_general(left, right, (((1,), (1,)), ((), ())), preferred_element_...]
  transfers between devices with their start and end apart: 63 -> 63, of which waited for: 23 -> 18; matrix products, arithmetic and copies ran while one was open for 24% -> 27% of each run, Pallas kernels for 17% -> 25%
where the time goes in v5:
time: 617 us; the launch traced here: 611 us
  waiting for transfers between devices  194 us (31%)
  Pallas kernels  155 us (25%)
  local copies, waits for them, and re-layouts  77.7 us (13%)
  starting transfers between devices  73.8 us (12%)
  other arithmetic  57.9 us (9%)
  matrix products  37.5 us (6%)
  between operations  15.4 us (2%)
    ppermute x53, waiting for transfers between devices, hop(): return lax.ppermute(value, axis, [(i, i ^ bits) for i in range(count)])  108 us
    ppermute x53, starting transfers between devices, hop(): return lax.ppermute(value, axis, [(i, i ^ bits) for i in range(count)])  39.4 us
    pallas_call x2, Pallas kernels, attention_grad(): pl.pallas_call(partial(attend_grad_kernel, heads, block), grid=(lat,), in...  36.2 us
    reduce_scatter x1, waiting for transfers between devices, on_device(): lax.psum_scatter(pack_last(proj_terms, grad_qkv.reshape(dp_n, rows, 3 * c...  35.3 us
    pallas_call x2, Pallas kernels, mlp(): pl.pallas_call(partial(mlp_kernel, count), grid=(per, tok // chunk), in_s...  33.4 us
    dot_general x7, matrix products, matmul_tn(): lax.dot_general(left, right, (((0,), (0,)), ((), ())), preferred_element_...  33.1 us
    all_gather x1, waiting for transfers between devices, on_device(): proj_mine = lax.all_gather(proj_here, 'dp', axis=0)  29.9 us
    all_to_all x4, starting transfers between devices, dp_exchange(): return lax.all_to_all(value, 'dp', 0, 0, tiled=True)  27 us
  transfers between devices with their start and end apart: 63, of which 18 were waited for; matrix products, arithmetic and copies ran while one was open for 27% of the time, Pallas kernels for 25%

profile of v5, /device:TPU:0, one launch (start us, length us, event | category | flops | bytes accessed | tf_op | source)
XLA Modules:
  0.0 610.8 jit_solution(5711441333154086118)
XLA Ops:
  12.8 4.0 collective-permute-start.6
  22.2 2.2 constant_dynamic-slice_fusion.5
  28.0 29.9 %all-gather.6.cloned.1.call-done = bf16[576,1152]{1,0:T(8,128)(2,1)} async-done(((bf16[72,1152]{1,0:T(8,128)(2,1)}), bf16[576,1152]{1,0:T(8,128)(2,1)}) %all-gather.6.cloned.1.call-update) | async-done | bytes 1327120 | tf_op jit(solution)/shard_map/all_gather | solution.py:512
  62.1 3.3 all-to-all-start
  67.7 4.6 all-to-all-done
  77.4 4.1 all-to-all-start.1
  81.8 3.7 collective-permute-start.8
  90.4 16.0 %collective-permute-done.8 = bf16[144,864]{1,0:T(8,128)(2,1)S(1)} collective-permute-done((bf16[144,864]{1,0:T(8,128)(2,1)}, bf16[144,864]{1,0:T(8,128)(2,1)S(1)}, u32[]{:S(2)}, u32[]{:S(2)}) %collective-permute-start.8) | collective-permute-done | bytes 248864 | tf_op jit(solution)/shard_map/ppermute | solution.py:23
  111.3 5.5 collective-permute-done.7
  118.2 7.6 %collective-permute-done.9 = bf16[144,864]{1,0:T(8,128)(2,1)S(1)} collective-permute-done((bf16[144,864]{1,0:T(8,128)(2,1)S(1)}, bf16[144,864]{1,0:T(8,128)(2,1)S(1)}, u32[]{:S(2)}, u32[]{:S(2)}) %collective-permute-start.9) | collective-permute-done | bytes 248864 | tf_op jit(solution)/shard_map/ppermute | solution.py:23
  129.0 8.0 %qkv_forward.2 = (bf16[1,4,256,1152]{3,2,1,0:T(8,128)(2,1)}, bf16[1,4,256,864]{3,2,1,0:T(8,128)(2,1)}) custom-call(bf16[2,256,1152]{2,1,0:T(8,128)(2,1)} %refs_0_.3, bf16[2,256,1152]{2,1,0:T(8,128)(2,1)} %collective-permute-done.refs_1_, bf16[2,256,1152]{2,1,0:T(8,128)(2,1)} %collective-permute-done.1.refs_2_, ...), custom_call_target="tpu_custom_call" | custom-call | tf_op jit(solution)/shard_map/qkv_forward/pallas_call | solution.py:227
  137.0 8.7 %attend.2 = (bf16[1,1024,288]{2,1,0:T(8,128)(2,1)}, f32[1,4,1024]{2,1,0:T(4,128)}) custom-call(bf16[1,1024,864]{2,1,0:T(8,128)(2,1)} %bitcast.319), custom_call_target="tpu_custom_call" | custom-call | tf_op jit(solution)/shard_map/attend/pallas_call | solution.py:171
  149.0 8.2 %qkv_forward.3 = (bf16[1,4,256,1152]{3,2,1,0:T(8,128)(2,1)}, bf16[1,4,256,864]{3,2,1,0:T(8,128)(2,1)}) custom-call(bf16[2,256,1152]{2,1,0:T(8,128)(2,1)} %refs_0_.3, bf16[2,256,1152]{2,1,0:T(8,128)(2,1)} %collective-permute-done.refs_1_, bf16[2,256,1152]{2,1,0:T(8,128)(2,1)} %collective-permute-done.1.refs_2_, ...), custom_call_target="tpu_custom_call" | custom-call | tf_op jit(solution)/shard_map/qkv_forward/pallas_call | solution.py:227
  157.2 8.8 %attend.3 = (bf16[1,1024,288]{2,1,0:T(8,128)(2,1)}, f32[1,4,1024]{2,1,0:T(4,128)}) custom-call(bf16[1,1024,864]{2,1,0:T(8,128)(2,1)} %bitcast.321, bf16[1,1024,288]{2,1,0:T(8,128)(2,1)} %get-tuple-element.55.refs_0_.mixed, bf16[2,256,1152]{2,1,0:T(8,128)(2,1)} %collective-permute-done.19.refs_7_.refs_1_), custom_call_target="tpu_custom_call" | custom-call | tf_op jit(solution)/shard_map/attend/pallas_call | solution.py:171
  172.2 2.2 collective-permute-done.22
  174.4 4.3 collective-permute-done.21
  180.9 2.9 maximum_select_fusion
  184.3 5.3 pad_maximum_fusion.refs_6_
  192.3 2.3 fusion.45
  200.4 12.4 %collective-permute-done.15.refs_2_ = bf16[1,256,1152]{2,1,0:T(8,128)(2,1)} collective-permute-done((bf16[1,256,1152]{2,1,0:T(8,128)(2,1)}, bf16[1,256,1152]{2,1,0:T(8,128)(2,1)}, u32[]{:S(2)}, u32[]{:S(2)}) %collective-permute-start.15) | collective-permute-done | bytes 589856 | tf_op jit(solution)/shard_map/ppermute | solution.py:23
  213.9 10.4 %collective-permute-done.24.refs_2_ = bf16[1,256,1152]{2,1,0:T(8,128)(2,1)} collective-permute-done((bf16[1,256,1152]{2,1,0:T(8,128)(2,1)}, bf16[1,256,1152]{2,1,0:T(8,128)(2,1)}, u32[]{:S(2)}, u32[]{:S(2)}) %collective-permute-start.24) | collective-permute-done | bytes 589856 | tf_op jit(solution)/shard_map/ppermute | solution.py:23
  224.4 7.3 %unpack.1 = (bf16[8,144,1152]{2,1,0:T(8,128)(2,1)}, bf16[8,144,1152]{2,1,0:T(8,128)(2,1)}) custom-call(bf16[8,288,1152]{2,1,0:T(8,128)(2,1)} %all-gather.4.cloned.1.call-done.joined, bf16[1,256,1152]{2,1,0:T(8,128)(2,1)} %add_convert_fusion.3.after.refs_0_), custom_call_target="tpu_custom_call" | custom-call | tf_op jit(solution)/shard_map/unpack/pallas_call | solution.py:444
  231.6 16.7 %mlp.2 = (bf16[1,4,256,1152]{3,2,1,0:T(8,128)(2,1)}, bf16[1,4,256,1152]{3,2,1,0:T(8,128)(2,1)}, bf16[1,4,256,1152]{3,2,1,0:T(8,128)(2,1)}, bf16[1,4,256,1152]{3,...) custom-call(bf16[1,256,1152]{2,1,0:T(8,128)(2,1)} %add_convert_fusion.3.after.refs_0_, ...), custom_call_target="tpu_custom_call" | custom-call | tf_op jit(solution)/shard_map/mlp/pallas_call | solution.py:287
  248.3 2.4 slice_bitcast_fusion.17
  251.2 16.7 %mlp.3 = (bf16[1,4,256,1152]{3,2,1,0:T(8,128)(2,1)}, bf16[1,4,256,1152]{3,2,1,0:T(8,128)(2,1)}, bf16[1,4,256,1152]{3,2,1,0:T(8,128)(2,1)}, bf16[1,4,256,1152]{3,...) custom-call(bf16[1,256,1152]{2,1,0:T(8,128)(2,1)} %add_convert_fusion.2.refs_0_, ...), custom_call_target="tpu_custom_call" | custom-call | tf_op jit(solution)/shard_map/mlp/pallas_call | solution.py:287
  268.0 2.3 slice_bitcast_fusion.19
  270.8 5.1 convolution_bitcast_fusion.2
  275.9 3.3 convolution_bitcast_fusion
  279.3 5.0 fusion.2
  284.4 5.1 fusion.3
  292.8 2.2 fusion.56
  296.4 7.2 %pack.3.refs_7_ = bf16[8,288,1152]{2,1,0:T(8,128)(2,1)} custom-call(bf16[8,144,1152]{2,1,0:T(8,128)(2,1)} %bitcast.335, bf16[8,144,1152]{2,1,0:T(8,128)(2,1)} %bitcast.336, f32[1152]{0:T(1024)} %copy-done.30), custom_call_target="tpu_custom_call" | custom-call | tf_op jit(solution)/shard_map/pack/pallas_call | solution.py:396
  303.7 4.3 collective-permute-done.28
  308.0 2.6 fusion.63.refs_0_
  310.6 6.6 %resid_grad.2 = (f32[1,256,1152]{2,1,0:T(8,128)}, bf16[1,256,1152]{2,1,0:T(8,128)(2,1)}, f32[1,1,1152]{2,1,0:T(1,128)}, f32[1,1,1152]{2,1,0:T(1,128)}, f32[1,1,1...) custom-call(f32[1,256,1152]{2,1,0:T(8,128)} %fusion.63.refs_0_, ...), custom_call_target="tpu_custom_call" | custom-call | tf_op jit(solution)/shard_map/resid_grad/pallas_call | solution.py:360
  317.2 7.3 %mlp_out_terms.3.refs_2_ = bf16[1,4,256,1152]{3,2,1,0:T(8,128)(2,1)} custom-call(bf16[1,4,256,1152]{3,2,1,0:T(8,128)(2,1)} %get-tuple-element.67.activated, bf16[1152,1152]{1,0:T(8,128)(2,1)} %bitcast.307, bf16[1,256,288]{2,1,0:T(8,128)(2,1)} %get-tuple-element.71.after.refs_0_), custom_call_target="tpu_custom_call" | custom-call | tf_op jit(solution)/shard_map/mlp_out_terms/pallas_call | solution.py:312
  324.5 7.2 %mlp_out_terms.2.refs_1_ = bf16[1,4,256,1152]{3,2,1,0:T(8,128)(2,1)} custom-call(bf16[1,4,256,1152]{3,2,1,0:T(8,128)(2,1)} %get-tuple-element.58.activated, bf16[1152,1152]{1,0:T(8,128)(2,1)} %bitcast.308, bf16[1,256,288]{2,1,0:T(8,128)(2,1)} %get-tuple-element.71.after.refs_0_), custom_call_target="tpu_custom_call" | custom-call | tf_op jit(solution)/shard_map/mlp_out_terms/pallas_call | solution.py:312
  331.7 2.7 fusion.57.refs_0_
  334.4 6.7 %resid_grad.3 = (f32[1,256,1152]{2,1,0:T(8,128)}, bf16[1,256,1152]{2,1,0:T(8,128)(2,1)}, f32[1,1,1152]{2,1,0:T(1,128)}, f32[1,1,1152]{2,1,0:T(1,128)}, f32[1,1,1...) custom-call(f32[1,256,1152]{2,1,0:T(8,128)} %fusion.57.refs_0_, ...), custom_call_target="tpu_custom_call" | custom-call | tf_op jit(solution)/shard_map/resid_grad/pallas_call | solution.py:360
  344.6 3.3 convolution_convert_fusion
  350.7 5.2 pad_maximum_fusion.1
  360.5 18.1 %attend_grad.2 = (bf16[1,1024,864]{2,1,0:T(8,128)(2,1)}, bf16[1,1024,1152]{2,1,0:T(8,128)(2,1)}) custom-call(bf16[1,1024,864]{2,1,0:T(8,128)(2,1)} %bitcast.320, bf16[1,1024,288]{2,1,0:T(8,128)(2,1)} %get-tuple-element.55.refs_0_.mixed, f32[1,4,1024]{2,1,0:T(4,128)} %get-tuple-element.74.log_sum, bf16[1,1024,288]{2,1,0:T(8,128)(2,1)} %pad_maximum_fusion.6.d_mixed, ...), custom_call_target="tpu_custom_call" | custom-call | tf_op jit(solution)/shard_map/attend_grad/pallas_call | solution.py:189
  381.1 18.1 %attend_grad.3 = (bf16[1,1024,864]{2,1,0:T(8,128)(2,1)}, bf16[1,1024,1152]{2,1,0:T(8,128)(2,1)}) custom-call(bf16[1,1024,864]{2,1,0:T(8,128)(2,1)} %bitcast.322, bf16[1,1024,288]{2,1,0:T(8,128)(2,1)} %get-tuple-element.60.mixed, f32[1,4,1024]{2,1,0:T(4,128)} %get-tuple-element.81.log_sum, bf16[1,1024,288]{2,1,0:T(8,128)(2,1)} %pad_maximum_fusion.7.d_mixed, ...), custom_call_target="tpu_custom_call" | custom-call | tf_op jit(solution)/shard_map/attend_grad/pallas_call | solution.py:189
  399.2 9.8 %fusion.11 = bf16[1152,864]{0,1:T(8,128)(2,1)} fusion(bf16[1024,864]{1,0:T(8,128)(2,1)} %bitcast.360, bf16[1024,864]{1,0:T(8,128)(2,1)} %bitcast.359, bf16[1024,1152]{1,0:T(8,128)(2,1)} %bitcast.358, bf16[1024,1152]{1,0:T(8,128)(2,1)} %bitcast.357), kind=kOutput, calls=%fused_computation.16 | convolution fusion | flops 4094373888 | bytes 10248192 | tf_op jit(solution)/shard_map/dot_general | solution.py:35
  410.1 4.1 copy.110
  421.4 2.1 fusion.52
  424.4 9.6 %collective-permute-done.31 = bf16[1,256,1152]{2,1,0:T(8,128)(2,1)S(1)} collective-permute-done((bf16[1,256,1152]{2,1,0:T(8,128)(2,1)S(1)}, bf16[1,256,1152]{2,1,0:T(8,128)(2,1)S(1)}, u32[]{:S(2)}, u32[]{:S(2)}) %collective-permute-start.31) | collective-permute-done | bytes 589856 | tf_op jit(solution)/shard_map/ppermute | solution.py:23
  435.0 11.7 %collective-permute-done.34 = bf16[1,256,1152]{2,1,0:T(8,128)(2,1)S(1)} collective-permute-done((bf16[1,256,1152]{2,1,0:T(8,128)(2,1)S(1)}, bf16[1,256,1152]{2,1,0:T(8,128)(2,1)S(1)}, u32[]{:S(2)}, u32[]{:S(2)}) %collective-permute-start.34) | collective-permute-done | bytes 589856 | tf_op jit(solution)/shard_map/ppermute | solution.py:23
  447.6 2.8 multiply_reduce_fusion.1
  451.6 19.9 %collective-permute-done.43 = bf16[1,256,1152]{2,1,0:T(8,128)(2,1)S(1)} collective-permute-done((bf16[1,256,1152]{2,1,0:T(8,128)(2,1)S(1)}, bf16[1,256,1152]{2,1,0:T(8,128)(2,1)S(1)}, u32[]{:S(2)}, u32[]{:S(2)}) %collective-permute-start.43) | collective-permute-done | bytes 589856 | tf_op jit(solution)/shard_map/ppermute | solution.py:23
  475.3 7.0 %pack_last.1 = bf16[8,144,1440]{2,1,0:T(8,128)(2,1)} custom-call(f32[8,72,1152]{2,1,0:T(8,128)} %convert_add_fusion.proj_terms, bf16[8,144,864]{2,1,0:T(8,128)(2,1)} %bitcast.318, bf16[288,1152]{1,0:T(8,128)(2,1)} %bitcast.333), custom_call_target="tpu_custom_call" | custom-call | tf_op jit(solution)/shard_map/pack_last/pallas_call | solution.py:420
  482.4 4.1 fusion.38
  489.1 3.2 collective-permute-done.51
  493.1 16.3 %all-to-all-start.2 = ((bf16[8,2,6912]{2,1,0:T(2,128)(2,1)}), bf16[8,2,6912]{2,1,0:T(2,128)(2,1)S(1)}, u32[]{:S(2)}, u32[]{:S(2)}) async-start(bf16[8,2,6912]{2,1,0:T(2,128)(2,1)} %broadcast_in_dim.115), calls=%async_computation.2 | async-start | bytes 442368 | tf_op jit(solution)/shard_map/all_to_all | solution.py:77
  509.4 2.5 fusion.37
  513.4 11.0 %all-to-all-done.2 = bf16[8,2,6912]{2,1,0:T(2,128)(2,1)S(1)} async-done(((bf16[8,2,6912]{2,1,0:T(2,128)(2,1)}), bf16[8,2,6912]{2,1,0:T(2,128)(2,1)S(1)}, u32[]{:S(2)}, u32[]{:S(2)}) %all-to-all-start.2) | async-done | bytes 221216 | tf_op jit(solution)/shard_map/all_to_all | solution.py:77
  525.9 3.3 all-to-all-start.3
  531.3 4.9 all-to-all-done.3
  539.0 3.5 all-to-all-start.5
  542.5 35.3 %reduce-scatter.5.cloned.1.call-done = bf16[1,144,1440]{2,1,0:T(8,128)(2,1)} async-done(((bf16[8,144,1440]{2,1,0:T(8,128)(2,1)}), bf16[1,144,1440]{2,1,0:T(8,128)(2,1)}) %reduce-scatter.5.cloned.1.call-update) | async-done | bytes 414736 | tf_op jit(solution)/shard_map/reduce_scatter | solution.py:639
  585.3 3.5 all-to-all-start.4
  590.8 2.4 copy.118
  595.2 3.1 copy.139
  598.3 3.1 reshape.630
  (341 shorter events, 122.5 us)
Async XLA Ops:
  7.2 65.3 %copy-start = (bf16[144,6912]{1,0:T(8,128)(2,1)S(1)}, bf16[144,6912]{1,0:T(8,128)(2,1)}, u32[]{:S(2)}) copy-start(bf16[144,6912]{1,0:T(8,128)(2,1)} %param.12) | copy-start | bytes 5971972
  7.2 50.7 %all-gather.6.cloned.1.call-start = ((), (), s32[]{:S(2)}) async-start(), calls=%async_computation.11 | async-start | bytes 1492992 | tf_op jit(solution)/shard_map/all_gather | solution.py:512
  9.0 215.3 %all-gather.4.cloned.1.call-start = ((), (), s32[]{:S(2)}) async-start(), calls=%async_computation.8 | async-start | bytes 5971968 | tf_op jit(solution)/shard_map/all_gather | solution.py:514
  12.8 77.6 %collective-permute-start.6 = (bf16[144,864]{1,0:T(8,128)(2,1)}, bf16[144,864]{1,0:T(8,128)(2,1)}, u32[]{:S(2)}, u32[]{:S(2)}) collective-permute-start(bf16[144,864]{1,0:T(8,128)(2,1)} %get-tuple-element.186), channel_id=1, source_target_pairs={{0,16},{4,20},{8,24},{12,28},{16,0},{20,4},{24,8},{28,12},{1,17},{... | collective-permute-start | bytes 746504 | tf_op jit(solution)/shard_map/ppermute | solution.py:23
  16.8 65.0 %collective-permute-start.4 = (bf16[144,864]{1,0:T(8,128)(2,1)}, bf16[144,864]{1,0:T(8,128)(2,1)}, u32[]{:S(2)}, u32[]{:S(2)}) collective-permute-start(bf16[144,864]{1,0:T(8,128)(2,1)} %get-tuple-element.186), channel_id=1, source_target_pairs={{0,8},{4,12},{8,0},{12,4},{16,24},{20,28},{24,16},{28,20},{1,9},{5... | collective-permute-start | bytes 746504 | tf_op jit(solution)/shard_map/ppermute | solution.py:23
  18.4 67.2 %collective-permute-start.3 = (bf16[144,864]{1,0:T(8,128)(2,1)}, bf16[144,864]{1,0:T(8,128)(2,1)}, u32[]{:S(2)}, u32[]{:S(2)}) collective-permute-start(bf16[144,864]{1,0:T(8,128)(2,1)} %get-tuple-element.186), channel_id=1, source_target_pairs={{0,4},{4,0},{8,12},{12,8},{16,20},{20,16},{24,28},{28,24},{1,5},{5... | collective-permute-start | bytes 746504 | tf_op jit(solution)/shard_map/ppermute | solution.py:23
  19.9 88.5 %collective-permute-start.1 = (bf16[2,256,1152]{2,1,0:T(8,128)(2,1)S(1)}, bf16[2,256,1152]{2,1,0:T(8,128)(2,1)}, u32[]{:S(2)}, u32[]{:S(2)}) collective-permute-start(bf16[2,256,1152]{2,1,0:T(8,128)(2,1)S(1)} %copy-done.2), channel_id=1, source_target_pairs={{0,2},{1,3},{2,0},{3,1},{4,6},{5,7},{6,4},{7,5},{8,10},{9,11},{10,... | collective-permute-start | bytes 3538952 | tf_op jit(solution)/shard_map/ppermute | solution.py:23
  62.1 10.2 %all-to-all-start = ((bf16[8,2,1224]{2,1,0:T(2,128)(2,1)}), bf16[8,2,1224]{2,1,0:T(2,128)(2,1)S(1)}, u32[]{:S(2)}, u32[]{:S(2)}) async-start(bf16[8,2,1224]{2,1,0:T(2,128)(2,1)} %reshape.664), calls=%async_computation | async-start | bytes 81920 | tf_op jit(solution)/shard_map/all_to_all | solution.py:77
  65.5 45.3 %collective-permute-start.18 = (bf16[2,256,1152]{2,1,0:T(8,128)(2,1)}, bf16[2,256,1152]{2,1,0:T(8,128)(2,1)}, u32[]{:S(2)}, u32[]{:S(2)}) collective-permute-start(bf16[2,256,1152]{2,1,0:T(8,128)(2,1)} %refs_3_.3), channel_id=1, source_target_pairs={{0,2},{1,3},{2,0},{3,1},{4,6},{5,7},{6,4},{7,5},{8,10},{9,11},{10,... | collective-permute-start | bytes 3538952 | tf_op jit(solution)/shard_map/ppermute | solution.py:23
  77.4 49.2 %all-to-all-start.1 = ((f32[8,2,6912]{2,1,0:T(2,128)}), f32[8,2,6912]{2,1,0:T(2,128)}, u32[]{:S(2)}, u32[]{:S(2)}) async-start(f32[8,2,6912]{2,1,0:T(2,128)} %reshape.585), calls=%async_computation.1 | async-start | bytes 884736 | tf_op jit(solution)/shard_map/all_to_all | solution.py:77
  81.5 393.8 %reduce-scatter.3.cloned.1.call-start = ((), (), s32[]{:S(2)}) async-start(), calls=%async_computation.9 | async-start | bytes 5971968 | tf_op jit(solution)/shard_map/reduce_scatter | solution.py:586
  81.8 24.6 %collective-permute-start.8 = (bf16[144,864]{1,0:T(8,128)(2,1)}, bf16[144,864]{1,0:T(8,128)(2,1)S(1)}, u32[]{:S(2)}, u32[]{:S(2)}) collective-permute-start(bf16[144,864]{1,0:T(8,128)(2,1)} %get-tuple-element.186), channel_id=1, source_target_pairs={{0,24},{4,28},{8,16},{12,20},{16,8},{20,12},{24,0},{28,4},{1,25},{... | collective-permute-start | bytes 746504 | tf_op jit(solution)/shard_map/ppermute | solution.py:23
  85.5 22.3 %collective-permute-start.5 = (bf16[144,864]{1,0:T(8,128)(2,1)}, bf16[144,864]{1,0:T(8,128)(2,1)S(1)}, u32[]{:S(2)}, u32[]{:S(2)}) collective-permute-start(bf16[144,864]{1,0:T(8,128)(2,1)} %collective-permute-done.4), channel_id=1, source_target_pairs={{0,4},{4,0},{8,12},{12,8},{16,20},{20,16},{24,28},{28,24},{1,5},{5... | collective-permute-start | bytes 746504 | tf_op jit(solution)/shard_map/ppermute | solution.py:23
  90.4 38.6 %collective-permute-start = (bf16[2,256,1152]{2,1,0:T(8,128)(2,1)S(1)}, bf16[2,256,1152]{2,1,0:T(8,128)(2,1)}, u32[]{:S(2)}, u32[]{:S(2)}) collective-permute-start(bf16[2,256,1152]{2,1,0:T(8,128)(2,1)S(1)} %copy-done.2), channel_id=1, source_target_pairs={{0,1},{1,0},{2,3},{3,2},{4,5},{5,4},{6,7},{7,6},{8,9},{9,8},{10,11... | collective-permute-start | bytes 3538952 | tf_op jit(solution)/shard_map/ppermute | solution.py:23
  106.4 10.4 %collective-permute-start.7 = (bf16[144,864]{1,0:T(8,128)(2,1)}, bf16[144,864]{1,0:T(8,128)(2,1)S(1)}, u32[]{:S(2)}, u32[]{:S(2)}) collective-permute-start(bf16[144,864]{1,0:T(8,128)(2,1)} %collective-permute-done.6), channel_id=1, source_target_pairs={{0,4},{4,0},{8,12},{12,8},{16,20},{20,16},{24,28},{28,24},{1,5},{5... | collective-permute-start | bytes 746504 | tf_op jit(solution)/shard_map/ppermute | solution.py:23
  107.8 18.0 %collective-permute-start.9 = (bf16[144,864]{1,0:T(8,128)(2,1)S(1)}, bf16[144,864]{1,0:T(8,128)(2,1)S(1)}, u32[]{:S(2)}, u32[]{:S(2)}) collective-permute-start(bf16[144,864]{1,0:T(8,128)(2,1)S(1)} %collective-permute-done.8), channel_id=1, source_target_pairs={{0,4},{4,0},{8,12},{12,8},{16,20},{20,16},{24,28},{28,24},{1,5},{5... | collective-permute-start | bytes 746504 | tf_op jit(solution)/shard_map/ppermute | solution.py:23
  108.4 20.6 %collective-permute-start.2 = (bf16[2,256,1152]{2,1,0:T(8,128)(2,1)}, bf16[2,256,1152]{2,1,0:T(8,128)(2,1)}, u32[]{:S(2)}, u32[]{:S(2)}) collective-permute-start(bf16[2,256,1152]{2,1,0:T(8,128)(2,1)} %collective-permute-done.1.refs_2_), channel_id=1, source_target_pairs={{0,1},{1,0},{2,3},{3,2},{4,5},{5,4},{6,7},{7,6},{8,9},{9,8},{10,11... | collective-permute-start | bytes 3538952 | tf_op jit(solution)/shard_map/ppermute | solution.py:23
  110.8 46.4 %collective-permute-start.19 = (bf16[2,256,1152]{2,1,0:T(8,128)(2,1)}, bf16[2,256,1152]{2,1,0:T(8,128)(2,1)}, u32[]{:S(2)}, u32[]{:S(2)}) collective-permute-start(bf16[2,256,1152]{2,1,0:T(8,128)(2,1)} %collective-permute-done.18.refs_6_), channel_id=1, source_target_pairs={{0,1},{1,0},{2,3},{3,2},{4,5},{5,4},{6,7},{7,6},{8,9},{9,8},{10,11... | collective-permute-start | bytes 3538952 | tf_op jit(solution)/shard_map/ppermute | solution.py:23
  117.5 63.4 %collective-permute-start.13 = (bf16[8,72,1152]{2,1,0:T(8,128)(2,1)}, bf16[8,72,1152]{2,1,0:T(8,128)(2,1)}, u32[]{:S(2)}, u32[]{:S(2)}) collective-permute-start(bf16[8,72,1152]{2,1,0:T(8,128)(2,1)} %bitcast.19.after), channel_id=1, source_target_pairs={{0,1},{1,0},{2,3},{3,2},{4,5},{5,4},{6,7},{7,6},{8,9},{9,8},{10,11... | collective-permute-start | bytes 3981320 | tf_op jit(solution)/shard_map/ppermute | solution.py:23
  147.0 21.2 %collective-permute-start.12 = (bf16[1,256,288]{2,1,0:T(8,128)(2,1)S(1)}, bf16[1,256,288]{2,1,0:T(8,128)(2,1)S(1)}, u32[]{:S(2)}, u32[]{:S(2)}) collective-permute-start(bf16[1,256,288]{2,1,0:T(8,128)(2,1)S(1)} %get-tuple-element.230), channel_id=1, source_target_pairs={{0,3},{1,2},{2,1},{3,0},{4,7},{5,6},{6,5},{7,4},{8,11},{9,10},{10,... | collective-permute-start | bytes 442376 | tf_op jit(solution)/shard_map/ppermute | solution.py:23
  147.1 21.9 %collective-permute-start.11 = (bf16[1,256,288]{2,1,0:T(8,128)(2,1)S(1)}, bf16[1,256,288]{2,1,0:T(8,128)(2,1)}, u32[]{:S(2)}, u32[]{:S(2)}) collective-permute-start(bf16[1,256,288]{2,1,0:T(8,128)(2,1)S(1)} %get-tuple-element.231), channel_id=1, source_target_pairs={{0,2},{1,3},{2,0},{3,1},{4,6},{5,7},{6,4},{7,5},{8,10},{9,11},{10,... | collective-permute-start | bytes 442376 | tf_op jit(solution)/shard_map/ppermute | solution.py:23
  148.4 21.4 %collective-permute-start.10 = (bf16[1,256,288]{2,1,0:T(8,128)(2,1)S(1)}, bf16[1,256,288]{2,1,0:T(8,128)(2,1)}, u32[]{:S(2)}, u32[]{:S(2)}) collective-permute-start(bf16[1,256,288]{2,1,0:T(8,128)(2,1)S(1)} %get-tuple-element.232), channel_id=1, source_target_pairs={{0,1},{1,0},{2,3},{3,2},{4,5},{5,4},{6,7},{7,6},{8,9},{9,8},{10,11... | collective-permute-start | bytes 442376 | tf_op jit(solution)/shard_map/ppermute | solution.py:23
  167.3 7.1 %collective-permute-start.22 = (bf16[1,256,288]{2,1,0:T(8,128)(2,1)S(1)}, bf16[1,256,288]{2,1,0:T(8,128)(2,1)}, u32[]{:S(2)}, u32[]{:S(2)}) collective-permute-start(bf16[1,256,288]{2,1,0:T(8,128)(2,1)S(1)} %get-tuple-element.234), channel_id=1, source_target_pairs={{0,3},{1,2},{2,1},{3,0},{4,7},{5,6},{6,5},{7,4},{8,11},{9,10},{10,... | collective-permute-start | bytes 442376 | tf_op jit(solution)/shard_map/ppermute | solution.py:23
  168.3 10.5 %collective-permute-start.21 = (bf16[1,256,288]{2,1,0:T(8,128)(2,1)S(1)}, bf16[1,256,288]{2,1,0:T(8,128)(2,1)S(1)}, u32[]{:S(2)}, u32[]{:S(2)}) collective-permute-start(bf16[1,256,288]{2,1,0:T(8,128)(2,1)S(1)} %get-tuple-element.235), channel_id=1, source_target_pairs={{0,2},{1,3},{2,0},{3,1},{4,6},{5,7},{6,4},{7,5},{8,10},{9,11},{10,... | collective-permute-start | bytes 442376 | tf_op jit(solution)/shard_map/ppermute | solution.py:23
  169.0 9.7 %collective-permute-start.20 = (bf16[1,256,288]{2,1,0:T(8,128)(2,1)S(1)}, bf16[1,256,288]{2,1,0:T(8,128)(2,1)}, u32[]{:S(2)}, u32[]{:S(2)}) collective-permute-start(bf16[1,256,288]{2,1,0:T(8,128)(2,1)S(1)} %get-tuple-element.236), channel_id=1, source_target_pairs={{0,1},{1,0},{2,3},{3,2},{4,5},{5,4},{6,7},{7,6},{8,9},{9,8},{10,11... | collective-permute-start | bytes 442376 | tf_op jit(solution)/shard_map/ppermute | solution.py:23
  169.8 61.8 %collective-permute-start.17 = (bf16[2,256,1152]{2,1,0:T(8,128)(2,1)}, bf16[2,256,1152]{2,1,0:T(8,128)(2,1)}, u32[]{:S(2)}, u32[]{:S(2)}) collective-permute-start(bf16[2,256,1152]{2,1,0:T(8,128)(2,1)} %refs_3_.3), channel_id=1, source_target_pairs={{0,1},{1,0},{2,3},{3,2},{4,5},{5,4},{6,7},{7,6},{8,9},{9,8},{10,11... | collective-permute-start | bytes 3538952 | tf_op jit(solution)/shard_map/ppermute | solution.py:23
  196.2 16.5 %collective-permute-start.15 = (bf16[1,256,1152]{2,1,0:T(8,128)(2,1)}, bf16[1,256,1152]{2,1,0:T(8,128)(2,1)}, u32[]{:S(2)}, u32[]{:S(2)}) collective-permute-start(bf16[1,256,1152]{2,1,0:T(8,128)(2,1)} %add_convert_fusion.3.after.refs_0_), channel_id=1, source_target_pairs={{0,2},{1,3},{2,0},{3,1},{4,6},{5,7},{6,4},{7,5},{8,10},{9,11},{10,... | collective-permute-start | bytes 1769480 | tf_op jit(solution)/shard_map/ppermute | solution.py:23
  198.9 25.4 %collective-permute-start.24 = (bf16[1,256,1152]{2,1,0:T(8,128)(2,1)}, bf16[1,256,1152]{2,1,0:T(8,128)(2,1)}, u32[]{:S(2)}, u32[]{:S(2)}) collective-permute-start(bf16[1,256,1152]{2,1,0:T(8,128)(2,1)} %add_convert_fusion.2.refs_0_), channel_id=1, source_target_pairs={{0,2},{1,3},{2,0},{3,1},{4,6},{5,7},{6,4},{7,5},{8,10},{9,11},{10,... | collective-permute-start | bytes 1769480 | tf_op jit(solution)/shard_map/ppermute | solution.py:23
  200.4 31.3 %collective-permute-start.14 = (bf16[1,256,1152]{2,1,0:T(8,128)(2,1)}, bf16[1,256,1152]{2,1,0:T(8,128)(2,1)}, u32[]{:S(2)}, u32[]{:S(2)}) collective-permute-start(bf16[1,256,1152]{2,1,0:T(8,128)(2,1)} %add_convert_fusion.3.after.refs_0_), channel_id=1, source_target_pairs={{0,1},{1,0},{2,3},{3,2},{4,5},{5,4},{6,7},{7,6},{8,9},{9,8},{10,11... | collective-permute-start | bytes 1769480 | tf_op jit(solution)/shard_map/ppermute | solution.py:23
  212.8 18.9 %collective-permute-start.16 = (bf16[1,256,1152]{2,1,0:T(8,128)(2,1)}, bf16[1,256,1152]{2,1,0:T(8,128)(2,1)}, u32[]{:S(2)}, u32[]{:S(2)}) collective-permute-start(bf16[1,256,1152]{2,1,0:T(8,128)(2,1)} %collective-permute-done.15.refs_2_), channel_id=1, source_target_pairs={{0,1},{1,0},{2,3},{3,2},{4,5},{5,4},{6,7},{7,6},{8,9},{9,8},{10,11... | collective-permute-start | bytes 1769480 | tf_op jit(solution)/shard_map/ppermute | solution.py:23
  213.4 37.8 %collective-permute-start.23 = (bf16[1,256,1152]{2,1,0:T(8,128)(2,1)}, bf16[1,256,1152]{2,1,0:T(8,128)(2,1)}, u32[]{:S(2)}, u32[]{:S(2)}) collective-permute-start(bf16[1,256,1152]{2,1,0:T(8,128)(2,1)} %add_convert_fusion.2.refs_0_), channel_id=1, source_target_pairs={{0,1},{1,0},{2,3},{3,2},{4,5},{5,4},{6,7},{7,6},{8,9},{9,8},{10,11... | collective-permute-start | bytes 1769480 | tf_op jit(solution)/shard_map/ppermute | solution.py:23
  224.3 26.9 %collective-permute-start.25 = (bf16[1,256,1152]{2,1,0:T(8,128)(2,1)}, bf16[1,256,1152]{2,1,0:T(8,128)(2,1)}, u32[]{:S(2)}, u32[]{:S(2)}) collective-permute-start(bf16[1,256,1152]{2,1,0:T(8,128)(2,1)} %collective-permute-done.24.refs_2_), channel_id=1, source_target_pairs={{0,1},{1,0},{2,3},{3,2},{4,5},{5,4},{6,7},{7,6},{8,9},{9,8},{10,11... | collective-permute-start | bytes 1769480 | tf_op jit(solution)/shard_map/ppermute | solution.py:23
  250.7 81.0 %collective-permute-start.35 = (bf16[1,256,1152]{2,1,0:T(8,128)(2,1)}, bf16[1,256,1152]{2,1,0:T(8,128)(2,1)}, u32[]{:S(2)}, u32[]{:S(2)}) collective-permute-start(bf16[1,256,1152]{2,1,0:T(8,128)(2,1)} %get-tuple-element.201), channel_id=1, source_target_pairs={{0,1},{1,0},{2,3},{3,2},{4,5},{5,4},{6,7},{7,6},{8,9},{9,8},{10,11... | collective-permute-start | bytes 1769480 | tf_op jit(solution)/shard_map/ppermute | solution.py:23
  251.2 41.6 %collective-permute-start.36 = (bf16[1,256,1152]{2,1,0:T(8,128)(2,1)}, bf16[1,256,1152]{2,1,0:T(8,128)(2,1)}, u32[]{:S(2)}, u32[]{:S(2)}) collective-permute-start(bf16[1,256,1152]{2,1,0:T(8,128)(2,1)} %get-tuple-element.202), channel_id=1, source_target_pairs={{0,1},{1,0},{2,3},{3,2},{4,5},{5,4},{6,7},{7,6},{8,9},{9,8},{10,11... | collective-permute-start | bytes 1769480 | tf_op jit(solution)/shard_map/ppermute | solution.py:23
  270.3 33.4 %collective-permute-start.26 = (bf16[1,256,1152]{2,1,0:T(8,128)(2,1)}, bf16[1,256,1152]{2,1,0:T(8,128)(2,1)}, u32[]{:S(2)}, u32[]{:S(2)}) collective-permute-start(bf16[1,256,1152]{2,1,0:T(8,128)(2,1)} %get-tuple-element.207), channel_id=1, source_target_pairs={{0,1},{1,0},{2,3},{3,2},{4,5},{5,4},{6,7},{7,6},{8,9},{9,8},{10,11... | collective-permute-start | bytes 1769480 | tf_op jit(solution)/shard_map/ppermute | solution.py:23
  270.7 18.8 %collective-permute-start.27 = (bf16[1,256,1152]{2,1,0:T(8,128)(2,1)S(1)}, bf16[1,256,1152]{2,1,0:T(8,128)(2,1)S(1)}, u32[]{:S(2)}, u32[]{:S(2)}) collective-permute-start(bf16[1,256,1152]{2,1,0:T(8,128)(2,1)S(1)} %get-tuple-element.208), channel_id=1, source_target_pairs={{0,1},{1,0},{2,3},{3,2},{4,5},{5,4},{6,7},{7,6},{8,9},{9,8},{10,11... | collective-permute-start | bytes 1769480 | tf_op jit(solution)/shard_map/ppermute | solution.py:23
  291.5 16.4 %collective-permute-start.28 = (bf16[1,256,1152]{2,1,0:T(8,128)(2,1)}, bf16[1,256,1152]{2,1,0:T(8,128)(2,1)}, u32[]{:S(2)}, u32[]{:S(2)}) collective-permute-start(bf16[1,256,1152]{2,1,0:T(8,128)(2,1)} %fusion.62), channel_id=1, source_target_pairs={{0,2},{1,3},{2,0},{3,1},{4,6},{5,7},{6,4},{7,5},{8,10},{9,11},{10,... | collective-permute-start | bytes 1769480 | tf_op jit(solution)/shard_map/ppermute | solution.py:23
  295.0 36.7 %collective-permute-start.37 = (bf16[1,256,1152]{2,1,0:T(8,128)(2,1)}, bf16[1,256,1152]{2,1,0:T(8,128)(2,1)}, u32[]{:S(2)}, u32[]{:S(2)}) collective-permute-start(bf16[1,256,1152]{2,1,0:T(8,128)(2,1)} %fusion.56), channel_id=1, source_target_pairs={{0,2},{1,3},{2,0},{3,1},{4,6},{5,7},{6,4},{7,5},{8,10},{9,11},{10,... | collective-permute-start | bytes 1769480 | tf_op jit(solution)/shard_map/ppermute | solution.py:23
  303.6 274.1 %reduce-scatter.5.cloned.1.call-start = ((), (), s32[]{:S(2)}) async-start(), calls=%async_computation.10 | async-start | bytes 3981312 | tf_op jit(solution)/shard_map/reduce_scatter | solution.py:639
  341.1 16.0 %collective-permute-start.38 = (bf16[1,256,288]{2,1,0:T(8,128)(2,1)}, bf16[1,256,288]{2,1,0:T(8,128)(2,1)S(1)}, u32[]{:S(2)}, u32[]{:S(2)}) collective-permute-start(bf16[1,256,288]{2,1,0:T(8,128)(2,1)} %get-tuple-element.76), channel_id=1, source_target_pairs={{0,1},{1,0},{2,3},{3,2},{4,5},{5,4},{6,7},{7,6},{8,9},{9,8},{10,11... | collective-permute-start | bytes 442376 | tf_op jit(solution)/shard_map/ppermute | solution.py:23
  341.2 17.5 %collective-permute-start.39 = (bf16[1,256,288]{2,1,0:T(8,128)(2,1)}, bf16[1,256,288]{2,1,0:T(8,128)(2,1)S(1)}, u32[]{:S(2)}, u32[]{:S(2)}) collective-permute-start(bf16[1,256,288]{2,1,0:T(8,128)(2,1)} %get-tuple-element.77), channel_id=1, source_target_pairs={{0,2},{1,3},{2,0},{3,1},{4,6},{5,7},{6,4},{7,5},{8,10},{9,11},{10,... | collective-permute-start | bytes 442376 | tf_op jit(solution)/shard_map/ppermute | solution.py:23
  342.4 17.0 %collective-permute-start.40 = (bf16[1,256,288]{2,1,0:T(8,128)(2,1)}, bf16[1,256,288]{2,1,0:T(8,128)(2,1)S(1)}, u32[]{:S(2)}, u32[]{:S(2)}) collective-permute-start(bf16[1,256,288]{2,1,0:T(8,128)(2,1)} %get-tuple-element.78), channel_id=1, source_target_pairs={{0,3},{1,2},{2,1},{3,0},{4,7},{5,6},{6,5},{7,4},{8,11},{9,10},{10,... | collective-permute-start | bytes 442376 | tf_op jit(solution)/shard_map/ppermute | solution.py:23
  343.0 35.6 %collective-permute-start.44 = (bf16[1,256,288]{2,1,0:T(8,128)(2,1)}, bf16[1,256,288]{2,1,0:T(8,128)(2,1)S(1)}, u32[]{:S(2)}, u32[]{:S(2)}) collective-permute-start(bf16[1,256,288]{2,1,0:T(8,128)(2,1)} %get-tuple-element.82), channel_id=1, source_target_pairs={{0,1},{1,0},{2,3},{3,2},{4,5},{5,4},{6,7},{7,6},{8,9},{9,8},{10,11... | collective-permute-start | bytes 442376 | tf_op jit(solution)/shard_map/ppermute | solution.py:23
  343.4 35.8 %collective-permute-start.45 = (bf16[1,256,288]{2,1,0:T(8,128)(2,1)}, bf16[1,256,288]{2,1,0:T(8,128)(2,1)S(1)}, u32[]{:S(2)}, u32[]{:S(2)}) collective-permute-start(bf16[1,256,288]{2,1,0:T(8,128)(2,1)} %get-tuple-element.83), channel_id=1, source_target_pairs={{0,2},{1,3},{2,0},{3,1},{4,6},{5,7},{6,4},{7,5},{8,10},{9,11},{10,... | collective-permute-start | bytes 442376 | tf_op jit(solution)/shard_map/ppermute | solution.py:23
  357.1 22.1 %collective-permute-start.46 = (bf16[1,256,288]{2,1,0:T(8,128)(2,1)}, bf16[1,256,288]{2,1,0:T(8,128)(2,1)}, u32[]{:S(2)}, u32[]{:S(2)}) collective-permute-start(bf16[1,256,288]{2,1,0:T(8,128)(2,1)} %get-tuple-element.84), channel_id=1, source_target_pairs={{0,3},{1,2},{2,1},{3,0},{4,7},{5,6},{6,5},{7,4},{8,11},{9,10},{10,... | collective-permute-start | bytes 442376 | tf_op jit(solution)/shard_map/ppermute | solution.py:23
  358.7 65.1 %collective-permute-start.29 = (bf16[1,256,1152]{2,1,0:T(8,128)(2,1)}, bf16[1,256,1152]{2,1,0:T(8,128)(2,1)}, u32[]{:S(2)}, u32[]{:S(2)}) collective-permute-start(bf16[1,256,1152]{2,1,0:T(8,128)(2,1)} %get-tuple-element.203), channel_id=1, source_target_pairs={{0,1},{1,0},{2,3},{3,2},{4,5},{5,4},{6,7},{7,6},{8,9},{9,8},{10,11... | collective-permute-start | bytes 1769480 | tf_op jit(solution)/shard_map/ppermute | solution.py:23
  359.5 56.7 %collective-permute-start.30 = (bf16[1,256,1152]{2,1,0:T(8,128)(2,1)}, bf16[1,256,1152]{2,1,0:T(8,128)(2,1)}, u32[]{:S(2)}, u32[]{:S(2)}) collective-permute-start(bf16[1,256,1152]{2,1,0:T(8,128)(2,1)} %get-tuple-element.204), channel_id=1, source_target_pairs={{0,1},{1,0},{2,3},{3,2},{4,5},{5,4},{6,7},{7,6},{8,9},{9,8},{10,11... | collective-permute-start | bytes 1769480 | tf_op jit(solution)/shard_map/ppermute | solution.py:23
  378.7 45.7 %collective-permute-start.32 = (bf16[1,256,1152]{2,1,0:T(8,128)(2,1)}, bf16[1,256,1152]{2,1,0:T(8,128)(2,1)}, u32[]{:S(2)}, u32[]{:S(2)}) collective-permute-start(bf16[1,256,1152]{2,1,0:T(8,128)(2,1)} %get-tuple-element.205), channel_id=1, source_target_pairs={{0,1},{1,0},{2,3},{3,2},{4,5},{5,4},{6,7},{7,6},{8,9},{9,8},{10,11... | collective-permute-start | bytes 1769480 | tf_op jit(solution)/shard_map/ppermute | solution.py:23
  379.2 38.6 %collective-permute-start.33 = (bf16[1,256,1152]{2,1,0:T(8,128)(2,1)}, bf16[1,256,1152]{2,1,0:T(8,128)(2,1)}, u32[]{:S(2)}, u32[]{:S(2)}) collective-permute-start(bf16[1,256,1152]{2,1,0:T(8,128)(2,1)} %get-tuple-element.206), channel_id=1, source_target_pairs={{0,1},{1,0},{2,3},{3,2},{4,5},{5,4},{6,7},{7,6},{8,9},{9,8},{10,11... | collective-permute-start | bytes 1769480 | tf_op jit(solution)/shard_map/ppermute | solution.py:23
  414.2 6.0 collective-permute-start.48
  416.1 7.4 %collective-permute-start.42 = (bf16[1,256,1152]{2,1,0:T(8,128)(2,1)S(1)}, bf16[1,256,1152]{2,1,0:T(8,128)(2,1)S(1)}, u32[]{:S(2)}, u32[]{:S(2)}) collective-permute-start(bf16[1,256,1152]{2,1,0:T(8,128)(2,1)S(1)} %get-tuple-element.200), channel_id=1, source_target_pairs={{0,1},{1,0},{2,3},{3,2},{4,5},{5,4},{6,7},{7,6},{8,9},{9,8},{10,11... | collective-permute-start | bytes 1769480 | tf_op jit(solution)/shard_map/ppermute | solution.py:23
  417.8 16.2 %collective-permute-start.31 = (bf16[1,256,1152]{2,1,0:T(8,128)(2,1)S(1)}, bf16[1,256,1152]{2,1,0:T(8,128)(2,1)S(1)}, u32[]{:S(2)}, u32[]{:S(2)}) collective-permute-start(bf16[1,256,1152]{2,1,0:T(8,128)(2,1)S(1)} %fusion.60), channel_id=1, source_target_pairs={{0,2},{1,3},{2,0},{3,1},{4,6},{5,7},{6,4},{7,5},{8,10},{9,11},{10,... | collective-permute-start | bytes 1769480 | tf_op jit(solution)/shard_map/ppermute | solution.py:23
  420.2 26.4 %collective-permute-start.34 = (bf16[1,256,1152]{2,1,0:T(8,128)(2,1)S(1)}, bf16[1,256,1152]{2,1,0:T(8,128)(2,1)S(1)}, u32[]{:S(2)}, u32[]{:S(2)}) collective-permute-start(bf16[1,256,1152]{2,1,0:T(8,128)(2,1)S(1)} %fusion.58), channel_id=1, source_target_pairs={{0,2},{1,3},{2,0},{3,1},{4,6},{5,7},{6,4},{7,5},{8,10},{9,11},{10,... | collective-permute-start | bytes 1769480 | tf_op jit(solution)/shard_map/ppermute | solution.py:23
  423.5 48.9 %collective-permute-start.52 = (bf16[8,72,1152]{2,1,0:T(8,128)(2,1)S(1)}, bf16[8,72,1152]{2,1,0:T(8,128)(2,1)S(1)}, u32[]{:S(2)}, u32[]{:S(2)}) collective-permute-start(bf16[8,72,1152]{2,1,0:T(8,128)(2,1)S(1)} %copy-done.26), channel_id=1, source_target_pairs={{0,1},{1,0},{2,3},{3,2},{4,5},{5,4},{6,7},{7,6},{8,9},{9,8},{10,11... | collective-permute-start | bytes 3981320 | tf_op jit(solution)/shard_map/ppermute | solution.py:23
  423.8 58.5 %collective-permute-start.47 = (bf16[1,256,1152]{2,1,0:T(8,128)(2,1)}, bf16[1,256,1152]{2,1,0:T(8,128)(2,1)}, u32[]{:S(2)}, u32[]{:S(2)}) collective-permute-start(bf16[1,256,1152]{2,1,0:T(8,128)(2,1)} %get-tuple-element.197), channel_id=1, source_target_pairs={{0,1},{1,0},{2,3},{3,2},{4,5},{5,4},{6,7},{7,6},{8,9},{9,8},{10,11... | collective-permute-start | bytes 1769480 | tf_op jit(solution)/shard_map/ppermute | solution.py:23
  424.4 27.2 %collective-permute-start.41 = (bf16[1,256,1152]{2,1,0:T(8,128)(2,1)S(1)}, bf16[1,256,1152]{2,1,0:T(8,128)(2,1)S(1)}, u32[]{:S(2)}, u32[]{:S(2)}) collective-permute-start(bf16[1,256,1152]{2,1,0:T(8,128)(2,1)S(1)} %get-tuple-element.199), channel_id=1, source_target_pairs={{0,1},{1,0},{2,3},{3,2},{4,5},{5,4},{6,7},{7,6},{8,9},{9,8},{10,11... | collective-permute-start | bytes 1769480 | tf_op jit(solution)/shard_map/ppermute | solution.py:23
  434.0 48.3 %collective-permute-start.49 = (bf16[1,256,1152]{2,1,0:T(8,128)(2,1)}, bf16[1,256,1152]{2,1,0:T(8,128)(2,1)}, u32[]{:S(2)}, u32[]{:S(2)}) collective-permute-start(bf16[1,256,1152]{2,1,0:T(8,128)(2,1)} %fusion.52), channel_id=1, source_target_pairs={{0,2},{1,3},{2,0},{3,1},{4,6},{5,7},{6,4},{7,5},{8,10},{9,11},{10,... | collective-permute-start | bytes 1769480 | tf_op jit(solution)/shard_map/ppermute | solution.py:23
  446.6 24.8 %collective-permute-start.43 = (bf16[1,256,1152]{2,1,0:T(8,128)(2,1)S(1)}, bf16[1,256,1152]{2,1,0:T(8,128)(2,1)S(1)}, u32[]{:S(2)}, u32[]{:S(2)}) collective-permute-start(bf16[1,256,1152]{2,1,0:T(8,128)(2,1)S(1)} %fusion.54), channel_id=1, source_target_pairs={{0,2},{1,3},{2,0},{3,1},{4,6},{5,7},{6,4},{7,5},{8,10},{9,11},{10,... | collective-permute-start | bytes 1769480 | tf_op jit(solution)/shard_map/ppermute | solution.py:23
  486.7 1.3 collective-permute-start.50
  488.1 4.2 collective-permute-start.51
  493.1 31.3 %all-to-all-start.2 = ((bf16[8,2,6912]{2,1,0:T(2,128)(2,1)}), bf16[8,2,6912]{2,1,0:T(2,128)(2,1)S(1)}, u32[]{:S(2)}, u32[]{:S(2)}) async-start(bf16[8,2,6912]{2,1,0:T(2,128)(2,1)} %broadcast_in_dim.115), calls=%async_computation.2 | async-start | bytes 442368 | tf_op jit(solution)/shard_map/all_to_all | solution.py:77
  525.9 10.2 %all-to-all-start.3 = ((f32[8,1,432]{2,1,0:T(1,128)}), f32[8,1,432]{2,1,0:T(1,128)S(1)}, u32[]{:S(2)}, u32[]{:S(2)}) async-start(f32[8,1,432]{2,1,0:T(1,128)} %all_to_all.30), calls=%async_computation.3 | async-start | bytes 32768 | tf_op jit(solution)/shard_map/all_to_all | solution.py:77
  539.0 46.3 %all-to-all-start.5 = ((bf16[4,288,288]{2,1,0:T(8,128)(2,1)}), bf16[4,288,288]{2,1,0:T(8,128)(2,1)S(1)}, u32[]{:S(2)}, u32[]{:S(2)}) async-start(bf16[4,288,288]{2,1,0:T(8,128)(2,1)} %pad_maximum_fusion.5), calls=%async_computation.7 | async-start | bytes 1769472 | tf_op jit(solution)/shard_map/all_to_all | solution.py:682
  585.3 16.1 %all-to-all-start.4 = ((bf16[4,216,288]{1,2,0:T(8,128)(2,1)}), bf16[4,216,288]{1,2,0:T(8,128)(2,1)S(1)}, u32[]{:S(2)}, u32[]{:S(2)}) async-start(bf16[4,216,288]{1,2,0:T(8,128)(2,1)} %copy.112), calls=%async_computation.6 | async-start | bytes 1179648 | tf_op jit(solution)/shard_map/all_to_all | solution.py:682
  (52 other events, 316.3 us)
Sparse Core Ops, SparseCore 0:
  10.8 47.0 all-gather.5
  60.6 111.1 all-gather.3
  303.7 115.3 reduce-scatter.2
  482.5 95.2 reduce-scatter.4

commit v6 on v5

--- a/solution.py
+++ b/solution.py
@@ -59,14 +59,29 @@
     return [slots[j] for j in range(len(slots))]
 
 
-def seq_reduce(slots):
+def seq_step(slots, bit):
+    kept = {j: v for j, v in slots.items() if not j & bit}
+    for j in slots:
+        if j & bit:
+            kept[j ^ bit] = kept[j ^ bit] + hop(slots[j].astype(BF), "seq", bit).astype(F32)
+    return kept
+
+
+def seq_near(slots):
     slots = dict(enumerate(slots))
     bit = 1
-    while len(slots) > 1:
-        for j in [j for j in slots if j & bit]:
-            slots[j ^ bit] = slots[j ^ bit] + hop(slots.pop(j).astype(BF), "seq", bit).astype(F32)
+    while len(slots) > 2:
+        slots = seq_step(slots, bit)
         bit *= 2
-    return slots[0]
+    return slots[0], slots[bit].astype(BF)
+
+
+def seq_far(kept, sent):
+    return kept + hop(sent, "seq", lax.axis_size("seq") // 2).astype(F32)
+
+
+def seq_reduce(slots):
+    return seq_far(*seq_near(slots))
 
 
 def seq_exchange(blocks):
@@ -455,6 +470,73 @@
     )(joined, after)
 
 
+def token_grad_kernel(per, d_first, e_first, d_resid, e_resid, tokens, scale, after, *outs):
+    grad_tokens, d_shift, d_scale = outs
+    early = pl.program_id(0) < per
+    grad = jnp.where(early, d_first[0], e_first[0])
+    normed, inv_std = ln_parts(tokens[0].astype(F32))
+    grad_tokens[0] = jnp.where(early, d_resid[0], e_resid[0]) + ln_backward(
+        grad * (1.0 + scale[0]), normed, inv_std
+    )
+
+    @pl.when(pl.program_id(1) == 0)
+    def _():
+        d_shift[...] = jnp.zeros_like(d_shift)
+        d_scale[...] = jnp.zeros_like(d_scale)
+
+    d_shift[0] += jnp.sum(grad, axis=0, keepdims=True)
+    d_scale[0] += jnp.sum(grad * normed, axis=0, keepdims=True)
+
+
+def token_grad(d_first, d_resid, tokens, scale, after):
+    lat, tok, width = tokens.shape
+    per = lat // 2
+    chunk = min(tok, 128)
+    early = pl.BlockSpec((1, chunk, width), lambda i, c: (jnp.minimum(i, per - 1), c, 0))
+    late = pl.BlockSpec((1, chunk, width), lambda i, c: (jnp.maximum(i, per) - per, c, 0))
+    block = pl.BlockSpec((1, chunk, width), lambda i, c: (i, c, 0))
+    row = pl.BlockSpec((1, 1, width), lambda i, c: (i, 0, 0))
+    row_shape = jax.ShapeDtypeStruct((lat, 1, width), F32)
+    return pl.pallas_call(
+        partial(token_grad_kernel, per),
+        grid=(lat, tok // chunk),
+        in_specs=[early, late, early, late, block, row, pl.BlockSpec(memory_space=pl.ANY)],
+        out_specs=[block, row, row],
+        out_shape=[jax.ShapeDtypeStruct((lat, tok, width), F32), row_shape, row_shape],
+        compiler_params=pltpu.CompilerParams(vmem_limit_bytes=VMEM_LIMIT),
+        name="token_grad",
+    )(*d_first, *d_resid, tokens, scale, after)
+
+
+def place_last_kernel(rows, owners, received, out_qkv, out_proj):
+    cols = received.shape[2]
+    half = rows // 2
+    for i in range(3):
+        out_qkv[:, i * cols : (i + 1) * cols] = received[owners[i], :rows].astype(F32)
+    for core in range(2):
+        total = received[core, rows:].astype(F32)
+        for j in range(core + 2, received.shape[0], 2):
+            total = total + received[j, rows:].astype(F32)
+        out_proj[core * half : (core + 1) * half] = total
+
+
+def place_last(received, rows, seq):
+    count, _, cols = received.shape
+    owners = (3 * seq + jnp.arange(3, dtype=jnp.int32)) % count
+    vmem = pl.BlockSpec(memory_space=pltpu.VMEM)
+    return pl.pallas_call(
+        partial(place_last_kernel, rows),
+        in_specs=[pl.BlockSpec(memory_space=pltpu.SMEM), vmem],
+        out_specs=[vmem, vmem],
+        out_shape=[
+            jax.ShapeDtypeStruct((rows, 3 * cols), F32),
+            jax.ShapeDtypeStruct((rows, cols), F32),
+        ],
+        compiler_params=pltpu.CompilerParams(vmem_limit_bytes=VMEM_LIMIT),
+        name="place_last",
+    )(owners, received)
+
+
 def on_device(tokens, conditioning, w_mod, b_mod, w_qkv, w_proj, w_fc1, b_fc1, w_fc2, cotangent):
     lat, tok, width = tokens.shape
     seq_n = lax.axis_size("seq")
@@ -511,7 +593,7 @@
     together = hid == width
     proj_mine = lax.all_gather(proj_here, "dp", axis=0)
     if together:
-        joined = lax.all_gather(pack(fc1_here[None], fc2_here[None], proj_mine)[0], "dp", axis=0)
+        joined = lax.all_gather(jnp.concatenate([fc1_here, fc2_here]), "dp", axis=0)
     else:
         fc1 = lax.all_gather(fc1_here, "dp", axis=0, tiled=True)
         fc2 = lax.all_gather(fc2_here, "dp", axis=0, tiled=True)
@@ -607,15 +689,11 @@
         d_gate_attn.append(outs[4][:, 0])
         d_attended.append(outs[5])
         d_mixed.append(jnp.concatenate(seq_exchange(outs[5:]), axis=1))
-    mlp_out, mlp_terms = [], []
+    mlp_terms, mlp_near = [], []
     for g in range(groups):
         terms = mlp_out_terms(activated[g], fc2, d_attended[-1])
         mlp_terms.append(terms)
-        mlp_out.append(seq_reduce([terms[:, j].astype(F32) for j in range(seq_n)]))
-    output = jnp.concatenate(
-        [(resid_mid[g] + gate_mlp[g] * mlp_out[g]).astype(BF) for g in range(groups)]
-    )
-    d_gate_mlp = stacked([jnp.sum(upstream[g] * mlp_out[g], axis=1) for g in range(groups)])
+        mlp_near.append(seq_near([terms[:, j].astype(F32) for j in range(seq_n)]))
     grad_proj = by_place(
         matmul_tn(stacked(attended), stacked(d_attn)).astype(BF).reshape(seq_n, cols, width)
     ).reshape(dp_n, 2, half, width)
@@ -629,30 +707,28 @@
     for g in range(groups):
         grads, terms = attention_grad(
             packed[g], mixed[g], log_sums[g], d_mixed[g], qkv,
-            first_terms if g else [d_attended[-1]] + mlp_terms, heads_here,
+            first_terms + [near[1] for near in mlp_near] if g else [d_attended[-1]] + mlp_terms,
+            heads_here,
         )
         d_packed.append(grads.reshape(per * seq_len, 3 * cols))
         first_terms.append(terms)
         terms = terms.reshape(per, seq_n, tok, width)
         d_first.append(seq_reduce([terms[:, j].astype(F32) for j in range(seq_n)]))
+    mlp_out = [seq_far(*near) for near in mlp_near]
+    output = jnp.concatenate(
+        [(resid_mid[g] + gate_mlp[g] * mlp_out[g]).astype(BF) for g in range(groups)]
+    )
+    d_gate_mlp = stacked([jnp.sum(upstream[g] * mlp_out[g], axis=1) for g in range(groups)])
     grad_qkv = matmul_tn(stacked(normed_all), stacked(d_packed)).astype(BF)
-    sum_last = lax.psum_scatter(
-        pack_last(proj_terms, grad_qkv.reshape(dp_n, rows, 3 * cols), sum_fc),
-        "dp",
-        scatter_dimension=0,
-    )
+    last = pack_last(proj_terms, grad_qkv.reshape(dp_n, rows, 3 * cols), sum_fc)
+    sum_last = lax.psum_scatter(last, "dp", scatter_dimension=0)
     sum_proj, sum_qkv = sum_last[:, : width // 2], sum_last[:, width // 2 :]
-    d_shift_attn, d_scale_attn, grad_tokens = [], [], []
-    for g in range(groups):
-        normed_tok, std_tok = ln_parts(token_values[g])
-        d_shift_attn.append(jnp.sum(d_first[g], axis=1))
-        d_scale_attn.append(jnp.sum(d_first[g] * normed_tok, axis=1))
-        grad_tokens.append(
-            d_resid[g] + ln_backward(d_first[g] * (1.0 + scale_attn[g]), normed_tok, std_tok)
-        )
+    grad_tokens, d_shift_attn, d_scale_attn = token_grad(
+        d_first, d_resid, tokens, modulation[:, None, width : 2 * width], last
+    )
 
     mod_part = jnp.concatenate(
-        [stacked(d_shift_attn), stacked(d_scale_attn), stacked(d_gate_attn)]
+        [d_shift_attn[:, 0], d_scale_attn[:, 0], stacked(d_gate_attn)]
         + [stacked(d_shift_mlp), stacked(d_scale_mlp), d_gate_mlp],
         axis=1,
     )
@@ -703,19 +779,13 @@
             for to in range(seq_n)
         ]
     )
-    received = to_owner(jnp.concatenate([proj_blocks, qkv_blocks], axis=1))
-    out_proj = jnp.sum(received[:, :half].reshape(seq_n // 2, 2, half, share), axis=0)
-    out_proj = out_proj.reshape(rows, share)
-    out_qkv = jnp.concatenate(
-        [
-            lax.dynamic_index_in_dim(received, (3 * seq + i) % seq_n, 0, keepdims=False)[half:]
-            for i in range(3)
-        ],
-        axis=1,
-    )
+    received = lax.all_to_all(
+        jnp.concatenate([qkv_blocks, proj_blocks], axis=1), "seq", 0, 0, tiled=True
+    )
+    out_qkv, out_proj = place_last(received, rows, seq)
     return (
         output,
-        stacked(grad_tokens),
+        grad_tokens,
         grad_cond,
         grad_wmod,
         grad_bmod,

time: 617 us -> 538 us (0.87)
  waiting for transfers between devices: 194 us -> 108 us
  Pallas kernels: 155 us -> 162 us
    ppermute x53, waiting for transfers between devices: 108 us -> 73.6 us  [hop(): return lax.ppermute(value, axis, [(i, i ^ bits) for i in range(count)])]
    all_gather x1, waiting for transfers between devices: 29.9 us -> 0.01 us  [on_device(): proj_mine = lax.all_gather(proj_here, 'dp', axis=0)]
    reduce_scatter x1, waiting for transfers between devices: 35.3 us -> 7.83 us  [on_device(): sum_last = lax.psum_scatter(last, 'dp', scatter_dimension=0)]
    all_to_all x4, waiting for transfers between devices: 20.4 us -> 8.87 us  [dp_exchange(): return lax.all_to_all(value, 'dp', 0, 0, tiled=True)]
    all_to_all x2 -> x1, waiting for transfers between devices: 0.01 us -> 9.12 us  [to_owner(): return lax.all_to_all(blocks, 'seq', 0, 0, tiled=True).astype(F32)]
    pallas_call x0 -> x2, Pallas kernels: none -> 8.95 us  [the longest x1 6.89 us: token_grad(): pl.pallas_call(partial(token_grad_kernel, per), grid=(lat, tok // chunk),...]
    all_to_all x0 -> x1, waiting for transfers between devices: none -> 8.88 us  [on_device(): lax.all_to_all(jnp.concatenate([qkv_blocks, proj_blocks], axis=1), 'seq',...]
    all_to_all x4, starting transfers between devices: 27 us -> 33.4 us  [dp_exchange(): return lax.all_to_all(value, 'dp', 0, 0, tiled=True)]
  transfers between devices with their start and end apart: 63 -> 63, of which waited for: 18 -> 16; matrix products, arithmetic and copies ran while one was open for 27% -> 29% of each run, Pallas kernels for 25% -> 30%
where the time goes in v6:
time: 538 us; the launch traced here: 532 us
  Pallas kernels  162 us (30%)
  waiting for transfers between devices  108 us (20%)
  starting transfers between devices  78.8 us (15%)
  local copies, waits for them, and re-layouts  73.6 us (14%)
  other arithmetic  57.3 us (11%)
  matrix products  36.3 us (7%)
  between operations  15.1 us (3%)
    ppermute x53, waiting for transfers between devices, hop(): return lax.ppermute(value, axis, [(i, i ^ bits) for i in range(count)])  73.6 us
    ppermute x53, starting transfers between devices, hop(): return lax.ppermute(value, axis, [(i, i ^ bits) for i in range(count)])  38.1 us
    pallas_call x2, Pallas kernels, attention_grad(): pl.pallas_call(partial(attend_grad_kernel, heads, block), grid=(lat,), in...  36.3 us
    pallas_call x2, Pallas kernels, mlp(): pl.pallas_call(partial(mlp_kernel, count), grid=(per, tok // chunk), in_s...  33.5 us
    all_to_all x4, starting transfers between devices, dp_exchange(): return lax.all_to_all(value, 'dp', 0, 0, tiled=True)  33.4 us
    dot_general x7, matrix products, matmul_tn(): lax.dot_general(left, right, (((0,), (0,)), ((), ())), preferred_element_...  32.2 us
    pallas_call x2, Pallas kernels, attention(): pl.pallas_call(partial(attend_kernel, heads, block), grid=(lat,), in_spec...  17.9 us
    pallas_call x2, Pallas kernels, qkv_forward(): pl.pallas_call(partial(qkv_kernel, count), grid=(per, tok // chunk), in_s...  16.1 us
  transfers between devices with their start and end apart: 63, of which 16 were waited for; matrix products, arithmetic and copies ran while one was open for 29% of the time, Pallas kernels for 30%

profile of v6, /device:TPU:0, one launch (start us, length us, event | category | flops | bytes accessed | tf_op | source)
XLA Modules:
  0.0 531.9 jit_solution(13339116034384102498)
XLA Ops:
  9.1 2.3 constant_dynamic-slice_fusion.6
  17.8 7.3 %all-to-all-start = ((bf16[8,2,1224]{2,1,0:T(2,128)(2,1)}), bf16[8,2,1224]{2,1,0:T(2,128)(2,1)S(1)}, u32[]{:S(2)}, u32[]{:S(2)}) async-start(bf16[8,2,1224]{2,1,0:T(2,128)(2,1)} %reshape.546), calls=%async_computation | async-start | bytes 81920 | tf_op jit(solution)/shard_map/all_to_all | solution.py:92
  30.3 2.9 collective-permute-start.6
  43.0 4.1 all-to-all-start.1
  47.3 3.7 collective-permute-start.8
  55.9 14.5 %collective-permute-done.8 = bf16[144,864]{1,0:T(8,128)(2,1)} collective-permute-done((bf16[144,864]{1,0:T(8,128)(2,1)}, bf16[144,864]{1,0:T(8,128)(2,1)}, u32[]{:S(2)}, u32[]{:S(2)}) %collective-permute-start.8) | collective-permute-done | bytes 248864 | tf_op jit(solution)/shard_map/ppermute | solution.py:23
  70.3 2.2 collective-permute-start.7
  74.2 3.8 collective-permute-done.18.refs_6_
  85.7 8.0 %qkv_forward.2 = (bf16[1,4,256,1152]{3,2,1,0:T(8,128)(2,1)}, bf16[1,4,256,864]{3,2,1,0:T(8,128)(2,1)}) custom-call(bf16[2,256,1152]{2,1,0:T(8,128)(2,1)} %tokens.1, bf16[2,256,1152]{2,1,0:T(8,128)(2,1)} %collective-permute-done.refs_1_, bf16[2,256,1152]{2,1,0:T(8,128)(2,1)} %collective-permute-done.1.refs_2_, ...), custom_call_target="tpu_custom_call" | custom-call | tf_op jit(solution)/shard_map/qkv_forward/pallas_call | solution.py:242
  93.7 8.7 %attend.2 = (bf16[1,1024,288]{2,1,0:T(8,128)(2,1)}, f32[1,4,1024]{2,1,0:T(4,128)}) custom-call(bf16[1,1024,864]{2,1,0:T(8,128)(2,1)} %bitcast.292), custom_call_target="tpu_custom_call" | custom-call | tf_op jit(solution)/shard_map/attend/pallas_call | solution.py:186
  105.7 8.1 %qkv_forward.3 = (bf16[1,4,256,1152]{3,2,1,0:T(8,128)(2,1)}, bf16[1,4,256,864]{3,2,1,0:T(8,128)(2,1)}) custom-call(bf16[2,256,1152]{2,1,0:T(8,128)(2,1)} %tokens.1, bf16[2,256,1152]{2,1,0:T(8,128)(2,1)} %collective-permute-done.refs_1_, bf16[2,256,1152]{2,1,0:T(8,128)(2,1)} %collective-permute-done.1.refs_2_, ...), custom_call_target="tpu_custom_call" | custom-call | tf_op jit(solution)/shard_map/qkv_forward/pallas_call | solution.py:242
  113.8 9.1 %attend.3 = (bf16[1,1024,288]{2,1,0:T(8,128)(2,1)}, f32[1,4,1024]{2,1,0:T(4,128)}) custom-call(bf16[1,1024,864]{2,1,0:T(8,128)(2,1)} %bitcast.294, bf16[1,1024,288]{2,1,0:T(8,128)(2,1)} %get-tuple-element.60.refs_0_.mixed, bf16[2,256,1152]{2,1,0:T(8,128)(2,1)} %collective-permute-done.19.refs_7_.refs_1_), custom_call_target="tpu_custom_call" | custom-call | tf_op jit(solution)/shard_map/attend/pallas_call | solution.py:186
  122.9 2.0 slice_bitcast_fusion.20
  129.2 2.9 collective-permute-done.22
  132.1 4.6 collective-permute-done.21
  136.7 2.1 concatenate.75
  138.8 3.0 maximum_select_fusion
  142.3 5.2 pad_maximum_fusion.refs_6_
  149.6 2.2 fusion.53
  156.0 12.8 %collective-permute-done.15.refs_2_ = bf16[1,256,1152]{2,1,0:T(8,128)(2,1)} collective-permute-done((bf16[1,256,1152]{2,1,0:T(8,128)(2,1)S(1)}, bf16[1,256,1152]{2,1,0:T(8,128)(2,1)}, u32[]{:S(2)}, u32[]{:S(2)}) %collective-permute-start.15) | collective-permute-done | bytes 589856 | tf_op jit(solution)/shard_map/ppermute | solution.py:23
  169.3 10.8 %collective-permute-done.24.refs_2_ = bf16[1,256,1152]{2,1,0:T(8,128)(2,1)} collective-permute-done((bf16[1,256,1152]{2,1,0:T(8,128)(2,1)}, bf16[1,256,1152]{2,1,0:T(8,128)(2,1)}, u32[]{:S(2)}, u32[]{:S(2)}) %collective-permute-start.24) | collective-permute-done | bytes 589856 | tf_op jit(solution)/shard_map/ppermute | solution.py:23
  181.5 7.3 %unpack.1 = (bf16[8,144,1152]{2,1,0:T(8,128)(2,1)}, bf16[8,144,1152]{2,1,0:T(8,128)(2,1)}) custom-call(bf16[8,288,1152]{2,1,0:T(8,128)(2,1)} %bitcast.297, bf16[1,256,1152]{2,1,0:T(8,128)(2,1)} %copy-done.12), custom_call_target="tpu_custom_call" | custom-call | tf_op jit(solution)/shard_map/unpack/pallas_call | solution.py:459
  188.8 16.7 %mlp.2 = (bf16[1,4,256,1152]{3,2,1,0:T(8,128)(2,1)}, bf16[1,4,256,1152]{3,2,1,0:T(8,128)(2,1)}, bf16[1,4,256,1152]{3,2,1,0:T(8,128)(2,1)}, bf16[1,4,256,1152]{3,...) custom-call(bf16[1,256,1152]{2,1,0:T(8,128)(2,1)} %copy-done.12, ...), custom_call_target="tpu_custom_call" | custom-call | tf_op jit(solution)/shard_map/mlp/pallas_call | solution.py:302
  205.5 2.4 slice_bitcast_fusion.17
  208.4 16.8 %mlp.3 = (bf16[1,4,256,1152]{3,2,1,0:T(8,128)(2,1)}, bf16[1,4,256,1152]{3,2,1,0:T(8,128)(2,1)}, bf16[1,4,256,1152]{3,2,1,0:T(8,128)(2,1)}, bf16[1,4,256,1152]{3,...) custom-call(bf16[1,256,1152]{2,1,0:T(8,128)(2,1)} %add_convert_fusion.2.refs_0_, ...), custom_call_target="tpu_custom_call" | custom-call | tf_op jit(solution)/shard_map/mlp/pallas_call | solution.py:302
  225.2 2.5 slice_bitcast_fusion.19
  228.2 5.1 convolution_bitcast_fusion.2
  233.4 3.3 convolution_bitcast_fusion
  236.8 5.0 fusion.2
  241.7 5.1 fusion.3
  247.5 7.2 %pack.1.refs_7_ = bf16[8,288,1152]{2,1,0:T(8,128)(2,1)} custom-call(bf16[8,144,1152]{2,1,0:T(8,128)(2,1)} %bitcast.305, bf16[8,144,1152]{2,1,0:T(8,128)(2,1)} %bitcast.306, f32[1152]{0:T(1024)} %add_reduce_fusion.after), custom_call_target="tpu_custom_call" | custom-call | tf_op jit(solution)/shard_map/pack/pallas_call | solution.py:411
  261.5 11.7 %collective-permute-done.28 = bf16[1,256,1152]{2,1,0:T(8,128)(2,1)} collective-permute-done((bf16[1,256,1152]{2,1,0:T(8,128)(2,1)}, bf16[1,256,1152]{2,1,0:T(8,128)(2,1)}, u32[]{:S(2)}, u32[]{:S(2)}) %collective-permute-start.28) | collective-permute-done | bytes 589856 | tf_op jit(solution)/shard_map/ppermute | solution.py:23
  273.2 2.6 fusion.41.refs_0_
  275.8 7.0 %resid_grad.2 = (f32[1,256,1152]{2,1,0:T(8,128)}, bf16[1,256,1152]{2,1,0:T(8,128)(2,1)}, f32[1,1,1152]{2,1,0:T(1,128)}, f32[1,1,1152]{2,1,0:T(1,128)}, f32[1,1,1...) custom-call(f32[1,256,1152]{2,1,0:T(8,128)} %fusion.41.refs_0_, ...), custom_call_target="tpu_custom_call" | custom-call | tf_op jit(solution)/shard_map/resid_grad/pallas_call | solution.py:375
  282.8 7.2 %mlp_out_terms.3.refs_2_ = bf16[1,4,256,1152]{3,2,1,0:T(8,128)(2,1)} custom-call(bf16[1,4,256,1152]{3,2,1,0:T(8,128)(2,1)} %get-tuple-element.72.activated, bf16[1152,1152]{1,0:T(8,128)(2,1)} %bitcast.281, bf16[1,256,288]{2,1,0:T(8,128)(2,1)} %get-tuple-element.76.after.refs_0_), custom_call_target="tpu_custom_call" | custom-call | tf_op jit(solution)/shard_map/mlp_out_terms/pallas_call | solution.py:327
  290.0 7.1 %mlp_out_terms.2.refs_1_ = bf16[1,4,256,1152]{3,2,1,0:T(8,128)(2,1)} custom-call(bf16[1,4,256,1152]{3,2,1,0:T(8,128)(2,1)} %get-tuple-element.63.activated, bf16[1152,1152]{1,0:T(8,128)(2,1)} %bitcast.282, bf16[1,256,288]{2,1,0:T(8,128)(2,1)} %get-tuple-element.76.after.refs_0_), custom_call_target="tpu_custom_call" | custom-call | tf_op jit(solution)/shard_map/mlp_out_terms/pallas_call | solution.py:327
  297.1 2.6 fusion.35.refs_0_
  299.8 6.9 %resid_grad.3 = (f32[1,256,1152]{2,1,0:T(8,128)}, bf16[1,256,1152]{2,1,0:T(8,128)(2,1)}, f32[1,1,1152]{2,1,0:T(1,128)}, f32[1,1,1152]{2,1,0:T(1,128)}, f32[1,1,1...) custom-call(f32[1,256,1152]{2,1,0:T(8,128)} %fusion.35.refs_0_, ...), custom_call_target="tpu_custom_call" | custom-call | tf_op jit(solution)/shard_map/resid_grad/pallas_call | solution.py:375
  310.7 3.0 convolution_convert_fusion
  318.3 5.2 pad_maximum_fusion.1
  326.2 18.0 %attend_grad.2 = (bf16[1,1024,864]{2,1,0:T(8,128)(2,1)}, bf16[1,1024,1152]{2,1,0:T(8,128)(2,1)}) custom-call(bf16[1,1024,864]{2,1,0:T(8,128)(2,1)} %bitcast.293, bf16[1,1024,288]{2,1,0:T(8,128)(2,1)} %get-tuple-element.60.refs_0_.mixed, f32[1,4,1024]{2,1,0:T(4,128)} %get-tuple-element.77.log_sum, bf16[1,1024,288]{2,1,0:T(8,128)(2,1)} %pad_maximum_fusion.4.d_mixed, ...), custom_call_target="tpu_custom_call" | custom-call | tf_op jit(solution)/shard_map/attend_grad/pallas_call | solution.py:204
  344.2 2.4 slice_bitcast_fusion.6
  349.5 2.0 fusion.38.refs_1_
  355.6 18.3 %attend_grad.3 = (bf16[1,1024,864]{2,1,0:T(8,128)(2,1)}, bf16[1,1024,1152]{2,1,0:T(8,128)(2,1)}) custom-call(bf16[1,1024,864]{2,1,0:T(8,128)(2,1)} %bitcast.295, bf16[1,1024,288]{2,1,0:T(8,128)(2,1)} %get-tuple-element.65.mixed, f32[1,4,1024]{2,1,0:T(4,128)} %get-tuple-element.84.log_sum, bf16[1,1024,288]{2,1,0:T(8,128)(2,1)} %pad_maximum_fusion.5.d_mixed, ...), custom_call_target="tpu_custom_call" | custom-call | tf_op jit(solution)/shard_map/attend_grad/pallas_call | solution.py:204
  373.9 9.2 %fusion.11 = bf16[1152,864]{0,1:T(8,128)(2,1)} fusion(bf16[1024,864]{1,0:T(8,128)(2,1)} %bitcast.332, bf16[1024,864]{1,0:T(8,128)(2,1)S(1)} %bitcast.331, bf16[1024,1152]{1,0:T(8,128)(2,1)} %bitcast.330, bf16[1024,1152]{1,0:T(8,128)(2,1)} %bitcast.329), kind=kOutput, calls=%fused_computation.16 | convolution fusion | flops 4094373888 | bytes 10248192 | tf_op jit(solution)/shard_map/dot_general | solution.py:35
  384.2 4.2 copy.96
  388.9 2.2 fusion.32
  393.5 4.4 multiply_reduce_fusion.1
  401.2 7.0 %pack_last.1.after = bf16[8,144,1440]{2,1,0:T(8,128)(2,1)} custom-call(f32[8,72,1152]{2,1,0:T(8,128)} %convert_add_fusion.proj_terms, bf16[8,144,864]{2,1,0:T(8,128)(2,1)} %bitcast.291, bf16[288,1152]{1,0:T(8,128)(2,1)} %bitcast.303), custom_call_target="tpu_custom_call" | custom-call | tf_op jit(solution)/shard_map/pack_last/pallas_call | solution.py:435
  408.2 2.6 fusion.33.d_first
  410.9 9.0 %collective-permute-done.49 = bf16[1,256,1152]{2,1,0:T(8,128)(2,1)S(1)} collective-permute-done((bf16[1,256,1152]{2,1,0:T(8,128)(2,1)S(1)}, bf16[1,256,1152]{2,1,0:T(8,128)(2,1)S(1)}, u32[]{:S(2)}, u32[]{:S(2)}) %collective-permute-start.49) | collective-permute-done | bytes 589856 | tf_op jit(solution)/shard_map/ppermute | solution.py:23
  419.9 2.5 fusion.31.e_first
  422.5 6.9 %token_grad.1 = (f32[2,256,1152]{2,1,0:T(8,128)}, f32[2,1,1152]{2,1,0:T(1,128)}, f32[2,1,1152]{2,1,0:T(1,128)}) custom-call(f32[1,256,1152]{2,1,0:T(8,128)} %fusion.33.d_first, f32[1,256,1152]{2,1,0:T(8,128)} %fusion.31.e_first, f32[1,256,1152]{2,1,0:T(8,128)} %get-tuple-element.89.d_resid, f32[1,256,1152]{2,1,0:T(8,128)} %get-tuple-element.90.e_resid, ...), custom_call_target="tpu_custom_call" | custom-call | tf_op jit(solution)/shard_map/token_grad/pallas_call | solution.py:500
  437.4 18.7 %all-to-all-start.2 = ((bf16[8,2,6912]{2,1,0:T(2,128)(2,1)}), bf16[8,2,6912]{2,1,0:T(2,128)(2,1)S(1)}, u32[]{:S(2)}, u32[]{:S(2)}) async-start(bf16[8,2,6912]{2,1,0:T(2,128)(2,1)} %broadcast_in_dim.103), calls=%async_computation.3 | async-start | bytes 442368 | tf_op jit(solution)/shard_map/all_to_all | solution.py:92
  457.3 8.9 %all-to-all-done.2 = bf16[8,2,6912]{2,1,0:T(2,128)(2,1)S(1)} async-done(((bf16[8,2,6912]{2,1,0:T(2,128)(2,1)}), bf16[8,2,6912]{2,1,0:T(2,128)(2,1)S(1)}, u32[]{:S(2)}, u32[]{:S(2)}) %all-to-all-start.2) | async-done | bytes 221216 | tf_op jit(solution)/shard_map/all_to_all | solution.py:92
  466.1 3.5 all-to-all-start.5
  473.2 9.1 %all-to-all-done.5 = bf16[4,288,288]{2,1,0:T(8,128)(2,1)S(1)} async-done(((bf16[4,288,288]{2,1,0:T(8,128)(2,1)}), bf16[4,288,288]{2,1,0:T(8,128)(2,1)S(1)}, u32[]{:S(2)}, u32[]{:S(2)}) %all-to-all-start.5) | async-done | bytes 663584 | tf_op jit(solution)/shard_map/all_to_all | solution.py:758
  482.3 3.3 all-to-all-start.3
  487.1 2.4 copy.104
  491.5 2.0 copy.129
  496.2 7.8 %reduce-scatter.5.cloned.1.call-done = bf16[1,144,1440]{2,1,0:T(8,128)(2,1)} async-done(((bf16[8,144,1440]{2,1,0:T(8,128)(2,1)}), bf16[1,144,1440]{2,1,0:T(8,128)(2,1)}) %reduce-scatter.5.cloned.1.call-update) | async-done | bytes 414736 | tf_op jit(solution)/shard_map/reduce_scatter | solution.py:724
  508.9 3.5 all-to-all-start.4
  513.0 8.9 %all-to-all-done.4 = bf16[4,216,288]{1,2,0:T(8,128)(2,1)S(1)} async-done(((bf16[4,216,288]{1,2,0:T(8,128)(2,1)}), bf16[4,216,288]{1,2,0:T(8,128)(2,1)S(1)}, u32[]{:S(2)}, u32[]{:S(2)}) %all-to-all-start.4) | async-done | bytes 497696 | tf_op jit(solution)/shard_map/all_to_all | solution.py:782
  523.0 2.1 place_last.1
  (313 shorter events, 112.8 us)
Async XLA Ops:
  7.2 30.9 %copy-start = (bf16[144,6912]{1,0:T(8,128)(2,1)S(1)}, bf16[144,6912]{1,0:T(8,128)(2,1)}, u32[]{:S(2)}) copy-start(bf16[144,6912]{1,0:T(8,128)(2,1)} %param.12) | copy-start | bytes 5971972
  7.2 72.8 %all-gather.5.cloned.1.call-start = ((), (), s32[]{:S(2)}) async-start(), calls=%async_computation.10 | async-start | bytes 1492992 | tf_op jit(solution)/shard_map/all_gather | solution.py:594
  9.0 172.5 %all-gather.7.cloned.1.call-start = ((), (), s32[]{:S(2)}) async-start(), calls=%async_computation.11 | async-start | bytes 5971968 | tf_op jit(solution)/shard_map/all_gather | solution.py:596
  17.8 19.4 %all-to-all-start = ((bf16[8,2,1224]{2,1,0:T(2,128)(2,1)}), bf16[8,2,1224]{2,1,0:T(2,128)(2,1)S(1)}, u32[]{:S(2)}, u32[]{:S(2)}) async-start(bf16[8,2,1224]{2,1,0:T(2,128)(2,1)} %reshape.546), calls=%async_computation | async-start | bytes 81920 | tf_op jit(solution)/shard_map/all_to_all | solution.py:92
  25.1 47.5 %collective-permute-start.1 = (bf16[2,256,1152]{2,1,0:T(8,128)(2,1)S(1)}, bf16[2,256,1152]{2,1,0:T(8,128)(2,1)}, u32[]{:S(2)}, u32[]{:S(2)}) collective-permute-start(bf16[2,256,1152]{2,1,0:T(8,128)(2,1)S(1)} %copy-done.8), channel_id=1, source_target_pairs={{0,2},{1,3},{2,0},{3,1},{4,6},{5,7},{6,4},{7,5},{8,10},{9,11},{10,... | collective-permute-start | bytes 3538952 | tf_op jit(solution)/shard_map/ppermute | solution.py:23
  30.3 25.6 %collective-permute-start.6 = (bf16[144,864]{1,0:T(8,128)(2,1)}, bf16[144,864]{1,0:T(8,128)(2,1)S(1)}, u32[]{:S(2)}, u32[]{:S(2)}) collective-permute-start(bf16[144,864]{1,0:T(8,128)(2,1)} %get-tuple-element.173), channel_id=1, source_target_pairs={{0,16},{4,20},{8,24},{12,28},{16,0},{20,4},{24,8},{28,12},{1,17},{... | collective-permute-start | bytes 746504 | tf_op jit(solution)/shard_map/ppermute | solution.py:23
  33.2 14.1 %collective-permute-start.4 = (bf16[144,864]{1,0:T(8,128)(2,1)}, bf16[144,864]{1,0:T(8,128)(2,1)}, u32[]{:S(2)}, u32[]{:S(2)}) collective-permute-start(bf16[144,864]{1,0:T(8,128)(2,1)} %get-tuple-element.173), channel_id=1, source_target_pairs={{0,8},{4,12},{8,0},{12,4},{16,24},{20,28},{24,16},{28,20},{1,9},{5... | collective-permute-start | bytes 746504 | tf_op jit(solution)/shard_map/ppermute | solution.py:23
  34.6 16.4 %collective-permute-start.3 = (bf16[144,864]{1,0:T(8,128)(2,1)}, bf16[144,864]{1,0:T(8,128)(2,1)}, u32[]{:S(2)}, u32[]{:S(2)}) collective-permute-start(bf16[144,864]{1,0:T(8,128)(2,1)} %get-tuple-element.173), channel_id=1, source_target_pairs={{0,4},{4,0},{8,12},{12,8},{16,20},{20,16},{24,28},{28,24},{1,5},{5... | collective-permute-start | bytes 746504 | tf_op jit(solution)/shard_map/ppermute | solution.py:23
  36.1 41.9 %collective-permute-start.18 = (bf16[2,256,1152]{2,1,0:T(8,128)(2,1)}, bf16[2,256,1152]{2,1,0:T(8,128)(2,1)}, u32[]{:S(2)}, u32[]{:S(2)}) collective-permute-start(bf16[2,256,1152]{2,1,0:T(8,128)(2,1)} %refs_3_.3), channel_id=1, source_target_pairs={{0,2},{1,3},{2,0},{3,1},{4,6},{5,7},{6,4},{7,5},{8,10},{9,11},{10,... | collective-permute-start | bytes 3538952 | tf_op jit(solution)/shard_map/ppermute | solution.py:23
  43.0 40.8 %all-to-all-start.1 = ((f32[8,2,6912]{2,1,0:T(2,128)}), f32[8,2,6912]{2,1,0:T(2,128)}, u32[]{:S(2)}, u32[]{:S(2)}) async-start(f32[8,2,6912]{2,1,0:T(2,128)} %reshape.470), calls=%async_computation.1 | async-start | bytes 884736 | tf_op jit(solution)/shard_map/all_to_all | solution.py:92
  47.1 354.1 %reduce-scatter.3.cloned.1.call-start = ((), (), s32[]{:S(2)}) async-start(), calls=%async_computation.8 | async-start | bytes 5971968 | tf_op jit(solution)/shard_map/reduce_scatter | solution.py:668
  47.3 23.0 %collective-permute-start.8 = (bf16[144,864]{1,0:T(8,128)(2,1)}, bf16[144,864]{1,0:T(8,128)(2,1)}, u32[]{:S(2)}, u32[]{:S(2)}) collective-permute-start(bf16[144,864]{1,0:T(8,128)(2,1)} %get-tuple-element.173), channel_id=1, source_target_pairs={{0,24},{4,28},{8,16},{12,20},{16,8},{20,12},{24,0},{28,4},{1,25},{... | collective-permute-start | bytes 746504 | tf_op jit(solution)/shard_map/ppermute | solution.py:23
  51.1 21.5 %collective-permute-start.5 = (bf16[144,864]{1,0:T(8,128)(2,1)}, bf16[144,864]{1,0:T(8,128)(2,1)S(1)}, u32[]{:S(2)}, u32[]{:S(2)}) collective-permute-start(bf16[144,864]{1,0:T(8,128)(2,1)} %collective-permute-done.4), channel_id=1, source_target_pairs={{0,4},{4,0},{8,12},{12,8},{16,20},{20,16},{24,28},{28,24},{1,5},{5... | collective-permute-start | bytes 746504 | tf_op jit(solution)/shard_map/ppermute | solution.py:23
  55.9 29.8 %collective-permute-start = (bf16[2,256,1152]{2,1,0:T(8,128)(2,1)S(1)}, bf16[2,256,1152]{2,1,0:T(8,128)(2,1)}, u32[]{:S(2)}, u32[]{:S(2)}) collective-permute-start(bf16[2,256,1152]{2,1,0:T(8,128)(2,1)S(1)} %copy-done.8), channel_id=1, source_target_pairs={{0,1},{1,0},{2,3},{3,2},{4,5},{5,4},{6,7},{7,6},{8,9},{9,8},{10,11... | collective-permute-start | bytes 3538952 | tf_op jit(solution)/shard_map/ppermute | solution.py:23
  70.3 8.9 %collective-permute-start.7 = (bf16[144,864]{1,0:T(8,128)(2,1)S(1)}, bf16[144,864]{1,0:T(8,128)(2,1)S(1)}, u32[]{:S(2)}, u32[]{:S(2)}) collective-permute-start(bf16[144,864]{1,0:T(8,128)(2,1)S(1)} %collective-permute-done.6), channel_id=1, source_target_pairs={{0,4},{4,0},{8,12},{12,8},{16,20},{20,16},{24,28},{28,24},{1,5},{5... | collective-permute-start | bytes 746504 | tf_op jit(solution)/shard_map/ppermute | solution.py:23
  72.6 9.5 %collective-permute-start.9 = (bf16[144,864]{1,0:T(8,128)(2,1)}, bf16[144,864]{1,0:T(8,128)(2,1)}, u32[]{:S(2)}, u32[]{:S(2)}) collective-permute-start(bf16[144,864]{1,0:T(8,128)(2,1)} %collective-permute-done.8), channel_id=1, source_target_pairs={{0,4},{4,0},{8,12},{12,8},{16,20},{20,16},{24,28},{28,24},{1,5},{5... | collective-permute-start | bytes 746504 | tf_op jit(solution)/shard_map/ppermute | solution.py:23
  72.6 13.1 %collective-permute-start.2 = (bf16[2,256,1152]{2,1,0:T(8,128)(2,1)}, bf16[2,256,1152]{2,1,0:T(8,128)(2,1)}, u32[]{:S(2)}, u32[]{:S(2)}) collective-permute-start(bf16[2,256,1152]{2,1,0:T(8,128)(2,1)} %collective-permute-done.1.refs_2_), channel_id=1, source_target_pairs={{0,1},{1,0},{2,3},{3,2},{4,5},{5,4},{6,7},{7,6},{8,9},{9,8},{10,11... | collective-permute-start | bytes 3538952 | tf_op jit(solution)/shard_map/ppermute | solution.py:23
  78.0 35.8 %collective-permute-start.19 = (bf16[2,256,1152]{2,1,0:T(8,128)(2,1)}, bf16[2,256,1152]{2,1,0:T(8,128)(2,1)}, u32[]{:S(2)}, u32[]{:S(2)}) collective-permute-start(bf16[2,256,1152]{2,1,0:T(8,128)(2,1)} %collective-permute-done.18.refs_6_), channel_id=1, source_target_pairs={{0,1},{1,0},{2,3},{3,2},{4,5},{5,4},{6,7},{7,6},{8,9},{9,8},{10,11... | collective-permute-start | bytes 3538952 | tf_op jit(solution)/shard_map/ppermute | solution.py:23
  80.0 58.8 %collective-permute-start.13 = (bf16[8,72,1152]{2,1,0:T(8,128)(2,1)}, bf16[8,72,1152]{2,1,0:T(8,128)(2,1)}, u32[]{:S(2)}, u32[]{:S(2)}) collective-permute-start(bf16[8,72,1152]{2,1,0:T(8,128)(2,1)} %bitcast.311), channel_id=1, source_target_pairs={{0,1},{1,0},{2,3},{3,2},{4,5},{5,4},{6,7},{7,6},{8,9},{9,8},{10,11... | collective-permute-start | bytes 3981320 | tf_op jit(solution)/shard_map/ppermute | solution.py:23
  103.7 22.8 %collective-permute-start.12 = (bf16[1,256,288]{2,1,0:T(8,128)(2,1)S(1)}, bf16[1,256,288]{2,1,0:T(8,128)(2,1)S(1)}, u32[]{:S(2)}, u32[]{:S(2)}) collective-permute-start(bf16[1,256,288]{2,1,0:T(8,128)(2,1)S(1)} %get-tuple-element.211), channel_id=1, source_target_pairs={{0,3},{1,2},{2,1},{3,0},{4,7},{5,6},{6,5},{7,4},{8,11},{9,10},{10,... | collective-permute-start | bytes 442376 | tf_op jit(solution)/shard_map/ppermute | solution.py:23
  105.1 21.9 %collective-permute-start.11 = (bf16[1,256,288]{2,1,0:T(8,128)(2,1)S(1)}, bf16[1,256,288]{2,1,0:T(8,128)(2,1)S(1)}, u32[]{:S(2)}, u32[]{:S(2)}) collective-permute-start(bf16[1,256,288]{2,1,0:T(8,128)(2,1)S(1)} %get-tuple-element.212), channel_id=1, source_target_pairs={{0,2},{1,3},{2,0},{3,1},{4,6},{5,7},{6,4},{7,5},{8,10},{9,11},{10,... | collective-permute-start | bytes 442376 | tf_op jit(solution)/shard_map/ppermute | solution.py:23
  105.5 21.5 %collective-permute-start.10 = (bf16[1,256,288]{2,1,0:T(8,128)(2,1)S(1)}, bf16[1,256,288]{2,1,0:T(8,128)(2,1)S(1)}, u32[]{:S(2)}, u32[]{:S(2)}) collective-permute-start(bf16[1,256,288]{2,1,0:T(8,128)(2,1)S(1)} %get-tuple-element.213), channel_id=1, source_target_pairs={{0,1},{1,0},{2,3},{3,2},{4,5},{5,4},{6,7},{7,6},{8,9},{9,8},{10,11... | collective-permute-start | bytes 442376 | tf_op jit(solution)/shard_map/ppermute | solution.py:23
  125.0 7.1 %collective-permute-start.22 = (bf16[1,256,288]{2,1,0:T(8,128)(2,1)}, bf16[1,256,288]{2,1,0:T(8,128)(2,1)}, u32[]{:S(2)}, u32[]{:S(2)}) collective-permute-start(bf16[1,256,288]{2,1,0:T(8,128)(2,1)} %get-tuple-element.215), channel_id=1, source_target_pairs={{0,3},{1,2},{2,1},{3,0},{4,7},{5,6},{6,5},{7,4},{8,11},{9,10},{10,... | collective-permute-start | bytes 442376 | tf_op jit(solution)/shard_map/ppermute | solution.py:23
  126.6 10.1 %collective-permute-start.21 = (bf16[1,256,288]{2,1,0:T(8,128)(2,1)}, bf16[1,256,288]{2,1,0:T(8,128)(2,1)}, u32[]{:S(2)}, u32[]{:S(2)}) collective-permute-start(bf16[1,256,288]{2,1,0:T(8,128)(2,1)} %get-tuple-element.216), channel_id=1, source_target_pairs={{0,2},{1,3},{2,0},{3,1},{4,6},{5,7},{6,4},{7,5},{8,10},{9,11},{10,... | collective-permute-start | bytes 442376 | tf_op jit(solution)/shard_map/ppermute | solution.py:23
  127.0 9.7 %collective-permute-start.20 = (bf16[1,256,288]{2,1,0:T(8,128)(2,1)S(1)}, bf16[1,256,288]{2,1,0:T(8,128)(2,1)}, u32[]{:S(2)}, u32[]{:S(2)}) collective-permute-start(bf16[1,256,288]{2,1,0:T(8,128)(2,1)S(1)} %get-tuple-element.217), channel_id=1, source_target_pairs={{0,1},{1,0},{2,3},{3,2},{4,5},{5,4},{6,7},{7,6},{8,9},{9,8},{10,11... | collective-permute-start | bytes 442376 | tf_op jit(solution)/shard_map/ppermute | solution.py:23
  127.0 61.8 %collective-permute-start.17 = (bf16[2,256,1152]{2,1,0:T(8,128)(2,1)}, bf16[2,256,1152]{2,1,0:T(8,128)(2,1)}, u32[]{:S(2)}, u32[]{:S(2)}) collective-permute-start(bf16[2,256,1152]{2,1,0:T(8,128)(2,1)} %refs_3_.3), channel_id=1, source_target_pairs={{0,1},{1,0},{2,3},{3,2},{4,5},{5,4},{6,7},{7,6},{8,9},{9,8},{10,11... | collective-permute-start | bytes 3538952 | tf_op jit(solution)/shard_map/ppermute | solution.py:23
  152.4 16.4 %collective-permute-start.15 = (bf16[1,256,1152]{2,1,0:T(8,128)(2,1)S(1)}, bf16[1,256,1152]{2,1,0:T(8,128)(2,1)}, u32[]{:S(2)}, u32[]{:S(2)}) collective-permute-start(bf16[1,256,1152]{2,1,0:T(8,128)(2,1)S(1)} %add_convert_fusion.3.after.refs_0_), channel_id=1, source_target_pairs={{0,2},{1,3},{2,0},{3,1},{4,6},{5,7},{6,4},{7,5},{8,10},{9,11},{10,... | collective-permute-start | bytes 1769480 | tf_op jit(solution)/shard_map/ppermute | solution.py:23
  155.5 24.5 %collective-permute-start.24 = (bf16[1,256,1152]{2,1,0:T(8,128)(2,1)}, bf16[1,256,1152]{2,1,0:T(8,128)(2,1)}, u32[]{:S(2)}, u32[]{:S(2)}) collective-permute-start(bf16[1,256,1152]{2,1,0:T(8,128)(2,1)} %add_convert_fusion.2.refs_0_), channel_id=1, source_target_pairs={{0,2},{1,3},{2,0},{3,1},{4,6},{5,7},{6,4},{7,5},{8,10},{9,11},{10,... | collective-permute-start | bytes 1769480 | tf_op jit(solution)/shard_map/ppermute | solution.py:23
  156.0 32.8 %collective-permute-start.14 = (bf16[1,256,1152]{2,1,0:T(8,128)(2,1)S(1)}, bf16[1,256,1152]{2,1,0:T(8,128)(2,1)}, u32[]{:S(2)}, u32[]{:S(2)}) collective-permute-start(bf16[1,256,1152]{2,1,0:T(8,128)(2,1)S(1)} %add_convert_fusion.3.after.refs_0_), channel_id=1, source_target_pairs={{0,1},{1,0},{2,3},{3,2},{4,5},{5,4},{6,7},{7,6},{8,9},{9,8},{10,11... | collective-permute-start | bytes 1769480 | tf_op jit(solution)/shard_map/ppermute | solution.py:23
  168.8 20.0 %collective-permute-start.16 = (bf16[1,256,1152]{2,1,0:T(8,128)(2,1)}, bf16[1,256,1152]{2,1,0:T(8,128)(2,1)}, u32[]{:S(2)}, u32[]{:S(2)}) collective-permute-start(bf16[1,256,1152]{2,1,0:T(8,128)(2,1)} %collective-permute-done.15.refs_2_), channel_id=1, source_target_pairs={{0,1},{1,0},{2,3},{3,2},{4,5},{5,4},{6,7},{7,6},{8,9},{9,8},{10,11... | collective-permute-start | bytes 1769480 | tf_op jit(solution)/shard_map/ppermute | solution.py:23
  168.8 39.6 %collective-permute-start.23 = (bf16[1,256,1152]{2,1,0:T(8,128)(2,1)}, bf16[1,256,1152]{2,1,0:T(8,128)(2,1)}, u32[]{:S(2)}, u32[]{:S(2)}) collective-permute-start(bf16[1,256,1152]{2,1,0:T(8,128)(2,1)} %add_convert_fusion.2.refs_0_), channel_id=1, source_target_pairs={{0,1},{1,0},{2,3},{3,2},{4,5},{5,4},{6,7},{7,6},{8,9},{9,8},{10,11... | collective-permute-start | bytes 1769480 | tf_op jit(solution)/shard_map/ppermute | solution.py:23
  180.1 28.3 %collective-permute-start.25 = (bf16[1,256,1152]{2,1,0:T(8,128)(2,1)}, bf16[1,256,1152]{2,1,0:T(8,128)(2,1)}, u32[]{:S(2)}, u32[]{:S(2)}) collective-permute-start(bf16[1,256,1152]{2,1,0:T(8,128)(2,1)} %collective-permute-done.24.refs_2_), channel_id=1, source_target_pairs={{0,1},{1,0},{2,3},{3,2},{4,5},{5,4},{6,7},{7,6},{8,9},{9,8},{10,11... | collective-permute-start | bytes 1769480 | tf_op jit(solution)/shard_map/ppermute | solution.py:23
  207.9 89.2 %collective-permute-start.35 = (bf16[1,256,1152]{2,1,0:T(8,128)(2,1)}, bf16[1,256,1152]{2,1,0:T(8,128)(2,1)}, u32[]{:S(2)}, u32[]{:S(2)}) collective-permute-start(bf16[1,256,1152]{2,1,0:T(8,128)(2,1)} %get-tuple-element.188), channel_id=1, source_target_pairs={{0,1},{1,0},{2,3},{3,2},{4,5},{5,4},{6,7},{7,6},{8,9},{9,8},{10,11... | collective-permute-start | bytes 1769480 | tf_op jit(solution)/shard_map/ppermute | solution.py:23
  208.4 50.2 %collective-permute-start.36 = (bf16[1,256,1152]{2,1,0:T(8,128)(2,1)}, bf16[1,256,1152]{2,1,0:T(8,128)(2,1)}, u32[]{:S(2)}, u32[]{:S(2)}) collective-permute-start(bf16[1,256,1152]{2,1,0:T(8,128)(2,1)} %get-tuple-element.189), channel_id=1, source_target_pairs={{0,1},{1,0},{2,3},{3,2},{4,5},{5,4},{6,7},{7,6},{8,9},{9,8},{10,11... | collective-permute-start | bytes 1769480 | tf_op jit(solution)/shard_map/ppermute | solution.py:23
  227.7 33.8 %collective-permute-start.26 = (bf16[1,256,1152]{2,1,0:T(8,128)(2,1)}, bf16[1,256,1152]{2,1,0:T(8,128)(2,1)}, u32[]{:S(2)}, u32[]{:S(2)}) collective-permute-start(bf16[1,256,1152]{2,1,0:T(8,128)(2,1)} %get-tuple-element.194), channel_id=1, source_target_pairs={{0,1},{1,0},{2,3},{3,2},{4,5},{5,4},{6,7},{7,6},{8,9},{9,8},{10,11... | collective-permute-start | bytes 1769480 | tf_op jit(solution)/shard_map/ppermute | solution.py:23
  228.2 26.6 %collective-permute-start.27 = (bf16[1,256,1152]{2,1,0:T(8,128)(2,1)}, bf16[1,256,1152]{2,1,0:T(8,128)(2,1)S(1)}, u32[]{:S(2)}, u32[]{:S(2)}) collective-permute-start(bf16[1,256,1152]{2,1,0:T(8,128)(2,1)} %get-tuple-element.195), channel_id=1, source_target_pairs={{0,1},{1,0},{2,3},{3,2},{4,5},{5,4},{6,7},{7,6},{8,9},{9,8},{10,11... | collective-permute-start | bytes 1769480 | tf_op jit(solution)/shard_map/ppermute | solution.py:23
  254.7 249.4 %reduce-scatter.5.cloned.1.call-start = ((), (), s32[]{:S(2)}) async-start(), calls=%async_computation.9 | async-start | bytes 3981312 | tf_op jit(solution)/shard_map/reduce_scatter | solution.py:724
  256.8 16.4 %collective-permute-start.28 = (bf16[1,256,1152]{2,1,0:T(8,128)(2,1)}, bf16[1,256,1152]{2,1,0:T(8,128)(2,1)}, u32[]{:S(2)}, u32[]{:S(2)}) collective-permute-start(bf16[1,256,1152]{2,1,0:T(8,128)(2,1)} %fusion.40), channel_id=1, source_target_pairs={{0,2},{1,3},{2,0},{3,1},{4,6},{5,7},{6,4},{7,5},{8,10},{9,11},{10,... | collective-permute-start | bytes 1769480 | tf_op jit(solution)/shard_map/ppermute | solution.py:23
  259.9 37.2 %collective-permute-start.37 = (bf16[1,256,1152]{2,1,0:T(8,128)(2,1)S(1)}, bf16[1,256,1152]{2,1,0:T(8,128)(2,1)}, u32[]{:S(2)}, u32[]{:S(2)}) collective-permute-start(bf16[1,256,1152]{2,1,0:T(8,128)(2,1)S(1)} %fusion.34), channel_id=1, source_target_pairs={{0,2},{1,3},{2,0},{3,1},{4,6},{5,7},{6,4},{7,5},{8,10},{9,11},{10,... | collective-permute-start | bytes 1769480 | tf_op jit(solution)/shard_map/ppermute | solution.py:23
  306.6 18.0 %collective-permute-start.38 = (bf16[1,256,288]{2,1,0:T(8,128)(2,1)}, bf16[1,256,288]{2,1,0:T(8,128)(2,1)S(1)}, u32[]{:S(2)}, u32[]{:S(2)}) collective-permute-start(bf16[1,256,288]{2,1,0:T(8,128)(2,1)} %get-tuple-element.80), channel_id=1, source_target_pairs={{0,1},{1,0},{2,3},{3,2},{4,5},{5,4},{6,7},{7,6},{8,9},{9,8},{10,11... | collective-permute-start | bytes 442376 | tf_op jit(solution)/shard_map/ppermute | solution.py:23
  306.7 17.9 %collective-permute-start.39 = (bf16[1,256,288]{2,1,0:T(8,128)(2,1)}, bf16[1,256,288]{2,1,0:T(8,128)(2,1)S(1)}, u32[]{:S(2)}, u32[]{:S(2)}) collective-permute-start(bf16[1,256,288]{2,1,0:T(8,128)(2,1)} %get-tuple-element.81), channel_id=1, source_target_pairs={{0,2},{1,3},{2,0},{3,1},{4,6},{5,7},{6,4},{7,5},{8,10},{9,11},{10,... | collective-permute-start | bytes 442376 | tf_op jit(solution)/shard_map/ppermute | solution.py:23
  308.6 16.4 %collective-permute-start.40 = (bf16[1,256,288]{2,1,0:T(8,128)(2,1)}, bf16[1,256,288]{2,1,0:T(8,128)(2,1)S(1)}, u32[]{:S(2)}, u32[]{:S(2)}) collective-permute-start(bf16[1,256,288]{2,1,0:T(8,128)(2,1)} %get-tuple-element.82), channel_id=1, source_target_pairs={{0,3},{1,2},{2,1},{3,0},{4,7},{5,6},{6,5},{7,4},{8,11},{9,10},{10,... | collective-permute-start | bytes 442376 | tf_op jit(solution)/shard_map/ppermute | solution.py:23
  308.7 38.0 %collective-permute-start.44 = (bf16[1,256,288]{2,1,0:T(8,128)(2,1)}, bf16[1,256,288]{2,1,0:T(8,128)(2,1)S(1)}, u32[]{:S(2)}, u32[]{:S(2)}) collective-permute-start(bf16[1,256,288]{2,1,0:T(8,128)(2,1)} %get-tuple-element.85), channel_id=1, source_target_pairs={{0,1},{1,0},{2,3},{3,2},{4,5},{5,4},{6,7},{7,6},{8,9},{9,8},{10,11... | collective-permute-start | bytes 442376 | tf_op jit(solution)/shard_map/ppermute | solution.py:23
  308.9 38.0 %collective-permute-start.45 = (bf16[1,256,288]{2,1,0:T(8,128)(2,1)}, bf16[1,256,288]{2,1,0:T(8,128)(2,1)}, u32[]{:S(2)}, u32[]{:S(2)}) collective-permute-start(bf16[1,256,288]{2,1,0:T(8,128)(2,1)} %get-tuple-element.86), channel_id=1, source_target_pairs={{0,2},{1,3},{2,0},{3,1},{4,6},{5,7},{6,4},{7,5},{8,10},{9,11},{10,... | collective-permute-start | bytes 442376 | tf_op jit(solution)/shard_map/ppermute | solution.py:23
  324.6 22.5 %collective-permute-start.46 = (bf16[1,256,288]{2,1,0:T(8,128)(2,1)}, bf16[1,256,288]{2,1,0:T(8,128)(2,1)}, u32[]{:S(2)}, u32[]{:S(2)}) collective-permute-start(bf16[1,256,288]{2,1,0:T(8,128)(2,1)} %get-tuple-element.87), channel_id=1, source_target_pairs={{0,3},{1,2},{2,1},{3,0},{4,7},{5,6},{6,5},{7,4},{8,11},{9,10},{10,... | collective-permute-start | bytes 442376 | tf_op jit(solution)/shard_map/ppermute | solution.py:23
  324.6 63.8 %collective-permute-start.29 = (bf16[1,256,1152]{2,1,0:T(8,128)(2,1)}, bf16[1,256,1152]{2,1,0:T(8,128)(2,1)}, u32[]{:S(2)}, u32[]{:S(2)}) collective-permute-start(bf16[1,256,1152]{2,1,0:T(8,128)(2,1)} %get-tuple-element.190), channel_id=1, source_target_pairs={{0,1},{1,0},{2,3},{3,2},{4,5},{5,4},{6,7},{7,6},{8,9},{9,8},{10,11... | collective-permute-start | bytes 1769480 | tf_op jit(solution)/shard_map/ppermute | solution.py:23
  325.0 24.5 %collective-permute-start.30 = (bf16[1,256,1152]{2,1,0:T(8,128)(2,1)S(1)}, bf16[1,256,1152]{2,1,0:T(8,128)(2,1)S(1)}, u32[]{:S(2)}, u32[]{:S(2)}) collective-permute-start(bf16[1,256,1152]{2,1,0:T(8,128)(2,1)S(1)} %get-tuple-element.191), channel_id=1, source_target_pairs={{0,1},{1,0},{2,3},{3,2},{4,5},{5,4},{6,7},{7,6},{8,9},{9,8},{10,11... | collective-permute-start | bytes 1769480 | tf_op jit(solution)/shard_map/ppermute | solution.py:23
  346.6 44.5 %collective-permute-start.32 = (bf16[1,256,1152]{2,1,0:T(8,128)(2,1)}, bf16[1,256,1152]{2,1,0:T(8,128)(2,1)}, u32[]{:S(2)}, u32[]{:S(2)}) collective-permute-start(bf16[1,256,1152]{2,1,0:T(8,128)(2,1)} %get-tuple-element.192), channel_id=1, source_target_pairs={{0,1},{1,0},{2,3},{3,2},{4,5},{5,4},{6,7},{7,6},{8,9},{9,8},{10,11... | collective-permute-start | bytes 1769480 | tf_op jit(solution)/shard_map/ppermute | solution.py:23
  346.9 6.4 %collective-permute-start.33 = (bf16[1,256,1152]{2,1,0:T(8,128)(2,1)S(1)}, bf16[1,256,1152]{2,1,0:T(8,128)(2,1)S(1)}, u32[]{:S(2)}, u32[]{:S(2)}) collective-permute-start(bf16[1,256,1152]{2,1,0:T(8,128)(2,1)S(1)} %get-tuple-element.193), channel_id=1, source_target_pairs={{0,1},{1,0},{2,3},{3,2},{4,5},{5,4},{6,7},{7,6},{8,9},{9,8},{10,11... | collective-permute-start | bytes 1769480 | tf_op jit(solution)/shard_map/ppermute | solution.py:23
  347.1 41.3 %collective-permute-start.42 = (bf16[1,256,1152]{2,1,0:T(8,128)(2,1)}, bf16[1,256,1152]{2,1,0:T(8,128)(2,1)}, u32[]{:S(2)}, u32[]{:S(2)}) collective-permute-start(bf16[1,256,1152]{2,1,0:T(8,128)(2,1)} %get-tuple-element.187), channel_id=1, source_target_pairs={{0,1},{1,0},{2,3},{3,2},{4,5},{5,4},{6,7},{7,6},{8,9},{9,8},{10,11... | collective-permute-start | bytes 1769480 | tf_op jit(solution)/shard_map/ppermute | solution.py:23
  351.5 39.7 %collective-permute-start.31 = (bf16[1,256,1152]{2,1,0:T(8,128)(2,1)}, bf16[1,256,1152]{2,1,0:T(8,128)(2,1)}, u32[]{:S(2)}, u32[]{:S(2)}) collective-permute-start(bf16[1,256,1152]{2,1,0:T(8,128)(2,1)} %fusion.38.refs_1_), channel_id=1, source_target_pairs={{0,2},{1,3},{2,0},{3,1},{4,6},{5,7},{6,4},{7,5},{8,10},{9,11},{10,... | collective-permute-start | bytes 1769480 | tf_op jit(solution)/shard_map/ppermute | solution.py:23
  355.4 36.3 %collective-permute-start.34 = (bf16[1,256,1152]{2,1,0:T(8,128)(2,1)}, bf16[1,256,1152]{2,1,0:T(8,128)(2,1)}, u32[]{:S(2)}, u32[]{:S(2)}) collective-permute-start(bf16[1,256,1152]{2,1,0:T(8,128)(2,1)} %fusion.36.refs_2_), channel_id=1, source_target_pairs={{0,2},{1,3},{2,0},{3,1},{4,6},{5,7},{6,4},{7,5},{8,10},{9,11},{10,... | collective-permute-start | bytes 1769480 | tf_op jit(solution)/shard_map/ppermute | solution.py:23
  388.4 11.0 %collective-permute-start.50 = (bf16[8,72,1152]{2,1,0:T(8,128)(2,1)}, bf16[8,72,1152]{2,1,0:T(8,128)(2,1)S(1)}, u32[]{:S(2)}, u32[]{:S(2)}) collective-permute-start(bf16[8,72,1152]{2,1,0:T(8,128)(2,1)} %dynamic-slice_bitcast_fusion), channel_id=1, source_target_pairs={{0,1},{1,0},{2,3},{3,2},{4,5},{5,4},{6,7},{7,6},{8,9},{9,8},{10,11... | collective-permute-start | bytes 3981320 | tf_op jit(solution)/shard_map/ppermute | solution.py:23
  388.4 9.4 %collective-permute-start.48 = (bf16[1,256,1152]{2,1,0:T(8,128)(2,1)}, bf16[1,256,1152]{2,1,0:T(8,128)(2,1)S(1)}, u32[]{:S(2)}, u32[]{:S(2)}) collective-permute-start(bf16[1,256,1152]{2,1,0:T(8,128)(2,1)} %get-tuple-element.185), channel_id=1, source_target_pairs={{0,1},{1,0},{2,3},{3,2},{4,5},{5,4},{6,7},{7,6},{8,9},{9,8},{10,11... | collective-permute-start | bytes 1769480 | tf_op jit(solution)/shard_map/ppermute | solution.py:23
  391.1 17.1 %collective-permute-start.41 = (bf16[1,256,1152]{2,1,0:T(8,128)(2,1)}, bf16[1,256,1152]{2,1,0:T(8,128)(2,1)}, u32[]{:S(2)}, u32[]{:S(2)}) collective-permute-start(bf16[1,256,1152]{2,1,0:T(8,128)(2,1)} %get-tuple-element.186), channel_id=1, source_target_pairs={{0,1},{1,0},{2,3},{3,2},{4,5},{5,4},{6,7},{7,6},{8,9},{9,8},{10,11... | collective-permute-start | bytes 1769480 | tf_op jit(solution)/shard_map/ppermute | solution.py:23
  391.2 19.7 %collective-permute-start.47 = (bf16[1,256,1152]{2,1,0:T(8,128)(2,1)}, bf16[1,256,1152]{2,1,0:T(8,128)(2,1)}, u32[]{:S(2)}, u32[]{:S(2)}) collective-permute-start(bf16[1,256,1152]{2,1,0:T(8,128)(2,1)} %get-tuple-element.184), channel_id=1, source_target_pairs={{0,1},{1,0},{2,3},{3,2},{4,5},{5,4},{6,7},{7,6},{8,9},{9,8},{10,11... | collective-permute-start | bytes 1769480 | tf_op jit(solution)/shard_map/ppermute | solution.py:23
  391.6 16.6 %collective-permute-start.43 = (bf16[1,256,1152]{2,1,0:T(8,128)(2,1)}, bf16[1,256,1152]{2,1,0:T(8,128)(2,1)}, u32[]{:S(2)}, u32[]{:S(2)}) collective-permute-start(bf16[1,256,1152]{2,1,0:T(8,128)(2,1)} %fusion.32), channel_id=1, source_target_pairs={{0,2},{1,3},{2,0},{3,1},{4,6},{5,7},{6,4},{7,5},{8,10},{9,11},{10,... | collective-permute-start | bytes 1769480 | tf_op jit(solution)/shard_map/ppermute | solution.py:23
  399.1 20.8 %collective-permute-start.49 = (bf16[1,256,1152]{2,1,0:T(8,128)(2,1)S(1)}, bf16[1,256,1152]{2,1,0:T(8,128)(2,1)S(1)}, u32[]{:S(2)}, u32[]{:S(2)}) collective-permute-start(bf16[1,256,1152]{2,1,0:T(8,128)(2,1)S(1)} %fusion.30), channel_id=1, source_target_pairs={{0,2},{1,3},{2,0},{3,1},{4,6},{5,7},{6,4},{7,5},{8,10},{9,11},{10,... | collective-permute-start | bytes 1769480 | tf_op jit(solution)/shard_map/ppermute | solution.py:23
  431.0 1.3 collective-permute-start.51
  432.3 4.3 collective-permute-start.52
  437.4 28.7 %all-to-all-start.2 = ((bf16[8,2,6912]{2,1,0:T(2,128)(2,1)}), bf16[8,2,6912]{2,1,0:T(2,128)(2,1)S(1)}, u32[]{:S(2)}, u32[]{:S(2)}) async-start(bf16[8,2,6912]{2,1,0:T(2,128)(2,1)} %broadcast_in_dim.103), calls=%async_computation.3 | async-start | bytes 442368 | tf_op jit(solution)/shard_map/all_to_all | solution.py:92
  466.1 16.2 %all-to-all-start.5 = ((bf16[4,288,288]{2,1,0:T(8,128)(2,1)}), bf16[4,288,288]{2,1,0:T(8,128)(2,1)S(1)}, u32[]{:S(2)}, u32[]{:S(2)}) async-start(bf16[4,288,288]{2,1,0:T(8,128)(2,1)} %pad_maximum_fusion.3), calls=%async_computation.7 | async-start | bytes 1769472 | tf_op jit(solution)/shard_map/all_to_all | solution.py:758
  482.3 13.1 %all-to-all-start.3 = ((f32[8,1,432]{2,1,0:T(1,128)}), f32[8,1,432]{2,1,0:T(1,128)S(1)}, u32[]{:S(2)}, u32[]{:S(2)}) async-start(f32[8,1,432]{2,1,0:T(1,128)} %all_to_all.30), calls=%async_computation.4 | async-start | bytes 32768 | tf_op jit(solution)/shard_map/all_to_all | solution.py:92
  508.9 13.0 %all-to-all-start.4 = ((bf16[4,216,288]{1,2,0:T(8,128)(2,1)}), bf16[4,216,288]{1,2,0:T(8,128)(2,1)S(1)}, u32[]{:S(2)}, u32[]{:S(2)}) async-start(bf16[4,216,288]{1,2,0:T(8,128)(2,1)} %copy.99), calls=%async_computation.6 | async-start | bytes 1179648 | tf_op jit(solution)/shard_map/all_to_all | solution.py:782
  (46 other events, 265.2 us)
Sparse Core Ops, SparseCore 0:
  10.8 63.0 all-gather.4
  76.6 86.3 all-gather.6
  254.8 118.7 reduce-scatter.2
  408.3 95.7 reduce-scatter.4

commit v7 on v6

--- a/solution.py
+++ b/solution.py
@@ -259,23 +259,26 @@
 
 def mlp_kernel(count, *refs):
     inputs, grads = refs[:count], refs[count : 2 * count]
-    gate, fc1, bias, fc2, x_all, g_all, activated, d_hidden, d_norm, d_bias = refs[2 * count :]
+    gate, fc1, bias, fc2 = refs[2 * count : 2 * count + 4]
+    x_all, g_all, activated, d_hidden, d_norm, d_bias = refs[-6:]
     chunk, width = inputs[0].shape[1:]
-    hid = fc1.shape[1]
+    hid = bias.shape[1]
+    fc1 = fc1[...].reshape(width, hid)
+    fc2 = fc2[...].reshape(hid, width)
     for j in range(count):
         x_all[0, j] = inputs[j][0]
         g_all[0, j] = (gate[0] * grads[j][0].astype(F32)).astype(BF)
     x = x_all[0].reshape(count * chunk, width)
     g = g_all[0].reshape(count * chunk, width)
-    hidden = matmul(x, fc1[...]) + bias[...]
+    hidden = matmul(x, fc1) + bias[...]
     square = hidden * hidden
     tanh = jnp.tanh(GELU_C * (hidden + GELU_A * hidden * square))
     half = 0.5 * (1.0 + tanh)
     activated[0] = (hidden * half).astype(BF).reshape(count, chunk, hid)
     slope = half + (0.5 * GELU_C) * hidden * (1.0 - tanh * tanh) * (1.0 + 3.0 * GELU_A * square)
-    d_h = (matmul_nt(g, fc2[...]) * slope).astype(BF)
+    d_h = (matmul_nt(g, fc2) * slope).astype(BF)
     d_hidden[0] = d_h.reshape(count, chunk, hid)
-    d_norm[0] = matmul_nt(d_h, fc1[...]).astype(BF).reshape(count, chunk, width)
+    d_norm[0] = matmul_nt(d_h, fc1).astype(BF).reshape(count, chunk, width)
 
     @pl.when((pl.program_id(0) == 0) & (pl.program_id(1) == 0))
     def _():
@@ -284,10 +287,15 @@
     d_bias[...] += jnp.sum(d_h.astype(F32), axis=0, keepdims=True)
 
 
-def mlp(inputs, grads, group, gate, fc1, bias, fc2):
+def stored_spec(stored):
+    array, rows, index = stored
+    return pl.BlockSpec((array.shape[0], rows, array.shape[2]), lambda i, c: (0, index, 0))
+
+
+def mlp(inputs, grads, group, gate, fc1, bias, fc2, after):
     count = len(inputs)
     per, tok, width = inputs[0].shape
-    hid = fc1.shape[1]
+    hid = bias.shape[1]
     chunk = max(16, 256 // count)
     slot = pl.BlockSpec((1, chunk, width), lambda i, c: (i, c, 0))
     late = pl.BlockSpec((1, chunk, width), lambda i, c: (group * per + i, c, 0))
@@ -305,38 +313,40 @@
         in_specs=[slot] * count
         + [late] * count
         + [pl.BlockSpec((1, 1, width), lambda i, c: (i, 0, 0))]
-        + [whole(width, hid), whole(1, hid), whole(hid, width)],
+        + [stored_spec(fc1), whole(1, hid), stored_spec(fc2)]
+        + [pl.BlockSpec(memory_space=pl.ANY)] * len(after),
         out_specs=[wide, wide, inner, inner, wide, whole(1, hid)],
         out_shape=[shape_wide, shape_wide, shape_inner, shape_inner, shape_wide]
         + [jax.ShapeDtypeStruct((1, hid), F32)],
         compiler_params=pltpu.CompilerParams(vmem_limit_bytes=VMEM_LIMIT),
         name="mlp",
-    )(*inputs, *grads, gate, fc1, bias, fc2)
+    )(*inputs, *grads, gate, fc1[0], bias, fc2[0], *after)
 
 
 def mlp_out_kernel(activated, fc2, after, out):
     count, chunk, hid = activated.shape[1:]
     rows = activated[0].reshape(count * chunk, hid)
-    out[0] = matmul(rows, fc2[...]).astype(BF).reshape(count, chunk, out.shape[3])
+    weight = fc2[...].reshape(hid, out.shape[3])
+    out[0] = matmul(rows, weight).astype(BF).reshape(count, chunk, out.shape[3])
 
 
 def mlp_out_terms(activated, fc2, after):
     per, count, tok, hid = activated.shape
-    width = fc2.shape[1]
+    width = fc2[0].shape[2]
     chunk = max(16, 256 // count)
     return pl.pallas_call(
         mlp_out_kernel,
         grid=(per, tok // chunk),
         in_specs=[
             pl.BlockSpec((1, count, chunk, hid), lambda i, c: (i, 0, c, 0)),
-            pl.BlockSpec((hid, width), lambda i, c: (0, 0)),
+            stored_spec(fc2),
             pl.BlockSpec(memory_space=pl.ANY),
         ],
         out_specs=pl.BlockSpec((1, count, chunk, width), lambda i, c: (i, 0, c, 0)),
         out_shape=jax.ShapeDtypeStruct((per, count, tok, width), BF),
         compiler_params=pltpu.CompilerParams(vmem_limit_bytes=VMEM_LIMIT),
         name="mlp_out_terms",
-    )(activated, fc2, after)
+    )(activated, fc2[0], after)
 
 
 def resid_grad_kernel(count, *refs):
@@ -425,8 +435,10 @@
 
 def pack_last_kernel(proj_terms, qkv_terms, after, out):
     half = proj_terms.shape[2] // 2
+    cols = qkv_terms.shape[2]
     folded = jnp.concatenate([proj_terms[0, :, :half], proj_terms[0, :, half:]], axis=0)
-    out[0] = jnp.concatenate([folded, qkv_terms[0].astype(F32)], axis=1).astype(BF)
+    out[0, :, :cols] = qkv_terms[0]
+    out[0, :, cols:] = folded.astype(BF)
 
 
 def pack_last(proj_terms, qkv_terms, after):
@@ -445,29 +457,6 @@
         compiler_params=pltpu.CompilerParams(vmem_limit_bytes=VMEM_LIMIT),
         name="pack_last",
     )(proj_terms, qkv_terms, after)
-
-
-def unpack_kernel(joined, after, *parts):
-    start = 0
-    for part in parts:
-        part[0] = joined[0, start : start + part.shape[1]]
-        start += part.shape[1]
-
-
-def unpack(joined, after, row_counts):
-    count, rows, width = joined.shape
-    return pl.pallas_call(
-        unpack_kernel,
-        grid=(count,),
-        in_specs=[
-            pl.BlockSpec((1, rows, width), lambda i: (i, 0, 0)),
-            pl.BlockSpec(memory_space=pl.ANY),
-        ],
-        out_specs=[pl.BlockSpec((1, n, width), lambda i: (i, 0, 0)) for n in row_counts],
-        out_shape=[jax.ShapeDtypeStruct((count, n, width), joined.dtype) for n in row_counts],
-        compiler_params=pltpu.CompilerParams(vmem_limit_bytes=VMEM_LIMIT),
-        name="unpack",
-    )(joined, after)
 
 
 def token_grad_kernel(per, d_first, e_first, d_resid, e_resid, tokens, scale, after, *outs):
@@ -594,9 +583,10 @@
     proj_mine = lax.all_gather(proj_here, "dp", axis=0)
     if together:
         joined = lax.all_gather(jnp.concatenate([fc1_here, fc2_here]), "dp", axis=0)
+        fc1, fc2 = (joined, rows, 0), (joined, hid_here, 1)
     else:
-        fc1 = lax.all_gather(fc1_here, "dp", axis=0, tiled=True)
-        fc2 = lax.all_gather(fc2_here, "dp", axis=0, tiled=True)
+        fc1 = (lax.all_gather(fc1_here, "dp", axis=0, tiled=True)[None], width, 0)
+        fc2 = (lax.all_gather(fc2_here, "dp", axis=0, tiled=True)[None], hid, 0)
 
     def part(g):
         return slice(g * per, (g + 1) * per)
@@ -606,13 +596,28 @@
         for i in range(6)
     ]
     token_values = [tokens[part(g)].astype(F32) for g in range(groups)]
+    proj_other = hop(proj_mine, "seq", 1)
+    proj = jnp.where(
+        core == 0,
+        jnp.stack([proj_mine, proj_other], axis=1),
+        jnp.stack([proj_other, proj_mine], axis=1),
+    ).reshape(seq_n, cols, width)
+
+    def by_place(blocks):
+        return jnp.concatenate(
+            [lax.dynamic_index_in_dim(blocks, seq ^ j, 0, keepdims=False) for j in range(seq_n)]
+        )
+
+    proj = by_place(proj)
+
     normed_all, packed, mixed, log_sums, attended = [], [], [], [], []
+    attn_out, resid_mid, normed_mlp, upstream = [], [], [], []
     for g in range(groups):
         normed, rows_packed = qkv_forward(tok_slots, g, per, shift_attn[g], scale_attn[g], qkv)
         normed_all.append(normed.reshape(per * seq_len, width))
         packed.append(rows_packed.reshape(per, seq_len, 3 * cols))
         out, log_sum = attention(
-            packed[g], mixed + cot_slots[-1:] if g else [], heads_here
+            packed[g], normed_mlp + cot_slots[-1:] if g else [], heads_here
         )
         mixed.append(out)
         log_sums.append(log_sum)
@@ -622,40 +627,21 @@
                 own, width
             )
         )
-
-    proj_other = hop(proj_mine, "seq", 1)
-    proj = jnp.where(
-        core == 0,
-        jnp.stack([proj_mine, proj_other], axis=1),
-        jnp.stack([proj_other, proj_mine], axis=1),
-    ).reshape(seq_n, cols, width)
-
-    def by_place(blocks):
-        return jnp.concatenate(
-            [lax.dynamic_index_in_dim(blocks, seq ^ j, 0, keepdims=False) for j in range(seq_n)]
-        )
-
-    proj = by_place(proj)
-
-    attn_out, resid_mid, normed_mlp, upstream = [], [], [], []
-    for g in range(groups):
         attn_out.append(matmul(attended[g], proj).reshape(per, tok, width))
         resid_mid.append(token_values[g] + gate_attn[g] * attn_out[g])
         normed_mlp.append(
             (ln_parts(resid_mid[g])[0] * (1.0 + scale_mlp[g]) + shift_mlp[g]).astype(BF)
         )
         upstream.append(cotangent[part(g)].astype(F32))
-    if together:
-        fc1, fc2 = unpack(joined, normed_mlp[0], [rows, hid_here])
-        fc1, fc2 = fc1.reshape(width, hid), fc2.reshape(hid, width)
 
     grad_fc1 = grad_fc2 = grad_bias1 = 0.0
-    d_norm, activated = [], []
+    d_near, activated = [], []
     for g in range(groups):
         x_all, d_mlp, active, d_hidden, terms, d_bias = mlp(
-            seq_gather(normed_mlp[g]), cot_slots, g, gate_mlp[g], fc1, fc1_bias[None], fc2
+            seq_gather(normed_mlp[g]), cot_slots, g, gate_mlp[g], fc1, fc1_bias[None], fc2,
+            [near[1] for near in d_near],
         )
-        d_norm.append(seq_reduce([terms[:, j].astype(F32) for j in range(seq_n)]))
+        d_near.append(seq_near([terms[:, j].astype(F32) for j in range(seq_n)]))
         activated.append(active)
         flat = per * seq_len
         grad_fc2 = grad_fc2 + matmul_tn(active.reshape(flat, hid), d_mlp.reshape(flat, width))
@@ -664,7 +650,7 @@
     grad_fc1 = grad_fc1.astype(BF).reshape(dp_n, rows, hid)
     grad_fc2 = grad_fc2.astype(BF).reshape(dp_n, hid_here, width)
     if together:
-        grad_fc = pack(grad_fc1, grad_fc2, grad_bias1)
+        grad_fc = pack(grad_fc1, grad_fc2, d_near[-1][1])
         sum_fc = lax.psum_scatter(grad_fc, "dp", scatter_dimension=0)
         sum_fc1, sum_fc2 = sum_fc[:rows], sum_fc[rows:]
     else:
@@ -679,8 +665,8 @@
     d_mixed = []
     for g in range(groups):
         outs = resid_grad(
-            d_norm[g], resid_mid[g], attn_out[g], cotangent, g, scale_mlp[g], gate_attn[g], proj,
-            grad_fc, seq_n,
+            seq_far(*d_near[g]), resid_mid[g], attn_out[g], cotangent, g, scale_mlp[g],
+            gate_attn[g], proj, d_attended[0] if g else grad_fc, seq_n,
         )
         d_resid.append(outs[0])
         d_attn.append(outs[1].reshape(own, width))
@@ -722,7 +708,7 @@
     grad_qkv = matmul_tn(stacked(normed_all), stacked(d_packed)).astype(BF)
     last = pack_last(proj_terms, grad_qkv.reshape(dp_n, rows, 3 * cols), sum_fc)
     sum_last = lax.psum_scatter(last, "dp", scatter_dimension=0)
-    sum_proj, sum_qkv = sum_last[:, : width // 2], sum_last[:, width // 2 :]
+    sum_qkv, sum_proj = sum_last[:, : 3 * cols], sum_last[:, 3 * cols :]
     grad_tokens, d_shift_attn, d_scale_attn = token_grad(
         d_first, d_resid, tokens, modulation[:, None, width : 2 * width], last
     )

time: 538 us -> 530 us (0.985)
  Pallas kernels: 162 us -> 155 us
    ppermute x53, waiting for transfers between devices: 73.6 us -> 65.6 us  [hop(): return lax.ppermute(value, axis, [(i, i ^ bits) for i in range(count)])]
    pallas_call x1 -> x0, Pallas kernels: 7.3 us -> none  [unpack(): pl.pallas_call(unpack_kernel, grid=(count,), in_specs=[pl.BlockSpec((1, r...]
  transfers between devices with their start and end apart: 63 -> 63, of which waited for: 16 -> 18; matrix products, arithmetic and copies ran while one was open for 29% -> 29% of each run, Pallas kernels for 30% -> 25%
where the time goes in v7:
time: 530 us; the launch traced here: 524 us
  Pallas kernels  155 us (29%)
  waiting for transfers between devices  103 us (19%)
  starting transfers between devices  79.6 us (15%)
  local copies, waits for them, and re-layouts  74 us (14%)
  other arithmetic  57.6 us (11%)
  matrix products  39.9 us (8%)
  between operations  14.9 us (3%)
    ppermute x53, waiting for transfers between devices, hop(): return lax.ppermute(value, axis, [(i, i ^ bits) for i in range(count)])  65.6 us
    ppermute x53, starting transfers between devices, hop(): return lax.ppermute(value, axis, [(i, i ^ bits) for i in range(count)])  39.7 us
    pallas_call x2, Pallas kernels, attention_grad(): pl.pallas_call(partial(attend_grad_kernel, heads, block), grid=(lat,), in...  36.5 us
    pallas_call x2, Pallas kernels, mlp(): pl.pallas_call(partial(mlp_kernel, count), grid=(per, tok // chunk), in_s...  33.6 us
    all_to_all x4, starting transfers between devices, dp_exchange(): return lax.all_to_all(value, 'dp', 0, 0, tiled=True)  32 us
    dot_general x7, matrix products, matmul_tn(): lax.dot_general(left, right, (((0,), (0,)), ((), ())), preferred_element_...  31.3 us
    pallas_call x2, Pallas kernels, attention(): pl.pallas_call(partial(attend_kernel, heads, block), grid=(lat,), in_spec...  17.6 us
    pallas_call x2, Pallas kernels, qkv_forward(): pl.pallas_call(partial(qkv_kernel, count), grid=(per, tok // chunk), in_s...  16.1 us
  transfers between devices with their start and end apart: 63, of which 18 were waited for; matrix products, arithmetic and copies ran while one was open for 29% of the time, Pallas kernels for 25%

profile of v7, /device:TPU:0, one launch (start us, length us, event | category | flops | bytes accessed | tf_op | source)
XLA Modules:
  0.0 524.1 jit_solution(9185228681107262113)
XLA Ops:
  12.8 3.0 collective-permute-start.1
  18.9 5.8 %all-to-all-start = ((bf16[8,2,1224]{2,1,0:T(2,128)(2,1)}), bf16[8,2,1224]{2,1,0:T(2,128)(2,1)S(1)}, u32[]{:S(2)}, u32[]{:S(2)}) async-start(bf16[8,2,1224]{2,1,0:T(2,128)(2,1)} %reshape.536), calls=%async_computation | async-start | bytes 81920 | tf_op jit(solution)/shard_map/all_to_all | solution.py:92
  28.3 3.0 collective-permute-start.6
  39.9 4.1 all-to-all-start.1
  44.6 3.7 collective-permute-start.8
  53.7 13.8 %collective-permute-done.8 = bf16[144,864]{1,0:T(8,128)(2,1)} collective-permute-done((bf16[144,864]{1,0:T(8,128)(2,1)}, bf16[144,864]{1,0:T(8,128)(2,1)}, u32[]{:S(2)}, u32[]{:S(2)}) %collective-permute-start.8) | collective-permute-done | bytes 248864 | tf_op jit(solution)/shard_map/ppermute | solution.py:23
  67.5 3.7 collective-permute-start.7
  72.8 4.0 collective-permute-done.7
  83.7 8.1 %qkv_forward.2 = (bf16[1,4,256,1152]{3,2,1,0:T(8,128)(2,1)}, bf16[1,4,256,864]{3,2,1,0:T(8,128)(2,1)}) custom-call(bf16[2,256,1152]{2,1,0:T(8,128)(2,1)} %tokens.1, bf16[2,256,1152]{2,1,0:T(8,128)(2,1)} %collective-permute-done.refs_1_, bf16[2,256,1152]{2,1,0:T(8,128)(2,1)} %collective-permute-done.1.refs_2_, ...), custom_call_target="tpu_custom_call" | custom-call | tf_op jit(solution)/shard_map/qkv_forward/pallas_call | solution.py:242
  91.8 8.8 %attend.2 = (bf16[1,1024,288]{2,1,0:T(8,128)(2,1)}, f32[1,4,1024]{2,1,0:T(4,128)}) custom-call(bf16[1,1024,864]{2,1,0:T(8,128)(2,1)} %bitcast.292), custom_call_target="tpu_custom_call" | custom-call | tf_op jit(solution)/shard_map/attend/pallas_call | solution.py:186
  102.6 2.1 collective-permute-start.11
  104.7 8.0 %qkv_forward.3 = (bf16[1,4,256,1152]{3,2,1,0:T(8,128)(2,1)}, bf16[1,4,256,864]{3,2,1,0:T(8,128)(2,1)}) custom-call(bf16[2,256,1152]{2,1,0:T(8,128)(2,1)} %tokens.1, bf16[2,256,1152]{2,1,0:T(8,128)(2,1)} %collective-permute-done.refs_1_, bf16[2,256,1152]{2,1,0:T(8,128)(2,1)} %collective-permute-done.1.refs_2_, ...), custom_call_target="tpu_custom_call" | custom-call | tf_op jit(solution)/shard_map/qkv_forward/pallas_call | solution.py:242
  114.3 2.1 concatenate.71
  116.5 3.0 maximum_select_fusion
  119.9 5.0 pad_maximum_fusion.refs_6_
  124.9 3.5 fusion.54
  130.5 8.8 %attend.3 = (bf16[1,1024,288]{2,1,0:T(8,128)(2,1)}, f32[1,4,1024]{2,1,0:T(4,128)}) custom-call(bf16[1,1024,864]{2,1,0:T(8,128)(2,1)} %bitcast.294, bf16[1,256,1152]{2,1,0:T(8,128)(2,1)} %add_convert_fusion.3.refs_0_, bf16[2,256,1152]{2,1,0:T(8,128)(2,1)} %collective-permute-done.19.refs_7_.refs_1_), custom_call_target="tpu_custom_call" | custom-call | tf_op jit(solution)/shard_map/attend/pallas_call | solution.py:186
  145.1 3.8 collective-permute-done.22
  148.9 3.7 collective-permute-done.21
  152.6 2.3 concatenate.75
  155.0 4.1 fusion.53
  159.3 6.0 %collective-permute-done.15.refs_2_ = bf16[1,256,1152]{2,1,0:T(8,128)(2,1)} collective-permute-done((bf16[1,256,1152]{2,1,0:T(8,128)(2,1)}, bf16[1,256,1152]{2,1,0:T(8,128)(2,1)}, u32[]{:S(2)}, u32[]{:S(2)}) %collective-permute-start.15) | collective-permute-done | bytes 589856 | tf_op jit(solution)/shard_map/ppermute | solution.py:23
  167.6 16.6 %mlp.2 = (bf16[1,4,256,1152]{3,2,1,0:T(8,128)(2,1)}, bf16[1,4,256,1152]{3,2,1,0:T(8,128)(2,1)}, bf16[1,4,256,1152]{3,2,1,0:T(8,128)(2,1)}, bf16[1,4,256,1152]{3,...) custom-call(bf16[1,256,1152]{2,1,0:T(8,128)(2,1)} %add_convert_fusion.3.refs_0_, ...), custom_call_target="tpu_custom_call" | custom-call | tf_op jit(solution)/shard_map/mlp/pallas_call | solution.py:310
  184.3 2.2 slice_bitcast_fusion.16
  188.4 2.1 fusion.41.refs_12_
  191.5 17.0 %mlp.3 = (bf16[1,4,256,1152]{3,2,1,0:T(8,128)(2,1)}, bf16[1,4,256,1152]{3,2,1,0:T(8,128)(2,1)}, bf16[1,4,256,1152]{3,2,1,0:T(8,128)(2,1)}, bf16[1,4,256,1152]{3,...) custom-call(bf16[1,256,1152]{2,1,0:T(8,128)(2,1)} %add_convert_fusion.2.refs_0_, ...), custom_call_target="tpu_custom_call" | custom-call | tf_op jit(solution)/shard_map/mlp/pallas_call | solution.py:310
  208.5 2.3 slice_bitcast_fusion.18
  211.0 5.1 convolution_bitcast_fusion.2
  216.1 3.3 convolution_bitcast_fusion
  219.5 4.9 fusion.2
  224.4 5.1 fusion.3
  231.6 7.2 %pack.1.refs_7_ = bf16[8,288,1152]{2,1,0:T(8,128)(2,1)} custom-call(bf16[8,144,1152]{2,1,0:T(8,128)(2,1)} %bitcast.304, bf16[8,144,1152]{2,1,0:T(8,128)(2,1)} %bitcast.305, bf16[1,256,1152]{2,1,0:T(8,128)(2,1)} %fusion.39.after), custom_call_target="tpu_custom_call" | custom-call | tf_op jit(solution)/shard_map/pack/pallas_call | solution.py:421
  242.0 14.1 %collective-permute-done.31 = bf16[1,256,1152]{2,1,0:T(8,128)(2,1)} collective-permute-done((bf16[1,256,1152]{2,1,0:T(8,128)(2,1)S(1)}, bf16[1,256,1152]{2,1,0:T(8,128)(2,1)}, u32[]{:S(2)}, u32[]{:S(2)}) %collective-permute-start.31) | collective-permute-done | bytes 589856 | tf_op jit(solution)/shard_map/ppermute | solution.py:23
  256.1 2.6 fusion.38.refs_0_
  258.7 7.1 %resid_grad.2 = (f32[1,256,1152]{2,1,0:T(8,128)}, bf16[1,256,1152]{2,1,0:T(8,128)(2,1)}, f32[1,1,1152]{2,1,0:T(1,128)}, f32[1,1,1152]{2,1,0:T(1,128)}, f32[1,1,1...) custom-call(f32[1,256,1152]{2,1,0:T(8,128)} %fusion.38.refs_0_, ...), custom_call_target="tpu_custom_call" | custom-call | tf_op jit(solution)/shard_map/resid_grad/pallas_call | solution.py:385
  269.1 4.8 collective-permute-done.39
  273.9 3.3 collective-permute-done.40
  279.2 2.6 fusion.40.refs_0_
  281.8 6.7 %resid_grad.3 = (f32[1,256,1152]{2,1,0:T(8,128)}, bf16[1,256,1152]{2,1,0:T(8,128)(2,1)}, f32[1,1,1152]{2,1,0:T(1,128)}, f32[1,1,1152]{2,1,0:T(1,128)}, f32[1,1,1...) custom-call(f32[1,256,1152]{2,1,0:T(8,128)} %fusion.40.refs_0_, ...), custom_call_target="tpu_custom_call" | custom-call | tf_op jit(solution)/shard_map/resid_grad/pallas_call | solution.py:385
  288.5 7.2 %mlp_out_terms.3.refs_2_ = bf16[1,4,256,1152]{3,2,1,0:T(8,128)(2,1)} custom-call(bf16[1,4,256,1152]{3,2,1,0:T(8,128)(2,1)} %get-tuple-element.69.activated, bf16[8,288,1152]{2,1,0:T(8,128)(2,1)} %bitcast.283, bf16[1,256,288]{2,1,0:T(8,128)(2,1)} %get-tuple-element.72.after.refs_0_), custom_call_target="tpu_custom_call" | custom-call | tf_op jit(solution)/shard_map/mlp_out_terms/pallas_call | solution.py:337
  295.7 7.2 %mlp_out_terms.2.refs_1_ = bf16[1,4,256,1152]{3,2,1,0:T(8,128)(2,1)} custom-call(bf16[1,4,256,1152]{3,2,1,0:T(8,128)(2,1)} %get-tuple-element.59.activated, bf16[8,288,1152]{2,1,0:T(8,128)(2,1)} %bitcast.284, bf16[1,256,288]{2,1,0:T(8,128)(2,1)} %get-tuple-element.72.after.refs_0_), custom_call_target="tpu_custom_call" | custom-call | tf_op jit(solution)/shard_map/mlp_out_terms/pallas_call | solution.py:337
  305.1 18.4 %attend_grad.2 = (bf16[1,1024,864]{2,1,0:T(8,128)(2,1)}, bf16[1,1024,1152]{2,1,0:T(8,128)(2,1)}) custom-call(bf16[1,1024,864]{2,1,0:T(8,128)(2,1)} %bitcast.293, bf16[1,1024,288]{2,1,0:T(8,128)(2,1)} %get-tuple-element.58.mixed, f32[1,4,1024]{2,1,0:T(4,128)} %get-tuple-element.73.log_sum, bf16[1,1024,288]{2,1,0:T(8,128)(2,1)} %pad_maximum_fusion.4.d_mixed, ...), custom_call_target="tpu_custom_call" | custom-call | tf_op jit(solution)/shard_map/attend_grad/pallas_call | solution.py:204
  323.5 2.3 slice_bitcast_fusion.6
  331.8 4.8 pad_maximum_fusion.1
  344.8 18.1 %attend_grad.3 = (bf16[1,1024,864]{2,1,0:T(8,128)(2,1)}, bf16[1,1024,1152]{2,1,0:T(8,128)(2,1)}) custom-call(bf16[1,1024,864]{2,1,0:T(8,128)(2,1)} %bitcast.295, bf16[1,1024,288]{2,1,0:T(8,128)(2,1)} %get-tuple-element.61.mixed, f32[1,4,1024]{2,1,0:T(4,128)} %get-tuple-element.78.log_sum, bf16[1,1024,288]{2,1,0:T(8,128)(2,1)} %pad_maximum_fusion.5.d_mixed, ...), custom_call_target="tpu_custom_call" | custom-call | tf_op jit(solution)/shard_map/attend_grad/pallas_call | solution.py:204
  362.9 9.7 %fusion.11 = bf16[1152,864]{0,1:T(8,128)(2,1)} fusion(bf16[1024,864]{1,0:T(8,128)(2,1)} %bitcast.331, bf16[1024,864]{1,0:T(8,128)(2,1)} %bitcast.330, bf16[1024,1152]{1,0:T(8,128)(2,1)} %bitcast.329, bf16[1024,1152]{1,0:T(8,128)(2,1)} %bitcast.328), kind=kOutput, calls=%fused_computation.16 | convolution fusion | flops 4094373888 | bytes 10248192 | tf_op jit(solution)/shard_map/dot_general | solution.py:35
  376.6 4.2 copy.96
  382.3 4.8 multiply_reduce_fusion.1
  389.6 3.2 convert_add_fusion.proj_terms
  392.8 7.1 %pack_last.1.after = bf16[8,144,1440]{2,1,0:T(8,128)(2,1)} custom-call(f32[8,72,1152]{2,1,0:T(8,128)} %convert_add_fusion.proj_terms, bf16[8,144,864]{2,1,0:T(8,128)(2,1)} %bitcast.291, bf16[288,1152]{1,0:T(8,128)(2,1)} %bitcast.302), custom_call_target="tpu_custom_call" | custom-call | tf_op jit(solution)/shard_map/pack_last/pallas_call | solution.py:447
  399.9 2.6 fusion.33.d_first
  402.5 6.9 %collective-permute-done.49 = bf16[1,256,1152]{2,1,0:T(8,128)(2,1)S(1)} collective-permute-done((bf16[1,256,1152]{2,1,0:T(8,128)(2,1)S(1)}, bf16[1,256,1152]{2,1,0:T(8,128)(2,1)S(1)}, u32[]{:S(2)}, u32[]{:S(2)}) %collective-permute-start.49) | collective-permute-done | bytes 589856 | tf_op jit(solution)/shard_map/ppermute | solution.py:23
  409.4 2.6 fusion.31.e_first
  412.0 6.7 %token_grad.1 = (f32[2,256,1152]{2,1,0:T(8,128)}, f32[2,1,1152]{2,1,0:T(1,128)}, f32[2,1,1152]{2,1,0:T(1,128)}) custom-call(f32[1,256,1152]{2,1,0:T(8,128)} %fusion.33.d_first, f32[1,256,1152]{2,1,0:T(8,128)} %fusion.31.e_first, f32[1,256,1152]{2,1,0:T(8,128)} %get-tuple-element.83.d_resid, f32[1,256,1152]{2,1,0:T(8,128)} %get-tuple-element.84.e_resid, ...), custom_call_target="tpu_custom_call" | custom-call | tf_op jit(solution)/shard_map/token_grad/pallas_call | solution.py:489
  423.6 2.3 collective-permute-done.52
  426.8 18.7 %all-to-all-start.2 = ((bf16[8,2,6912]{2,1,0:T(2,128)(2,1)}), bf16[8,2,6912]{2,1,0:T(2,128)(2,1)S(1)}, u32[]{:S(2)}, u32[]{:S(2)}) async-start(bf16[8,2,6912]{2,1,0:T(2,128)(2,1)} %broadcast_in_dim.103), calls=%async_computation.3 | async-start | bytes 442368 | tf_op jit(solution)/shard_map/all_to_all | solution.py:92
  446.7 10.6 %all-to-all-done.2 = bf16[8,2,6912]{2,1,0:T(2,128)(2,1)S(1)} async-done(((bf16[8,2,6912]{2,1,0:T(2,128)(2,1)}), bf16[8,2,6912]{2,1,0:T(2,128)(2,1)S(1)}, u32[]{:S(2)}, u32[]{:S(2)}) %all-to-all-start.2) | async-done | bytes 221216 | tf_op jit(solution)/shard_map/all_to_all | solution.py:92
  457.3 3.7 all-to-all-start.5
  464.5 9.1 %all-to-all-done.5 = bf16[4,288,288]{2,1,0:T(8,128)(2,1)S(1)} async-done(((bf16[4,288,288]{2,1,0:T(8,128)(2,1)}), bf16[4,288,288]{2,1,0:T(8,128)(2,1)S(1)}, u32[]{:S(2)}, u32[]{:S(2)}) %all-to-all-start.5) | async-done | bytes 663584 | tf_op jit(solution)/shard_map/all_to_all | solution.py:744
  473.7 3.3 all-to-all-start.3
  478.4 2.4 copy.104
  487.6 8.7 %reduce-scatter.5.cloned.1.call-done = bf16[1,144,1440]{2,1,0:T(8,128)(2,1)} async-done(((bf16[8,144,1440]{2,1,0:T(8,128)(2,1)}), bf16[1,144,1440]{2,1,0:T(8,128)(2,1)}) %reduce-scatter.5.cloned.1.call-update) | async-done | bytes 414736 | tf_op jit(solution)/shard_map/reduce_scatter | solution.py:710
  501.1 3.5 all-to-all-start.4
  505.2 8.9 %all-to-all-done.4 = bf16[4,216,288]{1,2,0:T(8,128)(2,1)S(1)} async-done(((bf16[4,216,288]{1,2,0:T(8,128)(2,1)}), bf16[4,216,288]{1,2,0:T(8,128)(2,1)S(1)}, u32[]{:S(2)}, u32[]{:S(2)}) %all-to-all-start.4) | async-done | bytes 497696 | tf_op jit(solution)/shard_map/all_to_all | solution.py:768
  (310 shorter events, 114.5 us)
Async XLA Ops:
  7.2 27.8 %copy-start = (bf16[144,6912]{1,0:T(8,128)(2,1)S(1)}, bf16[144,6912]{1,0:T(8,128)(2,1)}, u32[]{:S(2)}) copy-start(bf16[144,6912]{1,0:T(8,128)(2,1)} %param.12) | copy-start | bytes 5971972
  7.2 69.6 %all-gather.5.cloned.1.call-start = ((), (), s32[]{:S(2)}) async-start(), calls=%async_computation.10 | async-start | bytes 1492992 | tf_op jit(solution)/shard_map/all_gather | solution.py:583
  9.0 158.6 %all-gather.7.cloned.1.call-start = ((), (), s32[]{:S(2)}) async-start(), calls=%async_computation.11 | async-start | bytes 5971968 | tf_op jit(solution)/shard_map/all_gather | solution.py:585
  12.8 58.4 %collective-permute-start.1 = (bf16[2,256,1152]{2,1,0:T(8,128)(2,1)}, bf16[2,256,1152]{2,1,0:T(8,128)(2,1)}, u32[]{:S(2)}, u32[]{:S(2)}) collective-permute-start(bf16[2,256,1152]{2,1,0:T(8,128)(2,1)} %tokens.1), channel_id=1, source_target_pairs={{0,2},{1,3},{2,0},{3,1},{4,6},{5,7},{6,4},{7,5},{8,10},{9,11},{10,... | collective-permute-start | bytes 3538952 | tf_op jit(solution)/shard_map/ppermute | solution.py:23
  15.9 67.8 %collective-permute-start = (bf16[2,256,1152]{2,1,0:T(8,128)(2,1)}, bf16[2,256,1152]{2,1,0:T(8,128)(2,1)}, u32[]{:S(2)}, u32[]{:S(2)}) collective-permute-start(bf16[2,256,1152]{2,1,0:T(8,128)(2,1)} %tokens.1), channel_id=1, source_target_pairs={{0,1},{1,0},{2,3},{3,2},{4,5},{5,4},{6,7},{7,6},{8,9},{9,8},{10,11... | collective-permute-start | bytes 3538952 | tf_op jit(solution)/shard_map/ppermute | solution.py:23
  18.9 15.3 %all-to-all-start = ((bf16[8,2,1224]{2,1,0:T(2,128)(2,1)}), bf16[8,2,1224]{2,1,0:T(2,128)(2,1)S(1)}, u32[]{:S(2)}, u32[]{:S(2)}) async-start(bf16[8,2,1224]{2,1,0:T(2,128)(2,1)} %reshape.536), calls=%async_computation | async-start | bytes 81920 | tf_op jit(solution)/shard_map/all_to_all | solution.py:92
  28.3 24.9 %collective-permute-start.6 = (bf16[144,864]{1,0:T(8,128)(2,1)}, bf16[144,864]{1,0:T(8,128)(2,1)S(1)}, u32[]{:S(2)}, u32[]{:S(2)}) collective-permute-start(bf16[144,864]{1,0:T(8,128)(2,1)} %get-tuple-element.169), channel_id=1, source_target_pairs={{0,16},{4,20},{8,24},{12,28},{16,0},{20,4},{24,8},{28,12},{1,17},{... | collective-permute-start | bytes 746504 | tf_op jit(solution)/shard_map/ppermute | solution.py:23
  31.3 13.3 %collective-permute-start.4 = (bf16[144,864]{1,0:T(8,128)(2,1)}, bf16[144,864]{1,0:T(8,128)(2,1)}, u32[]{:S(2)}, u32[]{:S(2)}) collective-permute-start(bf16[144,864]{1,0:T(8,128)(2,1)} %get-tuple-element.169), channel_id=1, source_target_pairs={{0,8},{4,12},{8,0},{12,4},{16,24},{20,28},{24,16},{28,20},{1,9},{5... | collective-permute-start | bytes 746504 | tf_op jit(solution)/shard_map/ppermute | solution.py:23
  32.7 15.6 %collective-permute-start.3 = (bf16[144,864]{1,0:T(8,128)(2,1)}, bf16[144,864]{1,0:T(8,128)(2,1)}, u32[]{:S(2)}, u32[]{:S(2)}) collective-permute-start(bf16[144,864]{1,0:T(8,128)(2,1)} %get-tuple-element.169), channel_id=1, source_target_pairs={{0,4},{4,0},{8,12},{12,8},{16,20},{20,16},{24,28},{28,24},{1,5},{5... | collective-permute-start | bytes 746504 | tf_op jit(solution)/shard_map/ppermute | solution.py:23
  39.9 41.9 %all-to-all-start.1 = ((f32[8,2,6912]{2,1,0:T(2,128)}), f32[8,2,6912]{2,1,0:T(2,128)}, u32[]{:S(2)}, u32[]{:S(2)}) async-start(f32[8,2,6912]{2,1,0:T(2,128)} %reshape.463), calls=%async_computation.1 | async-start | bytes 884736 | tf_op jit(solution)/shard_map/all_to_all | solution.py:92
  44.0 348.8 %reduce-scatter.3.cloned.1.call-start = ((), (), s32[]{:S(2)}) async-start(), calls=%async_computation.8 | async-start | bytes 5971968 | tf_op jit(solution)/shard_map/reduce_scatter | solution.py:654
  44.6 22.9 %collective-permute-start.8 = (bf16[144,864]{1,0:T(8,128)(2,1)}, bf16[144,864]{1,0:T(8,128)(2,1)}, u32[]{:S(2)}, u32[]{:S(2)}) collective-permute-start(bf16[144,864]{1,0:T(8,128)(2,1)} %get-tuple-element.169), channel_id=1, source_target_pairs={{0,24},{4,28},{8,16},{12,20},{16,8},{20,12},{24,0},{28,4},{1,25},{... | collective-permute-start | bytes 746504 | tf_op jit(solution)/shard_map/ppermute | solution.py:23
  48.3 22.9 %collective-permute-start.5 = (bf16[144,864]{1,0:T(8,128)(2,1)}, bf16[144,864]{1,0:T(8,128)(2,1)S(1)}, u32[]{:S(2)}, u32[]{:S(2)}) collective-permute-start(bf16[144,864]{1,0:T(8,128)(2,1)} %collective-permute-done.4), channel_id=1, source_target_pairs={{0,4},{4,0},{8,12},{12,8},{16,20},{20,16},{24,28},{28,24},{1,5},{5... | collective-permute-start | bytes 746504 | tf_op jit(solution)/shard_map/ppermute | solution.py:23
  53.2 59.5 %collective-permute-start.18 = (bf16[2,256,1152]{2,1,0:T(8,128)(2,1)S(1)}, bf16[2,256,1152]{2,1,0:T(8,128)(2,1)}, u32[]{:S(2)}, u32[]{:S(2)}) collective-permute-start(bf16[2,256,1152]{2,1,0:T(8,128)(2,1)S(1)} %copy-done.2), channel_id=1, source_target_pairs={{0,2},{1,3},{2,0},{3,1},{4,6},{5,7},{6,4},{7,5},{8,10},{9,11},{10,... | collective-permute-start | bytes 3538952 | tf_op jit(solution)/shard_map/ppermute | solution.py:23
  67.5 9.3 %collective-permute-start.7 = (bf16[144,864]{1,0:T(8,128)(2,1)S(1)}, bf16[144,864]{1,0:T(8,128)(2,1)}, u32[]{:S(2)}, u32[]{:S(2)}) collective-permute-start(bf16[144,864]{1,0:T(8,128)(2,1)S(1)} %collective-permute-done.6), channel_id=1, source_target_pairs={{0,4},{4,0},{8,12},{12,8},{16,20},{20,16},{24,28},{28,24},{1,5},{5... | collective-permute-start | bytes 746504 | tf_op jit(solution)/shard_map/ppermute | solution.py:23
  71.2 8.9 %collective-permute-start.9 = (bf16[144,864]{1,0:T(8,128)(2,1)}, bf16[144,864]{1,0:T(8,128)(2,1)}, u32[]{:S(2)}, u32[]{:S(2)}) collective-permute-start(bf16[144,864]{1,0:T(8,128)(2,1)} %collective-permute-done.8), channel_id=1, source_target_pairs={{0,4},{4,0},{8,12},{12,8},{16,20},{20,16},{24,28},{28,24},{1,5},{5... | collective-permute-start | bytes 746504 | tf_op jit(solution)/shard_map/ppermute | solution.py:23
  71.3 12.4 %collective-permute-start.2 = (bf16[2,256,1152]{2,1,0:T(8,128)(2,1)}, bf16[2,256,1152]{2,1,0:T(8,128)(2,1)}, u32[]{:S(2)}, u32[]{:S(2)}) collective-permute-start(bf16[2,256,1152]{2,1,0:T(8,128)(2,1)} %collective-permute-done.1.refs_2_), channel_id=1, source_target_pairs={{0,1},{1,0},{2,3},{3,2},{4,5},{5,4},{6,7},{7,6},{8,9},{9,8},{10,11... | collective-permute-start | bytes 3538952 | tf_op jit(solution)/shard_map/ppermute | solution.py:23
  76.8 39.7 %collective-permute-start.13 = (bf16[8,72,1152]{2,1,0:T(8,128)(2,1)}, bf16[8,72,1152]{2,1,0:T(8,128)(2,1)}, u32[]{:S(2)}, u32[]{:S(2)}) collective-permute-start(bf16[8,72,1152]{2,1,0:T(8,128)(2,1)} %bitcast.311), channel_id=1, source_target_pairs={{0,1},{1,0},{2,3},{3,2},{4,5},{5,4},{6,7},{7,6},{8,9},{9,8},{10,11... | collective-permute-start | bytes 3981320 | tf_op jit(solution)/shard_map/ppermute | solution.py:23
  102.6 10.7 %collective-permute-start.12 = (bf16[1,256,288]{2,1,0:T(8,128)(2,1)}, bf16[1,256,288]{2,1,0:T(8,128)(2,1)}, u32[]{:S(2)}, u32[]{:S(2)}) collective-permute-start(bf16[1,256,288]{2,1,0:T(8,128)(2,1)} %get-tuple-element.209), channel_id=1, source_target_pairs={{0,3},{1,2},{2,1},{3,0},{4,7},{5,6},{6,5},{7,4},{8,11},{9,10},{10,... | collective-permute-start | bytes 442376 | tf_op jit(solution)/shard_map/ppermute | solution.py:23
  102.6 11.7 %collective-permute-start.11 = (bf16[1,256,288]{2,1,0:T(8,128)(2,1)}, bf16[1,256,288]{2,1,0:T(8,128)(2,1)}, u32[]{:S(2)}, u32[]{:S(2)}) collective-permute-start(bf16[1,256,288]{2,1,0:T(8,128)(2,1)} %get-tuple-element.210), channel_id=1, source_target_pairs={{0,2},{1,3},{2,0},{3,1},{4,6},{5,7},{6,4},{7,5},{8,10},{9,11},{10,... | collective-permute-start | bytes 442376 | tf_op jit(solution)/shard_map/ppermute | solution.py:23
  104.7 9.7 %collective-permute-start.10 = (bf16[1,256,288]{2,1,0:T(8,128)(2,1)}, bf16[1,256,288]{2,1,0:T(8,128)(2,1)}, u32[]{:S(2)}, u32[]{:S(2)}) collective-permute-start(bf16[1,256,288]{2,1,0:T(8,128)(2,1)} %get-tuple-element.211), channel_id=1, source_target_pairs={{0,1},{1,0},{2,3},{3,2},{4,5},{5,4},{6,7},{7,6},{8,9},{9,8},{10,11... | collective-permute-start | bytes 442376 | tf_op jit(solution)/shard_map/ppermute | solution.py:23
  112.7 54.6 %collective-permute-start.17 = (bf16[2,256,1152]{2,1,0:T(8,128)(2,1)S(1)}, bf16[2,256,1152]{2,1,0:T(8,128)(2,1)}, u32[]{:S(2)}, u32[]{:S(2)}) collective-permute-start(bf16[2,256,1152]{2,1,0:T(8,128)(2,1)S(1)} %copy-done.2), channel_id=1, source_target_pairs={{0,1},{1,0},{2,3},{3,2},{4,5},{5,4},{6,7},{7,6},{8,9},{9,8},{10,11... | collective-permute-start | bytes 3538952 | tf_op jit(solution)/shard_map/ppermute | solution.py:23
  113.3 17.3 %collective-permute-start.19 = (bf16[2,256,1152]{2,1,0:T(8,128)(2,1)}, bf16[2,256,1152]{2,1,0:T(8,128)(2,1)}, u32[]{:S(2)}, u32[]{:S(2)}) collective-permute-start(bf16[2,256,1152]{2,1,0:T(8,128)(2,1)} %collective-permute-done.18.refs_6_), channel_id=1, source_target_pairs={{0,1},{1,0},{2,3},{3,2},{4,5},{5,4},{6,7},{7,6},{8,9},{9,8},{10,11... | collective-permute-start | bytes 3538952 | tf_op jit(solution)/shard_map/ppermute | solution.py:23
  141.4 7.5 %collective-permute-start.22 = (bf16[1,256,288]{2,1,0:T(8,128)(2,1)}, bf16[1,256,288]{2,1,0:T(8,128)(2,1)}, u32[]{:S(2)}, u32[]{:S(2)}) collective-permute-start(bf16[1,256,288]{2,1,0:T(8,128)(2,1)} %get-tuple-element.205), channel_id=1, source_target_pairs={{0,3},{1,2},{2,1},{3,0},{4,7},{5,6},{6,5},{7,4},{8,11},{9,10},{10,... | collective-permute-start | bytes 442376 | tf_op jit(solution)/shard_map/ppermute | solution.py:23
  141.4 11.3 %collective-permute-start.21 = (bf16[1,256,288]{2,1,0:T(8,128)(2,1)}, bf16[1,256,288]{2,1,0:T(8,128)(2,1)}, u32[]{:S(2)}, u32[]{:S(2)}) collective-permute-start(bf16[1,256,288]{2,1,0:T(8,128)(2,1)} %get-tuple-element.206), channel_id=1, source_target_pairs={{0,2},{1,3},{2,0},{3,1},{4,6},{5,7},{6,4},{7,5},{8,10},{9,11},{10,... | collective-permute-start | bytes 442376 | tf_op jit(solution)/shard_map/ppermute | solution.py:23
  142.6 10.0 %collective-permute-start.20 = (bf16[1,256,288]{2,1,0:T(8,128)(2,1)}, bf16[1,256,288]{2,1,0:T(8,128)(2,1)}, u32[]{:S(2)}, u32[]{:S(2)}) collective-permute-start(bf16[1,256,288]{2,1,0:T(8,128)(2,1)} %get-tuple-element.207), channel_id=1, source_target_pairs={{0,1},{1,0},{2,3},{3,2},{4,5},{5,4},{6,7},{7,6},{8,9},{9,8},{10,11... | collective-permute-start | bytes 442376 | tf_op jit(solution)/shard_map/ppermute | solution.py:23
  144.6 20.7 %collective-permute-start.15 = (bf16[1,256,1152]{2,1,0:T(8,128)(2,1)}, bf16[1,256,1152]{2,1,0:T(8,128)(2,1)}, u32[]{:S(2)}, u32[]{:S(2)}) collective-permute-start(bf16[1,256,1152]{2,1,0:T(8,128)(2,1)} %add_convert_fusion.3.refs_0_), channel_id=1, source_target_pairs={{0,2},{1,3},{2,0},{3,1},{4,6},{5,7},{6,4},{7,5},{8,10},{9,11},{10,... | collective-permute-start | bytes 1769480 | tf_op jit(solution)/shard_map/ppermute | solution.py:23
  148.9 18.5 %collective-permute-start.14 = (bf16[1,256,1152]{2,1,0:T(8,128)(2,1)}, bf16[1,256,1152]{2,1,0:T(8,128)(2,1)}, u32[]{:S(2)}, u32[]{:S(2)}) collective-permute-start(bf16[1,256,1152]{2,1,0:T(8,128)(2,1)} %add_convert_fusion.3.refs_0_), channel_id=1, source_target_pairs={{0,1},{1,0},{2,3},{3,2},{4,5},{5,4},{6,7},{7,6},{8,9},{9,8},{10,11... | collective-permute-start | bytes 1769480 | tf_op jit(solution)/shard_map/ppermute | solution.py:23
  165.3 2.3 collective-permute-start.16
  166.5 20.4 %collective-permute-start.24 = (bf16[1,256,1152]{2,1,0:T(8,128)(2,1)}, bf16[1,256,1152]{2,1,0:T(8,128)(2,1)}, u32[]{:S(2)}, u32[]{:S(2)}) collective-permute-start(bf16[1,256,1152]{2,1,0:T(8,128)(2,1)} %add_convert_fusion.2.refs_0_), channel_id=1, source_target_pairs={{0,2},{1,3},{2,0},{3,1},{4,6},{5,7},{6,4},{7,5},{8,10},{9,11},{10,... | collective-permute-start | bytes 1769480 | tf_op jit(solution)/shard_map/ppermute | solution.py:23
  186.4 2.0 collective-permute-start.26
  186.6 3.9 collective-permute-start.23
  186.9 3.6 collective-permute-start.25
  210.8 18.7 %collective-permute-start.28 = (bf16[1,256,1152]{2,1,0:T(8,128)(2,1)S(1)}, bf16[1,256,1152]{2,1,0:T(8,128)(2,1)S(1)}, u32[]{:S(2)}, u32[]{:S(2)}) collective-permute-start(bf16[1,256,1152]{2,1,0:T(8,128)(2,1)S(1)} %get-tuple-element.191), channel_id=1, source_target_pairs={{0,1},{1,0},{2,3},{3,2},{4,5},{5,4},{6,7},{7,6},{8,9},{9,8},{10,11... | collective-permute-start | bytes 1769480 | tf_op jit(solution)/shard_map/ppermute | solution.py:23
  238.8 257.5 %reduce-scatter.5.cloned.1.call-start = ((), (), s32[]{:S(2)}) async-start(), calls=%async_computation.9 | async-start | bytes 3981312 | tf_op jit(solution)/shard_map/reduce_scatter | solution.py:710
  238.8 3.1 collective-permute-start.30
  239.8 16.3 %collective-permute-start.31 = (bf16[1,256,1152]{2,1,0:T(8,128)(2,1)S(1)}, bf16[1,256,1152]{2,1,0:T(8,128)(2,1)}, u32[]{:S(2)}, u32[]{:S(2)}) collective-permute-start(bf16[1,256,1152]{2,1,0:T(8,128)(2,1)S(1)} %copy-done.14), channel_id=1, source_target_pairs={{0,2},{1,3},{2,0},{3,1},{4,6},{5,7},{6,4},{7,5},{8,10},{9,11},{10,... | collective-permute-start | bytes 1769480 | tf_op jit(solution)/shard_map/ppermute | solution.py:23
  240.8 38.3 %collective-permute-start.27 = (bf16[1,256,1152]{2,1,0:T(8,128)(2,1)}, bf16[1,256,1152]{2,1,0:T(8,128)(2,1)}, u32[]{:S(2)}, u32[]{:S(2)}) collective-permute-start(bf16[1,256,1152]{2,1,0:T(8,128)(2,1)} %get-tuple-element.190), channel_id=1, source_target_pairs={{0,1},{1,0},{2,3},{3,2},{4,5},{5,4},{6,7},{7,6},{8,9},{9,8},{10,11... | collective-permute-start | bytes 1769480 | tf_op jit(solution)/shard_map/ppermute | solution.py:23
  240.9 38.2 %collective-permute-start.29 = (bf16[1,256,1152]{2,1,0:T(8,128)(2,1)S(1)}, bf16[1,256,1152]{2,1,0:T(8,128)(2,1)}, u32[]{:S(2)}, u32[]{:S(2)}) collective-permute-start(bf16[1,256,1152]{2,1,0:T(8,128)(2,1)S(1)} %copy-done.13), channel_id=1, source_target_pairs={{0,2},{1,3},{2,0},{3,1},{4,6},{5,7},{6,4},{7,5},{8,10},{9,11},{10,... | collective-permute-start | bytes 1769480 | tf_op jit(solution)/shard_map/ppermute | solution.py:23
  265.9 3.2 collective-permute-start.38
  265.9 8.0 %collective-permute-start.39 = (bf16[1,256,288]{2,1,0:T(8,128)(2,1)}, bf16[1,256,288]{2,1,0:T(8,128)(2,1)S(1)}, u32[]{:S(2)}, u32[]{:S(2)}) collective-permute-start(bf16[1,256,288]{2,1,0:T(8,128)(2,1)} %get-tuple-element.75), channel_id=1, source_target_pairs={{0,2},{1,3},{2,0},{3,1},{4,6},{5,7},{6,4},{7,5},{8,10},{9,11},{10,... | collective-permute-start | bytes 442376 | tf_op jit(solution)/shard_map/ppermute | solution.py:23
  266.9 10.3 %collective-permute-start.40 = (bf16[1,256,288]{2,1,0:T(8,128)(2,1)}, bf16[1,256,288]{2,1,0:T(8,128)(2,1)S(1)}, u32[]{:S(2)}, u32[]{:S(2)}) collective-permute-start(bf16[1,256,288]{2,1,0:T(8,128)(2,1)} %get-tuple-element.76), channel_id=1, source_target_pairs={{0,3},{1,2},{2,1},{3,0},{4,7},{5,6},{6,5},{7,4},{8,11},{9,10},{10,... | collective-permute-start | bytes 442376 | tf_op jit(solution)/shard_map/ppermute | solution.py:23
  303.0 34.8 %collective-permute-start.44 = (bf16[1,256,288]{2,1,0:T(8,128)(2,1)S(1)}, bf16[1,256,288]{2,1,0:T(8,128)(2,1)S(1)}, u32[]{:S(2)}, u32[]{:S(2)}) collective-permute-start(bf16[1,256,288]{2,1,0:T(8,128)(2,1)S(1)} %copy-done.45), channel_id=1, source_target_pairs={{0,1},{1,0},{2,3},{3,2},{4,5},{5,4},{6,7},{7,6},{8,9},{9,8},{10,11... | collective-permute-start | bytes 442376 | tf_op jit(solution)/shard_map/ppermute | solution.py:23
  303.7 34.6 %collective-permute-start.45 = (bf16[1,256,288]{2,1,0:T(8,128)(2,1)}, bf16[1,256,288]{2,1,0:T(8,128)(2,1)}, u32[]{:S(2)}, u32[]{:S(2)}) collective-permute-start(bf16[1,256,288]{2,1,0:T(8,128)(2,1)} %get-tuple-element.80), channel_id=1, source_target_pairs={{0,2},{1,3},{2,0},{3,1},{4,6},{5,7},{6,4},{7,5},{8,10},{9,11},{10,... | collective-permute-start | bytes 442376 | tf_op jit(solution)/shard_map/ppermute | solution.py:23
  304.6 33.7 %collective-permute-start.46 = (bf16[1,256,288]{2,1,0:T(8,128)(2,1)}, bf16[1,256,288]{2,1,0:T(8,128)(2,1)}, u32[]{:S(2)}, u32[]{:S(2)}) collective-permute-start(bf16[1,256,288]{2,1,0:T(8,128)(2,1)} %get-tuple-element.81), channel_id=1, source_target_pairs={{0,3},{1,2},{2,1},{3,0},{4,7},{5,6},{6,5},{7,4},{8,11},{9,10},{10,... | collective-permute-start | bytes 442376 | tf_op jit(solution)/shard_map/ppermute | solution.py:23
  325.9 47.8 %collective-permute-start.42 = (bf16[1,256,1152]{2,1,0:T(8,128)(2,1)S(1)}, bf16[1,256,1152]{2,1,0:T(8,128)(2,1)S(1)}, u32[]{:S(2)}, u32[]{:S(2)}) collective-permute-start(bf16[1,256,1152]{2,1,0:T(8,128)(2,1)S(1)} %get-tuple-element.183), channel_id=1, source_target_pairs={{0,1},{1,0},{2,3},{3,2},{4,5},{5,4},{6,7},{7,6},{8,9},{9,8},{10,11... | collective-permute-start | bytes 1769480 | tf_op jit(solution)/shard_map/ppermute | solution.py:23
  327.4 13.4 %collective-permute-start.33 = (bf16[1,256,1152]{2,1,0:T(8,128)(2,1)S(1)}, bf16[1,256,1152]{2,1,0:T(8,128)(2,1)S(1)}, u32[]{:S(2)}, u32[]{:S(2)}) collective-permute-start(bf16[1,256,1152]{2,1,0:T(8,128)(2,1)S(1)} %get-tuple-element.185), channel_id=1, source_target_pairs={{0,1},{1,0},{2,3},{3,2},{4,5},{5,4},{6,7},{7,6},{8,9},{9,8},{10,11... | collective-permute-start | bytes 1769480 | tf_op jit(solution)/shard_map/ppermute | solution.py:23
  337.8 35.9 %collective-permute-start.32 = (bf16[1,256,1152]{2,1,0:T(8,128)(2,1)}, bf16[1,256,1152]{2,1,0:T(8,128)(2,1)S(1)}, u32[]{:S(2)}, u32[]{:S(2)}) collective-permute-start(bf16[1,256,1152]{2,1,0:T(8,128)(2,1)} %get-tuple-element.184), channel_id=1, source_target_pairs={{0,1},{1,0},{2,3},{3,2},{4,5},{5,4},{6,7},{7,6},{8,9},{9,8},{10,11... | collective-permute-start | bytes 1769480 | tf_op jit(solution)/shard_map/ppermute | solution.py:23
  338.3 42.4 %collective-permute-start.35 = (bf16[1,256,1152]{2,1,0:T(8,128)(2,1)}, bf16[1,256,1152]{2,1,0:T(8,128)(2,1)}, u32[]{:S(2)}, u32[]{:S(2)}) collective-permute-start(bf16[1,256,1152]{2,1,0:T(8,128)(2,1)} %get-tuple-element.186), channel_id=1, source_target_pairs={{0,1},{1,0},{2,3},{3,2},{4,5},{5,4},{6,7},{7,6},{8,9},{9,8},{10,11... | collective-permute-start | bytes 1769480 | tf_op jit(solution)/shard_map/ppermute | solution.py:23
  338.4 4.4 collective-permute-start.36
  341.8 39.5 %collective-permute-start.34 = (bf16[1,256,1152]{2,1,0:T(8,128)(2,1)}, bf16[1,256,1152]{2,1,0:T(8,128)(2,1)}, u32[]{:S(2)}, u32[]{:S(2)}) collective-permute-start(bf16[1,256,1152]{2,1,0:T(8,128)(2,1)} %fusion.36.refs_1_), channel_id=1, source_target_pairs={{0,2},{1,3},{2,0},{3,1},{4,6},{5,7},{6,4},{7,5},{8,10},{9,11},{10,... | collective-permute-start | bytes 1769480 | tf_op jit(solution)/shard_map/ppermute | solution.py:23
  343.8 38.5 %collective-permute-start.37 = (bf16[1,256,1152]{2,1,0:T(8,128)(2,1)}, bf16[1,256,1152]{2,1,0:T(8,128)(2,1)}, u32[]{:S(2)}, u32[]{:S(2)}) collective-permute-start(bf16[1,256,1152]{2,1,0:T(8,128)(2,1)} %fusion.34.refs_2_), channel_id=1, source_target_pairs={{0,2},{1,3},{2,0},{3,1},{4,6},{5,7},{6,4},{7,5},{8,10},{9,11},{10,... | collective-permute-start | bytes 1769480 | tf_op jit(solution)/shard_map/ppermute | solution.py:23
  373.7 15.9 %collective-permute-start.50 = (bf16[8,72,1152]{2,1,0:T(8,128)(2,1)}, bf16[8,72,1152]{2,1,0:T(8,128)(2,1)}, u32[]{:S(2)}, u32[]{:S(2)}) collective-permute-start(bf16[8,72,1152]{2,1,0:T(8,128)(2,1)} %dynamic-slice_bitcast_fusion), channel_id=1, source_target_pairs={{0,1},{1,0},{2,3},{3,2},{4,5},{5,4},{6,7},{7,6},{8,9},{9,8},{10,11... | collective-permute-start | bytes 3981320 | tf_op jit(solution)/shard_map/ppermute | solution.py:23
  373.7 13.4 %collective-permute-start.48 = (bf16[1,256,1152]{2,1,0:T(8,128)(2,1)}, bf16[1,256,1152]{2,1,0:T(8,128)(2,1)}, u32[]{:S(2)}, u32[]{:S(2)}) collective-permute-start(bf16[1,256,1152]{2,1,0:T(8,128)(2,1)} %get-tuple-element.181), channel_id=1, source_target_pairs={{0,1},{1,0},{2,3},{3,2},{4,5},{5,4},{6,7},{7,6},{8,9},{9,8},{10,11... | collective-permute-start | bytes 1769480 | tf_op jit(solution)/shard_map/ppermute | solution.py:23
  380.7 19.1 %collective-permute-start.41 = (bf16[1,256,1152]{2,1,0:T(8,128)(2,1)}, bf16[1,256,1152]{2,1,0:T(8,128)(2,1)}, u32[]{:S(2)}, u32[]{:S(2)}) collective-permute-start(bf16[1,256,1152]{2,1,0:T(8,128)(2,1)} %get-tuple-element.182), channel_id=1, source_target_pairs={{0,1},{1,0},{2,3},{3,2},{4,5},{5,4},{6,7},{7,6},{8,9},{9,8},{10,11... | collective-permute-start | bytes 1769480 | tf_op jit(solution)/shard_map/ppermute | solution.py:23
  381.2 18.6 %collective-permute-start.43 = (bf16[1,256,1152]{2,1,0:T(8,128)(2,1)}, bf16[1,256,1152]{2,1,0:T(8,128)(2,1)}, u32[]{:S(2)}, u32[]{:S(2)}) collective-permute-start(bf16[1,256,1152]{2,1,0:T(8,128)(2,1)} %fusion.32), channel_id=1, source_target_pairs={{0,2},{1,3},{2,0},{3,1},{4,6},{5,7},{6,4},{7,5},{8,10},{9,11},{10,... | collective-permute-start | bytes 1769480 | tf_op jit(solution)/shard_map/ppermute | solution.py:23
  382.3 20.2 %collective-permute-start.47 = (bf16[1,256,1152]{2,1,0:T(8,128)(2,1)}, bf16[1,256,1152]{2,1,0:T(8,128)(2,1)}, u32[]{:S(2)}, u32[]{:S(2)}) collective-permute-start(bf16[1,256,1152]{2,1,0:T(8,128)(2,1)} %get-tuple-element.180), channel_id=1, source_target_pairs={{0,1},{1,0},{2,3},{3,2},{4,5},{5,4},{6,7},{7,6},{8,9},{9,8},{10,11... | collective-permute-start | bytes 1769480 | tf_op jit(solution)/shard_map/ppermute | solution.py:23
  388.5 20.9 %collective-permute-start.49 = (bf16[1,256,1152]{2,1,0:T(8,128)(2,1)S(1)}, bf16[1,256,1152]{2,1,0:T(8,128)(2,1)S(1)}, u32[]{:S(2)}, u32[]{:S(2)}) collective-permute-start(bf16[1,256,1152]{2,1,0:T(8,128)(2,1)S(1)} %fusion.30), channel_id=1, source_target_pairs={{0,2},{1,3},{2,0},{3,1},{4,6},{5,7},{6,4},{7,5},{8,10},{9,11},{10,... | collective-permute-start | bytes 1769480 | tf_op jit(solution)/shard_map/ppermute | solution.py:23
  420.3 1.3 collective-permute-start.51
  421.6 4.3 collective-permute-start.52
  426.8 30.5 %all-to-all-start.2 = ((bf16[8,2,6912]{2,1,0:T(2,128)(2,1)}), bf16[8,2,6912]{2,1,0:T(2,128)(2,1)S(1)}, u32[]{:S(2)}, u32[]{:S(2)}) async-start(bf16[8,2,6912]{2,1,0:T(2,128)(2,1)} %broadcast_in_dim.103), calls=%async_computation.3 | async-start | bytes 442368 | tf_op jit(solution)/shard_map/all_to_all | solution.py:92
  457.3 16.4 %all-to-all-start.5 = ((bf16[4,288,288]{2,1,0:T(8,128)(2,1)}), bf16[4,288,288]{2,1,0:T(8,128)(2,1)S(1)}, u32[]{:S(2)}, u32[]{:S(2)}) async-start(bf16[4,288,288]{2,1,0:T(8,128)(2,1)} %pad_maximum_fusion.3), calls=%async_computation.7 | async-start | bytes 1769472 | tf_op jit(solution)/shard_map/all_to_all | solution.py:744
  473.7 13.1 %all-to-all-start.3 = ((f32[8,1,432]{2,1,0:T(1,128)}), f32[8,1,432]{2,1,0:T(1,128)S(1)}, u32[]{:S(2)}, u32[]{:S(2)}) async-start(f32[8,1,432]{2,1,0:T(1,128)} %all_to_all.30), calls=%async_computation.4 | async-start | bytes 32768 | tf_op jit(solution)/shard_map/all_to_all | solution.py:92
  501.1 13.0 %all-to-all-start.4 = ((bf16[4,216,288]{1,2,0:T(8,128)(2,1)}), bf16[4,216,288]{1,2,0:T(8,128)(2,1)S(1)}, u32[]{:S(2)}, u32[]{:S(2)}) async-start(bf16[4,216,288]{1,2,0:T(8,128)(2,1)} %copy.99), calls=%async_computation.6 | async-start | bytes 1179648 | tf_op jit(solution)/shard_map/all_to_all | solution.py:768
  (45 other events, 244.7 us)
Sparse Core Ops, SparseCore 0:
  10.8 64.2 all-gather.4
  77.8 84.2 all-gather.6
  238.9 118.0 reduce-scatter.2
  400.0 96.3 reduce-scatter.4

commit v8 on v7

--- a/solution.py
+++ b/solution.py
@@ -76,12 +76,12 @@
     return slots[0], slots[bit].astype(BF)
 
 
+def far_hop(sent):
+    return hop(sent, "seq", lax.axis_size("seq") // 2)
+
+
 def seq_far(kept, sent):
-    return kept + hop(sent, "seq", lax.axis_size("seq") // 2).astype(F32)
-
-
-def seq_reduce(slots):
-    return seq_far(*seq_near(slots))
+    return kept + far_hop(sent).astype(F32)
 
 
 def seq_exchange(blocks):
@@ -142,8 +142,11 @@
     mixed[0] = mixed_t[...].T.astype(BF)
 
 
-def attend_grad_kernel(heads, block, packed, mixed, log_sum, d_mixed, qkv, *refs):
-    d_packed, terms, d_queries_t = refs[-3:]
+def attend_grad_kernel(heads, block, count, packed, mixed, log_sum, qkv, *refs):
+    d_packed, terms, d_queries_t, d_mixed = refs[-4:]
+    tok = refs[0].shape[1]
+    for j in range(count):
+        d_mixed[0, j * tok : (j + 1) * tok] = refs[j][0]
     seq_len = packed.shape[1]
     cols = heads * HEAD_DIM
     inv_root = HEAD_DIM ** (-0.5)
@@ -202,25 +205,25 @@
     lat, seq_len, _ = packed.shape
     cols = heads * HEAD_DIM
     return pl.pallas_call(
-        partial(attend_grad_kernel, heads, block),
+        partial(attend_grad_kernel, heads, block, len(d_mixed)),
         grid=(lat,),
         in_specs=[
             row_spec(seq_len, 3 * cols),
             row_spec(seq_len, cols),
             row_spec(heads, seq_len),
-            row_spec(seq_len, cols),
             pl.BlockSpec(qkv.shape, lambda i: (0, 0)),
         ]
+        + [row_spec(seq_len // len(d_mixed), cols)] * len(d_mixed)
         + [pl.BlockSpec(memory_space=pl.ANY)] * len(after),
         out_specs=[row_spec(seq_len, 3 * cols), row_spec(seq_len, qkv.shape[0])],
         out_shape=[
             jax.ShapeDtypeStruct((lat, seq_len, 3 * cols), BF),
             jax.ShapeDtypeStruct((lat, seq_len, qkv.shape[0]), BF),
         ],
-        scratch_shapes=[pltpu.VMEM((cols, seq_len), F32)],
+        scratch_shapes=[pltpu.VMEM((cols, seq_len), F32), pltpu.VMEM((1, seq_len, cols), BF)],
         compiler_params=pltpu.CompilerParams(vmem_limit_bytes=VMEM_LIMIT),
         name="attend_grad",
-    )(packed, mixed, log_sum, d_mixed, qkv, *after)
+    )(packed, mixed, log_sum, qkv, *d_mixed, *after)
 
 
 def qkv_kernel(count, *refs):
@@ -459,25 +462,32 @@
     )(proj_terms, qkv_terms, after)
 
 
-def token_grad_kernel(per, d_first, e_first, d_resid, e_resid, tokens, scale, after, *outs):
-    grad_tokens, d_shift, d_scale = outs
+def token_grad_kernel(per, *refs):
+    pairs, (tokens, cotangent, scale, gate) = refs[:12], refs[12:16]
+    output, grad_tokens, d_shift, d_scale, d_gate = refs[-5:]
     early = pl.program_id(0) < per
-    grad = jnp.where(early, d_first[0], e_first[0])
+
+    def pick(i):
+        return jnp.where(early, pairs[2 * i][0].astype(F32), pairs[2 * i + 1][0].astype(F32))
+
+    grad = pick(0) + pick(1)
     normed, inv_std = ln_parts(tokens[0].astype(F32))
-    grad_tokens[0] = jnp.where(early, d_resid[0], e_resid[0]) + ln_backward(
-        grad * (1.0 + scale[0]), normed, inv_std
-    )
+    grad_tokens[0] = pick(2) + ln_backward(grad * (1.0 + scale[0]), normed, inv_std)
+    mlp_out = pick(3) + pick(4)
+    output[0] = (pick(5) + gate[0] * mlp_out).astype(BF)
 
     @pl.when(pl.program_id(1) == 0)
     def _():
         d_shift[...] = jnp.zeros_like(d_shift)
         d_scale[...] = jnp.zeros_like(d_scale)
+        d_gate[...] = jnp.zeros_like(d_gate)
 
     d_shift[0] += jnp.sum(grad, axis=0, keepdims=True)
     d_scale[0] += jnp.sum(grad * normed, axis=0, keepdims=True)
-
-
-def token_grad(d_first, d_resid, tokens, scale, after):
+    d_gate[0] += jnp.sum(cotangent[0].astype(F32) * mlp_out, axis=0, keepdims=True)
+
+
+def token_grad(pairs, tokens, cotangent, scale, gate, after):
     lat, tok, width = tokens.shape
     per = lat // 2
     chunk = min(tok, 128)
@@ -489,12 +499,18 @@
     return pl.pallas_call(
         partial(token_grad_kernel, per),
         grid=(lat, tok // chunk),
-        in_specs=[early, late, early, late, block, row, pl.BlockSpec(memory_space=pl.ANY)],
-        out_specs=[block, row, row],
-        out_shape=[jax.ShapeDtypeStruct((lat, tok, width), F32), row_shape, row_shape],
+        in_specs=[early, late] * 6 + [block, block, row, row, pl.BlockSpec(memory_space=pl.ANY)],
+        out_specs=[block, block, row, row, row],
+        out_shape=[
+            jax.ShapeDtypeStruct((lat, tok, width), BF),
+            jax.ShapeDtypeStruct((lat, tok, width), F32),
+            row_shape,
+            row_shape,
+            row_shape,
+        ],
         compiler_params=pltpu.CompilerParams(vmem_limit_bytes=VMEM_LIMIT),
         name="token_grad",
-    )(*d_first, *d_resid, tokens, scale, after)
+    )(*[v for pair in pairs for v in pair], tokens, cotangent, scale, gate, after)
 
 
 def place_last_kernel(rows, owners, received, out_qkv, out_proj):
@@ -611,7 +627,7 @@
     proj = by_place(proj)
 
     normed_all, packed, mixed, log_sums, attended = [], [], [], [], []
-    attn_out, resid_mid, normed_mlp, upstream = [], [], [], []
+    attn_out, resid_mid, normed_mlp = [], [], []
     for g in range(groups):
         normed, rows_packed = qkv_forward(tok_slots, g, per, shift_attn[g], scale_attn[g], qkv)
         normed_all.append(normed.reshape(per * seq_len, width))
@@ -632,7 +648,6 @@
         normed_mlp.append(
             (ln_parts(resid_mid[g])[0] * (1.0 + scale_mlp[g]) + shift_mlp[g]).astype(BF)
         )
-        upstream.append(cotangent[part(g)].astype(F32))
 
     grad_fc1 = grad_fc2 = grad_bias1 = 0.0
     d_near, activated = [], []
@@ -674,7 +689,7 @@
         d_scale_mlp.append(outs[3][:, 0])
         d_gate_attn.append(outs[4][:, 0])
         d_attended.append(outs[5])
-        d_mixed.append(jnp.concatenate(seq_exchange(outs[5:]), axis=1))
+        d_mixed.append(seq_exchange(outs[5:]))
     mlp_terms, mlp_near = [], []
     for g in range(groups):
         terms = mlp_out_terms(activated[g], fc2, d_attended[-1])
@@ -693,29 +708,35 @@
     for g in range(groups):
         grads, terms = attention_grad(
             packed[g], mixed[g], log_sums[g], d_mixed[g], qkv,
-            first_terms + [near[1] for near in mlp_near] if g else [d_attended[-1]] + mlp_terms,
+            first_terms + [near[1] for near in mlp_near] + [proj_terms]
+            if g
+            else [d_attended[-1]] + mlp_terms,
             heads_here,
         )
         d_packed.append(grads.reshape(per * seq_len, 3 * cols))
         first_terms.append(terms)
         terms = terms.reshape(per, seq_n, tok, width)
-        d_first.append(seq_reduce([terms[:, j].astype(F32) for j in range(seq_n)]))
-    mlp_out = [seq_far(*near) for near in mlp_near]
-    output = jnp.concatenate(
-        [(resid_mid[g] + gate_mlp[g] * mlp_out[g]).astype(BF) for g in range(groups)]
-    )
-    d_gate_mlp = stacked([jnp.sum(upstream[g] * mlp_out[g], axis=1) for g in range(groups)])
+        d_first.append(seq_near([terms[:, j].astype(F32) for j in range(seq_n)]))
     grad_qkv = matmul_tn(stacked(normed_all), stacked(d_packed)).astype(BF)
     last = pack_last(proj_terms, grad_qkv.reshape(dp_n, rows, 3 * cols), sum_fc)
     sum_last = lax.psum_scatter(last, "dp", scatter_dimension=0)
     sum_qkv, sum_proj = sum_last[:, : 3 * cols], sum_last[:, 3 * cols :]
-    grad_tokens, d_shift_attn, d_scale_attn = token_grad(
-        d_first, d_resid, tokens, modulation[:, None, width : 2 * width], last
+    pairs = [
+        [near[0] for near in d_first],
+        [far_hop(near[1]) for near in d_first],
+        d_resid,
+        [near[0] for near in mlp_near],
+        [far_hop(near[1]) for near in mlp_near],
+        resid_mid,
+    ]
+    output, grad_tokens, d_shift_attn, d_scale_attn, d_gate_mlp = token_grad(
+        pairs, tokens, cotangent, modulation[:, None, width : 2 * width],
+        modulation[:, None, 5 * width :], last,
     )
 
     mod_part = jnp.concatenate(
         [d_shift_attn[:, 0], d_scale_attn[:, 0], stacked(d_gate_attn)]
-        + [stacked(d_shift_mlp), stacked(d_scale_mlp), d_gate_mlp],
+        + [stacked(d_shift_mlp), stacked(d_scale_mlp), d_gate_mlp[:, 0]],
         axis=1,
     )
     bit = 1

time: 530 us -> 509 us (0.960)
  other arithmetic: 57.6 us -> 43.9 us
  waiting for transfers between devices: 103 us -> 90.7 us
    reduce_scatter x1, waiting for transfers between devices: 8.73 us -> 0.01 us  [on_device(): sum_last = lax.psum_scatter(last, 'dp', scatter_dimension=0)]
    unnamed x101 -> x109, local copies, waits for them, and re-layouts: 10.4 us -> 11.9 us
  transfers between devices with their start and end apart: 63 -> 63, of which waited for: 18 -> 17; matrix products, arithmetic and copies ran while one was open for 29% -> 27% of each run, Pallas kernels for 25% -> 27%
where the time goes in v8:
time: 509 us; the launch traced here: 503 us
  Pallas kernels  160 us (31%)
  waiting for transfers between devices  90.7 us (18%)
  starting transfers between devices  79.8 us (16%)
  local copies, waits for them, and re-layouts  74.9 us (15%)
  other arithmetic  43.9 us (9%)
  matrix products  39.3 us (8%)
  between operations  14.9 us (3%)
    ppermute x53, waiting for transfers between devices, hop(): return lax.ppermute(value, axis, [(i, i ^ bits) for i in range(count)])  65.9 us
    ppermute x53, starting transfers between devices, hop(): return lax.ppermute(value, axis, [(i, i ^ bits) for i in range(count)])  39.8 us
    pallas_call x2, Pallas kernels, attention_grad(): pl.pallas_call(partial(attend_grad_kernel, heads, block, len(d_mixed)), g...  36.3 us
    pallas_call x2, Pallas kernels, mlp(): pl.pallas_call(partial(mlp_kernel, count), grid=(per, tok // chunk), in_s...  33.5 us
    all_to_all x4, starting transfers between devices, dp_exchange(): return lax.all_to_all(value, 'dp', 0, 0, tiled=True)  32.3 us
    dot_general x7, matrix products, matmul_tn(): lax.dot_general(left, right, (((0,), (0,)), ((), ())), preferred_element_...  30.7 us
    pallas_call x2, Pallas kernels, attention(): pl.pallas_call(partial(attend_kernel, heads, block), grid=(lat,), in_spec...  17.6 us
    pallas_call x2, Pallas kernels, qkv_forward(): pl.pallas_call(partial(qkv_kernel, count), grid=(per, tok // chunk), in_s...  16.1 us
  transfers between devices with their start and end apart: 63, of which 17 were waited for; matrix products, arithmetic and copies ran while one was open for 27% of the time, Pallas kernels for 27%

profile of v8, /device:TPU:0, one launch (start us, length us, event | category | flops | bytes accessed | tf_op | source)
XLA Modules:
  0.0 503.4 jit_solution(10623964386934348087)
XLA Ops:
  12.8 3.0 collective-permute-start.1
  18.9 5.8 %all-to-all-start = ((bf16[8,2,1224]{2,1,0:T(2,128)(2,1)}), bf16[8,2,1224]{2,1,0:T(2,128)(2,1)S(1)}, u32[]{:S(2)}, u32[]{:S(2)}) async-start(bf16[8,2,1224]{2,1,0:T(2,128)(2,1)} %reshape.526), calls=%async_computation | async-start | bytes 81920 | tf_op jit(solution)/shard_map/all_to_all | solution.py:92
  28.3 2.9 collective-permute-start.6
  37.8 2.0 reshape.455
  39.8 4.1 all-to-all-start.1
  44.5 3.7 collective-permute-start.8
  53.6 13.8 %collective-permute-done.8 = bf16[144,864]{1,0:T(8,128)(2,1)} collective-permute-done((bf16[144,864]{1,0:T(8,128)(2,1)}, bf16[144,864]{1,0:T(8,128)(2,1)}, u32[]{:S(2)}, u32[]{:S(2)}) %collective-permute-start.8) | collective-permute-done | bytes 248864 | tf_op jit(solution)/shard_map/ppermute | solution.py:23
  67.5 3.7 collective-permute-start.7
  72.7 4.0 collective-permute-done.7
  83.6 8.1 %qkv_forward.2 = (bf16[1,4,256,1152]{3,2,1,0:T(8,128)(2,1)}, bf16[1,4,256,864]{3,2,1,0:T(8,128)(2,1)}) custom-call(bf16[2,256,1152]{2,1,0:T(8,128)(2,1)} %refs_12_.1, bf16[2,256,1152]{2,1,0:T(8,128)(2,1)} %collective-permute-done.refs_1_, bf16[2,256,1152]{2,1,0:T(8,128)(2,1)} %collective-permute-done.1.refs_2_, ...), custom_call_target="tpu_custom_call" | custom-call | tf_op jit(solution)/shard_map/qkv_forward/pallas_call | solution.py:245
  91.8 8.8 %attend.2 = (bf16[1,1024,288]{2,1,0:T(8,128)(2,1)}, f32[1,4,1024]{2,1,0:T(4,128)}) custom-call(bf16[1,1024,864]{2,1,0:T(8,128)(2,1)} %bitcast.291), custom_call_target="tpu_custom_call" | custom-call | tf_op jit(solution)/shard_map/attend/pallas_call | solution.py:189
  100.5 2.1 slice_bitcast_fusion.24
  102.6 2.1 collective-permute-start.11
  104.7 8.0 %qkv_forward.3 = (bf16[1,4,256,1152]{3,2,1,0:T(8,128)(2,1)}, bf16[1,4,256,864]{3,2,1,0:T(8,128)(2,1)}) custom-call(bf16[2,256,1152]{2,1,0:T(8,128)(2,1)} %refs_12_.1, bf16[2,256,1152]{2,1,0:T(8,128)(2,1)} %collective-permute-done.refs_1_, bf16[2,256,1152]{2,1,0:T(8,128)(2,1)} %collective-permute-done.1.refs_2_, ...), custom_call_target="tpu_custom_call" | custom-call | tf_op jit(solution)/shard_map/qkv_forward/pallas_call | solution.py:245
  114.3 2.1 concatenate.59
  116.4 3.0 maximum_select_fusion
  119.9 5.0 pad_maximum_fusion.refs_6_
  124.9 3.5 fusion.50
  130.6 8.8 %attend.3 = (bf16[1,1024,288]{2,1,0:T(8,128)(2,1)}, f32[1,4,1024]{2,1,0:T(4,128)}) custom-call(bf16[1,1024,864]{2,1,0:T(8,128)(2,1)} %bitcast.293, bf16[1,256,1152]{2,1,0:T(8,128)(2,1)} %add_convert_fusion.1.refs_0_, bf16[2,256,1152]{2,1,0:T(8,128)(2,1)} %collective-permute-done.19.refs_7_.refs_1_), custom_call_target="tpu_custom_call" | custom-call | tf_op jit(solution)/shard_map/attend/pallas_call | solution.py:189
  139.4 2.0 slice_bitcast_fusion.20
  144.5 4.5 collective-permute-done.25
  149.0 3.7 collective-permute-done.24
  152.7 2.3 concatenate.63
  155.0 4.1 fusion.49
  159.4 6.0 %collective-permute-done.15.refs_2_ = bf16[1,256,1152]{2,1,0:T(8,128)(2,1)} collective-permute-done((bf16[1,256,1152]{2,1,0:T(8,128)(2,1)}, bf16[1,256,1152]{2,1,0:T(8,128)(2,1)}, u32[]{:S(2)}, u32[]{:S(2)}) %collective-permute-start.15) | collective-permute-done | bytes 589856 | tf_op jit(solution)/shard_map/ppermute | solution.py:23
  167.7 16.5 %mlp.2 = (bf16[1,4,256,1152]{3,2,1,0:T(8,128)(2,1)}, bf16[1,4,256,1152]{3,2,1,0:T(8,128)(2,1)}, bf16[1,4,256,1152]{3,2,1,0:T(8,128)(2,1)}, bf16[1,4,256,1152]{3,...) custom-call(bf16[1,256,1152]{2,1,0:T(8,128)(2,1)} %add_convert_fusion.1.refs_0_, ...), custom_call_target="tpu_custom_call" | custom-call | tf_op jit(solution)/shard_map/mlp/pallas_call | solution.py:313
  184.2 2.1 slice_bitcast_fusion.19
  188.4 2.0 fusion.36.refs_12_
  191.4 17.0 %mlp.3 = (bf16[1,4,256,1152]{3,2,1,0:T(8,128)(2,1)}, bf16[1,4,256,1152]{3,2,1,0:T(8,128)(2,1)}, bf16[1,4,256,1152]{3,2,1,0:T(8,128)(2,1)}, bf16[1,4,256,1152]{3,...) custom-call(bf16[1,256,1152]{2,1,0:T(8,128)(2,1)} %add_convert_fusion.refs_0_, ...), custom_call_target="tpu_custom_call" | custom-call | tf_op jit(solution)/shard_map/mlp/pallas_call | solution.py:313
  208.4 2.3 slice_bitcast_fusion.16
  210.9 5.1 %convolution_bitcast_fusion.2 = f32[1152,1152]{1,0:T(8,128)S(1)} fusion(bf16[1,4,256,1152]{3,2,1,0:T(8,128)(2,1)} %get-tuple-element.68, bf16[1,4,256,1152]{3,2,1,0:T(8,128)(2,1)S(1)} %copy-done.46), kind=kOutput, calls=%fused_computation.3 | convolution fusion | flops 2717908992 | bytes 10027008 | tf_op jit(solution)/shard_map/dot_general | solution.py:35
  216.0 3.3 convolution_bitcast_fusion
  219.4 5.1 %fusion.2 = bf16[1152,1152]{1,0:T(8,128)(2,1)} fusion(f32[1152,1152]{1,0:T(8,128)S(1)} %convolution_bitcast_fusion.2, bf16[1,4,256,1152]{3,2,1,0:T(8,128)(2,1)S(1)} %copy-done.44, bf16[1,4,256,1152]{3,2,1,0:T(8,128)(2,1)S(1)} %copy-done.43), kind=kOutput, calls=%fused_computation.7 | convolution fusion | flops 2720563200 | bytes 12681216 | tf_op jit(solution)/shard_map/dot_general | solution.py:35
  224.5 5.1 %fusion.3 = bf16[1152,1152]{1,0:T(8,128)(2,1)} fusion(f32[1152,1152]{1,0:T(8,128)S(1)} %convolution_bitcast_fusion, bf16[1,4,256,1152]{3,2,1,0:T(8,128)(2,1)S(1)} %copy-done.42, bf16[1,4,256,1152]{3,2,1,0:T(8,128)(2,1)S(1)} %copy-done.12), kind=kOutput, calls=%fused_computation.8 | convolution fusion | flops 2720563200 | bytes 12681216 | tf_op jit(solution)/shard_map/dot_general | solution.py:35
  229.6 2.1 fusion.35.after
  231.6 7.1 %pack.1.refs_7_ = bf16[8,288,1152]{2,1,0:T(8,128)(2,1)} custom-call(bf16[8,144,1152]{2,1,0:T(8,128)(2,1)} %bitcast.303, bf16[8,144,1152]{2,1,0:T(8,128)(2,1)} %bitcast.304, bf16[1,256,1152]{2,1,0:T(8,128)(2,1)} %fusion.35.after), custom_call_target="tpu_custom_call" | custom-call | tf_op jit(solution)/shard_map/pack/pallas_call | solution.py:424
  241.9 14.1 %collective-permute-done.22 = bf16[1,256,1152]{2,1,0:T(8,128)(2,1)} collective-permute-done((bf16[1,256,1152]{2,1,0:T(8,128)(2,1)S(1)}, bf16[1,256,1152]{2,1,0:T(8,128)(2,1)}, u32[]{:S(2)}, u32[]{:S(2)}) %collective-permute-start.22) | collective-permute-done | bytes 589856 | tf_op jit(solution)/shard_map/ppermute | solution.py:23
  256.1 2.6 fusion.37.refs_0_
  258.7 7.1 %resid_grad.2 = (f32[1,256,1152]{2,1,0:T(8,128)}, bf16[1,256,1152]{2,1,0:T(8,128)(2,1)}, f32[1,1,1152]{2,1,0:T(1,128)}, f32[1,1,1152]{2,1,0:T(1,128)}, f32[1,1,1...) custom-call(f32[1,256,1152]{2,1,0:T(8,128)} %fusion.37.refs_0_, ...), custom_call_target="tpu_custom_call" | custom-call | tf_op jit(solution)/shard_map/resid_grad/pallas_call | solution.py:388
  268.1 2.6 fusion.34.refs_0_
  270.8 6.8 %resid_grad.3 = (f32[1,256,1152]{2,1,0:T(8,128)}, bf16[1,256,1152]{2,1,0:T(8,128)(2,1)}, f32[1,1,1152]{2,1,0:T(1,128)}, f32[1,1,1152]{2,1,0:T(1,128)}, f32[1,1,1...) custom-call(f32[1,256,1152]{2,1,0:T(8,128)} %fusion.34.refs_0_, ...), custom_call_target="tpu_custom_call" | custom-call | tf_op jit(solution)/shard_map/resid_grad/pallas_call | solution.py:388
  277.6 7.3 %mlp_out_terms.3.refs_6_ = bf16[1,4,256,1152]{3,2,1,0:T(8,128)(2,1)} custom-call(bf16[1,4,256,1152]{3,2,1,0:T(8,128)(2,1)} %get-tuple-element.71.activated, bf16[8,288,1152]{2,1,0:T(8,128)(2,1)} %bitcast.283, bf16[1,256,288]{2,1,0:T(8,128)(2,1)} %get-tuple-element.78.after.refs_4_.refs_0_), custom_call_target="tpu_custom_call" | custom-call | tf_op jit(solution)/shard_map/mlp_out_terms/pallas_call | solution.py:340
  284.8 7.3 %mlp_out_terms.2.refs_5_ = bf16[1,4,256,1152]{3,2,1,0:T(8,128)(2,1)} custom-call(bf16[1,4,256,1152]{3,2,1,0:T(8,128)(2,1)} %get-tuple-element.69.activated, bf16[8,288,1152]{2,1,0:T(8,128)(2,1)} %bitcast.284, bf16[1,256,288]{2,1,0:T(8,128)(2,1)} %get-tuple-element.78.after.refs_4_.refs_0_), custom_call_target="tpu_custom_call" | custom-call | tf_op jit(solution)/shard_map/mlp_out_terms/pallas_call | solution.py:340
  293.8 18.3 %attend_grad.2 = (bf16[1,1024,864]{2,1,0:T(8,128)(2,1)}, bf16[1,1024,1152]{2,1,0:T(8,128)(2,1)}) custom-call(bf16[1,1024,864]{2,1,0:T(8,128)(2,1)} %bitcast.292, bf16[1,1024,288]{2,1,0:T(8,128)(2,1)} %get-tuple-element.60.mixed, f32[1,4,1024]{2,1,0:T(4,128)} %get-tuple-element.61.log_sum, bf16[1152,864]{1,0:T(8,128)(2,1)} %bitcast.10.refs_6_.qkv, ...), custom_call_target="tpu_custom_call" | custom-call | tf_op jit(solution)/shard_map/attend_grad/pallas_call | solution.py:207
  316.8 4.8 pad_maximum_fusion.1
  336.3 18.0 %attend_grad.3 = (bf16[1,1024,864]{2,1,0:T(8,128)(2,1)}, bf16[1,1024,1152]{2,1,0:T(8,128)(2,1)}) custom-call(bf16[1,1024,864]{2,1,0:T(8,128)(2,1)} %bitcast.294, bf16[1,1024,288]{2,1,0:T(8,128)(2,1)} %get-tuple-element.66.mixed, f32[1,4,1024]{2,1,0:T(4,128)} %get-tuple-element.80.log_sum, bf16[1152,864]{1,0:T(8,128)(2,1)} %bitcast.10.refs_6_.qkv, ...), custom_call_target="tpu_custom_call" | custom-call | tf_op jit(solution)/shard_map/attend_grad/pallas_call | solution.py:207
  354.3 2.5 slice_bitcast_fusion.4
  357.3 8.9 %fusion.11 = bf16[1152,864]{0,1:T(8,128)(2,1)} fusion(bf16[1024,864]{1,0:T(8,128)(2,1)} %bitcast.329, bf16[1024,864]{1,0:T(8,128)(2,1)} %bitcast.328, bf16[1024,1152]{1,0:T(8,128)(2,1)} %bitcast.327, bf16[1024,1152]{1,0:T(8,128)(2,1)S(1)} %bitcast.326), kind=kOutput, calls=%fused_computation.16 | convolution fusion | flops 4094373888 | bytes 10248192 | tf_op jit(solution)/shard_map/dot_general | solution.py:35
  366.3 4.1 copy.101
  370.3 7.0 %pack_last.1.refs_16_ = bf16[8,144,1440]{2,1,0:T(8,128)(2,1)} custom-call(f32[8,72,1152]{2,1,0:T(8,128)} %convert_add_fusion.refs_7_.proj_terms, bf16[8,144,864]{2,1,0:T(8,128)(2,1)} %bitcast.290, bf16[288,1152]{1,0:T(8,128)(2,1)} %bitcast.301), custom_call_target="tpu_custom_call" | custom-call | tf_op jit(solution)/shard_map/pack_last/pallas_call | solution.py:450
  377.4 3.1 fusion.30
  383.4 13.1 %collective-permute-done.46.refs_3_ = bf16[1,256,1152]{2,1,0:T(8,128)(2,1)} collective-permute-done((bf16[1,256,1152]{2,1,0:T(8,128)(2,1)}, bf16[1,256,1152]{2,1,0:T(8,128)(2,1)}, u32[]{:S(2)}, u32[]{:S(2)}) %collective-permute-start.46) | collective-permute-done | bytes 589856 | tf_op jit(solution)/shard_map/ppermute | solution.py:23
  396.6 11.8 %token_grad.1 = (bf16[2,256,1152]{2,1,0:T(8,128)(2,1)}, f32[2,256,1152]{2,1,0:T(8,128)}, f32[2,1,1152]{2,1,0:T(1,128)}, f32[2,1,1152]{2,1,0:T(1,128)}, f32[2,1,1152]{2,1,0:T(1,128)}) custom-call(f32[1,256,1152]{2,1,0:T(8,128)} %get-tuple-element.191.refs_0_, f32[1,256,1152]{2,1,0:T(8,128)} %get-tuple-element.187.refs_1_, ...), custom_call_target="tpu_custom_call" | custom-call | tf_op jit(solution)/shard_map/token_grad/pallas_call | solution.py:499
  414.9 2.1 collective-permute-done.52
  418.7 19.0 %all-to-all-start.2 = ((bf16[8,2,6912]{2,1,0:T(2,128)(2,1)}), bf16[8,2,6912]{2,1,0:T(2,128)(2,1)S(1)}, u32[]{:S(2)}, u32[]{:S(2)}) async-start(bf16[8,2,6912]{2,1,0:T(2,128)(2,1)} %broadcast_in_dim.107), calls=%async_computation.3 | async-start | bytes 442368 | tf_op jit(solution)/shard_map/all_to_all | solution.py:92
  438.9 6.8 %all-to-all-done.2 = bf16[8,2,6912]{2,1,0:T(2,128)(2,1)S(1)} async-done(((bf16[8,2,6912]{2,1,0:T(2,128)(2,1)}), bf16[8,2,6912]{2,1,0:T(2,128)(2,1)S(1)}, u32[]{:S(2)}, u32[]{:S(2)}) %all-to-all-start.2) | async-done | bytes 221216 | tf_op jit(solution)/shard_map/all_to_all | solution.py:92
  445.7 3.5 all-to-all-start.5
  452.7 9.1 %all-to-all-done.5 = bf16[4,288,288]{2,1,0:T(8,128)(2,1)S(1)} async-done(((bf16[4,288,288]{2,1,0:T(8,128)(2,1)}), bf16[4,288,288]{2,1,0:T(8,128)(2,1)S(1)}, u32[]{:S(2)}, u32[]{:S(2)}) %all-to-all-start.5) | async-done | bytes 663584 | tf_op jit(solution)/shard_map/all_to_all | solution.py:765
  461.8 3.3 all-to-all-start.3
  466.5 2.4 copy.110
  470.9 2.0 copy.137
  480.5 3.5 all-to-all-start.4
  484.6 8.9 %all-to-all-done.4 = bf16[4,216,288]{1,2,0:T(8,128)(2,1)S(1)} async-done(((bf16[4,216,288]{1,2,0:T(8,128)(2,1)}), bf16[4,216,288]{1,2,0:T(8,128)(2,1)S(1)}, u32[]{:S(2)}, u32[]{:S(2)}) %all-to-all-start.4) | async-done | bytes 497696 | tf_op jit(solution)/shard_map/all_to_all | solution.py:789
  494.6 2.1 place_last.1
  (311 shorter events, 101.2 us)
Async XLA Ops:
  7.2 27.7 %copy-start = (bf16[144,6912]{1,0:T(8,128)(2,1)S(1)}, bf16[144,6912]{1,0:T(8,128)(2,1)}, u32[]{:S(2)}) copy-start(bf16[144,6912]{1,0:T(8,128)(2,1)} %param.12) | copy-start | bytes 5971972
  7.2 69.6 %all-gather.5.cloned.1.call-start = ((), (), s32[]{:S(2)}) async-start(), calls=%async_computation.10 | async-start | bytes 1492992 | tf_op jit(solution)/shard_map/all_gather | solution.py:599
  9.0 158.7 %all-gather.7.cloned.1.call-start = ((), (), s32[]{:S(2)}) async-start(), calls=%async_computation.11 | async-start | bytes 5971968 | tf_op jit(solution)/shard_map/all_gather | solution.py:601
  12.8 58.4 %collective-permute-start.1 = (bf16[2,256,1152]{2,1,0:T(8,128)(2,1)}, bf16[2,256,1152]{2,1,0:T(8,128)(2,1)}, u32[]{:S(2)}, u32[]{:S(2)}) collective-permute-start(bf16[2,256,1152]{2,1,0:T(8,128)(2,1)} %refs_12_.1), channel_id=1, source_target_pairs={{0,2},{1,3},{2,0},{3,1},{4,6},{5,7},{6,4},{7,5},{8,10},{9,11},{10,... | collective-permute-start | bytes 3538952 | tf_op jit(solution)/shard_map/ppermute | solution.py:23
  15.9 67.8 %collective-permute-start = (bf16[2,256,1152]{2,1,0:T(8,128)(2,1)}, bf16[2,256,1152]{2,1,0:T(8,128)(2,1)}, u32[]{:S(2)}, u32[]{:S(2)}) collective-permute-start(bf16[2,256,1152]{2,1,0:T(8,128)(2,1)} %refs_12_.1), channel_id=1, source_target_pairs={{0,1},{1,0},{2,3},{3,2},{4,5},{5,4},{6,7},{7,6},{8,9},{9,8},{10,11... | collective-permute-start | bytes 3538952 | tf_op jit(solution)/shard_map/ppermute | solution.py:23
  18.9 15.3 %all-to-all-start = ((bf16[8,2,1224]{2,1,0:T(2,128)(2,1)}), bf16[8,2,1224]{2,1,0:T(2,128)(2,1)S(1)}, u32[]{:S(2)}, u32[]{:S(2)}) async-start(bf16[8,2,1224]{2,1,0:T(2,128)(2,1)} %reshape.526), calls=%async_computation | async-start | bytes 81920 | tf_op jit(solution)/shard_map/all_to_all | solution.py:92
  28.3 24.9 %collective-permute-start.6 = (bf16[144,864]{1,0:T(8,128)(2,1)}, bf16[144,864]{1,0:T(8,128)(2,1)S(1)}, u32[]{:S(2)}, u32[]{:S(2)}) collective-permute-start(bf16[144,864]{1,0:T(8,128)(2,1)} %get-tuple-element.169), channel_id=1, source_target_pairs={{0,16},{4,20},{8,24},{12,28},{16,0},{20,4},{24,8},{28,12},{1,17},{... | collective-permute-start | bytes 746504 | tf_op jit(solution)/shard_map/ppermute | solution.py:23
  31.2 13.3 %collective-permute-start.4 = (bf16[144,864]{1,0:T(8,128)(2,1)}, bf16[144,864]{1,0:T(8,128)(2,1)}, u32[]{:S(2)}, u32[]{:S(2)}) collective-permute-start(bf16[144,864]{1,0:T(8,128)(2,1)} %get-tuple-element.169), channel_id=1, source_target_pairs={{0,8},{4,12},{8,0},{12,4},{16,24},{20,28},{24,16},{28,20},{1,9},{5... | collective-permute-start | bytes 746504 | tf_op jit(solution)/shard_map/ppermute | solution.py:23
  32.7 15.6 %collective-permute-start.3 = (bf16[144,864]{1,0:T(8,128)(2,1)}, bf16[144,864]{1,0:T(8,128)(2,1)}, u32[]{:S(2)}, u32[]{:S(2)}) collective-permute-start(bf16[144,864]{1,0:T(8,128)(2,1)} %get-tuple-element.169), channel_id=1, source_target_pairs={{0,4},{4,0},{8,12},{12,8},{16,20},{20,16},{24,28},{28,24},{1,5},{5... | collective-permute-start | bytes 746504 | tf_op jit(solution)/shard_map/ppermute | solution.py:23
  39.8 41.9 %all-to-all-start.1 = ((f32[8,2,6912]{2,1,0:T(2,128)}), f32[8,2,6912]{2,1,0:T(2,128)}, u32[]{:S(2)}, u32[]{:S(2)}) async-start(f32[8,2,6912]{2,1,0:T(2,128)} %reshape.455), calls=%async_computation.1 | async-start | bytes 884736 | tf_op jit(solution)/shard_map/all_to_all | solution.py:92
  44.0 326.4 %reduce-scatter.3.cloned.1.call-start = ((), (), s32[]{:S(2)}) async-start(), calls=%async_computation.8 | async-start | bytes 5971968 | tf_op jit(solution)/shard_map/reduce_scatter | solution.py:669
  44.5 22.9 %collective-permute-start.8 = (bf16[144,864]{1,0:T(8,128)(2,1)}, bf16[144,864]{1,0:T(8,128)(2,1)}, u32[]{:S(2)}, u32[]{:S(2)}) collective-permute-start(bf16[144,864]{1,0:T(8,128)(2,1)} %get-tuple-element.169), channel_id=1, source_target_pairs={{0,24},{4,28},{8,16},{12,20},{16,8},{20,12},{24,0},{28,4},{1,25},{... | collective-permute-start | bytes 746504 | tf_op jit(solution)/shard_map/ppermute | solution.py:23
  48.3 22.9 %collective-permute-start.5 = (bf16[144,864]{1,0:T(8,128)(2,1)}, bf16[144,864]{1,0:T(8,128)(2,1)S(1)}, u32[]{:S(2)}, u32[]{:S(2)}) collective-permute-start(bf16[144,864]{1,0:T(8,128)(2,1)} %collective-permute-done.4), channel_id=1, source_target_pairs={{0,4},{4,0},{8,12},{12,8},{16,20},{20,16},{24,28},{28,24},{1,5},{5... | collective-permute-start | bytes 746504 | tf_op jit(solution)/shard_map/ppermute | solution.py:23
  53.1 59.5 %collective-permute-start.18 = (bf16[2,256,1152]{2,1,0:T(8,128)(2,1)S(1)}, bf16[2,256,1152]{2,1,0:T(8,128)(2,1)}, u32[]{:S(2)}, u32[]{:S(2)}) collective-permute-start(bf16[2,256,1152]{2,1,0:T(8,128)(2,1)S(1)} %copy-done.2), channel_id=1, source_target_pairs={{0,2},{1,3},{2,0},{3,1},{4,6},{5,7},{6,4},{7,5},{8,10},{9,11},{10,... | collective-permute-start | bytes 3538952 | tf_op jit(solution)/shard_map/ppermute | solution.py:23
  67.5 9.3 %collective-permute-start.7 = (bf16[144,864]{1,0:T(8,128)(2,1)S(1)}, bf16[144,864]{1,0:T(8,128)(2,1)}, u32[]{:S(2)}, u32[]{:S(2)}) collective-permute-start(bf16[144,864]{1,0:T(8,128)(2,1)S(1)} %collective-permute-done.6), channel_id=1, source_target_pairs={{0,4},{4,0},{8,12},{12,8},{16,20},{20,16},{24,28},{28,24},{1,5},{5... | collective-permute-start | bytes 746504 | tf_op jit(solution)/shard_map/ppermute | solution.py:23
  71.2 8.9 %collective-permute-start.9 = (bf16[144,864]{1,0:T(8,128)(2,1)}, bf16[144,864]{1,0:T(8,128)(2,1)}, u32[]{:S(2)}, u32[]{:S(2)}) collective-permute-start(bf16[144,864]{1,0:T(8,128)(2,1)} %collective-permute-done.8), channel_id=1, source_target_pairs={{0,4},{4,0},{8,12},{12,8},{16,20},{20,16},{24,28},{28,24},{1,5},{5... | collective-permute-start | bytes 746504 | tf_op jit(solution)/shard_map/ppermute | solution.py:23
  71.2 12.4 %collective-permute-start.2 = (bf16[2,256,1152]{2,1,0:T(8,128)(2,1)}, bf16[2,256,1152]{2,1,0:T(8,128)(2,1)}, u32[]{:S(2)}, u32[]{:S(2)}) collective-permute-start(bf16[2,256,1152]{2,1,0:T(8,128)(2,1)} %collective-permute-done.1.refs_2_), channel_id=1, source_target_pairs={{0,1},{1,0},{2,3},{3,2},{4,5},{5,4},{6,7},{7,6},{8,9},{9,8},{10,11... | collective-permute-start | bytes 3538952 | tf_op jit(solution)/shard_map/ppermute | solution.py:23
  76.7 39.7 %collective-permute-start.13 = (bf16[8,72,1152]{2,1,0:T(8,128)(2,1)}, bf16[8,72,1152]{2,1,0:T(8,128)(2,1)}, u32[]{:S(2)}, u32[]{:S(2)}) collective-permute-start(bf16[8,72,1152]{2,1,0:T(8,128)(2,1)} %bitcast.309), channel_id=1, source_target_pairs={{0,1},{1,0},{2,3},{3,2},{4,5},{5,4},{6,7},{7,6},{8,9},{9,8},{10,11... | collective-permute-start | bytes 3981320 | tf_op jit(solution)/shard_map/ppermute | solution.py:23
  102.6 10.6 %collective-permute-start.12 = (bf16[1,256,288]{2,1,0:T(8,128)(2,1)}, bf16[1,256,288]{2,1,0:T(8,128)(2,1)}, u32[]{:S(2)}, u32[]{:S(2)}) collective-permute-start(bf16[1,256,288]{2,1,0:T(8,128)(2,1)} %get-tuple-element.215), channel_id=1, source_target_pairs={{0,3},{1,2},{2,1},{3,0},{4,7},{5,6},{6,5},{7,4},{8,11},{9,10},{10,... | collective-permute-start | bytes 442376 | tf_op jit(solution)/shard_map/ppermute | solution.py:23
  102.6 11.7 %collective-permute-start.11 = (bf16[1,256,288]{2,1,0:T(8,128)(2,1)}, bf16[1,256,288]{2,1,0:T(8,128)(2,1)}, u32[]{:S(2)}, u32[]{:S(2)}) collective-permute-start(bf16[1,256,288]{2,1,0:T(8,128)(2,1)} %get-tuple-element.216), channel_id=1, source_target_pairs={{0,2},{1,3},{2,0},{3,1},{4,6},{5,7},{6,4},{7,5},{8,10},{9,11},{10,... | collective-permute-start | bytes 442376 | tf_op jit(solution)/shard_map/ppermute | solution.py:23
  104.7 9.7 %collective-permute-start.10 = (bf16[1,256,288]{2,1,0:T(8,128)(2,1)}, bf16[1,256,288]{2,1,0:T(8,128)(2,1)}, u32[]{:S(2)}, u32[]{:S(2)}) collective-permute-start(bf16[1,256,288]{2,1,0:T(8,128)(2,1)} %get-tuple-element.217), channel_id=1, source_target_pairs={{0,1},{1,0},{2,3},{3,2},{4,5},{5,4},{6,7},{7,6},{8,9},{9,8},{10,11... | collective-permute-start | bytes 442376 | tf_op jit(solution)/shard_map/ppermute | solution.py:23
  112.7 54.8 %collective-permute-start.17 = (bf16[2,256,1152]{2,1,0:T(8,128)(2,1)S(1)}, bf16[2,256,1152]{2,1,0:T(8,128)(2,1)}, u32[]{:S(2)}, u32[]{:S(2)}) collective-permute-start(bf16[2,256,1152]{2,1,0:T(8,128)(2,1)S(1)} %copy-done.2), channel_id=1, source_target_pairs={{0,1},{1,0},{2,3},{3,2},{4,5},{5,4},{6,7},{7,6},{8,9},{9,8},{10,11... | collective-permute-start | bytes 3538952 | tf_op jit(solution)/shard_map/ppermute | solution.py:23
  113.2 17.4 %collective-permute-start.19 = (bf16[2,256,1152]{2,1,0:T(8,128)(2,1)}, bf16[2,256,1152]{2,1,0:T(8,128)(2,1)}, u32[]{:S(2)}, u32[]{:S(2)}) collective-permute-start(bf16[2,256,1152]{2,1,0:T(8,128)(2,1)} %collective-permute-done.18.refs_6_), channel_id=1, source_target_pairs={{0,1},{1,0},{2,3},{3,2},{4,5},{5,4},{6,7},{7,6},{8,9},{9,8},{10,11... | collective-permute-start | bytes 3538952 | tf_op jit(solution)/shard_map/ppermute | solution.py:23
  141.4 7.5 %collective-permute-start.25 = (bf16[1,256,288]{2,1,0:T(8,128)(2,1)}, bf16[1,256,288]{2,1,0:T(8,128)(2,1)}, u32[]{:S(2)}, u32[]{:S(2)}) collective-permute-start(bf16[1,256,288]{2,1,0:T(8,128)(2,1)} %get-tuple-element.211), channel_id=1, source_target_pairs={{0,3},{1,2},{2,1},{3,0},{4,7},{5,6},{6,5},{7,4},{8,11},{9,10},{10,... | collective-permute-start | bytes 442376 | tf_op jit(solution)/shard_map/ppermute | solution.py:23
  141.5 11.2 %collective-permute-start.24 = (bf16[1,256,288]{2,1,0:T(8,128)(2,1)}, bf16[1,256,288]{2,1,0:T(8,128)(2,1)}, u32[]{:S(2)}, u32[]{:S(2)}) collective-permute-start(bf16[1,256,288]{2,1,0:T(8,128)(2,1)} %get-tuple-element.212), channel_id=1, source_target_pairs={{0,2},{1,3},{2,0},{3,1},{4,6},{5,7},{6,4},{7,5},{8,10},{9,11},{10,... | collective-permute-start | bytes 442376 | tf_op jit(solution)/shard_map/ppermute | solution.py:23
  142.7 10.0 %collective-permute-start.23 = (bf16[1,256,288]{2,1,0:T(8,128)(2,1)}, bf16[1,256,288]{2,1,0:T(8,128)(2,1)}, u32[]{:S(2)}, u32[]{:S(2)}) collective-permute-start(bf16[1,256,288]{2,1,0:T(8,128)(2,1)} %get-tuple-element.213), channel_id=1, source_target_pairs={{0,1},{1,0},{2,3},{3,2},{4,5},{5,4},{6,7},{7,6},{8,9},{9,8},{10,11... | collective-permute-start | bytes 442376 | tf_op jit(solution)/shard_map/ppermute | solution.py:23
  144.0 21.3 %collective-permute-start.15 = (bf16[1,256,1152]{2,1,0:T(8,128)(2,1)}, bf16[1,256,1152]{2,1,0:T(8,128)(2,1)}, u32[]{:S(2)}, u32[]{:S(2)}) collective-permute-start(bf16[1,256,1152]{2,1,0:T(8,128)(2,1)} %add_convert_fusion.1.refs_0_), channel_id=1, source_target_pairs={{0,2},{1,3},{2,0},{3,1},{4,6},{5,7},{6,4},{7,5},{8,10},{9,11},{10,... | collective-permute-start | bytes 1769480 | tf_op jit(solution)/shard_map/ppermute | solution.py:23
  149.0 18.5 %collective-permute-start.14 = (bf16[1,256,1152]{2,1,0:T(8,128)(2,1)}, bf16[1,256,1152]{2,1,0:T(8,128)(2,1)}, u32[]{:S(2)}, u32[]{:S(2)}) collective-permute-start(bf16[1,256,1152]{2,1,0:T(8,128)(2,1)} %add_convert_fusion.1.refs_0_), channel_id=1, source_target_pairs={{0,1},{1,0},{2,3},{3,2},{4,5},{5,4},{6,7},{7,6},{8,9},{9,8},{10,11... | collective-permute-start | bytes 1769480 | tf_op jit(solution)/shard_map/ppermute | solution.py:23
  165.3 2.3 collective-permute-start.16
  166.6 20.3 %collective-permute-start.27 = (bf16[1,256,1152]{2,1,0:T(8,128)(2,1)}, bf16[1,256,1152]{2,1,0:T(8,128)(2,1)}, u32[]{:S(2)}, u32[]{:S(2)}) collective-permute-start(bf16[1,256,1152]{2,1,0:T(8,128)(2,1)} %add_convert_fusion.refs_0_), channel_id=1, source_target_pairs={{0,2},{1,3},{2,0},{3,1},{4,6},{5,7},{6,4},{7,5},{8,10},{9,11},{10,... | collective-permute-start | bytes 1769480 | tf_op jit(solution)/shard_map/ppermute | solution.py:23
  186.3 2.0 collective-permute-start.21
  186.5 3.9 collective-permute-start.26
  186.9 3.5 collective-permute-start.28
  210.7 18.9 %collective-permute-start.29 = (bf16[1,256,1152]{2,1,0:T(8,128)(2,1)S(1)}, bf16[1,256,1152]{2,1,0:T(8,128)(2,1)S(1)}, u32[]{:S(2)}, u32[]{:S(2)}) collective-permute-start(bf16[1,256,1152]{2,1,0:T(8,128)(2,1)S(1)} %get-tuple-element.195), channel_id=1, source_target_pairs={{0,1},{1,0},{2,3},{3,2},{4,5},{5,4},{6,7},{7,6},{8,9},{9,8},{10,11... | collective-permute-start | bytes 1769480 | tf_op jit(solution)/shard_map/ppermute | solution.py:23
  238.8 236.9 %reduce-scatter.5.cloned.1.call-start = ((), (), s32[]{:S(2)}) async-start(), calls=%async_computation.9 | async-start | bytes 3981312 | tf_op jit(solution)/shard_map/reduce_scatter | solution.py:722
  238.8 3.1 collective-permute-start.20
  239.8 16.3 %collective-permute-start.22 = (bf16[1,256,1152]{2,1,0:T(8,128)(2,1)S(1)}, bf16[1,256,1152]{2,1,0:T(8,128)(2,1)}, u32[]{:S(2)}, u32[]{:S(2)}) collective-permute-start(bf16[1,256,1152]{2,1,0:T(8,128)(2,1)S(1)} %copy-done.10), channel_id=1, source_target_pairs={{0,2},{1,3},{2,0},{3,1},{4,6},{5,7},{6,4},{7,5},{8,10},{9,11},{10,... | collective-permute-start | bytes 1769480 | tf_op jit(solution)/shard_map/ppermute | solution.py:23
  240.8 26.9 %collective-permute-start.33 = (bf16[1,256,1152]{2,1,0:T(8,128)(2,1)}, bf16[1,256,1152]{2,1,0:T(8,128)(2,1)}, u32[]{:S(2)}, u32[]{:S(2)}) collective-permute-start(bf16[1,256,1152]{2,1,0:T(8,128)(2,1)} %get-tuple-element.194), channel_id=1, source_target_pairs={{0,1},{1,0},{2,3},{3,2},{4,5},{5,4},{6,7},{7,6},{8,9},{9,8},{10,11... | collective-permute-start | bytes 1769480 | tf_op jit(solution)/shard_map/ppermute | solution.py:23
  240.9 27.2 %collective-permute-start.34 = (bf16[1,256,1152]{2,1,0:T(8,128)(2,1)S(1)}, bf16[1,256,1152]{2,1,0:T(8,128)(2,1)}, u32[]{:S(2)}, u32[]{:S(2)}) collective-permute-start(bf16[1,256,1152]{2,1,0:T(8,128)(2,1)S(1)} %copy-done.11), channel_id=1, source_target_pairs={{0,2},{1,3},{2,0},{3,1},{4,6},{5,7},{6,4},{7,5},{8,10},{9,11},{10,... | collective-permute-start | bytes 1769480 | tf_op jit(solution)/shard_map/ppermute | solution.py:23
  265.8 27.2 %collective-permute-start.30 = (bf16[1,256,288]{2,1,0:T(8,128)(2,1)}, bf16[1,256,288]{2,1,0:T(8,128)(2,1)S(1)}, u32[]{:S(2)}, u32[]{:S(2)}) collective-permute-start(bf16[1,256,288]{2,1,0:T(8,128)(2,1)} %get-tuple-element.75), channel_id=1, source_target_pairs={{0,1},{1,0},{2,3},{3,2},{4,5},{5,4},{6,7},{7,6},{8,9},{9,8},{10,11... | collective-permute-start | bytes 442376 | tf_op jit(solution)/shard_map/ppermute | solution.py:23
  265.9 27.1 %collective-permute-start.31 = (bf16[1,256,288]{2,1,0:T(8,128)(2,1)}, bf16[1,256,288]{2,1,0:T(8,128)(2,1)S(1)}, u32[]{:S(2)}, u32[]{:S(2)}) collective-permute-start(bf16[1,256,288]{2,1,0:T(8,128)(2,1)} %get-tuple-element.76), channel_id=1, source_target_pairs={{0,2},{1,3},{2,0},{3,1},{4,6},{5,7},{6,4},{7,5},{8,10},{9,11},{10,... | collective-permute-start | bytes 442376 | tf_op jit(solution)/shard_map/ppermute | solution.py:23
  266.9 26.1 %collective-permute-start.32 = (bf16[1,256,288]{2,1,0:T(8,128)(2,1)}, bf16[1,256,288]{2,1,0:T(8,128)(2,1)S(1)}, u32[]{:S(2)}, u32[]{:S(2)}) collective-permute-start(bf16[1,256,288]{2,1,0:T(8,128)(2,1)} %get-tuple-element.77), channel_id=1, source_target_pairs={{0,3},{1,2},{2,1},{3,0},{4,7},{5,6},{6,5},{7,4},{8,11},{9,10},{10,... | collective-permute-start | bytes 442376 | tf_op jit(solution)/shard_map/ppermute | solution.py:23
  292.1 42.4 %collective-permute-start.36 = (bf16[1,256,288]{2,1,0:T(8,128)(2,1)}, bf16[1,256,288]{2,1,0:T(8,128)(2,1)S(1)}, u32[]{:S(2)}, u32[]{:S(2)}) collective-permute-start(bf16[1,256,288]{2,1,0:T(8,128)(2,1)} %get-tuple-element.81), channel_id=1, source_target_pairs={{0,1},{1,0},{2,3},{3,2},{4,5},{5,4},{6,7},{7,6},{8,9},{9,8},{10,11... | collective-permute-start | bytes 442376 | tf_op jit(solution)/shard_map/ppermute | solution.py:23
  292.1 43.4 %collective-permute-start.37 = (bf16[1,256,288]{2,1,0:T(8,128)(2,1)}, bf16[1,256,288]{2,1,0:T(8,128)(2,1)S(1)}, u32[]{:S(2)}, u32[]{:S(2)}) collective-permute-start(bf16[1,256,288]{2,1,0:T(8,128)(2,1)} %get-tuple-element.82), channel_id=1, source_target_pairs={{0,2},{1,3},{2,0},{3,1},{4,6},{5,7},{6,4},{7,5},{8,10},{9,11},{10,... | collective-permute-start | bytes 442376 | tf_op jit(solution)/shard_map/ppermute | solution.py:23
  313.6 9.8 %collective-permute-start.43 = (bf16[1,256,1152]{2,1,0:T(8,128)(2,1)S(1)}, bf16[1,256,1152]{2,1,0:T(8,128)(2,1)S(1)}, u32[]{:S(2)}, u32[]{:S(2)}) collective-permute-start(bf16[1,256,1152]{2,1,0:T(8,128)(2,1)S(1)} %get-tuple-element.192), channel_id=1, source_target_pairs={{0,1},{1,0},{2,3},{3,2},{4,5},{5,4},{6,7},{7,6},{8,9},{9,8},{10,11... | collective-permute-start | bytes 1769480 | tf_op jit(solution)/shard_map/ppermute | solution.py:23
  313.9 9.9 %collective-permute-start.35 = (bf16[1,256,1152]{2,1,0:T(8,128)(2,1)S(1)}, bf16[1,256,1152]{2,1,0:T(8,128)(2,1)S(1)}, u32[]{:S(2)}, u32[]{:S(2)}) collective-permute-start(bf16[1,256,1152]{2,1,0:T(8,128)(2,1)S(1)} %get-tuple-element.193), channel_id=1, source_target_pairs={{0,1},{1,0},{2,3},{3,2},{4,5},{5,4},{6,7},{7,6},{8,9},{9,8},{10,11... | collective-permute-start | bytes 1769480 | tf_op jit(solution)/shard_map/ppermute | solution.py:23
  314.3 11.2 %collective-permute-start.47 = (bf16[1,256,1152]{2,1,0:T(8,128)(2,1)S(1)}, bf16[1,256,1152]{2,1,0:T(8,128)(2,1)S(1)}, u32[]{:S(2)}, u32[]{:S(2)}) collective-permute-start(bf16[1,256,1152]{2,1,0:T(8,128)(2,1)S(1)} %get-tuple-element.184), channel_id=1, source_target_pairs={{0,1},{1,0},{2,3},{3,2},{4,5},{5,4},{6,7},{7,6},{8,9},{9,8},{10,11... | collective-permute-start | bytes 1769480 | tf_op jit(solution)/shard_map/ppermute | solution.py:23
  323.4 2.4 collective-permute-start.39
  323.8 7.8 %collective-permute-start.41 = (bf16[8,72,1152]{2,1,0:T(8,128)(2,1)S(1)}, bf16[8,72,1152]{2,1,0:T(8,128)(2,1)S(1)}, u32[]{:S(2)}, u32[]{:S(2)}) collective-permute-start(bf16[8,72,1152]{2,1,0:T(8,128)(2,1)S(1)} %dynamic-slice_bitcast_fusion), channel_id=1, source_target_pairs={{0,1},{1,0},{2,3},{3,2},{4,5},{5,4},{6,7},{7,6},{8,9},{9,8},{10,11... | collective-permute-start | bytes 3981320 | tf_op jit(solution)/shard_map/ppermute | solution.py:23
  325.5 2.7 collective-permute-start.48
  325.8 3.5 collective-permute-start.40
  328.2 7.3 %collective-permute-start.38 = (bf16[1,256,288]{2,1,0:T(8,128)(2,1)S(1)}, bf16[1,256,288]{2,1,0:T(8,128)(2,1)S(1)}, u32[]{:S(2)}, u32[]{:S(2)}) collective-permute-start(bf16[1,256,288]{2,1,0:T(8,128)(2,1)S(1)} %copy-done.49), channel_id=1, source_target_pairs={{0,3},{1,2},{2,1},{3,0},{4,7},{5,6},{6,5},{7,4},{8,11},{9,10},{10,... | collective-permute-start | bytes 442376 | tf_op jit(solution)/shard_map/ppermute | solution.py:23
  329.3 54.1 %collective-permute-start.44 = (bf16[1,256,1152]{2,1,0:T(8,128)(2,1)}, bf16[1,256,1152]{2,1,0:T(8,128)(2,1)}, u32[]{:S(2)}, u32[]{:S(2)}) collective-permute-start(bf16[1,256,1152]{2,1,0:T(8,128)(2,1)} %get-tuple-element.190), channel_id=1, source_target_pairs={{0,2},{1,3},{2,0},{3,1},{4,6},{5,7},{6,4},{7,5},{8,10},{9,11},{10,... | collective-permute-start | bytes 1769480 | tf_op jit(solution)/shard_map/ppermute | solution.py:23
  331.5 51.9 %collective-permute-start.49 = (bf16[1,256,1152]{2,1,0:T(8,128)(2,1)S(1)}, bf16[1,256,1152]{2,1,0:T(8,128)(2,1)}, u32[]{:S(2)}, u32[]{:S(2)}) collective-permute-start(bf16[1,256,1152]{2,1,0:T(8,128)(2,1)S(1)} %get-tuple-element.183.refs_5_), channel_id=1, source_target_pairs={{0,2},{1,3},{2,0},{3,1},{4,6},{5,7},{6,4},{7,5},{8,10},{9,11},{10,... | collective-permute-start | bytes 1769480 | tf_op jit(solution)/shard_map/ppermute | solution.py:23
  334.5 48.9 %collective-permute-start.50 = (bf16[1,256,1152]{2,1,0:T(8,128)(2,1)S(1)}, bf16[1,256,1152]{2,1,0:T(8,128)(2,1)}, u32[]{:S(2)}, u32[]{:S(2)}) collective-permute-start(bf16[1,256,1152]{2,1,0:T(8,128)(2,1)S(1)} %get-tuple-element.179.refs_6_), channel_id=1, source_target_pairs={{0,2},{1,3},{2,0},{3,1},{4,6},{5,7},{6,4},{7,5},{8,10},{9,11},{10,... | collective-permute-start | bytes 1769480 | tf_op jit(solution)/shard_map/ppermute | solution.py:23
  356.8 20.6 %collective-permute-start.45 = (bf16[1,256,1152]{2,1,0:T(8,128)(2,1)}, bf16[1,256,1152]{2,1,0:T(8,128)(2,1)}, u32[]{:S(2)}, u32[]{:S(2)}) collective-permute-start(bf16[1,256,1152]{2,1,0:T(8,128)(2,1)} %get-tuple-element.188), channel_id=1, source_target_pairs={{0,1},{1,0},{2,3},{3,2},{4,5},{5,4},{6,7},{7,6},{8,9},{9,8},{10,11... | collective-permute-start | bytes 1769480 | tf_op jit(solution)/shard_map/ppermute | solution.py:23
  357.3 20.1 %collective-permute-start.42 = (bf16[1,256,1152]{2,1,0:T(8,128)(2,1)}, bf16[1,256,1152]{2,1,0:T(8,128)(2,1)}, u32[]{:S(2)}, u32[]{:S(2)}) collective-permute-start(bf16[1,256,1152]{2,1,0:T(8,128)(2,1)} %get-tuple-element.189), channel_id=1, source_target_pairs={{0,1},{1,0},{2,3},{3,2},{4,5},{5,4},{6,7},{7,6},{8,9},{9,8},{10,11... | collective-permute-start | bytes 1769480 | tf_op jit(solution)/shard_map/ppermute | solution.py:23
  380.5 16.0 %collective-permute-start.46 = (bf16[1,256,1152]{2,1,0:T(8,128)(2,1)}, bf16[1,256,1152]{2,1,0:T(8,128)(2,1)}, u32[]{:S(2)}, u32[]{:S(2)}) collective-permute-start(bf16[1,256,1152]{2,1,0:T(8,128)(2,1)} %get-tuple-element.186), channel_id=1, source_target_pairs={{0,2},{1,3},{2,0},{3,1},{4,6},{5,7},{6,4},{7,5},{8,10},{9,11},{10,... | collective-permute-start | bytes 1769480 | tf_op jit(solution)/shard_map/ppermute | solution.py:23
  410.7 1.2 collective-permute-start.51
  412.6 4.5 collective-permute-start.52
  418.7 26.9 %all-to-all-start.2 = ((bf16[8,2,6912]{2,1,0:T(2,128)(2,1)}), bf16[8,2,6912]{2,1,0:T(2,128)(2,1)S(1)}, u32[]{:S(2)}, u32[]{:S(2)}) async-start(bf16[8,2,6912]{2,1,0:T(2,128)(2,1)} %broadcast_in_dim.107), calls=%async_computation.3 | async-start | bytes 442368 | tf_op jit(solution)/shard_map/all_to_all | solution.py:92
  445.7 16.2 %all-to-all-start.5 = ((bf16[4,288,288]{2,1,0:T(8,128)(2,1)}), bf16[4,288,288]{2,1,0:T(8,128)(2,1)S(1)}, u32[]{:S(2)}, u32[]{:S(2)}) async-start(bf16[4,288,288]{2,1,0:T(8,128)(2,1)} %pad_maximum_fusion.2), calls=%async_computation.7 | async-start | bytes 1769472 | tf_op jit(solution)/shard_map/all_to_all | solution.py:765
  461.8 13.0 %all-to-all-start.3 = ((f32[8,1,432]{2,1,0:T(1,128)}), f32[8,1,432]{2,1,0:T(1,128)S(1)}, u32[]{:S(2)}, u32[]{:S(2)}) async-start(f32[8,1,432]{2,1,0:T(1,128)} %all_to_all.30), calls=%async_computation.4 | async-start | bytes 32768 | tf_op jit(solution)/shard_map/all_to_all | solution.py:92
  480.5 13.0 %all-to-all-start.4 = ((bf16[4,216,288]{1,2,0:T(8,128)(2,1)}), bf16[4,216,288]{1,2,0:T(8,128)(2,1)S(1)}, u32[]{:S(2)}, u32[]{:S(2)}) async-start(bf16[4,216,288]{1,2,0:T(8,128)(2,1)} %copy.105), calls=%async_computation.6 | async-start | bytes 1179648 | tf_op jit(solution)/shard_map/all_to_all | solution.py:789
  (49 other events, 284.0 us)
Sparse Core Ops, SparseCore 0:
  10.8 64.1 all-gather.4
  77.8 84.2 all-gather.6
  238.9 118.1 reduce-scatter.2
  377.5 95.7 reduce-scatter.4
